TPU v7x, 32 devices: a whole 2x2x4 slice. The times are simulated.
32 devices in a mesh: dp: 4 (over y, x), mp: 8 (over z, core).
Axes of the slice: x: 2, y: 2, z: 4, core: 2. Of those that a mesh axis runs over, the one named last changes fastest.
Arguments:
- tokens: bfloat16 [16384, 1024], P(('dp', 'mp')), may hold values from -6 to 6
- cotangent: bfloat16 [16384, 1024], P(('dp', 'mp')), may hold values from -6 to 6
- first_gain: float32 [1024], P(('dp', 'mp')), may hold values from 0.5 to 1.5
- second_gain: float32 [1024], P(('dp', 'mp')), may hold values from 0.5 to 1.5
- w_query: float32 [1024, 1024], P(('dp', 'mp')), may hold values from -0.1875 to 0.1875
- w_key: float32 [1024, 1024], P(('dp', 'mp')), may hold values from -0.1875 to 0.1875
- w_value: float32 [1024, 1024], P(('dp', 'mp')), may hold values from -0.1875 to 0.1875
- w_out: float32 [1024, 1024], P(('dp', 'mp')), may hold values from -2 to 2
- w_up: float32 [1024, 4096], P(('dp', 'mp')), may hold values from -0.1875 to 0.1875
- w_down: float32 [4096, 1024], P(None, ('dp', 'mp')), may hold values from -0.09375 to 0.09375
- state_rate: float32 [1024, 16], P('mp', 'dp'), may hold values from 0 to 1, as said below
- state_in: float32 [1024, 16], P('mp', 'dp'), may hold values from -1.25 to 1.25
- state_out: float32 [1024, 16], P('mp', 'dp'), may hold values from -0.3125 to 0.3125
- state_bank: float32 [4, 1024, 16], P('dp', 'mp'), may hold values from -24 to 24
- prev_link: int32 [4], replicated, may hold values from 0 to 3, each once
Outputs:
- mixed: bfloat16 [16384, 1024], P(('dp', 'mp'))
- grad_tokens: bfloat16 [16384, 1024], P(('dp', 'mp'))
- grad_first_gain: float32 [1024], P(('dp', 'mp'))
- grad_second_gain: float32 [1024], P(('dp', 'mp'))
- grad_w_query: float32 [1024, 1024], P(('dp', 'mp'))
- grad_w_key: float32 [1024, 1024], P(('dp', 'mp'))
- grad_w_value: float32 [1024, 1024], P(('dp', 'mp'))
- grad_w_out: float32 [1024, 1024], P(('dp', 'mp'))
- grad_w_up: float32 [1024, 4096], P('dp', 'mp')
- grad_w_down: float32 [4096, 1024], P('mp', 'dp')
- grad_state_rate: float32 [1024, 16], P('mp', 'dp')
- grad_state_in: float32 [1024, 16], P('mp', 'dp')
- grad_state_out: float32 [1024, 16], P('mp', 'dp')
- grad_state_bank: float32 [4, 1024, 16], P('dp', 'mp')
Inputs may be any that keep to these rules, and one draw needn't show every extreme that they name: `state_rate`: rates per channel and state entry, between 0.3 / 4096 and 1 / 30. `prev_link`: every row of state_bank is named once.
All inputs are finite; a program needn't handle non-finite values.
Results may differ from a plain program's by a relative error of at most 0.013.
Values may be sent and summed in bfloat16 or wider, within the bound.
No kernel may reach another device: no remote copies, remote signals or barrier semaphores. Data moves between devices by JAX's collectives and lax.ppermute only.
A program may use at most 256 MiB of HBM per device.

v0:
```python
import jax
import jax.numpy as jnp
from jax import lax
from jax.sharding import PartitionSpec as P

D = 1024
H = 8
HD = 128
LEN = 4096
BLK = 512
CTX = 128
SEG = 128


precise = lax.Precision.HIGHEST


def layer_norm(values, gain):
    center = values - jnp.mean(values, axis=-1, keepdims=True)
    spread = jnp.mean(center * center, axis=-1, keepdims=True)
    return center * lax.rsqrt(spread + 1e-05) * gain


def gelu_exact(values):
    return jax.nn.gelu(values, approximate=False)


def recurrence(inputs, rate, gain_in, gain_out, initial):
    windows = inputs.shape[0]
    channels = inputs.shape[2]
    counts = LEN // SEG
    offsets = jnp.arange(SEG, dtype=jnp.int32)
    powers = jnp.exp(-rate[None, :, :] * offsets.astype(jnp.float32)[:, None, None])
    shifted = powers * jnp.exp(-rate)[None]
    kernel = jnp.einsum("tcn,cn->tc", powers, gain_in * gain_out, precision=precise)
    lag_steps = offsets[:, None] - offsets[None, :]
    selector = (lag_steps[:, :, None] == offsets[None, None, :]).astype(jnp.float32)
    toeplitz = jnp.einsum("tsk,kc->tsc", selector, kernel, precision=precise)
    blocks = inputs.reshape(windows, counts, SEG, channels)
    inside = jnp.einsum("tsc,wksc->wktc", toeplitz, blocks, precision=precise)
    tail_gain = jnp.flip(powers, 0) * gain_in[None]
    pushed = jnp.einsum("scn,wksc->wkcn", tail_gain, blocks, precision=precise)
    jump_decay = jnp.exp(-rate * SEG)

    def advance(state_now, pushed_in):
        return (jump_decay * state_now + pushed_in, state_now)

    _, starts = lax.scan(advance, initial, jnp.moveaxis(pushed, 1, 0))
    starts = jnp.moveaxis(starts, 0, 1)
    reader = shifted * gain_out[None]
    carried = jnp.einsum("tcn,wkcn->wktc", reader, starts, precision=precise)
    return (inside + carried).reshape(windows, LEN, channels)


def context_rows(recur):
    channels = recur.shape[-1]
    block_tails = recur.reshape(-1, BLK, channels)[:, BLK - CTX :, :]
    return jnp.concatenate([jnp.zeros_like(block_tails[:1]), block_tails[:-1]], axis=0)


def forward_dot(left, right):
    return jnp.dot(left, right, preferred_element_type=jnp.float32)


def trans_dot(left, right):
    return lax.dot_general(
        left, right, (((0,), (0,)), ((), ())), preferred_element_type=jnp.float32
    )


def back_dot(left, right):
    return lax.dot_general(
        left, right, (((1,), (1,)), ((), ())), preferred_element_type=jnp.float32
    )


def block_scores(queries, keys_all, opened):
    scores = jnp.einsum(
        "qhd,khd->hqk", queries, keys_all, preferred_element_type=jnp.float32
    ) * HD ** (-0.5)
    row_index = jnp.arange(BLK, dtype=jnp.int32)[:, None]
    col_index = jnp.arange(CTX + BLK, dtype=jnp.int32)[None, :]
    allowed = jnp.where(col_index < CTX, opened, col_index - CTX <= row_index)
    return jnp.where(allowed[None], scores, -jnp.inf)


def attend_forward(packed):
    queries, keys_all, values_all, opened = packed
    scores = block_scores(queries, keys_all, opened)
    peak_score = jnp.max(scores, -1, keepdims=True)
    lifted = jnp.exp(scores - peak_score)
    denominator = jnp.sum(lifted, -1, keepdims=True)
    prob_b = (lifted / denominator).astype(jnp.bfloat16)
    mixed_heads = jnp.einsum("hqk,khd->qhd", prob_b, values_all, preferred_element_type=jnp.float32)
    return (mixed_heads.astype(jnp.bfloat16), (peak_score + jnp.log(denominator))[..., 0])


def attend_backward(packed):
    queries, keys_all, values_all, opened, log_total, grad_mixed = packed
    scale = HD ** (-0.5)
    scores = block_scores(queries, keys_all, opened)
    attn_prob = jnp.exp(scores - log_total[..., None])
    prob_b = attn_prob.astype(jnp.bfloat16)
    grad_prob = jnp.einsum(
        "qhd,khd->hqk", grad_mixed, values_all, preferred_element_type=jnp.float32
    )
    grad_scores = (
        attn_prob * (grad_prob - jnp.sum(attn_prob * grad_prob, -1, keepdims=True))
    ).astype(jnp.bfloat16)
    grad_queries = (
        jnp.einsum("hqk,khd->qhd", grad_scores, keys_all, preferred_element_type=jnp.float32)
        * scale
    ).astype(jnp.bfloat16)
    grad_keys = (
        jnp.einsum("hqk,qhd->khd", grad_scores, queries, preferred_element_type=jnp.float32) * scale
    ).astype(jnp.bfloat16)
    grad_values = jnp.einsum(
        "hqk,qhd->khd", prob_b, grad_mixed, preferred_element_type=jnp.float32
    ).astype(jnp.bfloat16)
    return (grad_queries, grad_keys, grad_values)


def body(
    tokens,
    cotangent,
    first_gain,
    second_gain,
    w_query,
    w_key,
    w_value,
    w_out,
    w_up,
    w_down,
    state_rate,
    state_in,
    state_out,
    state_bank,
    prev_link,
):
    half = jnp.bfloat16
    gain_one, query_w, key_w, value_w, out_w = (
        lax.all_gather(first_gain.astype(half), ("dp", "mp"), axis=0, tiled=True),
        lax.all_gather(w_query.astype(half), ("dp", "mp"), axis=0, tiled=True),
        lax.all_gather(w_key.astype(half), ("dp", "mp"), axis=0, tiled=True),
        lax.all_gather(w_value.astype(half), ("dp", "mp"), axis=0, tiled=True),
        lax.all_gather(w_out.astype(half), ("dp", "mp"), axis=0, tiled=True),
    )
    rate_all, in_all, out_all, bank_all = (
        lax.all_gather(state_rate, "dp", axis=1, tiled=True),
        lax.all_gather(state_in, "dp", axis=1, tiled=True),
        lax.all_gather(state_out, "dp", axis=1, tiled=True),
        lax.all_gather(state_bank, "dp", axis=0, tiled=True),
    )
    dp_index = lax.axis_index("dp")
    mp_index = lax.axis_index("mp")
    tok_rows = tokens.shape[0]
    group_rows = tok_rows * lax.axis_size("mp")
    window_count = group_rows // LEN
    block_count = tok_rows // BLK
    own_links = lax.dynamic_slice_in_dim(prev_link, dp_index * window_count, window_count)
    selector = (
        own_links[:, None] == jnp.arange(prev_link.shape[0], dtype=jnp.int32)[None, :]
    ).astype(jnp.float32)
    initial = jnp.einsum("wv,vcn->wcn", selector, bank_all, precision=precise)
    token_f = tokens.astype(jnp.float32)
    normed, norm_pull = jax.vjp(layer_norm, token_f, gain_one.astype(jnp.float32))
    normed_b = normed.astype(half)
    channel_in = lax.all_to_all(normed_b, "mp", split_axis=1, concat_axis=0, tiled=True)
    channels = channel_in.shape[1]

    def local_state(values, rate, gain_in, gain_out, begin_state):
        recur = recurrence(
            values.reshape(window_count, LEN, channels), rate, gain_in, gain_out, begin_state
        )
        return context_rows(recur).reshape(-1, channels)

    context_ch, state_pull = jax.vjp(
        local_state, channel_in.astype(jnp.float32), rate_all, in_all, out_all, initial
    )

    def split_heads(values, rows):
        return values.reshape(block_count, rows, H, HD)

    queries = split_heads(forward_dot(normed_b, query_w).astype(half), BLK)
    self_keys = forward_dot(normed_b, key_w).astype(half)
    self_values = forward_dot(normed_b, value_w).astype(half)
    context = lax.all_to_all(context_ch.astype(half), "mp", split_axis=0, concat_axis=1, tiled=True)
    ctx_keys = forward_dot(context, key_w).astype(half)
    ctx_values = forward_dot(context, value_w).astype(half)
    keys_all = jnp.concatenate([split_heads(ctx_keys, CTX), split_heads(self_keys, BLK)], 1)
    values_all = jnp.concatenate([split_heads(ctx_values, CTX), split_heads(self_values, BLK)], 1)
    row_first = (dp_index * lax.axis_size("mp") + mp_index) * tok_rows
    opened = (row_first + jnp.arange(block_count, dtype=jnp.int32) * BLK) % LEN != 0
    mixed_heads, log_total = lax.map(attend_forward, (queries, keys_all, values_all, opened))
    attended = mixed_heads.reshape(tok_rows, D)
    middle = token_f + forward_dot(attended, out_w)
    gain_two, up_w, down_w = (
        lax.all_gather(second_gain.astype(half), ("dp", "mp"), axis=0, tiled=True),
        lax.all_gather(w_up.astype(half), ("dp", "mp"), axis=0, tiled=True),
        lax.all_gather(w_down.astype(half), ("dp", "mp"), axis=1, tiled=True),
    )
    second, second_pull = jax.vjp(layer_norm, middle, gain_two.astype(jnp.float32))
    second_b = second.astype(half)
    hidden = forward_dot(second_b, up_w)
    active, gelu_pull = jax.vjp(gelu_exact, hidden)
    active_b = active.astype(half)
    mixed = (middle + forward_dot(active_b, down_w)).astype(half)
    grad_active = back_dot(cotangent, down_w)
    grad_hidden = gelu_pull(grad_active)[0].astype(half)
    grad_second = back_dot(grad_hidden, up_w)
    grad_middle_norm, grad_gain_two = second_pull(grad_second)
    grad_middle = cotangent.astype(jnp.float32) + grad_middle_norm
    hidden_cols, active_cols = (
        lax.all_to_all(grad_hidden, "mp", split_axis=1, concat_axis=0, tiled=True),
        lax.all_to_all(active_b, "mp", split_axis=1, concat_axis=0, tiled=True),
    )
    second_piece = lax.all_gather(second_b, "mp", axis=0, tiled=True)
    cot_piece = lax.all_gather(cotangent, "mp", axis=0, tiled=True)
    up_part = trans_dot(second_piece, hidden_cols)
    down_part = trans_dot(active_cols, cot_piece)
    grad_up, grad_down = (
        lax.psum_scatter(
            up_part.astype(jnp.bfloat16), "dp", scatter_dimension=0, tiled=True
        ).astype(jnp.float32),
        lax.psum_scatter(
            down_part.astype(jnp.bfloat16), "dp", scatter_dimension=1, tiled=True
        ).astype(jnp.float32),
    )
    grad_branch = grad_middle.astype(half)
    grad_attended = back_dot(grad_branch, out_w).astype(half)
    grad_queries, grad_keys_all, grad_values_all = lax.map(
        attend_backward,
        (queries, keys_all, values_all, opened, log_total, split_heads(grad_attended, BLK)),
    )
    grad_queries = grad_queries.reshape(tok_rows, D)
    grad_ctx_keys = grad_keys_all[:, :CTX].reshape(block_count * CTX, D)
    grad_self_keys = grad_keys_all[:, CTX:].reshape(tok_rows, D)
    grad_ctx_values = grad_values_all[:, :CTX].reshape(block_count * CTX, D)
    grad_self_values = grad_values_all[:, CTX:].reshape(tok_rows, D)
    grad_context = (back_dot(grad_ctx_keys, key_w) + back_dot(grad_ctx_values, value_w)).astype(
        half
    )
    back_channels = lax.all_to_all(grad_context, "mp", split_axis=1, concat_axis=0, tiled=True)
    grad_inputs, grad_rate, grad_in, grad_out_map, grad_initial = state_pull(
        back_channels.astype(jnp.float32)
    )
    grad_bank = jnp.einsum("wv,wcn->vcn", selector, grad_initial, precision=precise)
    state_shares = (
        lax.psum_scatter(
            grad_rate.astype(jnp.bfloat16), "dp", scatter_dimension=1, tiled=True
        ).astype(jnp.float32),
        lax.psum_scatter(
            grad_in.astype(jnp.bfloat16), "dp", scatter_dimension=1, tiled=True
        ).astype(jnp.float32),
        lax.psum_scatter(
            grad_out_map.astype(jnp.bfloat16), "dp", scatter_dimension=1, tiled=True
        ).astype(jnp.float32),
        lax.psum_scatter(
            grad_bank.astype(jnp.bfloat16), "dp", scatter_dimension=0, tiled=True
        ).astype(jnp.float32),
    )
    grad_sent = lax.all_to_all(
        grad_inputs.astype(half), "mp", split_axis=0, concat_axis=1, tiled=True
    )
    grad_normed = (
        back_dot(grad_queries, query_w)
        + back_dot(grad_self_keys, key_w)
        + back_dot(grad_self_values, value_w)
        + grad_sent.astype(jnp.float32)
    )
    grad_token_norm, grad_gain_one = norm_pull(grad_normed)
    grad_tokens = (grad_middle + grad_token_norm).astype(half)
    grad_out_w = trans_dot(attended, grad_branch)
    grad_query_w = trans_dot(normed_b, grad_queries)
    grad_key_w = trans_dot(normed_b, grad_self_keys) + trans_dot(context, grad_ctx_keys)
    grad_value_w = trans_dot(normed_b, grad_self_values) + trans_dot(context, grad_ctx_values)
    attn_shares = (
        lax.psum_scatter(grad_gain_one, ("dp", "mp"), scatter_dimension=0, tiled=True),
        lax.psum_scatter(grad_gain_two, ("dp", "mp"), scatter_dimension=0, tiled=True),
        lax.psum_scatter(grad_query_w, ("dp", "mp"), scatter_dimension=0, tiled=True),
        lax.psum_scatter(grad_key_w, ("dp", "mp"), scatter_dimension=0, tiled=True),
        lax.psum_scatter(grad_value_w, ("dp", "mp"), scatter_dimension=0, tiled=True),
        lax.psum_scatter(grad_out_w, ("dp", "mp"), scatter_dimension=0, tiled=True),
    )
    share_one, share_two = (attn_shares[0], attn_shares[1])
    mat_query, mat_key, mat_value, mat_out = (
        attn_shares[2],
        attn_shares[3],
        attn_shares[4],
        attn_shares[5],
    )
    return (
        mixed,
        grad_tokens,
        share_one,
        share_two,
        mat_query,
        mat_key,
        mat_value,
        mat_out,
        grad_up,
        grad_down,
        state_shares[0],
        state_shares[1],
        state_shares[2],
        state_shares[3],
    )


def solution(mesh):
    return jax.shard_map(
        body,
        mesh=mesh,
        in_specs=(
            P(("dp", "mp"), None),
            P(("dp", "mp"), None),
            P(("dp", "mp")),
            P(("dp", "mp")),
            P(("dp", "mp"), None),
            P(("dp", "mp"), None),
            P(("dp", "mp"), None),
            P(("dp", "mp"), None),
            P(("dp", "mp"), None),
            P(None, ("dp", "mp")),
            P("mp", "dp"),
            P("mp", "dp"),
            P("mp", "dp"),
            P("dp", "mp", None),
            P(),
        ),
        out_specs=(
            P(("dp", "mp"), None),
            P(("dp", "mp"), None),
            P(("dp", "mp")),
            P(("dp", "mp")),
            P(("dp", "mp"), None),
            P(("dp", "mp"), None),
            P(("dp", "mp"), None),
            P(("dp", "mp"), None),
            P("dp", "mp"),
            P("mp", "dp"),
            P("mp", "dp"),
            P("mp", "dp"),
            P("mp", "dp"),
            P("dp", "mp", None),
        ),
        check_vma=False,
    )
```

profile of v0, /device:TPU:0, one launch (start us, length us, event | category | flops | bytes accessed | tf_op | source)
XLA Modules:
  0.0 1358.6 jit_solution(10846917883447503699)
XLA Ops:
  17.3 42.1 %all-reduce.12 = (bf16[1024]{0:T(1024)(128)(2,1)S(1)}, bf16[1024]{0:T(1024)(128)(2,1)}) all-reduce(bf16[1024]{0:T(1024)(128)(2,1)S(1)} %dynamic-update-slice, bf16[1024]{0:T(1024)(128)(2,1)S(1)} %dynamic-update-slice.1), channel_id=1, replica_groups=mesh['dp'=4,'mp'=8] {'dp','mp'}, use_global_device_ids=true, to_apply=%add.3 | all-reduce | flops 2048 | bytes 8192
  64.9 3.7 all-to-all-start
  70.4 9.2 all-gather.1
  79.7 7.0 all-gather
  86.8 8.1 all-gather.2
  96.3 8.0 fusion.9
  104.3 9.3 copy.163
  119.1 7.4 all_gather.46
  131.6 4.4 convolution_bitcast_fusion.4
  138.3 22.6 %while.9 = (s32[]{:T(128)}, f32[1,128,16]{1,2,0:T(8,128)S(1)}, f32[32,1,128,16]{2,3,1,0:T(8,128)S(1)}, f32[1,128,16]{1,2,0:T(8,128)S(1)}, f32[32,1,128,16]{2,3,1,0:T(8,128)}, /*index=5*/s32[]{:T(128)}) while((s32[]{:T(128)}, f32[1,128,16]{1,2,0:T(8,128)S(1)}, f32[32,1,128,16]{2,3,1,0:T(8,128)S(1)}, f32[1,128,16]{1,2,0:T(8,128)S(1)}, ...), condition=%wide.region_3.4_spmd, body=%wide.region_2.3_spmd.sunk | while | flops 4098 | bytes 49237 | solution.py:48
  162.4 9.0 fusion.98
  171.5 4.3 fusion.37
  179.0 5.1 all-to-all-start.1
  184.6 2.9 convolution_convert_fusion.4
  188.8 2.8 fusion.36
  193.0 3.2 all-to-all-done.1
  197.5 4.3 convolution_convert_fusion.5
  206.4 4.3 fusion.96
  214.7 4.4 fusion.30
  219.1 35.8 %all-gather.18.cloned.1.call-done = bf16[1024,1024]{1,0:T(8,128)(2,1)} async-done(((bf16[32,1024]{1,0:T(8,128)(2,1)}), bf16[1024,1024]{1,0:T(8,128)(2,1)}) %all-gather.18.cloned.1.call-update) | async-done | bytes 2097168 | tf_op jit(solution)/shard_map/all_gather | solution.py:146
  254.9 3.3 fusion.97
  260.7 73.2 %all-gather.20.cloned.1.call-done = bf16[1024,4096]{1,0:T(8,128)(2,1)} async-done(((bf16[32,4096]{1,0:T(8,128)(2,1)}), bf16[1024,4096]{1,0:T(8,128)(2,1)}) %all-gather.20.cloned.1.call-update) | async-done | bytes 8388624 | tf_op jit(solution)/shard_map/all_gather | solution.py:199
  333.9 11.5 fusion.99
  345.4 67.4 %all-gather.22.cloned.1.call-done = bf16[4096,1024]{0,1:T(8,128)(2,1)} async-done(((bf16[4096,32]{0,1:T(8,128)(2,1)}), bf16[4096,1024]{0,1:T(8,128)(2,1)}) %all-gather.22.cloned.1.call-update) | async-done | bytes 8388624 | tf_op jit(solution)/shard_map/all_gather | solution.py:200
  412.8 26.6 %add_convert_fusion = (bf16[512,4096]{1,0:T(8,128)(2,1)S(1)}, f32[512,4096]{1,0:T(8,128)}) fusion(f32[512,4096]{1,0:T(8,128)} %fusion.99, bf16[512,1024]{1,0:T(8,128)(2,1)S(1)} %copy-done.21, bf16[4096,1024]{0,1:T(8,128)(2,1)} %all-gather.22.cloned.1.call-done), kind=kOutput, calls=%fused_computation.17 | convolution fusion | flops 4445962240 | bytes 30408704 | tf_op jit(solution)/shard_map/dot_general | solution.py:72
  439.4 2.7 copy.225
  442.7 4.6 all-to-all-start.4
  447.3 7.9 multiply_convert_fusion.1
  459.6 174.5 %all-to-all-done.4 = bf16[512,8,512]{2,0,1:T(8,128)(2,1)} async-done(((bf16[512,8,512]{2,0,1:T(8,128)(2,1)}), bf16[512,8,512]{2,0,1:T(8,128)(2,1)}, u32[]{:S(2)}, u32[]{:S(2)}) %all-to-all-start.4) | async-done | bytes 4194336 | tf_op jit(solution)/shard_map/all_to_all | solution.py:214
  634.1 4.8 all-to-all-start.5
  639.0 11.5 multiply_reduce_fusion.1
  650.5 10.2 convolution_convert_fusion.1
  670.2 4.4 all-gather.26.cloned.1.call-done
  674.6 66.0 %all-to-all-done.5 = bf16[512,8,512]{2,0,1:T(8,128)(2,1)} async-done(((bf16[512,8,512]{2,0,1:T(8,128)(2,1)}), bf16[512,8,512]{2,0,1:T(8,128)(2,1)}, u32[]{:S(2)}, u32[]{:S(2)}) %all-to-all-start.5) | async-done | bytes 4194336 | tf_op jit(solution)/shard_map/all_to_all | solution.py:215
  740.6 10.1 convolution_convert_fusion
  750.8 6.6 multiply_reduce_fusion
  766.0 3.4 fusion.103
  770.6 3.5 fusion.34
  775.8 3.4 convolution_add_fusion.1
  779.3 6.3 fusion.31
  786.7 3.3 convolution_add_fusion
  793.2 2.4 fusion.102
  795.6 2.4 fusion.41
  798.8 3.4 all-to-all-start.2
  802.5 4.8 fusion.106
  807.4 10.3 add_convert_fusion.3
  817.7 2.6 fusion.100
  820.3 2.6 fusion.101
  824.5 3.2 convolution_bitcast_fusion.3
  828.9 64.8 %while.10 = (s32[]{:T(128)}, f32[128,16]{0,1:T(8,128)}, f32[1,128,16]{1,2,0:T(8,128)S(1)}, f32[32,1,128,16]{2,3,1,0:T(8,128)S(1)}, f32[32,1,128,16]{2,3,1,0:T(8,...) while((s32[]{:T(128)}, f32[128,16]{0,1:T(8,128)}, ...), condition=%wide.region_12.13_spmd.clone, body=%wide.region_11.12_spmd.clone.sunk | while | flops 16388 | bytes 83596 | solution.py:48
  894.3 3.8 fusion.57
  898.1 7.3 fusion.35
  905.3 2.7 copy.206
  908.1 5.2 all-to-all-start.3
  914.7 9.7 fusion.2
  927.0 4.8 multiply_reduce_fusion.4
  933.6 2.7 fusion.51
  937.4 16.5 %all-reduce.13 = (bf16[128,16]{0,1:T(8,128)(2,1)S(1)}, bf16[128,16]{0,1:T(8,128)(2,1)S(1)}, bf16[128,16]{0,1:T(8,128)(2,1)S(1)}, bf16[4,128,16]{1,2,0:T(8,128)(2,1)S(1)}) all-reduce(bf16[128,16]{0,1:T(8,128)(2,1)S(1)} %add_convert_fusion.5, bf16[128,16]{0,1:T(8,128)(2,1)S(1)} %copy.192, ...), channel_id=10, replica_groups=mesh['dp'=4,'mp'=8] {'dp'}, use_global_device_ids=true, to_apply=%region_27.28.clone | all-reduce | flops 14336 | bytes 57344
  956.4 4.6 fusion.26
  963.3 40.2 %all-reduce.11 = (f32[1024]{0:T(1024)S(1)}, f32[1024]{0:T(1024)S(1)}) all-reduce(f32[1024]{0:T(1024)S(1)} %get-tuple-element.325, f32[1024]{0:T(1024)S(1)} %copy-done.70), channel_id=2, replica_groups=mesh['dp'=4,'mp'=8] {'dp','mp'}, use_global_device_ids=true, to_apply=%region_16.17.clone | all-reduce | flops 2048 | bytes 16384
  1004.7 3.2 add_convert_fusion.1
  1011.5 55.7 %reduce-scatter.9.cloned.1.call-done = f32[32,1024]{1,0:T(8,128)} async-done(((f32[1024,1024]{1,0:T(8,128)}), f32[32,1024]{1,0:T(8,128)}) %reduce-scatter.9.cloned.1.call-update) | async-done | bytes 131088 | tf_op jit(solution)/shard_map/reduce_scatter | solution.py:281
  1067.2 142.4 %reduce-scatter.11.cloned.1.call-done = f32[32,1024]{1,0:T(8,128)} async-done(((f32[1024,1024]{1,0:T(8,128)}), f32[32,1024]{1,0:T(8,128)}) %reduce-scatter.11.cloned.1.call-update) | async-done | bytes 131088 | tf_op jit(solution)/shard_map/reduce_scatter | solution.py:282
  1209.7 142.2 %reduce-scatter.13.cloned.1.call-done = f32[32,1024]{1,0:T(8,128)} async-done(((f32[1024,1024]{1,0:T(8,128)}), f32[32,1024]{1,0:T(8,128)}) %reduce-scatter.13.cloned.1.call-update) | async-done | bytes 131088 | tf_op jit(solution)/shard_map/reduce_scatter | solution.py:283
  (480 shorter events, 189.2 us)
Async XLA Ops:
  7.2 55.9 %copy-start.1 = (bf16[512,1024]{1,0:T(8,128)(2,1)S(1)}, bf16[512,1024]{1,0:T(8,128)(2,1)}, u32[]{:S(2)}) copy-start(bf16[512,1024]{1,0:T(8,128)(2,1)} %param.19) | copy-start | bytes 3145732
  7.2 177.4 %all-gather.14.cloned.1.call-start = ((), (), s32[]{:S(2)}) async-start(), calls=%async_computation.13 | async-start | bytes 2162688 | tf_op jit(solution)/shard_map/all_gather | solution.py:143
  8.9 179.9 %all-gather.16.cloned.1.call-start = ((), (), s32[]{:S(2)}) async-start(), calls=%async_computation.14 | async-start | bytes 2162688 | tf_op jit(solution)/shard_map/all_gather | solution.py:144
  10.5 187.0 %all-gather.12.cloned.1.call-start = ((), (), s32[]{:S(2)}) async-start(), calls=%async_computation.12 | async-start | bytes 2162688 | tf_op jit(solution)/shard_map/all_gather | solution.py:145
  12.1 242.8 %all-gather.18.cloned.1.call-start = ((), (), s32[]{:S(2)}) async-start(), calls=%async_computation.15 | async-start | bytes 2162688 | tf_op jit(solution)/shard_map/all_gather | solution.py:146
  13.7 320.2 %all-gather.20.cloned.1.call-start = ((), (), s32[]{:S(2)}) async-start(), calls=%async_computation.16 | async-start | bytes 8650752 | tf_op jit(solution)/shard_map/all_gather | solution.py:199
  60.8 9.6 copy-start.74
  60.8 18.8 %copy-start.75 = (f32[128,4]{0,1:T(4,128)S(1)}, f32[128,4]{0,1:T(4,128)}, u32[]{:S(2)}) copy-start(f32[128,4]{0,1:T(4,128)} %param.30) | copy-start | bytes 6148
  60.9 26.0 %copy-start.76 = (f32[128,4]{0,1:T(4,128)S(1)}, f32[128,4]{0,1:T(4,128)}, u32[]{:S(2)}) copy-start(f32[128,4]{0,1:T(4,128)} %param.29) | copy-start | bytes 6148
  63.5 125.2 %copy-start.12 = (bf16[512,1024]{1,0:T(8,128)(2,1)}, bf16[512,1024]{1,0:T(8,128)(2,1)S(1)}, u32[]{:S(2)}) copy-start(bf16[512,1024]{1,0:T(8,128)(2,1)S(1)} %fusion.23) | copy-start | bytes 3145732
  64.9 63.4 %all-to-all-start = ((bf16[512,8,128]{0,2,1:T(8,128)(2,1)}), bf16[512,8,128]{0,2,1:T(8,128)(2,1)S(1)}, u32[]{:S(2)}, u32[]{:S(2)}) async-start(bf16[512,8,128]{0,2,1:T(8,128)(2,1)} %bitcast.286), calls=%async_computation | async-start | bytes 2097152 | tf_op jit(solution)/shard_map/all_to_all | solution.py:168
  68.5 344.3 %all-gather.22.cloned.1.call-start = ((), (), s32[]{:S(2)}) async-start(), calls=%async_computation.17 | async-start | bytes 8650752 | tf_op jit(solution)/shard_map/all_gather | solution.py:200
  70.4 43.2 %copy-start.71 = (f32[128]{0:T(128)}, f32[128]{0:T(128)S(1)}, u32[]{:S(2)}) copy-start(f32[128]{0:T(128)S(1)} %iota_convert_fusion) | copy-start | bytes 1540
  70.4 33.9 %copy-start.47 = (s32[128,128]{1,0:T(8,128)}, s32[128,128]{1,0:T(8,128)S(1)}, u32[]{:S(2)}) copy-start(s32[128,128]{1,0:T(8,128)S(1)} %iota_subtract_fusion) | copy-start | bytes 196612
  79.7 91.8 %copy-start.41 = (f32[16,128]{0,1:T(8,128)}, f32[16,128]{0,1:T(8,128)S(1)}, u32[]{:S(2)}) copy-start(f32[16,128]{0,1:T(8,128)S(1)} %copy.161) | copy-start | bytes 24580
  86.8 44.7 %copy-start.33 = (f32[16,128]{0,1:T(8,128)}, f32[16,128]{0,1:T(8,128)S(1)}, u32[]{:S(2)}) copy-start(f32[16,128]{0,1:T(8,128)S(1)} %copy.160) | copy-start | bytes 24580
  95.0 9.3 copy-start.61
  95.0 22.2 %copy-start.55 = (f32[4,4,128]{2,1,0:T(4,128)}, f32[4,4,128]{2,1,0:T(4,128)S(1)}, u32[]{:S(2)}) copy-start(f32[4,4,128]{2,1,0:T(4,128)S(1)} %neg.40) | copy-start | bytes 24580
  95.1 76.4 %copy-start.49 = (f32[128,16]{1,0:T(8,128)}, f32[128,16]{1,0:T(8,128)S(1)}, u32[]{:S(2)}) copy-start(f32[128,16]{1,0:T(8,128)S(1)} %copy.162) | copy-start | bytes 24580
  104.3 13.7 %copy-start.77 = (bf16[1024]{0:T(1024)(128)(2,1)S(1)}, bf16[1024]{0:T(1024)(128)(2,1)}, u32[]{:S(2)}) copy-start(bf16[1024]{0:T(1024)(128)(2,1)} %get-tuple-element.357) | copy-start | bytes 6148
  104.3 14.3 %copy-start.80 = (s32[4]{0:T(128)S(1)}, s32[4]{0:T(128)}, u32[]{:S(2)}) copy-start(s32[4]{0:T(128)} %param.33) | copy-start | bytes 52
  104.3 14.8 %copy-start.69 = (f32[1,128,16]{1,2,0:T(8,128)S(1)}, f32[1,128,16]{1,2,0:T(8,128)}, u32[]{:S(2)}) copy-start(f32[1,128,16]{1,2,0:T(8,128)} %param.32) | copy-start | bytes 24580
  131.5 39.9 %copy-start.3 = (bf16[32,128,128]{1,0,2:T(8,128)(2,1)}, bf16[32,128,128]{1,0,2:T(8,128)(2,1)S(1)}, u32[]{:S(2)}) copy-start(bf16[32,128,128]{1,0,2:T(8,128)(2,1)S(1)} %reshape.330) | copy-start | bytes 3145732
  160.9 10.5 copy-start.40
  160.9 10.5 copy-start.45
  162.4 9.1 copy-start.27
  162.4 9.1 copy-start.52
  162.4 9.1 copy-start.72
  179.0 17.2 %all-to-all-start.1 = ((bf16[8,128,128]{1,2,0:T(8,128)(2,1)}), bf16[8,128,128]{1,2,0:T(8,128)(2,1)S(1)}, u32[]{:S(2)}, u32[]{:S(2)}) async-start(bf16[8,128,128]{1,2,0:T(8,128)(2,1)} %concatenate.9), calls=%async_computation.1 | async-start | bytes 524288 | tf_op jit(solution)/shard_map/all_to_all | solution.py:187
  184.1 466.4 %all-gather.24.cloned.1.call-start = ((), (), s32[]{:S(2)}) async-start(), calls=%async_computation.22 | async-start | bytes 9437184 | tf_op jit(solution)/shard_map/all_gather | solution.py:217
  196.2 7.9 copy-start.25
  259.9 414.6 %all-gather.26.cloned.1.call-start = ((), (), s32[]{:S(2)}) async-start(), calls=%async_computation.24 | async-start | bytes 9437184 | tf_op jit(solution)/shard_map/all_gather | solution.py:218
  260.7 152.1 %copy-start.21 = (bf16[512,1024]{1,0:T(8,128)(2,1)S(1)}, bf16[512,1024]{1,0:T(8,128)(2,1)}, u32[]{:S(2)}) copy-start(bf16[512,1024]{1,0:T(8,128)(2,1)} %param.20) | copy-start | bytes 3145732
  442.7 191.4 %all-to-all-start.4 = ((bf16[512,8,512]{2,0,1:T(8,128)(2,1)}), bf16[512,8,512]{2,0,1:T(8,128)(2,1)}, u32[]{:S(2)}, u32[]{:S(2)}) async-start(bf16[512,8,512]{2,0,1:T(8,128)(2,1)} %bitcast.271), calls=%async_computation.8 | async-start | bytes 8388608 | tf_op jit(solution)/shard_map/all_to_all | solution.py:214
  634.1 106.5 %all-to-all-start.5 = ((bf16[512,8,512]{2,0,1:T(8,128)(2,1)}), bf16[512,8,512]{2,0,1:T(8,128)(2,1)}, u32[]{:S(2)}, u32[]{:S(2)}) async-start(bf16[512,8,512]{2,0,1:T(8,128)(2,1)} %bitcast.270), calls=%async_computation.10 | async-start | bytes 8388608 | tf_op jit(solution)/shard_map/all_to_all | solution.py:215
  638.9 369.1 %reduce-scatter.15.cloned.1.call-start = ((), (), s32[]{:S(2)}) async-start(), calls=%async_computation.23 | async-start | bytes 1310720 | tf_op jit(solution)/shard_map/reduce_scatter | solution.py:222
  660.7 349.0 %reduce-scatter.17.cloned.1.call-start = ((), (), s32[]{:S(2)}) async-start(), calls=%async_computation.25 | async-start | bytes 1310720 | tf_op jit(solution)/shard_map/reduce_scatter | solution.py:225
  670.1 80.7 %copy-start.18 = (bf16[512,1024]{0,1:T(8,128)(2,1)}, bf16[512,1024]{0,1:T(8,128)(2,1)S(1)}, u32[]{:S(2)}) copy-start(bf16[512,1024]{0,1:T(8,128)(2,1)S(1)} %copy.209) | copy-start | bytes 3145732
  750.8 260.8 %reduce-scatter.7.cloned.1.call-start = ((), (), s32[]{:S(2)}) async-start(), calls=%async_computation.18 | async-start | bytes 4325376 | tf_op jit(solution)/shard_map/reduce_scatter | solution.py:280
  750.8 6.7 slice-start
  750.8 7.0 slice-start.1
  750.8 7.6 slice-start.2
  769.4 297.9 %reduce-scatter.9.cloned.1.call-start = ((), (), s32[]{:S(2)}) async-start(), calls=%async_computation.19 | async-start | bytes 4325376 | tf_op jit(solution)/shard_map/reduce_scatter | solution.py:281
  779.2 430.5 %reduce-scatter.11.cloned.1.call-start = ((), (), s32[]{:S(2)}) async-start(), calls=%async_computation.20 | async-start | bytes 4325376 | tf_op jit(solution)/shard_map/reduce_scatter | solution.py:282
  798.8 24.2 %all-to-all-start.2 = ((bf16[128,8,128]{2,0,1:T(8,128)(2,1)}), bf16[128,8,128]{2,0,1:T(8,128)(2,1)S(1)}, u32[]{:S(2)}, u32[]{:S(2)}) async-start(bf16[128,8,128]{2,0,1:T(8,128)(2,1)} %bitcast.254), calls=%async_computation.2 | async-start | bytes 524288 | tf_op jit(solution)/shard_map/all_to_all | solution.py:243
  802.2 549.6 %reduce-scatter.13.cloned.1.call-start = ((), (), s32[]{:S(2)}) async-start(), calls=%async_computation.21 | async-start | bytes 4325376 | tf_op jit(solution)/shard_map/reduce_scatter | solution.py:283
  807.4 10.4 copy-start.79
  807.4 10.3 copy-start.82
  823.1 71.1 %copy-start.15 = (f32[128,128,16]{0,2,1:T(8,128)S(1)}, f32[128,128,16]{0,2,1:T(8,128)}, u32[]{:S(2)}) copy-start(f32[128,128,16]{0,2,1:T(8,128)} %rev.8) | copy-start | bytes 3145732
  823.1 71.1 %copy-start.34 = (f32[16,128]{0,1:T(8,128)S(1)}, f32[16,128]{0,1:T(8,128)}, u32[]{:S(2)}) copy-start(f32[16,128]{0,1:T(8,128)} %copy-done.33) | copy-start | bytes 24580
  824.5 88.8 %copy-start.17 = (bf16[1,32,128,128]{2,1,3,0:T(8,128)(2,1)}, bf16[1,32,128,128]{2,1,3,0:T(8,128)(2,1)S(1)}, u32[]{:S(2)}) copy-start(bf16[1,32,128,128]{2,1,3,0:T(8,128)(2,1)S(1)} %copy.205) | copy-start | bytes 3145732
  905.3 8.0 copy-start.4
  908.1 48.3 %all-to-all-start.3 = ((bf16[8,512,128]{2,1,0:T(8,128)(2,1)}), bf16[8,512,128]{2,1,0:T(8,128)(2,1)}, u32[]{:S(2)}, u32[]{:S(2)}) async-start(bf16[8,512,128]{2,1,0:T(8,128)(2,1)} %bitcast.287), calls=%async_computation.3 | async-start | bytes 2097152 | tf_op jit(solution)/shard_map/all_to_all | solution.py:262
  914.6 9.7 copy-start.20
  925.4 11.9 copy-start.78
  926.9 10.5 copy-start.51
  926.9 10.5 copy-start.56
  926.9 29.5 %copy-start.2 = (bf16[512,1024]{1,0:T(8,128)(2,1)S(1)}, bf16[512,1024]{1,0:T(8,128)(2,1)}, u32[]{:S(2)}) copy-start(bf16[512,1024]{1,0:T(8,128)(2,1)} %param.19) | copy-start | bytes 3145732
  926.9 29.5 %copy-start.7 = (bf16[1024,1024]{1,0:T(8,128)(2,1)S(1)}, bf16[1024,1024]{1,0:T(8,128)(2,1)}, u32[]{:S(2)}) copy-start(bf16[1024,1024]{1,0:T(8,128)(2,1)} %all-gather.12.cloned.1.call-done) | copy-start | bytes 6291460
  927.0 29.5 %copy-start.58 = (f32[1024]{0:T(1024)S(1)}, f32[1024]{0:T(1024)}, u32[]{:S(2)}) copy-start(f32[1024]{0:T(1024)} %copy-done.57) | copy-start | bytes 12292
  927.0 29.5 %copy-start.60 = (f32[512]{0:T(512)S(1)}, f32[512]{0:T(512)}, u32[]{:S(2)}) copy-start(f32[512]{0:T(512)} %copy-done.59) | copy-start | bytes 6148
  956.4 7.0 copy-start.70
  956.4 48.3 %copy-start.66 = (f32[512]{0:T(512)S(1)}, f32[512]{0:T(512)}, u32[]{:S(2)}) copy-start(f32[512]{0:T(512)} %copy-done.65) | copy-start | bytes 6148
  961.0 43.7 %copy-start.10 = (f32[512,1024]{1,0:T(8,128)S(1)}, f32[512,1024]{1,0:T(8,128)}, u32[]{:S(2)}) copy-start(f32[512,1024]{1,0:T(8,128)} %copy-done.9) | copy-start | bytes 6291460
  (43 other events, 131.5 us)
Sparse Core Ops, SparseCore 0:
  11.6 59.2 all-gather.13
  74.4 60.5 all-gather.15
  138.6 56.2 all-gather.11
  198.3 56.5 all-gather.17
  257.8 76.1 all-gather.19
  336.8 75.9 all-gather.21
  414.4 124.0 all-gather.23
  540.1 134.4 all-gather.25
  677.5 33.0 reduce-scatter.14
  750.9 26.0 reduce-scatter.16
  779.9 143.6 reduce-scatter.6
  926.3 140.9 reduce-scatter.8
  1070.1 139.5 reduce-scatter.10
  1212.4 139.4 reduce-scatter.12
where the time goes:
time: 1370 us; the launch traced here: 1360 us
  waiting for transfers between devices  766 us (56%)
  matrix products  217 us (16%)
  other arithmetic  134 us (10%)
  blocking collectives  130 us (9%)
  local copies, waits for them, and re-layouts  66.7 us (5%)
  starting transfers between devices  28.6 us (2%)
  between operations  16.1 us (1%)
    all_to_all x1, waiting for transfers between devices, body(): lax.all_to_all(grad_hidden, 'mp', split_axis=1, concat_axis=0, tiled=True)  175 us
    reduce_scatter x1, waiting for transfers between devices, body(): lax.psum_scatter(grad_value_w, ('dp', 'mp'), scatter_dimension=0, tiled=T...  142 us
    reduce_scatter x1, waiting for transfers between devices, body(): lax.psum_scatter(grad_out_w, ('dp', 'mp'), scatter_dimension=0, tiled=True)  142 us
    unnamed x3, blocking collectives  98.8 us
    all_gather x1, waiting for transfers between devices, body(): lax.all_gather(w_up.astype(half), ('dp', 'mp'), axis=0, tiled=True)  73.2 us
    all_gather x1, waiting for transfers between devices, body(): lax.all_gather(w_down.astype(half), ('dp', 'mp'), axis=1, tiled=True)  67.4 us
    all_to_all x1, waiting for transfers between devices, body(): lax.all_to_all(active_b, 'mp', split_axis=1, concat_axis=0, tiled=True)  66 us
    add_any x64, other arithmetic, advance(): return (jump_decay * state_now + pushed_in, state_now)  64.6 us
  transfers between devices with their start and end apart: 20, of which 10 were waited for; matrix products, arithmetic and copies ran while one was open for 29% of the time, Pallas kernels for 0%

commit v1 on v0

v1 whole, which is shorter than its diff:
```python
import functools

import jax
import jax.numpy as jnp
from jax import lax
from jax.experimental import pallas as pl
from jax.experimental.pallas import tpu as pltpu
from jax.sharding import PartitionSpec as P

D = 1024
H = 8
HD = 128
FF = 4096
NS = 16
LEN = 4096
BLK = 512
CTX = 128
OWN = BLK - CTX
HALF = D // 2
SCALE = HD ** (-0.5)
AXES = ("dp", "mp")
f32 = jnp.float32
bf16 = jnp.bfloat16
VMEM = pl.BlockSpec(memory_space=pltpu.VMEM)
SMEM = pl.BlockSpec(memory_space=pltpu.SMEM)
ANY = pl.BlockSpec(memory_space=pl.ANY)
NT = (((1,), (1,)), ((), ()))
TN = (((0,), (0,)), ((), ()))


def params(mib):
    return pltpu.CompilerParams(vmem_limit_bytes=mib * 1024 * 1024)


def cost(flops, bytes_accessed, trans=0):
    return pl.CostEstimate(flops=flops, bytes_accessed=bytes_accessed, transcendentals=trans)


def bits_of(n):
    return n.bit_length() - 1


def swap_bits(word, count):
    out = 0
    for i in range(count):
        out = out | (((word >> i) & 1) << (count - 1 - i))
    return out


class Links:
    def __init__(self):
        self.ndp = lax.axis_size("dp")
        self.nmp = lax.axis_size("mp")
        self.nz = self.nmp // 2
        self.dp = lax.axis_index("dp")
        self.mp = lax.axis_index("mp")
        self.z = self.mp // 2
        self.core = self.mp % 2
        self.dp_bits = bits_of(self.ndp)
        self.mp_bits = bits_of(self.nmp)

    def send(self, values, target):
        pairs = []
        for d in range(self.ndp):
            for m in range(self.nmp):
                to = target(d, m)
                if to is not None:
                    pairs.append((d * self.nmp + m, to[0] * self.nmp + to[1]))
        return lax.ppermute(values, AXES, pairs)

    def mp_swap(self, values, bit):
        return self.send(values, lambda d, m: (d, m ^ (1 << bit)))

    def dp_swap(self, values, bit):
        return self.send(values, lambda d, m: (d ^ (1 << bit), m))

    def core_swap(self, values):
        return self.mp_swap(values, 0)

    def fan(self, values, level):
        other = self.dp_bits - 1 - level
        return self.send(
            values, lambda d, m: (d ^ (1 << (other if m % 2 else level)), m)
        )

    def block_at(self, position):
        mirrored = swap_bits(position, self.dp_bits)
        return self.dp ^ jnp.where(self.core == 0, mirrored, position)

    def window_shift(self, values, step):
        per = LEN // BLK

        def target(d, m):
            inside = m % per + step
            return (d, m + step) if 0 <= inside < per else None

        return self.send(values, target)


def by_core(links, first, second, axis):
    return jnp.where(
        links.core == 0,
        jnp.concatenate([first, second], axis),
        jnp.concatenate([second, first], axis),
    )


def spread_rows(src_ref, dst_ref, rows, start=0):
    for r in range(0, rows, 16):
        block = src_ref[start + r : start + r + 16, :].astype(f32)
        for j in range(8):
            dst_ref[r : r + 16, j, :] = block[:, j * 128 : (j + 1) * 128]


def gather_rows(src_ref, dst_ref, rows):
    for r in range(0, rows, 16):
        for j in range(8):
            dst_ref[r : r + 16, j * 128 : (j + 1) * 128] = src_ref[r : r + 16, j, :].astype(
                dst_ref.dtype
            )


def scan_kernel(rows, x_ref, rate_ref, out_ref, xs):
    spread_rows(x_ref, xs, rows)
    decay = jnp.exp(-rate_ref[...])
    zero = jnp.zeros((NS, 8, 128), f32)

    def step(i, carry):
        u, v = carry
        for k in range(8):
            v = decay * v + u
            u = decay * u + xs[i * 8 + k][None]
        return u, v

    u, v = lax.fori_loop(0, rows // 8, step, (zero, zero))
    out_ref[0] = u
    out_ref[1] = v


def state_scan(values, rate):
    rows = values.shape[0]
    return pl.pallas_call(
        functools.partial(scan_kernel, rows),
        out_shape=jax.ShapeDtypeStruct((2, NS, 8, 128), f32),
        in_specs=[VMEM, VMEM],
        out_specs=VMEM,
        scratch_shapes=[pltpu.VMEM((rows, 8, 128), f32)],
        compiler_params=params(24),
        cost_estimate=cost(rows * 64 * 1024, rows * 2048),
        name="state_scan",
    )(values, rate)


def context_kernel(x_ref, start_ref, decay_ref, weight_ref, out_ref, xs, ys):
    spread_rows(x_ref, xs, CTX)
    decay = decay_ref[...]
    weight = weight_ref[...]

    def step(i, y):
        for k in range(8):
            y = decay * y + weight * xs[i * 8 + k][None]
            ys[i * 8 + k] = jnp.sum(y, axis=0)
        return y

    lax.fori_loop(0, CTX // 8, step, start_ref[...])
    gather_rows(ys, out_ref, CTX)


def context_states(tail, start, decay, weight):
    return pl.pallas_call(
        context_kernel,
        out_shape=jax.ShapeDtypeStruct((CTX, D), bf16),
        in_specs=[VMEM] * 4,
        out_specs=VMEM,
        scratch_shapes=[pltpu.VMEM((CTX, 8, 128), f32)] * 2,
        compiler_params=params(16),
        cost_estimate=cost(CTX * 64 * 1024, CTX * 4096),
        name="context_states",
    )(tail, start, decay, weight)


def state_sums_kernel(g_ref, x_ref, start_ref, decay_ref, sums_ref, gs, xs):
    spread_rows(g_ref, gs, CTX)
    spread_rows(x_ref, xs, CTX)
    part = NS // 2
    for n in range(0, NS, part):
        decay = decay_ref[n : n + part]
        zero = jnp.zeros((part, 8, 128), f32)

        def step(i, carry):
            u, v, su, sv = carry
            for k in range(4):
                v = decay * v + u
                u = decay * u + xs[i * 4 + k][None]
                g = gs[i * 4 + k][None]
                su = su + g * u
                sv = sv + g * v
            return u, v, su, sv

        _, _, su, sv = lax.fori_loop(
            0,
            CTX // 4,
            step,
            (start_ref[0, n : n + part], start_ref[1, n : n + part], zero, zero),
        )
        sums_ref[0, n : n + part] = su
        sums_ref[1, n : n + part] = sv
    decay = decay_ref[...]
    zero = jnp.zeros((NS, 8, 128), f32)

    def back(i, carry):
        low, slope = carry
        for k in range(8):
            slope = decay * slope + low
            low = decay * low + gs[CTX - 1 - (i * 8 + k)][None]
        return low, slope

    low, slope = lax.fori_loop(0, CTX // 8, back, (zero, zero))
    sums_ref[2] = low
    sums_ref[3] = slope


def state_sums(grad_context, tail, start, decay):
    return pl.pallas_call(
        state_sums_kernel,
        out_shape=jax.ShapeDtypeStruct((4, NS, 8, 128), f32),
        in_specs=[VMEM] * 4,
        out_specs=VMEM,
        scratch_shapes=[pltpu.VMEM((CTX, 8, 128), f32)] * 2,
        compiler_params=params(16),
        cost_estimate=cost(CTX * 192 * 1024, CTX * 4096),
        name="state_sums",
    )(grad_context, tail, start, decay)


def sent_tail_kernel(g_ref, start_ref, decay_ref, weight_ref, out_ref, gs, ys):
    spread_rows(g_ref, gs, CTX)
    decay = decay_ref[...]
    weight = weight_ref[...]

    def back(i, y):
        for k in range(8):
            t = CTX - 1 - (i * 8 + k)
            y = decay * y + weight * gs[t][None]
            ys[t] = jnp.sum(y, axis=0)
        return y

    lax.fori_loop(0, CTX // 8, back, start_ref[...])
    gather_rows(ys, out_ref, CTX)


def sent_tail(grad_context, start, decay, weight):
    return pl.pallas_call(
        sent_tail_kernel,
        out_shape=jax.ShapeDtypeStruct((CTX, D), bf16),
        in_specs=[VMEM] * 4,
        out_specs=VMEM,
        scratch_shapes=[pltpu.VMEM((CTX, 8, 128), f32)] * 2,
        compiler_params=params(16),
        cost_estimate=cost(CTX * 64 * 1024, CTX * 4096),
        name="sent_tail",
    )(grad_context, start, decay, weight)


def sent_own_kernel(start_ref, decay_ref, out_ref, ys):
    decay = decay_ref[...]

    def back(i, y):
        for k in range(8):
            y = decay * y
            ys[OWN - 1 - (i * 8 + k)] = jnp.sum(y, axis=0)
        return y

    lax.fori_loop(0, OWN // 8, back, start_ref[...])
    gather_rows(ys, out_ref, OWN)


def sent_own(start, decay):
    return pl.pallas_call(
        sent_own_kernel,
        out_shape=jax.ShapeDtypeStruct((OWN, D), bf16),
        in_specs=[VMEM] * 2,
        out_specs=VMEM,
        scratch_shapes=[pltpu.VMEM((OWN, 8, 128), f32)],
        compiler_params=params(16),
        cost_estimate=cost(OWN * 32 * 1024, OWN * 2048),
        name="sent_own",
    )(start, decay)


def attention_mask(keys, queries, first_query, opened):
    row = lax.broadcasted_iota(jnp.int32, (keys, queries), 0)
    col = lax.broadcasted_iota(jnp.int32, (keys, queries), 1) + first_query
    return jnp.where(row < CTX, (1 - opened) * BLK, row - CTX) <= col


def head_parts(own_ref, ctx_ref, offset):
    q = own_ref[:, pl.ds(offset, HD)]
    k = jnp.concatenate(
        [ctx_ref[:, pl.ds(offset, HD)], own_ref[:, pl.ds(HALF + offset, HD)]], 0
    )
    v = jnp.concatenate(
        [ctx_ref[:, pl.ds(HALF + offset, HD)], own_ref[:, pl.ds(2 * HALF + offset, HD)]], 0
    )
    return q, k, v


def probabilities(k, q, first_query, opened):
    scores = lax.dot_general(k, q, NT, preferred_element_type=f32) * SCALE
    scores = jnp.where(
        attention_mask(k.shape[0], q.shape[0], first_query, opened), scores, -jnp.inf
    )
    lifted = jnp.exp(scores - jnp.max(scores, axis=0, keepdims=True))
    return lifted * (1.0 / jnp.sum(lifted, axis=0, keepdims=True))


QT = BLK // 2


def attend_kernel(info, own_ref, other_ref, ctx_own_ref, ctx_other_ref, out_ref):
    opened = info[1]
    sides = ((own_ref, ctx_own_ref), (other_ref, ctx_other_ref))

    @pl.loop(0, H // 2)
    def _(h):
        offset = pl.multiple_of(h * HD, HD)
        for side, (qkv, ctx) in enumerate(sides):
            q, k, v = head_parts(qkv, ctx, offset)
            v_t = v.T
            home = pl.multiple_of((side ^ info[0]) * HALF + h * HD, HD)
            for first in range(0, BLK, QT):
                keys = CTX + first + QT
                p = probabilities(k[:keys], q[first : first + QT], first, opened).astype(bf16)
                mixed = jnp.dot(v_t[:, :keys], p, preferred_element_type=f32)
                out_ref[first : first + QT, pl.ds(home, HD)] = mixed.T.astype(bf16)


def attend(info, own, other, ctx_own, ctx_other):
    return pl.pallas_call(
        attend_kernel,
        out_shape=jax.ShapeDtypeStruct((BLK, D), bf16),
        in_specs=[SMEM] + [VMEM] * 4,
        out_specs=VMEM,
        compiler_params=params(32),
        cost_estimate=cost(4 * BLK * 640 * D, 6 * 2**20, H * 640 * BLK),
        name="attend",
    )(info, own, other, ctx_own, ctx_other)


def attend_back_kernel(
    info, own_ref, other_ref, ctx_own_ref, ctx_other_ref, grad_ref, g_own_ref, g_other_ref, acc
):
    opened = info[1]
    sides = ((own_ref, ctx_own_ref, g_own_ref), (other_ref, ctx_other_ref, g_other_ref))
    for _, _, g in sides:
        g[:CTX, :HALF] = jnp.zeros((CTX, HALF), bf16)

    @pl.loop(0, H // 2)
    def _(h):
        offset = pl.multiple_of(h * HD, HD)
        for side, (qkv, ctx, g) in enumerate(sides):
            q, k, v = head_parts(qkv, ctx, offset)
            k_t = k.T
            home = pl.multiple_of((side ^ info[0]) * HALF + h * HD, HD)
            for first in range(0, BLK, QT):
                keys = CTX + first + QT
                q_now = q[first : first + QT]
                go = grad_ref[first : first + QT, pl.ds(home, HD)]
                p = probabilities(k[:keys], q_now, first, opened)
                gp = lax.dot_general(v[:keys], go, NT, preferred_element_type=f32)
                mean = jnp.sum(p * gp, axis=0, keepdims=True)
                gs = (p * (gp - mean)).astype(bf16)
                gq_t = jnp.dot(k_t[:, :keys], gs, preferred_element_type=f32) * SCALE
                g[CTX + first : CTX + first + QT, pl.ds(offset, HD)] = gq_t.T.astype(bf16)
                gk = jnp.dot(gs, q_now, preferred_element_type=f32)
                gv = jnp.dot(p.astype(bf16), go, preferred_element_type=f32)
                if first == 0:
                    acc[0, :keys] = gk
                    acc[1, :keys] = gv
                else:
                    early = CTX + QT
                    gk_all = jnp.concatenate([gk[:early] + acc[0, :early], gk[early:]], 0)
                    gv_all = jnp.concatenate([gv[:early] + acc[1, :early], gv[early:]], 0)
                    g[:, pl.ds(HALF + offset, HD)] = (gk_all * SCALE).astype(bf16)
                    g[:, pl.ds(2 * HALF + offset, HD)] = gv_all.astype(bf16)


def attend_back(info, own, other, ctx_own, ctx_other, grad):
    out = jax.ShapeDtypeStruct((CTX + BLK, 3 * HALF), bf16)
    return pl.pallas_call(
        attend_back_kernel,
        out_shape=(out, out),
        in_specs=[SMEM] + [VMEM] * 5,
        out_specs=(VMEM, VMEM),
        scratch_shapes=[pltpu.VMEM((2, CTX + QT, HD), f32)],
        compiler_params=params(32),
        cost_estimate=cost(10 * BLK * 640 * D, 10 * 2**20, H * 640 * BLK),
        name="attend_back",
    )(info, own, other, ctx_own, ctx_other, grad)


def gelu_parts(x):
    cdf = 0.5 * (1.0 + lax.erf(x * 0.7071067811865476))
    slope = cdf + x * (jnp.exp(-0.5 * x * x) * 0.3989422804014327)
    return x * cdf, slope


def feed_kernel(
    ndp, nz, width, earlier, last, info, s_own, s_par, c_own, c_par, st_own, st_par, ct_own, ct_par,
    w_low, w_high, *rest
):
    rows = s_own.shape[0]
    tokens = 2 * rows
    block = D // ndp
    group = nz * width
    half = ndp // 2
    if earlier:
        m_in, g_in, *rest = rest
    if last:
        m_own, m_par, g_own, g_par, keep_out, send_out, *rest = rest
    else:
        m_out, g_out, keep_out, send_out, *rest = rest
    s, c, st, ct, w, act, gh, acc_m, acc_g, keep, send, sems, out_sems = rest
    at = [pl.multiple_of(info[p] * block, block) for p in range(ndp)]
    z = info[ndp]
    copies = {}
    count = [0]

    def start(name, src, dst):
        sem = sems.at[count[0]]
        count[0] += 1
        copy = pltpu.make_async_copy(src, dst, sem)
        copy.start()
        copies.setdefault(name, []).append(copy)

    def wait(name):
        for copy in copies.pop(name):
            copy.wait()

    def columns(name, own, par, dst):
        for p in range(ndp):
            for i, src in enumerate((own, par)):
                start(
                    name,
                    src.at[:, pl.ds(at[p], block)],
                    dst.at[i * rows : (i + 1) * rows, p * block : (p + 1) * block],
                )

    def rows_of(name, own, par, dst):
        for p in range(ndp):
            for i, src in enumerate((own, par)):
                start(
                    name,
                    src.at[pl.ds(at[p], block), :],
                    dst.at[p * block : (p + 1) * block, i * rows : (i + 1) * rows],
                )

    columns("s", s_own, s_par, s)
    for p in range(ndp):
        src = w_low if p < half else w_high
        start("w", src.at[p % half], w.at[p * block : (p + 1) * block, :])
    columns("c", c_own, c_par, c)
    rows_of("st", st_own, st_par, st)
    rows_of("ct", ct_own, ct_par, ct)
    if earlier:
        start("m", m_in, acc_m)
        start("g", g_in, acc_g)
    wait("s")
    wait("w")
    wait("c")

    @pl.loop(0, nz)
    def _(b):
        up = pl.ds(pl.multiple_of(b * width, width), width)
        down = pl.ds(pl.multiple_of(group + b * width, width), width)
        for i in range(2):
            part = slice(i * rows, (i + 1) * rows)
            hidden = jnp.dot(s[part, :], w[:, up], preferred_element_type=f32)
            grad = jnp.dot(c[part, :], w[:, down], preferred_element_type=f32)
            active, slope = gelu_parts(hidden)
            act[part, up] = active.astype(bf16)
            gh[part, up] = (grad * slope).astype(bf16)

    wait("st")
    wait("ct")

    @pl.loop(0, nz)
    def _(r):
        cols = pl.ds(pl.multiple_of((z ^ r) * width, width), width)
        for part, dst in ((0, keep), (1, send)):
            span = slice(part * half * block, (part + 1) * half * block)
            up = jnp.dot(st[span, :], gh[:, cols], preferred_element_type=f32).astype(bf16)
            down = jnp.dot(ct[span, :], act[:, cols], preferred_element_type=f32).astype(bf16)
            for p in range(half):
                dst[p, r, 0] = up[p * block : (p + 1) * block]
                dst[p, r, 1] = down[p * block : (p + 1) * block]

    outs = [
        pltpu.make_async_copy(keep, keep_out, out_sems.at[0]),
        pltpu.make_async_copy(send, send_out, out_sems.at[1]),
    ]
    for copy in outs:
        copy.start()
    if earlier:
        wait("m")
        wait("g")
    for name, left, acc, first in (("g", gh, acc_g, 0), ("m", act, acc_m, group)):
        for p in range(ndp):
            right = w[p * block : (p + 1) * block, first : first + group]
            for i in range(2):
                part = slice(i * rows, (i + 1) * rows)
                value = lax.dot_general(left[part, :], right, NT, preferred_element_type=f32)
                cols = pl.ds(at[p], block)
                if earlier:
                    value = value + acc[part, cols]
                if not last:
                    acc[part, cols] = value
                elif i == 0:
                    (g_own if name == "g" else m_own)[:, cols] = value
                else:
                    (g_par if name == "g" else m_par)[:, cols] = value.astype(bf16)
    if not last:
        outs.append(pltpu.make_async_copy(acc_m, m_out, out_sems.at[2]))
        outs.append(pltpu.make_async_copy(acc_g, g_out, out_sems.at[3]))
        for copy in outs[2:]:
            copy.start()
    for copy in outs:
        copy.wait()


def feed(links, info, acts, weights, earlier, last):
    ndp, nz = links.ndp, links.nz
    rows = acts[0].shape[0]
    tokens = 2 * rows
    block = D // ndp
    group = weights[0].shape[2] // 2
    width = group // nz
    half = ndp // 2
    full = jax.ShapeDtypeStruct((tokens, D), f32)
    own = jax.ShapeDtypeStruct((rows, D), f32)
    par = jax.ShapeDtypeStruct((rows, D), bf16)
    grads = jax.ShapeDtypeStruct((half, nz, 2, block, width), bf16)
    out_shape = (own, par, own, par, grads, grads) if last else (full, full, grads, grads)
    out_specs = (VMEM,) * 4 + (ANY,) * 2 if last else (ANY,) * 4
    inputs = (info, *acts, *weights) + (tuple(earlier) if earlier else ())
    n_copies = 8 * ndp + ndp + 2
    return pl.pallas_call(
        functools.partial(feed_kernel, ndp, nz, width, bool(earlier), last),
        out_shape=out_shape,
        in_specs=[SMEM] + [ANY] * (len(inputs) - 1),
        out_specs=out_specs,
        scratch_shapes=[
            pltpu.VMEM((tokens, D), bf16),
            pltpu.VMEM((tokens, D), bf16),
            pltpu.VMEM((D, tokens), bf16),
            pltpu.VMEM((D, tokens), bf16),
            pltpu.VMEM((D, 2 * group), bf16),
            pltpu.VMEM((tokens, group), bf16),
            pltpu.VMEM((tokens, group), bf16),
            pltpu.VMEM((tokens, D), f32),
            pltpu.VMEM((tokens, D), f32),
            pltpu.VMEM((half, nz, 2, block, width), bf16),
            pltpu.VMEM((half, nz, 2, block, width), bf16),
            pltpu.SemaphoreType.DMA((n_copies,)),
            pltpu.SemaphoreType.DMA((4,)),
        ],
        compiler_params=params(58),
        cost_estimate=cost(12 * tokens * D * group, 30 * 2**20, 2 * tokens * group),
        name="feed_last" if last else "feed_first",
    )(*inputs)


def place_kernel(ndp, half, block, info, low, high, out, sems):
    copies = []
    for p in range(ndp):
        src = low if p < half else high
        row = pl.multiple_of(info[p] * block, block)
        copies.append(
            pltpu.make_async_copy(src.at[p % half], out.at[pl.ds(row, block), :], sems.at[p])
        )
    for copy in copies:
        copy.start()
    for copy in copies:
        copy.wait()


def place(links, info, low, high):
    half, block, cols = low.shape
    ndp = links.ndp
    return pl.pallas_call(
        functools.partial(place_kernel, ndp, half, block),
        out_shape=jax.ShapeDtypeStruct((ndp * block, cols), low.dtype),
        in_specs=[SMEM, ANY, ANY],
        out_specs=ANY,
        scratch_shapes=[pltpu.SemaphoreType.DMA((ndp,))],
        cost_estimate=cost(0, 4 * ndp * block * cols),
        name="place",
    )(info, low, high)


def gather_z(links, values):
    current = values[None]
    for bit in reversed(range(1, links.mp_bits)):
        received = links.mp_swap(current, bit)
        mine = (links.mp >> bit) & 1
        current = jnp.where(
            mine == 0,
            jnp.stack([current, received], 1),
            jnp.stack([received, current], 1),
        )
        current = current.reshape(-1, *values.shape)
    return current.reshape(-1, values.shape[1])


def gather_dp(links, values):
    current = values[None]
    for level in reversed(range(links.dp_bits)):
        received = links.fan(current, level)
        if level == 0:
            return current, received
        current = jnp.concatenate([current, received], 0)


def add_b(left, right):
    return (left.astype(f32) + right.astype(f32)).astype(bf16)


def scatter_dp(links, keep, send):
    for level in range(links.dp_bits):
        received = links.fan(send, level)
        current = add_b(keep, received)
        half = current.shape[0] // 2
        if level < links.dp_bits - 1:
            keep, send = current[:half], current[half:]
    return current[0]


def scatter_z(links, values, relative):
    for bit in range(1, links.mp_bits):
        split = values.reshape(-1, 2, *values.shape[1:])
        if relative:
            keep, send = split[:, 0], split[:, 1]
        else:
            mine = (links.mp >> bit) & 1
            keep = jnp.where(mine == 0, split[:, 0], split[:, 1])
            send = jnp.where(mine == 0, split[:, 1], split[:, 0])
        received = links.mp_swap(send, bit)
        if bit == links.mp_bits - 1:
            return (keep.astype(f32) + received.astype(f32))[0]
        values = add_b(keep, received)


def gather_small(links, values):
    current = values[None]
    for bit in range(links.mp_bits):
        received = links.mp_swap(current, bit)
        current = jnp.where(
            (links.mp >> bit) & 1 == 0,
            jnp.concatenate([current, received], 0),
            jnp.concatenate([received, current], 0),
        )
    for bit in range(links.dp_bits):
        received = links.dp_swap(current, bit)
        current = jnp.where(
            (links.dp >> bit) & 1 == 0,
            jnp.concatenate([current, received], 0),
            jnp.concatenate([received, current], 0),
        )
    return current.reshape(links.ndp, links.nmp, -1)


def norm_parts(values):
    center = values - jnp.mean(values, axis=-1, keepdims=True)
    spread = jnp.mean(center * center, axis=-1, keepdims=True)
    inverse = lax.rsqrt(spread + 1e-05)
    return center * inverse, inverse


def norm_back(grad, unit, inverse, gain):
    scaled = grad * gain
    return (
        scaled
        - jnp.mean(scaled, axis=-1, keepdims=True)
        - unit * jnp.mean(scaled * unit, axis=-1, keepdims=True)
    ) * inverse


def dot(left, right):
    return jnp.dot(left, right, preferred_element_type=f32)


def dot_nt(left, right):
    return lax.dot_general(left, right, NT, preferred_element_type=f32)


def dot_tn(left, right):
    return lax.dot_general(left, right, TN, preferred_element_type=f32)


def body(
    tokens, cotangent, first_gain, second_gain, w_query, w_key, w_value, w_out, w_up, w_down,
    state_rate, state_in, state_out, state_bank, prev_link,
):
    links = Links()
    ndp, nmp, nz = links.ndp, links.nmp, links.nz
    rows = tokens.shape[0]
    per_window = LEN // BLK
    place_in = links.mp % per_window
    window = links.dp * (nmp // per_window) + links.mp // per_window
    link = lax.dynamic_index_in_dim(prev_link, window, keepdims=False)
    info = jnp.stack([links.block_at(p) for p in range(ndp)] + [links.z]).astype(jnp.int32)
    attend_info = jnp.stack([links.core, (place_in != 0).astype(jnp.int32)]).astype(jnp.int32)

    channels = state_rate.shape[0]
    maps_here = state_rate.shape[1]
    banks_here = state_bank.shape[0]
    pieces = [
        first_gain,
        second_gain,
        state_rate.T.reshape(-1),
        state_in.T.reshape(-1),
        state_out.T.reshape(-1),
        state_bank.transpose(0, 2, 1).reshape(-1),
    ]
    sizes = [piece.shape[0] for piece in pieces]
    packed = jnp.concatenate(pieces)
    packed = jnp.pad(packed, (0, -packed.shape[0] % 128)).reshape(-1, 128)
    small = gather_small(links, packed)
    starts = [sum(sizes[:i]) for i in range(len(sizes))]
    parts = [small[:, :, a : a + n] for a, n in zip(starts, sizes)]
    gain_one = lax.reduce_precision(parts[0].reshape(1, D), 8, 7)
    gain_two = lax.reduce_precision(parts[1].reshape(1, D), 8, 7)

    def full_map(values):
        values = values.reshape(ndp, nmp, maps_here, channels).transpose(0, 2, 1, 3)
        return values.reshape(NS, 8, 128)

    rate, gain_in, gain_out = (full_map(part) for part in parts[2:5])
    banks = parts[5].reshape(ndp, nmp, banks_here, NS, channels)
    bank = lax.dynamic_index_in_dim(banks, link // banks_here, 0, keepdims=False)
    bank = lax.dynamic_index_in_dim(bank, link % banks_here, 1, keepdims=False)
    initial = bank.transpose(1, 0, 2).reshape(NS, 8, 128)

    mats = jnp.stack([w_query, w_key, w_value, w_out], 1).astype(bf16)
    mats = mats.reshape(mats.shape[0], 4, 2, HALF)
    mats_keep = jnp.where(links.core == 0, mats[:, :, 0], mats[:, :, 1])
    mats_send = jnp.where(links.core == 0, mats[:, :, 1], mats[:, :, 0])
    mats_keep = mats_keep.reshape(-1, 4 * HALF)
    mats_send = mats_send.reshape(-1, 4 * HALF)
    mats_pair = by_core(links, mats_keep, links.core_swap(mats_send), 0)
    w_own = place(links, info, *gather_dp(links, gather_z(links, mats_pair)))
    w_other = links.core_swap(w_own)

    chunk = FF // nmp
    groups = 2 if chunk >= 256 else 1
    width = chunk // groups
    both = jnp.stack([w_up, w_down.T], 1).astype(bf16)
    both = both.reshape(both.shape[0], 2, nz, 2, groups, width)
    ff_keep = jnp.where(links.core == 0, both[:, :, :, 0], both[:, :, :, 1])
    ff_send = jnp.where(links.core == 0, both[:, :, :, 1], both[:, :, :, 0])

    def feed_group(values, g):
        return values[:, :, :, g].reshape(-1, 2 * nz * width)

    ff_pair = [
        by_core(links, feed_group(ff_keep, g), links.core_swap(feed_group(ff_send, g)), 0)
        for g in range(groups)
    ]
    ff_weights = [gather_dp(links, gather_z(links, pair)) for pair in ff_pair]

    token_f = tokens.astype(f32)
    unit_one, inverse_one = norm_parts(token_f)
    normed_b = (unit_one * gain_one).astype(bf16)
    tail = links.window_shift(normed_b[OWN:], 1)
    scan_own = state_scan(normed_b[:OWN], rate)
    scan_tail = state_scan(tail, rate)

    def decay_by(steps):
        return jnp.exp(-rate * steps)

    def forward(state, steps):
        far = decay_by(steps)
        near = decay_by(steps - 1.0) * steps
        return jnp.stack([far * state[0], far * state[1] + near * state[0]])

    total = forward(scan_tail, float(OWN)) + scan_own
    before = jnp.zeros_like(total)
    for bit in range(bits_of(per_window)):
        received = links.mp_swap(total, bit)
        mine = (links.mp >> bit) & 1
        inside = (place_in % (1 << bit)).astype(f32) * BLK
        before = before + jnp.where(mine == 1, forward(received, inside), 0.0)
        low = jnp.where(mine == 1, received, total)
        high = jnp.where(mine == 1, total, received)
        total = forward(low, float(BLK << bit)) + high
    decay = decay_by(1.0)
    tail_start = place_in.astype(f32) * BLK - CTX
    inside_window = (place_in != 0).astype(f32)
    carried = decay_by(tail_start) * initial * inside_window
    context = context_states(
        tail, gain_out * (gain_in * before[0] + carried), decay, gain_out * gain_in
    )

    qkv_own = dot(normed_b, w_own[:, : 3 * HALF]).astype(bf16)
    qkv_other = dot(normed_b, w_other[:, : 3 * HALF]).astype(bf16)
    ctx_own = dot(context, w_own[:, HALF : 3 * HALF]).astype(bf16)
    ctx_other = dot(context, w_other[:, HALF : 3 * HALF]).astype(bf16)
    attended = attend(attend_info, qkv_own, qkv_other, ctx_own, ctx_other)
    out_own = w_own[:, 3 * HALF :]
    out_other = w_other[:, 3 * HALF :]
    middle = token_f + by_core(links, dot(attended, out_own), dot(attended, out_other), 1)
    unit_two, inverse_two = norm_parts(middle)
    second_b = (unit_two * gain_two).astype(bf16)

    second_par = links.core_swap(second_b)
    cot_par = links.core_swap(cotangent)
    acts = (
        second_b, second_par, cotangent, cot_par, second_b.T, second_par.T, cotangent.T, cot_par.T,
    )
    scattered = []
    earlier = None
    for g in range(groups):
        last = g == groups - 1
        *sums, keep, send = feed(links, info, acts, ff_weights[g], earlier, last)
        earlier = sums
        scattered.append((keep, send))
    mix_own, mix_par, back_own, back_par = earlier
    mixed = (middle + (mix_own + links.core_swap(mix_par).astype(f32))).astype(bf16)
    grad_second = back_own + links.core_swap(back_par).astype(f32)
    ff_shares = [
        scatter_z(links, scatter_dp(links, keep, send), True) for keep, send in scattered
    ]
    grad_up = jnp.concatenate([share[0] for share in ff_shares], 1)
    grad_down = jnp.concatenate([share[1] for share in ff_shares], 1).T

    grad_gain_two = jnp.sum(grad_second * unit_two, axis=0)
    grad_middle = cotangent.astype(f32) + norm_back(grad_second, unit_two, inverse_two, gain_two)
    grad_branch = grad_middle.astype(bf16)
    branch_halves = grad_branch.reshape(rows, 2, HALF)
    branch_own = jnp.where(links.core == 0, branch_halves[:, 0], branch_halves[:, 1])
    branch_other = jnp.where(links.core == 0, branch_halves[:, 1], branch_halves[:, 0])
    grad_attended = (dot_nt(branch_own, out_own) + dot_nt(branch_other, out_other)).astype(bf16)
    g_own, g_other = attend_back(
        attend_info, qkv_own, qkv_other, ctx_own, ctx_other, grad_attended
    )
    grad_context = (
        dot_nt(g_own[:CTX, HALF:], w_own[:, HALF : 3 * HALF])
        + dot_nt(g_other[:CTX, HALF:], w_other[:, HALF : 3 * HALF])
    ).astype(bf16)

    sums = state_sums(grad_context, tail, before, decay)
    far = decay_by(tail_start)
    sum_init = far * decay * sums[2]
    sum_slope = far * ((tail_start + 1.0) * sums[2] + decay * sums[3])
    init_here = initial * inside_window
    grad_in = gain_out * sums[0]
    grad_out_map = gain_in * sums[0] + init_here * sum_init
    grad_rate = -decay * gain_out * (gain_in * sums[1] + init_here * sum_slope)
    grad_initial = gain_out * sum_init * inside_window

    total_back = sums[2]
    after = jnp.zeros_like(total_back)
    for bit in range(bits_of(per_window)):
        received = links.mp_swap(total_back, bit)
        mine = (links.mp >> bit) & 1
        inside = ((1 << bit) - 1 - place_in % (1 << bit)).astype(f32) * BLK
        after = after + jnp.where(mine == 0, decay_by(inside) * received, 0.0)
        low = jnp.where(mine == 1, received, total_back)
        high = jnp.where(mine == 1, total_back, received)
        total_back = low + decay_by(float(BLK << bit)) * high
    weight = gain_in * gain_out
    back_start = weight * after
    tail_sent = sent_tail(grad_context, decay_by(float(OWN)) * back_start, decay, weight)
    own_sent = sent_own(back_start, decay)
    last_sent = links.window_shift(tail_sent, -1)
    grad_sent = jnp.concatenate([own_sent, last_sent], 0)

    def by_owner(values):
        values = values.reshape(ndp, maps_here, nmp, channels).transpose(0, 2, 1, 3)
        return values.reshape(ndp, nmp, -1)

    chosen = jnp.arange(ndp * banks_here, dtype=jnp.int32) == link
    bank_share = grad_initial.reshape(NS, nmp, channels).transpose(1, 0, 2)[None]
    bank_share = jnp.where(chosen[:, None, None, None], bank_share, 0.0)
    bank_share = bank_share.reshape(ndp, banks_here, nmp, NS * channels).transpose(0, 2, 1, 3)
    shares = jnp.concatenate(
        [
            by_owner(grad_rate),
            by_owner(grad_in),
            by_owner(grad_out_map),
            bank_share.reshape(ndp, nmp, -1),
            grad_gain_two.reshape(ndp, nmp, -1),
        ],
        2,
    ).astype(bf16)
    share_len = shares.shape[2]
    line = 4 * HALF
    shares = jnp.pad(shares, ((0, 0), (0, 0), (0, -share_len % line)))
    shares = shares.reshape(ndp, nz, 2, -1, line)
    shares_keep = jnp.where(links.core == 0, shares[:, :, 0], shares[:, :, 1])
    shares_send = jnp.where(links.core == 0, shares[:, :, 1], shares[:, :, 0])
    shares = add_b(shares_keep, links.core_swap(shares_send))

    inputs_kv = jnp.concatenate([context, normed_b], 0)
    inputs_par = links.core_swap(inputs_kv)
    attended_par = links.core_swap(attended)
    g_par = links.core_swap(g_other)
    branch_par = links.core_swap(branch_other)
    grad_qkv = (dot_tn(inputs_kv, g_own) + dot_tn(inputs_par, g_par)).astype(bf16)
    grad_out = (dot_tn(attended, branch_own) + dot_tn(attended_par, branch_par)).astype(bf16)
    mat_rows = D // (ndp * nz)
    grad_mats = jnp.concatenate([grad_qkv, grad_out], 1).reshape(ndp, nz, mat_rows, line)
    grad_mats = jnp.concatenate([grad_mats, shares], 2)

    def blocks(first, count):
        return jnp.concatenate(
            [
                lax.dynamic_slice_in_dim(grad_mats, links.block_at(first + p), 1, 0)
                for p in range(count)
            ],
            0,
        )

    half = ndp // 2
    mats_share = scatter_z(
        links, scatter_dp(links, blocks(0, half), blocks(half, half)), False
    )
    flat = mats_share[mat_rows:].reshape(-1)[:share_len]
    map_size = maps_here * channels
    grad_maps = [
        flat[i * map_size : (i + 1) * map_size].reshape(maps_here, channels).T for i in range(3)
    ]
    bank_end = share_len - D // (ndp * nmp)
    grad_bank = flat[3 * map_size : bank_end].reshape(banks_here, NS, channels)
    grad_bank = grad_bank.transpose(0, 2, 1)
    share_two = flat[bank_end:]
    mine_rows = mats_share[:mat_rows].reshape(2, mat_rows // 2, 4, HALF)
    rows_keep = jnp.where(links.core == 0, mine_rows[0], mine_rows[1])
    rows_send = jnp.where(links.core == 0, mine_rows[1], mine_rows[0])
    grad_rows = by_core(links, rows_keep, links.core_swap(rows_send), 2)

    grad_normed = (
        dot_nt(g_own[CTX:], w_own[:, : 3 * HALF])
        + dot_nt(g_other[CTX:], w_other[:, : 3 * HALF])
        + grad_sent.astype(f32)
    )
    grad_gain_one = jnp.sum(grad_normed * unit_one, axis=0)
    grad_tokens = (grad_middle + norm_back(grad_normed, unit_one, inverse_one, gain_one)).astype(bf16)
    gain_parts = lax.all_to_all(
        grad_gain_one.reshape(ndp * nmp, -1), AXES, split_axis=0, concat_axis=0, tiled=True
    )
    share_one = jnp.sum(gain_parts, axis=0)
    return (
        mixed, grad_tokens, share_one, share_two,
        grad_rows[:, 0], grad_rows[:, 1], grad_rows[:, 2], grad_rows[:, 3],
        grad_up, grad_down, grad_maps[0], grad_maps[1], grad_maps[2], grad_bank,
    )


def solution(mesh):
    split = P(AXES, None)
    gain = P(AXES)
    maps = P("mp", "dp")
    bank = P("dp", "mp", None)
    return jax.shard_map(
        body,
        mesh=mesh,
        in_specs=(
            split, split, gain, gain, split, split, split, split, split, P(None, AXES),
            maps, maps, maps, bank, P(),
        ),
        out_specs=(
            split, split, gain, gain, split, split, split, split, P("dp", "mp"), P("mp", "dp"),
            maps, maps, maps, bank,
        ),
        check_vma=False,
    )
```

time: 1370 us -> 541 us (0.39)
  waiting for transfers between devices: 766 us -> 98.9 us
  Pallas kernels: 0 us -> 216 us
  matrix products: 217 us -> 38.9 us
  blocking collectives: 130 us -> 0 us
  other arithmetic: 134 us -> 62.3 us
  starting transfers between devices: 28.6 us -> 60.5 us
  local copies, waits for them, and re-layouts: 66.7 us -> 51.2 us
    reduce_scatter x6 -> x0, waiting for transfers between devices: 340 us -> none  [the longest x1 142 us: body(): lax.psum_scatter(grad_value_w, ('dp', 'mp'), scatter_dimension=0, tiled=T...]
    all_to_all x6 -> x1, waiting for transfers between devices: 244 us -> 0.01 us  [body(): lax.all_to_all(grad_gain_one.reshape(ndp * nmp, -1), AXES, split_axis=0,...]
    pallas_call x0 -> x11, Pallas kernels: none -> 216 us  [the longest x1 129 us: place(): pl.pallas_call(functools.partial(place_kernel, ndp, half, block), out_sha...]
    all_gather x8 -> x0, waiting for transfers between devices: 181 us -> none  [the longest x1 73.2 us: body(): lax.all_gather(w_up.astype(half), ('dp', 'mp'), axis=0, tiled=True)]
    dot_general x44 -> x16, matrix products: 217 us -> 38.9 us  [the longest x6 16.3 us: dot_nt(): return lax.dot_general(left, right, NT, preferred_element_type=f32)]
    ppermute x0 -> x51, waiting for transfers between devices: none -> 98.9 us  [send(): return lax.ppermute(values, AXES, pairs)]
    unnamed x3 -> x0, blocking collectives: 98.8 us -> none
    add_any x65 -> x0, other arithmetic: 65.5 us -> none  [the longest x64 64.6 us: advance(): return (jump_decay * state_now + pushed_in, state_now)]
  transfers between devices with their start and end apart: 20 -> 52, of which waited for: 10 -> 17; matrix products, arithmetic and copies ran while one was open for 29% -> 26% of each run, Pallas kernels for 0% -> 36%
where the time goes in v1:
time: 541 us; the launch traced here: 532 us
  Pallas kernels  216 us (40%)
  waiting for transfers between devices  98.9 us (18%)
  other arithmetic  62.3 us (12%)
  starting transfers between devices  60.5 us (11%)
  local copies, waits for them, and re-layouts  51.2 us (9%)
  matrix products  38.9 us (7%)
    pallas_call x1, Pallas kernels, place(): pl.pallas_call(functools.partial(place_kernel, ndp, half, block), out_sha...  129 us
    ppermute x51, waiting for transfers between devices, send(): return lax.ppermute(values, AXES, pairs)  98.9 us
    ppermute x51, starting transfers between devices, send(): return lax.ppermute(values, AXES, pairs)  55.3 us
    pallas_call x2, Pallas kernels, feed(): pl.pallas_call(functools.partial(feed_kernel, ndp, nz, width, bool(earlie...  47.2 us
    dot_general x6, matrix products, dot_nt(): return lax.dot_general(left, right, NT, preferred_element_type=f32)  16.3 us
    unnamed x134, local copies, waits for them, and re-layouts  15.9 us
    pallas_call x1, Pallas kernels, attend_back(): pl.pallas_call(attend_back_kernel, out_shape=(out, out), in_specs=[SMEM]...  13.4 us
    convert_element_type x7, other arithmetic, add_b(): return (left.astype(f32) + right.astype(f32)).astype(bf16)  13.4 us
  transfers between devices with their start and end apart: 52, of which 17 were waited for; matrix products, arithmetic and copies ran while one was open for 26% of the time, Pallas kernels for 36%

profile of v1, /device:TPU:0, one launch (start us, length us, event | category | flops | bytes accessed | tf_op | source)
XLA Modules:
  0.0 532.4 jit_solution(742919244979910364)
XLA Ops:
  11.5 3.7 collective-permute-start.6
  22.2 2.4 collective-permute-start.2
  24.6 4.1 collective-permute-done.6
  32.3 2.9 collective-permute-start.23
  35.2 12.7 %collective-permute-done.7 = bf16[2,64,2048]{2,1,0:T(8,128)(2,1)S(1)} collective-permute-done((bf16[2,64,2048]{2,1,0:T(8,128)(2,1)S(1)}, bf16[2,64,2048]{2,1,0:T(8,128)(2,1)S(1)}, u32[]{:S(2)}, u32[]{:S(2)}) %collective-permute-start.7) | collective-permute-done | bytes 524320 | tf_op jit(solution)/shard_map/ppermute | solution.py:69
  49.8 2.7 collective-permute-start.18
  53.9 2.5 collective-permute-start.24
  56.4 7.1 %collective-permute-done.18 = bf16[1,64,2048]{2,1,0:T(8,128)(2,1)S(1)} collective-permute-done((bf16[1,64,2048]{2,1,0:T(8,128)(2,1)S(1)}, bf16[1,64,2048]{2,1,0:T(8,128)(2,1)S(1)}, u32[]{:S(2)}, u32[]{:S(2)}) %collective-permute-start.18) | collective-permute-done | bytes 262176 | tf_op jit(solution)/shard_map/ppermute | solution.py:69
  75.3 4.6 state_scan.3
  81.7 2.4 collective-permute-start.12
  84.1 9.6 %collective-permute-done.9.high = bf16[2,256,2048]{2,1,0:T(8,128)(2,1)} collective-permute-done((bf16[2,256,2048]{2,1,0:T(8,128)(2,1)}, bf16[2,256,2048]{2,1,0:T(8,128)(2,1)}, u32[]{:S(2)}, u32[]{:S(2)}) %collective-permute-start.9) | collective-permute-done | bytes 2097184 | tf_op jit(solution)/shard_map/ppermute | solution.py:69
  93.8 128.9 %place.1 = bf16[1024,2048]{1,0:T(8,128)(2,1)} custom-call(s32[5]{0:T(128)} %stack.171.info, bf16[2,256,2048]{2,1,0:T(8,128)(2,1)} %pad_maximum_fusion.2.low, bf16[2,256,2048]{2,1,0:T(8,128)(2,1)} %collective-permute-done.9.high), custom_call_target="tpu_custom_call" | custom-call | bytes 8388608 | tf_op jit(solution)/shard_map/place/pallas_call | solution.py:590
  231.4 4.0 collective-permute-start.14
  235.4 6.1 %collective-permute-done.14 = f32[2,16,8,128]{3,2,1,0:T(8,128)S(1)} collective-permute-done((f32[2,16,8,128]{3,2,1,0:T(8,128)S(1)}, f32[2,16,8,128]{3,2,1,0:T(8,128)S(1)}, u32[]{:S(2)}, u32[]{:S(2)}) %collective-permute-start.14) | collective-permute-done | bytes 131104 | tf_op jit(solution)/shard_map/ppermute | solution.py:69
  241.6 2.1 context_states.1
  247.1 1.8 convolution_convert_fusion.1.own_ref
  249.0 2.6 fusion.36.ctx_other_ref
  251.6 3.7 convolution_convert_fusion.other_ref
  255.3 8.0 %attend.1 = bf16[512,1024]{1,0:T(8,128)(2,1)S(1)} custom-call(s32[2]{0:T(128)S(1)} %pad_add_fusion.info, bf16[512,1536]{1,0:T(8,128)(2,1)S(1)} %convolution_convert_fusion.1.own_ref, bf16[512,1536]{1,0:T(8,128)(2,1)S(1)} %convolution_convert_fusion.other_ref, bf16[128,1024]{1,0:T(8,128)(2,1)S(1)} %fusion.33.ctx_own_ref, ...), custom_call_target="tpu_custom_call" | custom-call | flops 1342177280 | bytes 6291456 | tf_op jit(solution)/shard_map/attend/pallas_call | solution.py:339
  264.0 1.9 fusion.51
  270.1 2.3 copy.253.c_par
  272.3 2.9 fusion.122
  275.2 2.3 copy.254.st_own
  277.5 2.3 copy.255.st_par
  279.8 23.8 %feed_first.1 = (f32[1024,1024]{1,0:T(8,128)}, f32[1024,1024]{1,0:T(8,128)}, bf16[2,4,2,256,256]{4,3,2,1,0:T(8,128)(2,1)}, bf16[2,4,2,256,256]{4,3,2,1,0:T(8,128)(2,1)}) custom-call(s32[5]{0:T(128)} %stack.171.info, bf16[512,1024]{1,0:T(8,128)(2,1)} %multiply_convert_fusion.s_own, bf16[512,1024]{1,0:T(8,128)(2,1)} %collective-permute-done.15.s_par, ...), custom_call_target="tpu_custom_call" | custom-call | flops 12884901888 | bytes 31457280 | tf_op jit(solution)/shard_map/feed_first/pallas_call | solution.py:547
  303.6 23.5 %feed_last.1 = (f32[512,1024]{1,0:T(8,128)}, bf16[512,1024]{1,0:T(8,128)(2,1)}, f32[512,1024]{1,0:T(8,128)}, bf16[512,1024]{1,0:T(8,128)(2,1)}, bf16[2,4,2,256,2...) custom-call(s32[5]{0:T(128)} %stack.171.info, bf16[512,1024]{1,0:T(8,128)(2,1)} %multiply_convert_fusion.s_own, ...), custom_call_target="tpu_custom_call" | custom-call | flops 12884901888 | bytes 31457280 | tf_op jit(solution)/shard_map/feed_last/pallas_call | solution.py:547
  329.8 2.4 pad_maximum_fusion.5
  334.7 3.5 multiply_reduce_fusion
  338.2 3.8 fusion.96
  342.1 2.6 reshape.1254
  344.7 3.4 fusion.100
  348.3 2.2 fusion.49
  352.7 13.4 %attend_back.1 = (bf16[640,1536]{1,0:T(8,128)(2,1)S(1)}, bf16[640,1536]{1,0:T(8,128)(2,1)}) custom-call(s32[2]{0:T(128)S(1)} %pad_add_fusion.info, bf16[512,1536]{1,0:T(8,128)(2,1)S(1)} %copy-done.3, bf16[512,1536]{1,0:T(8,128)(2,1)S(1)} %copy-done.5, bf16[128,1024]{1,0:T(8,128)(2,1)S(1)} %fusion.33.ctx_own_ref, bf16[128,1024]{1,0:T(8,128)(2,1)S(1)} %fusion.36.ctx_other_ref, ...), custom_call_target="tpu_custom_call" | custom-call | flops 3355443200 | bytes 10485760 | tf_op jit(solution)/shard_map/attend_back/pallas_call | solution.py:390
  366.1 3.2 fusion.20
  370.2 4.4 state_sums.1
  376.3 5.5 %fusion = f32[512,1024]{1,0:T(8,128)} fusion(bf16[1024,2048]{1,0:T(8,128)(2,1)} %collective-permute-done.10, bf16[640,1536]{1,0:T(8,128)(2,1)} %get-tuple-element.33), kind=kOutput, calls=%fused_computation.18 | convolution fusion | flops 1610612736 | bytes 6815744 | tf_op jit(solution)/shard_map/dot_general | solution.py:693
  381.8 2.1 fusion.60
  387.8 4.2 collective-permute-done.30
  393.5 2.2 collective-permute-start.31
  395.9 4.0 collective-permute-done.31
  399.9 2.1 sent_tail.1
  402.0 3.6 sent_own.1
  407.3 2.0 add_convert_fusion.7
  409.3 2.2 add_convert_fusion.3
  414.3 2.2 add_convert_fusion.2
  419.6 4.5 fusion.108
  424.1 2.9 add_convert_fusion
  427.7 1.7 fusion.45
  429.7 3.1 copy.265
  433.7 3.8 fusion.18
  438.2 5.2 all-to-all-start
  446.0 2.0 copy.288
  448.0 1.9 collective-permute-start.45
  453.4 9.0 %collective-permute-done.38 = bf16[2,4,66,2048]{3,1,2,0:T(4,128)(2,1)} collective-permute-done((bf16[2,4,66,2048]{3,1,2,0:T(4,128)(2,1)}, bf16[2,4,66,2048]{3,1,2,0:T(4,128)(2,1)}, u32[]{:S(2)}, u32[]{:S(2)}) %collective-permute-start.38) | collective-permute-done | bytes 2162720 | tf_op jit(solution)/shard_map/ppermute | solution.py:69
  462.5 3.8 add_convert_fusion.1
  466.4 1.8 copy.267
  468.9 1.7 fusion.17
  479.1 4.6 collective-permute-done.39
  483.7 2.0 add_convert_fusion.4
  486.6 9.7 %collective-permute-done.46 = bf16[1,2,256,256]{2,3,1,0:T(8,128)(2,1)S(1)} collective-permute-done((bf16[1,2,256,256]{2,3,1,0:T(8,128)(2,1)S(1)}, bf16[1,2,256,256]{2,3,1,0:T(8,128)(2,1)S(1)}, u32[]{:S(2)}, u32[]{:S(2)}) %collective-permute-start.46) | collective-permute-done | bytes 262176 | tf_op jit(solution)/shard_map/ppermute | solution.py:69
  496.4 4.5 collective-permute-done.50
  500.9 9.5 %collective-permute-done.40 = bf16[2,66,2048]{2,0,1:T(2,128)(2,1)S(1)} collective-permute-done((bf16[2,66,2048]{2,0,1:T(2,128)(2,1)S(1)}, bf16[2,66,2048]{2,0,1:T(2,128)(2,1)S(1)}, u32[]{:S(2)}, u32[]{:S(2)}) %collective-permute-start.40) | collective-permute-done | bytes 540704 | tf_op jit(solution)/shard_map/ppermute | solution.py:69
  510.9 2.0 collective-permute-start.41
  514.8 11.5 %collective-permute-done.41 = bf16[1,66,2048]{2,1,0:T(8,128)(2,1)S(1)} collective-permute-done((bf16[1,66,2048]{2,1,0:T(8,128)(2,1)S(1)}, bf16[1,66,2048]{2,1,0:T(8,128)(2,1)S(1)}, u32[]{:S(2)}, u32[]{:S(2)}) %collective-permute-start.41) | collective-permute-done | bytes 270368 | tf_op jit(solution)/shard_map/ppermute | solution.py:69
  (364 shorter events, 102.5 us)
Async XLA Ops:
  4.7 27.5 %collective-permute-start.22 = (bf16[32,2048]{1,0:T(8,128)(2,1)}, bf16[32,2048]{1,0:T(8,128)(2,1)S(1)}, u32[]{:S(2)}, u32[]{:S(2)}) collective-permute-start(bf16[32,2048]{1,0:T(8,128)(2,1)} %reshape_squeeze.18), channel_id=1, source_target_pairs={{0,1},{1,0},{2,3},{3,2},{4,5},{5,4},{6,7},{7,6},{8,9},{9,8},{10,11... | collective-permute-start | bytes 393224 | tf_op jit(solution)/shard_map/ppermute | solution.py:69
  6.5 8.7 %collective-permute-start = (f32[1,29,128]{2,1,0:T(8,128)}, f32[1,29,128]{2,1,0:T(8,128)}, u32[]{:S(2)}, u32[]{:S(2)}) collective-permute-start(f32[1,29,128]{2,1,0:T(8,128)} %pad_bitcast_fusion), channel_id=1, source_target_pairs={{0,1},{1,0},{2,3},{3,2},{4,5},{5,4},{6,7},{7,6},{8,9},{9,8},{10,11... | collective-permute-start | bytes 44552 | tf_op jit(solution)/shard_map/ppermute | solution.py:69
  8.0 3.5 collective-permute-start.5
  9.8 7.9 %copy-start.56 = (s32[4]{0:T(128)S(1)}, s32[4]{0:T(128)}, u32[]{:S(2)}) copy-start(s32[4]{0:T(128)} %param.29) | copy-start | bytes 52
  9.8 260.3 %collective-permute-start.16 = (bf16[512,1024]{0,1:T(8,128)(2,1)}, bf16[512,1024]{0,1:T(8,128)(2,1)}, u32[]{:S(2)}, u32[]{:S(2)}) collective-permute-start(bf16[512,1024]{0,1:T(8,128)(2,1)} %copy.241), channel_id=1, source_target_pairs={{0,1},{1,0},{2,3},{3,2},{4,5},{5,4},{6,7},{7,6},{8,9},{9,8},{10,11... | collective-permute-start | bytes 3145736 | tf_op jit(solution)/shard_map/ppermute | solution.py:69
  10.0 39.7 %collective-permute-start.17 = (bf16[32,2048]{1,0:T(8,128)(2,1)S(1)}, bf16[32,2048]{1,0:T(8,128)(2,1)S(1)}, u32[]{:S(2)}, u32[]{:S(2)}) collective-permute-start(bf16[32,2048]{1,0:T(8,128)(2,1)S(1)} %reshape_squeeze.17), channel_id=1, source_target_pairs={{0,1},{1,0},{2,3},{3,2},{4,5},{5,4},{6,7},{7,6},{8,9},{9,8},{10,11... | collective-permute-start | bytes 393224 | tf_op jit(solution)/shard_map/ppermute | solution.py:69
  10.7 60.6 %copy-start.47 = (f32[512]{0:T(512)}, f32[512]{0:T(512)S(1)}, u32[]{:S(2)}) copy-start(f32[512]{0:T(512)S(1)} %broadcast_multiply_fusion.5) | copy-start | bytes 6148
  11.5 59.9 %copy-start.49 = (f32[512]{0:T(512)}, f32[512]{0:T(512)S(1)}, u32[]{:S(2)}) copy-start(f32[512]{0:T(512)S(1)} %add_rsqrt_fusion.1) | copy-start | bytes 6148
  11.5 17.2 %collective-permute-start.6 = (bf16[1,64,2048]{2,1,0:T(8,128)(2,1)S(1)}, bf16[1,64,2048]{2,1,0:T(8,128)(2,1)S(1)}, u32[]{:S(2)}, u32[]{:S(2)}) collective-permute-start(bf16[1,64,2048]{2,1,0:T(8,128)(2,1)S(1)} %maximum_select_fusion.11), channel_id=1, source_target_pairs={{0,4},{1,5},{2,6},{3,7},{4,0},{5,1},{6,2},{7,3},{8,12},{9,13},{10,... | collective-permute-start | bytes 786440 | tf_op jit(solution)/shard_map/ppermute | solution.py:69
  16.0 6.1 %collective-permute-start.1 = (f32[2,29,128]{2,1,0:T(8,128)S(1)}, f32[2,29,128]{2,1,0:T(8,128)S(1)}, u32[]{:S(2)}, u32[]{:S(2)}) collective-permute-start(f32[2,29,128]{2,1,0:T(8,128)S(1)} %maximum_select_fusion.19), channel_id=1, source_target_pairs={{0,2},{1,3},{2,0},{3,1},{4,6},{5,7},{6,4},{7,5},{8,10},{9,11},{10,... | collective-permute-start | bytes 89096 | tf_op jit(solution)/shard_map/ppermute | solution.py:69
  22.2 8.4 %collective-permute-start.2 = (f32[4,29,128]{2,1,0:T(8,128)S(1)}, f32[4,29,128]{2,1,0:T(8,128)S(1)}, u32[]{:S(2)}, u32[]{:S(2)}) collective-permute-start(f32[4,29,128]{2,1,0:T(8,128)S(1)} %maximum_select_fusion.18), channel_id=1, source_target_pairs={{0,4},{1,5},{2,6},{3,7},{4,0},{5,1},{6,2},{7,3},{8,12},{9,13},{10,... | collective-permute-start | bytes 178184 | tf_op jit(solution)/shard_map/ppermute | solution.py:69
  28.8 19.2 %collective-permute-start.7 = (bf16[2,64,2048]{2,1,0:T(8,128)(2,1)S(1)}, bf16[2,64,2048]{2,1,0:T(8,128)(2,1)S(1)}, u32[]{:S(2)}, u32[]{:S(2)}) collective-permute-start(bf16[2,64,2048]{2,1,0:T(8,128)(2,1)S(1)} %maximum_select_fusion.5), channel_id=1, source_target_pairs={{0,2},{1,3},{2,0},{3,1},{4,6},{5,7},{6,4},{7,5},{8,10},{9,11},{10,... | collective-permute-start | bytes 1572872 | tf_op jit(solution)/shard_map/ppermute | solution.py:69
  30.6 21.9 %collective-permute-start.3 = (f32[8,29,128]{2,1,0:T(8,128)S(1)}, f32[8,29,128]{2,1,0:T(8,128)S(1)}, u32[]{:S(2)}, u32[]{:S(2)}) collective-permute-start(f32[8,29,128]{2,1,0:T(8,128)S(1)} %maximum_select_fusion.14), channel_id=1, source_target_pairs={{0,8},{1,9},{2,10},{3,11},{4,12},{5,13},{6,14},{7,15},{8,0},{9,1},... | collective-permute-start | bytes 356360 | tf_op jit(solution)/shard_map/ppermute | solution.py:69
  32.3 20.8 %collective-permute-start.23 = (bf16[1,64,2048]{2,1,0:T(8,128)(2,1)S(1)}, bf16[1,64,2048]{2,1,0:T(8,128)(2,1)S(1)}, u32[]{:S(2)}, u32[]{:S(2)}) collective-permute-start(bf16[1,64,2048]{2,1,0:T(8,128)(2,1)S(1)} %maximum_select_fusion.13), channel_id=1, source_target_pairs={{0,4},{1,5},{2,6},{3,7},{4,0},{5,1},{6,2},{7,3},{8,12},{9,13},{10,... | collective-permute-start | bytes 786440 | tf_op jit(solution)/shard_map/ppermute | solution.py:69
  48.3 17.7 %collective-permute-start.8 = (bf16[1,256,2048]{2,1,0:T(8,128)(2,1)S(1)}, bf16[1,256,2048]{2,1,0:T(8,128)(2,1)S(1)}, u32[]{:S(2)}, u32[]{:S(2)}) collective-permute-start(bf16[1,256,2048]{2,1,0:T(8,128)(2,1)S(1)} %bitcast.310), channel_id=1, source_target_pairs={{0,16},{1,9},{2,18},{3,11},{4,20},{5,13},{6,22},{7,15},{8,24},{9,1... | collective-permute-start | bytes 3145736 | tf_op jit(solution)/shard_map/ppermute | solution.py:69
  49.8 13.8 %collective-permute-start.18 = (bf16[1,64,2048]{2,1,0:T(8,128)(2,1)S(1)}, bf16[1,64,2048]{2,1,0:T(8,128)(2,1)S(1)}, u32[]{:S(2)}, u32[]{:S(2)}) collective-permute-start(bf16[1,64,2048]{2,1,0:T(8,128)(2,1)S(1)} %maximum_select_fusion.12), channel_id=1, source_target_pairs={{0,4},{1,5},{2,6},{3,7},{4,0},{5,1},{6,2},{7,3},{8,12},{9,13},{10,... | collective-permute-start | bytes 786440 | tf_op jit(solution)/shard_map/ppermute | solution.py:69
  52.5 16.4 %collective-permute-start.4 = (f32[16,29,128]{2,1,0:T(8,128)S(1)}, f32[16,29,128]{2,1,0:T(8,128)S(1)}, u32[]{:S(2)}, u32[]{:S(2)}) collective-permute-start(f32[16,29,128]{2,1,0:T(8,128)S(1)} %maximum_select_fusion.10), channel_id=1, source_target_pairs={{0,16},{1,17},{2,18},{3,19},{4,20},{5,21},{6,22},{7,23},{8,24},{9,... | collective-permute-start | bytes 712712 | tf_op jit(solution)/shard_map/ppermute | solution.py:69
  53.9 172.1 %collective-permute-start.24 = (bf16[2,64,2048]{2,1,0:T(8,128)(2,1)}, bf16[2,64,2048]{2,1,0:T(8,128)(2,1)}, u32[]{:S(2)}, u32[]{:S(2)}) collective-permute-start(bf16[2,64,2048]{2,1,0:T(8,128)(2,1)} %maximum_select_fusion.8), channel_id=1, source_target_pairs={{0,2},{1,3},{2,0},{3,1},{4,6},{5,7},{6,4},{7,5},{8,10},{9,11},{10,... | collective-permute-start | bytes 1572872 | tf_op jit(solution)/shard_map/ppermute | solution.py:69
  64.4 164.8 %collective-permute-start.19 = (bf16[2,64,2048]{2,1,0:T(8,128)(2,1)}, bf16[2,64,2048]{2,1,0:T(8,128)(2,1)}, u32[]{:S(2)}, u32[]{:S(2)}) collective-permute-start(bf16[2,64,2048]{2,1,0:T(8,128)(2,1)} %maximum_select_fusion.6), channel_id=1, source_target_pairs={{0,2},{1,3},{2,0},{3,1},{4,6},{5,7},{6,4},{7,5},{8,10},{9,11},{10,... | collective-permute-start | bytes 1572872 | tf_op jit(solution)/shard_map/ppermute | solution.py:69
  67.4 26.4 %collective-permute-start.9 = (bf16[2,256,2048]{2,1,0:T(8,128)(2,1)}, bf16[2,256,2048]{2,1,0:T(8,128)(2,1)}, u32[]{:S(2)}, u32[]{:S(2)}) collective-permute-start(bf16[2,256,2048]{2,1,0:T(8,128)(2,1)} %pad_maximum_fusion.2.low), channel_id=1, source_target_pairs={{0,8},{1,17},{2,10},{3,19},{4,12},{5,21},{6,14},{7,23},{8,0},{9,25... | collective-permute-start | bytes 6291464 | tf_op jit(solution)/shard_map/ppermute | solution.py:69
  71.8 8.3 %collective-permute-start.11 = (bf16[128,1024]{1,0:T(8,128)(2,1)S(1)}, bf16[128,1024]{1,0:T(8,128)(2,1)S(1)}, u32[]{:S(2)}, u32[]{:S(2)}) collective-permute-start(bf16[128,1024]{1,0:T(8,128)(2,1)S(1)} %slice.430), channel_id=1, source_target_pairs={{0,1},{1,2},{2,3},{3,4},{4,5},{5,6},{6,7},{8,9},{9,10},{10,11},{11... | collective-permute-start | bytes 786440 | tf_op jit(solution)/shard_map/ppermute | solution.py:69
  73.9 148.9 %copy-start.36 = (f32[4,8,128]{2,1,0:T(8,128)}, f32[4,8,128]{2,1,0:T(8,128)S(1)}, u32[]{:S(2)}) copy-start(f32[4,8,128]{2,1,0:T(8,128)S(1)} %get-tuple-element.174) | copy-start | bytes 49156
  73.9 148.9 %copy-start.38 = (f32[4,8,128]{2,1,0:T(8,128)}, f32[4,8,128]{2,1,0:T(8,128)S(1)}, u32[]{:S(2)}) copy-start(f32[4,8,128]{2,1,0:T(8,128)S(1)} %get-tuple-element.175) | copy-start | bytes 49156
  73.9 148.9 %copy-start.39 = (f32[4,8,128]{2,1,0:T(8,128)}, f32[4,8,128]{2,1,0:T(8,128)S(1)}, u32[]{:S(2)}) copy-start(f32[4,8,128]{2,1,0:T(8,128)S(1)} %get-tuple-element.176) | copy-start | bytes 49156
  80.1 161.5 %copy-start.29 = (f32[4,8,1,16,128]{4,1,3,2,0:T(8,128)}, f32[4,8,1,16,128]{4,1,3,2,0:T(8,128)S(1)}, u32[]{:S(2)}) copy-start(f32[4,8,1,16,128]{4,1,3,2,0:T(8,128)S(1)} %slice_bitcast_fusion.8) | copy-start | bytes 786436
  81.7 141.1 %copy-start.40 = (f32[4,8,128]{2,1,0:T(8,128)S(1)}, f32[4,8,128]{2,1,0:T(8,128)}, u32[]{:S(2)}) copy-start(f32[4,8,128]{2,1,0:T(8,128)} %get-tuple-element.177) | copy-start | bytes 49156
  81.7 142.7 %collective-permute-start.12 = (f32[2,16,8,128]{3,2,1,0:T(8,128)S(1)}, f32[2,16,8,128]{3,2,1,0:T(8,128)S(1)}, u32[]{:S(2)}, u32[]{:S(2)}) collective-permute-start(f32[2,16,8,128]{3,2,1,0:T(8,128)S(1)} %maximum_add_fusion), channel_id=1, source_target_pairs={{0,1},{1,0},{2,3},{3,2},{4,5},{5,4},{6,7},{7,6},{8,9},{9,8},{10,11... | collective-permute-start | bytes 393224 | tf_op jit(solution)/shard_map/ppermute | solution.py:69
  222.6 26.3 %collective-permute-start.10 = (bf16[1024,2048]{1,0:T(8,128)(2,1)}, bf16[1024,2048]{1,0:T(8,128)(2,1)}, u32[]{:S(2)}, u32[]{:S(2)}) collective-permute-start(bf16[1024,2048]{1,0:T(8,128)(2,1)} %place.1), channel_id=1, source_target_pairs={{0,1},{1,0},{2,3},{3,2},{4,5},{5,4},{6,7},{7,6},{8,9},{9,8},{10,11... | collective-permute-start | bytes 12582920 | tf_op jit(solution)/shard_map/ppermute | solution.py:69
  223.6 18.0 %copy-start.30 = (f32[4,32,128]{2,1,0:T(8,128)}, f32[4,32,128]{2,1,0:T(8,128)S(1)}, u32[]{:S(2)}) copy-start(f32[4,32,128]{2,1,0:T(8,128)S(1)} %get-tuple-element.218) | copy-start | bytes 196612
  225.4 5.9 %collective-permute-start.13 = (f32[2,16,8,128]{3,2,1,0:T(8,128)S(1)}, f32[2,16,8,128]{3,2,1,0:T(8,128)S(1)}, u32[]{:S(2)}, u32[]{:S(2)}) collective-permute-start(f32[2,16,8,128]{3,2,1,0:T(8,128)S(1)} %maximum_add_fusion.1), channel_id=1, source_target_pairs={{0,2},{1,3},{2,0},{3,1},{4,6},{5,7},{6,4},{7,5},{8,10},{9,11},{10,... | collective-permute-start | bytes 393224 | tf_op jit(solution)/shard_map/ppermute | solution.py:69
  227.6 13.9 %copy-start.33 = (f32[4,32,128]{2,1,0:T(8,128)S(1)}, f32[4,32,128]{2,1,0:T(8,128)}, u32[]{:S(2)}) copy-start(f32[4,32,128]{2,1,0:T(8,128)} %get-tuple-element.206) | copy-start | bytes 196612
  227.6 16.1 %collective-permute-start.25 = (bf16[1,256,2048]{2,1,0:T(8,128)(2,1)S(1)}, bf16[1,256,2048]{2,1,0:T(8,128)(2,1)S(1)}, u32[]{:S(2)}, u32[]{:S(2)}) collective-permute-start(bf16[1,256,2048]{2,1,0:T(8,128)(2,1)S(1)} %bitcast.308), channel_id=1, source_target_pairs={{0,16},{1,9},{2,18},{3,11},{4,20},{5,13},{6,22},{7,15},{8,24},{9,1... | collective-permute-start | bytes 3145736 | tf_op jit(solution)/shard_map/ppermute | solution.py:69
  230.6 37.4 %collective-permute-start.20 = (bf16[1,256,2048]{2,1,0:T(8,128)(2,1)S(1)}, bf16[1,256,2048]{2,1,0:T(8,128)(2,1)S(1)}, u32[]{:S(2)}, u32[]{:S(2)}) collective-permute-start(bf16[1,256,2048]{2,1,0:T(8,128)(2,1)S(1)} %bitcast.306), channel_id=1, source_target_pairs={{0,16},{1,9},{2,18},{3,11},{4,20},{5,13},{6,22},{7,15},{8,24},{9,1... | collective-permute-start | bytes 3145736 | tf_op jit(solution)/shard_map/ppermute | solution.py:69
  231.4 10.1 %collective-permute-start.14 = (f32[2,16,8,128]{3,2,1,0:T(8,128)S(1)}, f32[2,16,8,128]{3,2,1,0:T(8,128)S(1)}, u32[]{:S(2)}, u32[]{:S(2)}) collective-permute-start(f32[2,16,8,128]{3,2,1,0:T(8,128)S(1)} %maximum_add_fusion.2), channel_id=1, source_target_pairs={{0,4},{1,5},{2,6},{3,7},{4,0},{5,1},{6,2},{7,3},{8,12},{9,13},{10,... | collective-permute-start | bytes 393224 | tf_op jit(solution)/shard_map/ppermute | solution.py:69
  245.2 34.6 %collective-permute-start.26 = (bf16[2,256,2048]{2,1,0:T(8,128)(2,1)}, bf16[2,256,2048]{2,1,0:T(8,128)(2,1)}, u32[]{:S(2)}, u32[]{:S(2)}) collective-permute-start(bf16[2,256,2048]{2,1,0:T(8,128)(2,1)} %pad_maximum_fusion.4.w_low), channel_id=1, source_target_pairs={{0,8},{1,17},{2,10},{3,19},{4,12},{5,21},{6,14},{7,23},{8,0},{9,25... | collective-permute-start | bytes 6291464 | tf_op jit(solution)/shard_map/ppermute | solution.py:69
  255.3 8.0 %copy-start.4 = (bf16[512,1536]{1,0:T(8,128)(2,1)}, bf16[512,1536]{1,0:T(8,128)(2,1)S(1)}, u32[]{:S(2)}) copy-start(bf16[512,1536]{1,0:T(8,128)(2,1)S(1)} %convolution_convert_fusion.other_ref) | copy-start | bytes 4718596
  268.0 9.5 %collective-permute-start.15 = (bf16[512,1024]{1,0:T(8,128)(2,1)}, bf16[512,1024]{1,0:T(8,128)(2,1)}, u32[]{:S(2)}, u32[]{:S(2)}) collective-permute-start(bf16[512,1024]{1,0:T(8,128)(2,1)} %multiply_convert_fusion.s_own), channel_id=1, source_target_pairs={{0,1},{1,0},{2,3},{3,2},{4,5},{5,4},{6,7},{7,6},{8,9},{9,8},{10,11... | collective-permute-start | bytes 3145736 | tf_op jit(solution)/shard_map/ppermute | solution.py:69
  269.5 34.1 %collective-permute-start.21 = (bf16[2,256,2048]{2,1,0:T(8,128)(2,1)}, bf16[2,256,2048]{2,1,0:T(8,128)(2,1)}, u32[]{:S(2)}, u32[]{:S(2)}) collective-permute-start(bf16[2,256,2048]{2,1,0:T(8,128)(2,1)} %pad_maximum_fusion.3.w_low), channel_id=1, source_target_pairs={{0,8},{1,17},{2,10},{3,19},{4,12},{5,21},{6,14},{7,23},{8,0},{9,25... | collective-permute-start | bytes 6291464 | tf_op jit(solution)/shard_map/ppermute | solution.py:69
  327.1 7.6 %collective-permute-start.28 = (bf16[512,1024]{1,0:T(8,128)(2,1)}, bf16[512,1024]{1,0:T(8,128)(2,1)}, u32[]{:S(2)}, u32[]{:S(2)}) collective-permute-start(bf16[512,1024]{1,0:T(8,128)(2,1)} %get-tuple-element.31), channel_id=1, source_target_pairs={{0,1},{1,0},{2,3},{3,2},{4,5},{5,4},{6,7},{7,6},{8,9},{9,8},{10,11... | collective-permute-start | bytes 3145736 | tf_op jit(solution)/shard_map/ppermute | solution.py:69
  328.3 9.9 %collective-permute-start.27 = (bf16[512,1024]{1,0:T(8,128)(2,1)}, bf16[512,1024]{1,0:T(8,128)(2,1)S(1)}, u32[]{:S(2)}, u32[]{:S(2)}) collective-permute-start(bf16[512,1024]{1,0:T(8,128)(2,1)} %get-tuple-element.29), channel_id=1, source_target_pairs={{0,1},{1,0},{2,3},{3,2},{4,5},{5,4},{6,7},{7,6},{8,9},{9,8},{10,11... | collective-permute-start | bytes 3145736 | tf_op jit(solution)/shard_map/ppermute | solution.py:69
  332.2 60.7 %collective-permute-start.35 = (bf16[512,1024]{1,0:T(8,128)(2,1)S(1)}, bf16[512,1024]{1,0:T(8,128)(2,1)}, u32[]{:S(2)}, u32[]{:S(2)}) collective-permute-start(bf16[512,1024]{1,0:T(8,128)(2,1)S(1)} %attend.1), channel_id=1, source_target_pairs={{0,1},{1,0},{2,3},{3,2},{4,5},{5,4},{6,7},{7,6},{8,9},{9,8},{10,11... | collective-permute-start | bytes 3145736 | tf_op jit(solution)/shard_map/ppermute | solution.py:69
  332.6 76.7 %collective-permute-start.43 = (bf16[2,4,2,256,256]{4,3,2,1,0:T(8,128)(2,1)}, bf16[2,4,2,256,256]{4,3,2,1,0:T(8,128)(2,1)}, u32[]{:S(2)}, u32[]{:S(2)}) collective-permute-start(bf16[2,4,2,256,256]{4,3,2,1,0:T(8,128)(2,1)} %get-tuple-element.35), channel_id=1, source_target_pairs={{0,8},{1,17},{2,10},{3,19},{4,12},{5,21},{6,14},{7,23},{8,0},{9,25... | collective-permute-start | bytes 6291464 | tf_op jit(solution)/shard_map/ppermute | solution.py:69
  333.1 80.1 %collective-permute-start.47 = (bf16[2,4,2,256,256]{4,3,2,1,0:T(8,128)(2,1)}, bf16[2,4,2,256,256]{4,3,2,1,0:T(8,128)(2,1)}, u32[]{:S(2)}, u32[]{:S(2)}) collective-permute-start(bf16[2,4,2,256,256]{4,3,2,1,0:T(8,128)(2,1)} %get-tuple-element.37), channel_id=1, source_target_pairs={{0,8},{1,17},{2,10},{3,19},{4,12},{5,21},{6,14},{7,23},{8,0},{9,25... | collective-permute-start | bytes 6291464 | tf_op jit(solution)/shard_map/ppermute | solution.py:69
  375.8 43.8 %collective-permute-start.34 = (bf16[640,1536]{1,0:T(8,128)(2,1)}, bf16[640,1536]{1,0:T(8,128)(2,1)}, u32[]{:S(2)}, u32[]{:S(2)}) collective-permute-start(bf16[640,1536]{1,0:T(8,128)(2,1)} %get-tuple-element.33), channel_id=1, source_target_pairs={{0,1},{1,0},{2,3},{3,2},{4,5},{5,4},{6,7},{7,6},{8,9},{9,8},{10,11... | collective-permute-start | bytes 5898248 | tf_op jit(solution)/shard_map/ppermute | solution.py:69
  375.8 8.1 %collective-permute-start.29 = (f32[16,8,128]{2,1,0:T(8,128)S(1)}, f32[16,8,128]{2,1,0:T(8,128)S(1)}, u32[]{:S(2)}, u32[]{:S(2)}) collective-permute-start(f32[16,8,128]{2,1,0:T(8,128)S(1)} %get-tuple-element.180), channel_id=1, source_target_pairs={{0,1},{1,0},{2,3},{3,2},{4,5},{5,4},{6,7},{7,6},{8,9},{9,8},{10,11... | collective-permute-start | bytes 196616 | tf_op jit(solution)/shard_map/ppermute | solution.py:69
  387.5 19.8 %copy-start.15 = (f32[1024,512]{1,0:T(8,128)S(1)}, f32[1024,512]{1,0:T(8,128)}, u32[]{:S(2)}) copy-start(f32[1024,512]{1,0:T(8,128)} %fusion.60) | copy-start | bytes 6291460
  387.5 4.5 collective-permute-start.30
  392.0 1.5 collective-permute-start.37
  392.9 12.7 %collective-permute-start.36 = (bf16[512,512]{1,0:T(8,128)(2,1)}, bf16[512,512]{1,0:T(8,128)(2,1)S(1)}, u32[]{:S(2)}, u32[]{:S(2)}) collective-permute-start(bf16[512,512]{1,0:T(8,128)(2,1)} %copy-done.26), channel_id=1, source_target_pairs={{0,1},{1,0},{2,3},{3,2},{4,5},{5,4},{6,7},{7,6},{8,9},{9,8},{10,11... | collective-permute-start | bytes 1572872 | tf_op jit(solution)/shard_map/ppermute | solution.py:69
  393.5 6.4 %collective-permute-start.31 = (f32[16,8,128]{2,1,0:T(8,128)S(1)}, f32[16,8,128]{2,1,0:T(8,128)S(1)}, u32[]{:S(2)}, u32[]{:S(2)}) collective-permute-start(f32[16,8,128]{2,1,0:T(8,128)S(1)} %multiply_add_fusion.1), channel_id=1, source_target_pairs={{0,4},{1,5},{2,6},{3,7},{4,0},{5,1},{6,2},{7,3},{8,12},{9,13},{10,... | collective-permute-start | bytes 196616 | tf_op jit(solution)/shard_map/ppermute | solution.py:69
  399.9 19.7 %collective-permute-start.33 = (bf16[640,1024]{1,0:T(8,128)(2,1)}, bf16[640,1024]{1,0:T(8,128)(2,1)S(1)}, u32[]{:S(2)}, u32[]{:S(2)}) collective-permute-start(bf16[640,1024]{1,0:T(8,128)(2,1)} %pad_maximum_fusion.5), channel_id=1, source_target_pairs={{0,1},{1,0},{2,3},{3,2},{4,5},{5,4},{6,7},{7,6},{8,9},{9,8},{10,11... | collective-permute-start | bytes 3932168 | tf_op jit(solution)/shard_map/ppermute | solution.py:69
  405.6 28.1 %collective-permute-start.32 = (bf16[128,1024]{1,0:T(8,128)(2,1)S(1)}, bf16[128,1024]{1,0:T(8,128)(2,1)S(1)}, u32[]{:S(2)}, u32[]{:S(2)}) collective-permute-start(bf16[128,1024]{1,0:T(8,128)(2,1)S(1)} %sent_tail.1), channel_id=1, source_target_pairs={{1,0},{2,1},{3,2},{4,3},{5,4},{6,5},{7,6},{9,8},{10,9},{11,10},{12... | collective-permute-start | bytes 786440 | tf_op jit(solution)/shard_map/ppermute | solution.py:69
  412.6 30.8 %collective-permute-start.44 = (bf16[1,4,2,256,256]{4,3,2,1,0:T(8,128)(2,1)}, bf16[1,4,2,256,256]{4,3,2,1,0:T(8,128)(2,1)S(1)}, u32[]{:S(2)}, u32[]{:S(2)}) collective-permute-start(bf16[1,4,2,256,256]{4,3,2,1,0:T(8,128)(2,1)} %slice.492), channel_id=1, source_target_pairs={{0,16},{1,9},{2,18},{3,11},{4,20},{5,13},{6,22},{7,15},{8,24},{9,1... | collective-permute-start | bytes 3145736 | tf_op jit(solution)/shard_map/ppermute | solution.py:69
  419.0 30.9 %collective-permute-start.48 = (bf16[1,4,2,256,256]{4,3,2,1,0:T(8,128)(2,1)}, bf16[1,4,2,256,256]{4,3,2,1,0:T(8,128)(2,1)}, u32[]{:S(2)}, u32[]{:S(2)}) collective-permute-start(bf16[1,4,2,256,256]{4,3,2,1,0:T(8,128)(2,1)} %slice.499), channel_id=1, source_target_pairs={{0,16},{1,9},{2,18},{3,11},{4,20},{5,13},{6,22},{7,15},{8,24},{9,1... | collective-permute-start | bytes 3145736 | tf_op jit(solution)/shard_map/ppermute | solution.py:69
  432.8 29.7 %collective-permute-start.38 = (bf16[2,4,66,2048]{3,1,2,0:T(4,128)(2,1)}, bf16[2,4,66,2048]{3,1,2,0:T(4,128)(2,1)}, u32[]{:S(2)}, u32[]{:S(2)}) collective-permute-start(bf16[2,4,66,2048]{3,1,2,0:T(4,128)(2,1)} %copy.265), channel_id=1, source_target_pairs={{0,8},{1,17},{2,10},{3,19},{4,12},{5,21},{6,14},{7,23},{8,0},{9,25... | collective-permute-start | bytes 6488072 | tf_op jit(solution)/shard_map/ppermute | solution.py:69
  438.2 32.4 %all-to-all-start = ((f32[32,1,32]{2,1,0:T(1,128)}), f32[32,1,32]{2,1,0:T(1,128)S(1)}, u32[]{:S(2)}, u32[]{:S(2)}) async-start(f32[32,1,32]{2,1,0:T(1,128)} %all_to_all.6), calls=%async_computation | async-start | bytes 32768 | tf_op jit(solution)/shard_map/all_to_all | solution.py:949
  448.0 25.6 %collective-permute-start.45 = (bf16[2,2,256,256]{2,3,1,0:T(8,128)(2,1)}, bf16[2,2,256,256]{2,3,1,0:T(8,128)(2,1)}, u32[]{:S(2)}, u32[]{:S(2)}) collective-permute-start(bf16[2,2,256,256]{2,3,1,0:T(8,128)(2,1)} %bitcast.325), channel_id=1, source_target_pairs={{0,2},{1,3},{2,0},{3,1},{4,6},{5,7},{6,4},{7,5},{8,10},{9,11},{10,... | collective-permute-start | bytes 1572872 | tf_op jit(solution)/shard_map/ppermute | solution.py:69
  453.3 23.0 %collective-permute-start.49 = (bf16[2,2,256,256]{2,3,1,0:T(8,128)(2,1)}, bf16[2,2,256,256]{2,3,1,0:T(8,128)(2,1)}, u32[]{:S(2)}, u32[]{:S(2)}) collective-permute-start(bf16[2,2,256,256]{2,3,1,0:T(8,128)(2,1)} %bitcast.103), channel_id=1, source_target_pairs={{0,2},{1,3},{2,0},{3,1},{4,6},{5,7},{6,4},{7,5},{8,10},{9,11},{10,... | collective-permute-start | bytes 1572872 | tf_op jit(solution)/shard_map/ppermute | solution.py:69
  468.2 15.5 %collective-permute-start.39 = (bf16[1,4,66,2048]{3,1,2,0:T(4,128)(2,1)}, bf16[1,4,66,2048]{3,1,2,0:T(4,128)(2,1)}, u32[]{:S(2)}, u32[]{:S(2)}) collective-permute-start(bf16[1,4,66,2048]{3,1,2,0:T(4,128)(2,1)} %copy.267), channel_id=1, source_target_pairs={{0,16},{1,9},{2,18},{3,11},{4,20},{5,13},{6,22},{7,15},{8,24},{9,1... | collective-permute-start | bytes 3244040 | tf_op jit(solution)/shard_map/ppermute | solution.py:69
  474.8 21.5 %collective-permute-start.46 = (bf16[1,2,256,256]{2,3,1,0:T(8,128)(2,1)S(1)}, bf16[1,2,256,256]{2,3,1,0:T(8,128)(2,1)S(1)}, u32[]{:S(2)}, u32[]{:S(2)}) collective-permute-start(bf16[1,2,256,256]{2,3,1,0:T(8,128)(2,1)S(1)} %slice_bitcast_fusion.6), channel_id=1, source_target_pairs={{0,4},{1,5},{2,6},{3,7},{4,0},{5,1},{6,2},{7,3},{8,12},{9,13},{10,... | collective-permute-start | bytes 786440 | tf_op jit(solution)/shard_map/ppermute | solution.py:69
  477.5 23.4 %collective-permute-start.50 = (bf16[1,2,256,256]{2,3,1,0:T(8,128)(2,1)S(1)}, bf16[1,2,256,256]{2,3,1,0:T(8,128)(2,1)S(1)}, u32[]{:S(2)}, u32[]{:S(2)}) collective-permute-start(bf16[1,2,256,256]{2,3,1,0:T(8,128)(2,1)S(1)} %slice_bitcast_fusion.3), channel_id=1, source_target_pairs={{0,4},{1,5},{2,6},{3,7},{4,0},{5,1},{6,2},{7,3},{8,12},{9,13},{10,... | collective-permute-start | bytes 786440 | tf_op jit(solution)/shard_map/ppermute | solution.py:69
  486.3 24.2 %collective-permute-start.40 = (bf16[2,66,2048]{2,0,1:T(2,128)(2,1)S(1)}, bf16[2,66,2048]{2,0,1:T(2,128)(2,1)S(1)}, u32[]{:S(2)}, u32[]{:S(2)}) collective-permute-start(bf16[2,66,2048]{2,0,1:T(2,128)(2,1)S(1)} %copy.269), channel_id=1, source_target_pairs={{0,2},{1,3},{2,0},{3,1},{4,6},{5,7},{6,4},{7,5},{8,10},{9,11},{10,... | collective-permute-start | bytes 1622024 | tf_op jit(solution)/shard_map/ppermute | solution.py:69
  510.9 15.4 %collective-permute-start.41 = (bf16[1,66,2048]{2,1,0:T(8,128)(2,1)S(1)}, bf16[1,66,2048]{2,1,0:T(8,128)(2,1)S(1)}, u32[]{:S(2)}, u32[]{:S(2)}) collective-permute-start(bf16[1,66,2048]{2,1,0:T(8,128)(2,1)S(1)} %select_bitcast_fusion.2), channel_id=1, source_target_pairs={{0,4},{1,5},{2,6},{3,7},{4,0},{5,1},{6,2},{7,3},{8,12},{9,13},{10,... | collective-permute-start | bytes 811016 | tf_op jit(solution)/shard_map/ppermute | solution.py:69
  526.6 2.0 collective-permute-start.42
  (46 other events, 164.1 us)

commit v2 on v1

v2 whole, which is shorter than its diff:
```python
import functools

import jax
import jax.numpy as jnp
from jax import lax
from jax.experimental import pallas as pl
from jax.experimental.pallas import tpu as pltpu
from jax.sharding import PartitionSpec as P

D = 1024
H = 8
HD = 128
FF = 4096
NS = 16
LEN = 4096
BLK = 512
CTX = 128
OWN = BLK - CTX
HALF = D // 2
SCALE = HD ** (-0.5)
AXES = ("dp", "mp")
f32 = jnp.float32
bf16 = jnp.bfloat16
VMEM = pl.BlockSpec(memory_space=pltpu.VMEM)
SMEM = pl.BlockSpec(memory_space=pltpu.SMEM)
ANY = pl.BlockSpec(memory_space=pl.ANY)
QKV_COLS = pl.BlockSpec((D, 3 * HALF), lambda i: (0, 0))
OUT_COLS = pl.BlockSpec((D, HALF), lambda i: (0, 3))
NT = (((1,), (1,)), ((), ()))
TN = (((0,), (0,)), ((), ()))


def params(mib):
    return pltpu.CompilerParams(vmem_limit_bytes=mib * 1024 * 1024)


COST = pl.CostEstimate(flops=1, bytes_accessed=1, transcendentals=0)


def bits_of(n):
    return n.bit_length() - 1


def swap_bits(word, count):
    out = 0
    for i in range(count):
        out = out | (((word >> i) & 1) << (count - 1 - i))
    return out


class Links:
    def __init__(self):
        self.ndp = lax.axis_size("dp")
        self.nmp = lax.axis_size("mp")
        self.nz = self.nmp // 2
        self.dp = lax.axis_index("dp")
        self.mp = lax.axis_index("mp")
        self.z = self.mp // 2
        self.core = self.mp % 2
        self.dp_bits = bits_of(self.ndp)
        self.mp_bits = bits_of(self.nmp)

    def send(self, values, target):
        pairs = []
        for d in range(self.ndp):
            for m in range(self.nmp):
                to = target(d, m)
                if to is not None:
                    pairs.append((d * self.nmp + m, to[0] * self.nmp + to[1]))
        return lax.ppermute(values, AXES, pairs)

    def mp_swap(self, values, bit):
        return self.send(values, lambda d, m: (d, m ^ (1 << bit)))

    def dp_swap(self, values, bit):
        return self.send(values, lambda d, m: (d ^ (1 << bit), m))

    def core_swap(self, values):
        return self.mp_swap(values, 0)

    def fan(self, values, level):
        other = self.dp_bits - 1 - level
        return self.send(
            values, lambda d, m: (d ^ (1 << (other if m % 2 else level)), m)
        )

    def block_at(self, position):
        mirrored = swap_bits(position, self.dp_bits)
        return self.dp ^ jnp.where(self.core == 0, mirrored, position)

    def window_shift(self, values, step):
        per = LEN // BLK

        def target(d, m):
            inside = m % per + step
            return (d, m + step) if 0 <= inside < per else None

        return self.send(values, target)


def by_core(links, first, second, axis):
    return jnp.where(
        links.core == 0,
        jnp.concatenate([first, second], axis),
        jnp.concatenate([second, first], axis),
    )


def spread_rows(src_ref, dst_ref, rows, start=0):
    for r in range(0, rows, 16):
        block = src_ref[start + r : start + r + 16, :].astype(f32)
        for j in range(8):
            dst_ref[r : r + 16, j, :] = block[:, j * 128 : (j + 1) * 128]


def gather_rows(src_ref, dst_ref, rows):
    for r in range(0, rows, 16):
        for j in range(8):
            dst_ref[r : r + 16, j * 128 : (j + 1) * 128] = src_ref[r : r + 16, j, :].astype(
                dst_ref.dtype
            )


def move_on(state, rate, steps):
    far = jnp.exp(-rate * steps)
    near = jnp.exp(-rate * (steps - 1.0)) * steps
    return far * state[0], far * state[1] + near * state[0]


def scan_rows(xs, rows, decay):
    zero = jnp.zeros((NS, 8, 128), f32)

    def step(i, carry):
        u, v = carry
        for k in range(8):
            v = decay * v + u
            u = decay * u + xs[i * 8 + k][None]
        return u, v

    return lax.fori_loop(0, rows // 8, step, (zero, zero))


def scan_own_kernel(x_ref, rate_ref, out_ref, xs):
    spread_rows(x_ref, xs, OWN)
    u, v = scan_rows(xs, OWN, jnp.exp(-rate_ref[...]))
    out_ref[0] = u
    out_ref[1] = v


def scan_tail_kernel(x_ref, own_ref, rate_ref, out_ref, xs):
    spread_rows(x_ref, xs, CTX)
    state = scan_rows(xs, CTX, jnp.exp(-rate_ref[...]))
    u, v = move_on(state, rate_ref[...], float(OWN))
    out_ref[0] = u + own_ref[0]
    out_ref[1] = v + own_ref[1]


STATE = jax.ShapeDtypeStruct((2, NS, 8, 128), f32)


def scan_own(values, rate):
    return pl.pallas_call(
        scan_own_kernel,
        out_shape=STATE,
        in_specs=[VMEM, VMEM],
        out_specs=VMEM,
        scratch_shapes=[pltpu.VMEM((OWN, 8, 128), f32)],
        compiler_params=params(24),
        cost_estimate=COST,
        name="scan_own",
    )(values, rate)


def scan_tail(values, own, rate):
    return pl.pallas_call(
        scan_tail_kernel,
        out_shape=STATE,
        in_specs=[VMEM] * 3,
        out_specs=VMEM,
        scratch_shapes=[pltpu.VMEM((CTX, 8, 128), f32)],
        compiler_params=params(24),
        cost_estimate=COST,
        name="scan_tail",
    )(values, own, rate)


def exchange_kernel(scal, total_ref, recv_ref, before_ref, rate_ref, total_out, before_out):
    mine, inside, span = scal[0], scal[1], scal[2]
    rate = rate_ref[...]
    recv = (recv_ref[0], recv_ref[1])
    total = (total_ref[0], total_ref[1])
    moved = move_on(recv, rate, inside)
    low = tuple(mine * r + (1.0 - mine) * t for r, t in zip(recv, total))
    high = tuple(mine * t + (1.0 - mine) * r for r, t in zip(recv, total))
    far = move_on(low, rate, span)
    for i in range(2):
        before_out[i] = before_ref[i] + mine * moved[i]
        total_out[i] = far[i] + high[i]


def exchange_step(scal, total, received, before, rate):
    return pl.pallas_call(
        exchange_kernel,
        out_shape=(STATE, STATE),
        in_specs=[SMEM] + [VMEM] * 4,
        out_specs=(VMEM, VMEM),
        compiler_params=params(16),
        cost_estimate=COST,
        name="exchange_step",
    )(scal, total, received, before, rate)


def exchange_back_kernel(scal, total_ref, recv_ref, after_ref, rate_ref, total_out, after_out):
    mine, inside, span = scal[0], scal[1], scal[2]
    rate = rate_ref[...]
    recv, total = recv_ref[...], total_ref[...]
    after_out[...] = after_ref[...] + (1.0 - mine) * (jnp.exp(-rate * inside) * recv)
    low = mine * recv + (1.0 - mine) * total
    high = mine * total + (1.0 - mine) * recv
    total_out[...] = low + jnp.exp(-rate * span) * high


def exchange_back_step(scal, total, received, after, rate):
    one = jax.ShapeDtypeStruct((NS, 8, 128), f32)
    return pl.pallas_call(
        exchange_back_kernel,
        out_shape=(one, one),
        in_specs=[SMEM] + [VMEM] * 4,
        out_specs=(VMEM, VMEM),
        compiler_params=params(16),
        cost_estimate=COST,
        name="exchange_back_step",
    )(scal, total, received, after, rate)


def context_kernel(
    scal, x_ref, own_ref, before_ref, initial_ref, rate_ref, in_ref, out_map_ref, out_ref, xs, ys
):
    out_ref[CTX:, :] = own_ref[...]
    spread_rows(x_ref, xs, CTX)
    rate = rate_ref[...]
    decay = jnp.exp(-rate)
    weight = in_ref[...] * out_map_ref[...]
    carried = jnp.exp(-rate * scal[0]) * initial_ref[...] * scal[1]
    start = out_map_ref[...] * (in_ref[...] * before_ref[0] + carried)

    def step(i, y):
        for k in range(8):
            y = decay * y + weight * xs[i * 8 + k][None]
            ys[i * 8 + k] = jnp.sum(y, axis=0)
        return y

    lax.fori_loop(0, CTX // 8, step, start)
    gather_rows(ys, out_ref, CTX)


def context_states(scal, tail, own, before, initial, rate, gain_in, gain_out):
    return pl.pallas_call(
        context_kernel,
        out_shape=jax.ShapeDtypeStruct((CTX + BLK, D), bf16),
        in_specs=[SMEM] + [VMEM] * 7,
        out_specs=VMEM,
        scratch_shapes=[pltpu.VMEM((CTX, 8, 128), f32)] * 2,
        compiler_params=params(24),
        cost_estimate=COST,
        name="context_states",
    )(scal, tail, own, before, initial, rate, gain_in, gain_out)


def state_low_kernel(g_ref, rate_ref, out_ref, gs):
    spread_rows(g_ref, gs, CTX)
    decay = jnp.exp(-rate_ref[...])
    zero = jnp.zeros((NS, 8, 128), f32)

    def back(i, carry):
        low, slope = carry
        for k in range(8):
            slope = decay * slope + low
            low = decay * low + gs[CTX - 1 - (i * 8 + k)][None]
        return low, slope

    low, slope = lax.fori_loop(0, CTX // 8, back, (zero, zero))
    out_ref[0] = low
    out_ref[1] = slope


def state_low(grad_context, rate):
    return pl.pallas_call(
        state_low_kernel,
        out_shape=jax.ShapeDtypeStruct((2, NS, 8, 128), f32),
        in_specs=[VMEM] * 2,
        out_specs=VMEM,
        scratch_shapes=[pltpu.VMEM((CTX, 8, 128), f32)],
        compiler_params=params(16),
        cost_estimate=COST,
        name="state_low",
    )(grad_context, rate)


def state_sums_kernel(
    scal, g_ref, x_ref, start_ref, lows_ref, initial_ref, rate_ref, in_ref, out_map_ref, out_ref,
    gs, xs,
):
    spread_rows(g_ref, gs, CTX)
    spread_rows(x_ref, xs, CTX)
    part = NS // 2
    for n in range(0, NS, part):
        span = slice(n, n + part)
        rate = rate_ref[span]
        decay = jnp.exp(-rate)
        zero = jnp.zeros((part, 8, 128), f32)

        def step(i, carry):
            u, v, su, sv = carry
            for k in range(4):
                v = decay * v + u
                u = decay * u + xs[i * 4 + k][None]
                g = gs[i * 4 + k][None]
                su = su + g * u
                sv = sv + g * v
            return u, v, su, sv

        _, _, su, sv = lax.fori_loop(
            0, CTX // 4, step, (start_ref[0, span], start_ref[1, span], zero, zero)
        )
        far = jnp.exp(-rate * scal[0])
        low, slope = lows_ref[0, span], lows_ref[1, span]
        sum_init = far * decay * low
        sum_slope = far * ((scal[0] + 1.0) * low + decay * slope)
        initial = initial_ref[span] * scal[1]
        gain_in, gain_out = in_ref[span], out_map_ref[span]
        out_ref[0, span] = -decay * gain_out * (gain_in * sv + initial * sum_slope)
        out_ref[1, span] = gain_out * su
        out_ref[2, span] = gain_in * su + initial * sum_init
        out_ref[3, span] = gain_out * sum_init * scal[1]


def state_sums(scal, grad_context, tail, start, lows, initial, rate, gain_in, gain_out):
    return pl.pallas_call(
        state_sums_kernel,
        out_shape=jax.ShapeDtypeStruct((4, NS, 8, 128), f32),
        in_specs=[SMEM] + [VMEM] * 8,
        out_specs=VMEM,
        scratch_shapes=[pltpu.VMEM((CTX, 8, 128), f32)] * 2,
        compiler_params=params(24),
        cost_estimate=COST,
        name="state_sums",
    )(scal, grad_context, tail, start, lows, initial, rate, gain_in, gain_out)


def sent_tail_kernel(g_ref, after_ref, rate_ref, in_ref, out_map_ref, out_ref, gs, ys):
    spread_rows(g_ref, gs, CTX)
    rate = rate_ref[...]
    decay = jnp.exp(-rate)
    weight = in_ref[...] * out_map_ref[...]
    start = jnp.exp(-rate * float(OWN)) * weight * after_ref[...]

    def back(i, y):
        for k in range(8):
            t = CTX - 1 - (i * 8 + k)
            y = decay * y + weight * gs[t][None]
            ys[t] = jnp.sum(y, axis=0)
        return y

    lax.fori_loop(0, CTX // 8, back, start)
    gather_rows(ys, out_ref, CTX)


def sent_tail(grad_context, after, rate, gain_in, gain_out):
    return pl.pallas_call(
        sent_tail_kernel,
        out_shape=jax.ShapeDtypeStruct((CTX, D), bf16),
        in_specs=[VMEM] * 5,
        out_specs=VMEM,
        scratch_shapes=[pltpu.VMEM((CTX, 8, 128), f32)] * 2,
        compiler_params=params(24),
        cost_estimate=COST,
        name="sent_tail",
    )(grad_context, after, rate, gain_in, gain_out)


def sent_own_kernel(after_ref, rate_ref, in_ref, out_map_ref, out_ref, ys):
    decay = jnp.exp(-rate_ref[...])

    def back(i, y):
        for k in range(8):
            y = decay * y
            ys[OWN - 1 - (i * 8 + k)] = jnp.sum(y, axis=0)
        return y

    lax.fori_loop(0, OWN // 8, back, in_ref[...] * out_map_ref[...] * after_ref[...])
    gather_rows(ys, out_ref, OWN)


def sent_own(after, rate, gain_in, gain_out):
    return pl.pallas_call(
        sent_own_kernel,
        out_shape=jax.ShapeDtypeStruct((OWN, D), bf16),
        in_specs=[VMEM] * 4,
        out_specs=VMEM,
        scratch_shapes=[pltpu.VMEM((OWN, 8, 128), f32)],
        compiler_params=params(24),
        cost_estimate=COST,
        name="sent_own",
    )(after, rate, gain_in, gain_out)


def attention_mask(keys, queries, first_query, opened):
    row = lax.broadcasted_iota(jnp.int32, (keys, queries), 0)
    col = lax.broadcasted_iota(jnp.int32, (keys, queries), 1) + first_query
    return jnp.where(row < CTX, (1 - opened) * BLK, row - CTX) <= col


def head_parts(ref, offset):
    q = ref[CTX:, pl.ds(offset, HD)]
    k = ref[:, pl.ds(HALF + offset, HD)]
    v = ref[:, pl.ds(2 * HALF + offset, HD)]
    return q, k, v


def probabilities(k, q, first_query, opened):
    scores = lax.dot_general(k, q, NT, preferred_element_type=f32) * SCALE
    scores = jnp.where(
        attention_mask(k.shape[0], q.shape[0], first_query, opened), scores, -jnp.inf
    )
    lifted = jnp.exp(scores - jnp.max(scores, axis=0, keepdims=True))
    return lifted * (1.0 / jnp.sum(lifted, axis=0, keepdims=True))


QT = BLK // 2


def attend_kernel(info, own_ref, other_ref, out_ref):
    opened = info[1]

    @pl.loop(0, H // 2)
    def _(h):
        offset = pl.multiple_of(h * HD, HD)
        for side, qkv in enumerate((own_ref, other_ref)):
            q, k, v = head_parts(qkv, offset)
            v_t = v.T
            home = pl.multiple_of((side ^ info[0]) * HALF + h * HD, HD)
            for first in range(0, BLK, QT):
                keys = CTX + first + QT
                p = probabilities(k[:keys], q[first : first + QT], first, opened).astype(bf16)
                mixed = jnp.dot(v_t[:, :keys], p, preferred_element_type=f32)
                out_ref[first : first + QT, pl.ds(home, HD)] = mixed.T.astype(bf16)


def attend(info, own, other):
    return pl.pallas_call(
        attend_kernel,
        out_shape=jax.ShapeDtypeStruct((BLK, D), bf16),
        in_specs=[SMEM] + [VMEM] * 2,
        out_specs=VMEM,
        compiler_params=params(32),
        cost_estimate=COST,
        name="attend",
    )(info, own, other)


def attend_back_kernel(
    info, own_ref, other_ref, grad_ref, g_own_ref, g_other_ref, acc
):
    opened = info[1]
    sides = ((own_ref, g_own_ref), (other_ref, g_other_ref))
    for _, g in sides:
        g[:CTX, :HALF] = jnp.zeros((CTX, HALF), bf16)

    @pl.loop(0, H // 2)
    def _(h):
        offset = pl.multiple_of(h * HD, HD)
        for side, (qkv, g) in enumerate(sides):
            q, k, v = head_parts(qkv, offset)
            k_t = k.T
            home = pl.multiple_of((side ^ info[0]) * HALF + h * HD, HD)
            for first in range(0, BLK, QT):
                keys = CTX + first + QT
                q_now = q[first : first + QT]
                go = grad_ref[first : first + QT, pl.ds(home, HD)]
                p = probabilities(k[:keys], q_now, first, opened)
                gp = lax.dot_general(v[:keys], go, NT, preferred_element_type=f32)
                mean = jnp.sum(p * gp, axis=0, keepdims=True)
                gs = (p * (gp - mean)).astype(bf16)
                gq_t = jnp.dot(k_t[:, :keys], gs, preferred_element_type=f32) * SCALE
                g[CTX + first : CTX + first + QT, pl.ds(offset, HD)] = gq_t.T.astype(bf16)
                gk = jnp.dot(gs, q_now, preferred_element_type=f32)
                gv = jnp.dot(p.astype(bf16), go, preferred_element_type=f32)
                if first == 0:
                    acc[0, :keys] = gk
                    acc[1, :keys] = gv
                else:
                    early = CTX + QT
                    gk_all = jnp.concatenate([gk[:early] + acc[0, :early], gk[early:]], 0)
                    gv_all = jnp.concatenate([gv[:early] + acc[1, :early], gv[early:]], 0)
                    g[:, pl.ds(HALF + offset, HD)] = (gk_all * SCALE).astype(bf16)
                    g[:, pl.ds(2 * HALF + offset, HD)] = gv_all.astype(bf16)


def attend_back(info, own, other, grad):
    out = jax.ShapeDtypeStruct((CTX + BLK, 3 * HALF), bf16)
    return pl.pallas_call(
        attend_back_kernel,
        out_shape=(out, out),
        in_specs=[SMEM] + [VMEM] * 3,
        out_specs=(VMEM, VMEM),
        scratch_shapes=[pltpu.VMEM((2, CTX + QT, HD), f32)],
        compiler_params=params(32),
        cost_estimate=COST,
        name="attend_back",
    )(info, own, other, grad)


def gelu_parts(x):
    cdf = 0.5 * (1.0 + lax.erf(x * 0.7071067811865476))
    slope = cdf + x * (jnp.exp(-0.5 * x * x) * 0.3989422804014327)
    return x * cdf, slope


def feed_kernel(
    ndp, nz, width, index, groups, earlier, last, info, s_own, s_par, c_own, c_par, st_own, st_par, ct_own, ct_par,
    *rest
):
    rows = s_own.shape[0]
    tokens = 2 * rows
    block = D // ndp
    group = nz * width
    half = ndp // 2
    weights, *rest = rest
    if earlier:
        m_in, g_in, *rest = rest
    if last:
        m_own, m_par, g_own, g_par, keep_out, send_out, *rest = rest
    else:
        m_out, g_out, keep_out, send_out, *rest = rest
    s, c, st, ct, w, act, gh, acc_m, acc_g, keep, send, sems, out_sems = rest
    at = [pl.multiple_of(info[p] * block, block) for p in range(ndp)]
    z = info[ndp]
    copies = {}
    count = [0]

    def start(name, src, dst):
        sem = sems.at[count[0]]
        count[0] += 1
        copy = pltpu.make_async_copy(src, dst, sem)
        copy.start()
        copies.setdefault(name, []).append(copy)

    def wait(name):
        for copy in copies.pop(name):
            copy.wait()

    def rows_of(name, own, par, dst):
        for p in range(ndp):
            for i, src in enumerate((own, par)):
                start(
                    name,
                    src.at[pl.ds(at[p], block), :],
                    dst.at[p * block : (p + 1) * block, i * rows : (i + 1) * rows],
                )

    for i, src in enumerate((s_own, s_par)):
        start("s", src, s.at[i * rows : (i + 1) * rows, :])
    at_core = pl.multiple_of((info[ndp + 1] * groups + index) * 2 * group, 128)
    start("w", weights.at[:, pl.ds(at_core, 2 * group)], w)
    for i, src in enumerate((c_own, c_par)):
        start("c", src, c.at[i * rows : (i + 1) * rows, :])
    rows_of("st", st_own, st_par, st)
    rows_of("ct", ct_own, ct_par, ct)
    if earlier:
        start("m", m_in, acc_m)
        start("g", g_in, acc_g)
    wait("s")
    wait("w")
    wait("c")

    @pl.loop(0, nz)
    def _(b):
        up = pl.ds(pl.multiple_of(b * width, width), width)
        down = pl.ds(pl.multiple_of(group + b * width, width), width)
        for i in range(2):
            part = slice(i * rows, (i + 1) * rows)
            hidden = jnp.dot(s[part, :], w[:, up], preferred_element_type=f32)
            grad = jnp.dot(c[part, :], w[:, down], preferred_element_type=f32)
            active, slope = gelu_parts(hidden)
            act[part, up] = active.astype(bf16)
            gh[part, up] = (grad * slope).astype(bf16)

    wait("st")
    wait("ct")

    @pl.loop(0, nz)
    def _(r):
        cols = pl.ds(pl.multiple_of((z ^ swap_bits(r, bits_of(nz))) * width, width), width)
        for part, dst in ((0, keep), (1, send)):
            span = slice(part * half * block, (part + 1) * half * block)
            up = jnp.dot(st[span, :], gh[:, cols], preferred_element_type=f32).astype(bf16)
            down = jnp.dot(ct[span, :], act[:, cols], preferred_element_type=f32).astype(bf16)
            for p in range(half):
                dst[p, r, 0] = up[p * block : (p + 1) * block]
                dst[p, r, 1] = down[p * block : (p + 1) * block]

    outs = [
        pltpu.make_async_copy(keep, keep_out, out_sems.at[0]),
        pltpu.make_async_copy(send, send_out, out_sems.at[1]),
    ]
    for copy in outs:
        copy.start()
    if earlier:
        wait("m")
        wait("g")
    for name, left, acc, first in (("g", gh, acc_g, 0), ("m", act, acc_m, group)):
        for p in range(ndp):
            right = w[p * block : (p + 1) * block, first : first + group]
            for i in range(2):
                part = slice(i * rows, (i + 1) * rows)
                value = lax.dot_general(left[part, :], right, NT, preferred_element_type=f32)
                cols = slice(p * block, (p + 1) * block)
                if earlier:
                    value = value + acc[part, cols]
                if not last:
                    acc[part, cols] = value
                elif i == 0:
                    (g_own if name == "g" else m_own)[:, cols] = value
                else:
                    (g_par if name == "g" else m_par)[:, cols] = value.astype(bf16)
    if not last:
        outs.append(pltpu.make_async_copy(acc_m, m_out, out_sems.at[2]))
        outs.append(pltpu.make_async_copy(acc_g, g_out, out_sems.at[3]))
        for copy in outs[2:]:
            copy.start()
    for copy in outs:
        copy.wait()


def feed(links, info, acts, weights, group, index, groups, earlier, last):
    ndp, nz = links.ndp, links.nz
    rows = acts[0].shape[0]
    tokens = 2 * rows
    block = D // ndp
    width = group // nz
    half = ndp // 2
    full = jax.ShapeDtypeStruct((tokens, D), f32)
    own = jax.ShapeDtypeStruct((rows, D), f32)
    par = jax.ShapeDtypeStruct((rows, D), bf16)
    grads = jax.ShapeDtypeStruct((half, nz, 2, block, width), bf16)
    out_shape = (own, par, own, par, grads, grads) if last else (full, full, grads, grads)
    out_specs = (VMEM,) * 4 + (ANY,) * 2 if last else (ANY,) * 4
    inputs = (info, *acts, weights) + (tuple(earlier) if earlier else ())
    n_copies = 4 * ndp + 7
    return pl.pallas_call(
        functools.partial(feed_kernel, ndp, nz, width, index, groups, bool(earlier), last),
        out_shape=out_shape,
        in_specs=[SMEM] + [ANY] * (len(inputs) - 1),
        out_specs=out_specs,
        scratch_shapes=[
            pltpu.VMEM((tokens, D), bf16),
            pltpu.VMEM((tokens, D), bf16),
            pltpu.VMEM((D, tokens), bf16),
            pltpu.VMEM((D, tokens), bf16),
            pltpu.VMEM((D, 2 * group), bf16),
            pltpu.VMEM((tokens, group), bf16),
            pltpu.VMEM((tokens, group), bf16),
            pltpu.VMEM((tokens, D), f32),
            pltpu.VMEM((tokens, D), f32),
            pltpu.VMEM((half, nz, 2, block, width), bf16),
            pltpu.VMEM((half, nz, 2, block, width), bf16),
            pltpu.SemaphoreType.DMA((n_copies,)),
            pltpu.SemaphoreType.DMA((4,)),
        ],
        compiler_params=params(58),
        cost_estimate=COST,
        name="feed_last" if last else "feed_first",
    )(*inputs)


def norm_parts(values):
    center = values - jnp.mean(values, axis=-1, keepdims=True)
    spread = jnp.mean(center * center, axis=-1, keepdims=True)
    inverse = lax.rsqrt(spread + 1e-05)
    return center * inverse, inverse


def norm_back(grad, unit, inverse, gain):
    scaled = grad * gain
    return (
        scaled
        - jnp.mean(scaled, axis=-1, keepdims=True)
        - unit * jnp.mean(scaled * unit, axis=-1, keepdims=True)
    ) * inverse


def dot(left, right):
    return jnp.dot(left, right, preferred_element_type=f32)


def dot_nt(left, right):
    return lax.dot_general(left, right, NT, preferred_element_type=f32)


ROWS = 128


def norm_kernel(x_ref, gain_ref, out_ref, tail_ref):
    for r in range(0, x_ref.shape[0], ROWS):
        unit, _ = norm_parts(x_ref[r : r + ROWS, :].astype(f32))
        out_ref[r : r + ROWS, :] = (unit * gain_ref[...]).astype(bf16)
    tail_ref[...] = out_ref[OWN:, :]


def norm_first(tokens, gain):
    return pl.pallas_call(
        norm_kernel,
        out_shape=(
            jax.ShapeDtypeStruct(tokens.shape, bf16),
            jax.ShapeDtypeStruct((CTX, D), bf16),
        ),
        in_specs=[VMEM] * 2,
        out_specs=(VMEM, VMEM),
        compiler_params=params(16),
        cost_estimate=COST,
        name="norm_first",
    )(tokens, gain)


def middle_kernel(
    info, att_ref, tok_ref, o_own, o_other, gain_ref, mid_ref, second_ref, second_t_ref
):
    att = att_ref[...]
    for side, weight in enumerate((o_own, o_other)):
        cols = pl.ds(pl.multiple_of((side ^ info[0]) * HALF, HALF), HALF)
        mid_ref[:, cols] = tok_ref[:, cols].astype(f32) + dot(att, weight[...])
    for r in range(0, att_ref.shape[0], ROWS):
        unit, _ = norm_parts(mid_ref[r : r + ROWS, :])
        second = unit * gain_ref[...]
        second_ref[r : r + ROWS, :] = second.astype(bf16)
        second_t_ref[:, r : r + ROWS] = second.T.astype(bf16)


def middle_norm(info, attended, tokens, o_own, o_other, gain):
    rows = tokens.shape[0]
    return pl.pallas_call(
        middle_kernel,
        out_shape=(
            jax.ShapeDtypeStruct((rows, D), f32),
            jax.ShapeDtypeStruct((rows, D), bf16),
            jax.ShapeDtypeStruct((D, rows), bf16),
        ),
        grid=(1,),
        in_specs=[SMEM, VMEM, VMEM, OUT_COLS, OUT_COLS, VMEM],
        out_specs=(VMEM,) * 3,
        compiler_params=params(32),
        cost_estimate=COST,
        name="middle_norm",
    )(info, attended, tokens, o_own, o_other, gain)


def back_middle_kernel(
    info, mid_ref, own_ref, recv_ref, cot_ref, gain_ref, o_own, o_other,
    grad_ref, b_own_ref, b_other_ref, att_ref, gain_grad_ref, branch,
):
    total = jnp.zeros((1, D), f32)
    for r in range(0, mid_ref.shape[0], ROWS):
        span = slice(r, r + ROWS)
        unit, inverse = norm_parts(mid_ref[span, :])
        grad = own_ref[span, :] + recv_ref[span, :].astype(f32)
        total = total + jnp.sum(grad * unit, axis=0, keepdims=True)
        back = cot_ref[span, :].astype(f32) + norm_back(grad, unit, inverse, gain_ref[...])
        grad_ref[span, :] = back
        branch[span, :] = back.astype(bf16)
    gain_grad_ref[...] = total
    for side, out in enumerate((b_own_ref, b_other_ref)):
        out[...] = branch[:, pl.ds(pl.multiple_of((side ^ info[0]) * HALF, HALF), HALF)]
    att = dot_nt(b_own_ref[...], o_own[...]) + dot_nt(b_other_ref[...], o_other[...])
    att_ref[...] = att.astype(bf16)


def back_middle(info, middle, own, received, cotangent, gain, o_own, o_other):
    rows = middle.shape[0]
    part = jax.ShapeDtypeStruct((rows, HALF), bf16)
    return pl.pallas_call(
        back_middle_kernel,
        out_shape=(
            jax.ShapeDtypeStruct((rows, D), f32),
            part,
            part,
            jax.ShapeDtypeStruct((rows, D), bf16),
            jax.ShapeDtypeStruct((1, D), f32),
        ),
        grid=(1,),
        in_specs=[SMEM] + [VMEM] * 5 + [OUT_COLS] * 2,
        out_specs=(VMEM,) * 5,
        scratch_shapes=[pltpu.VMEM((rows, D), bf16)],
        compiler_params=params(40),
        cost_estimate=COST,
        name="back_middle",
    )(info, middle, own, received, cotangent, gain, o_own, o_other)


def project_kernel(x_ref, w_ref, out_ref):
    for first in range(0, 3 * HALF, HALF):
        cols = slice(first, first + HALF)
        out_ref[:, cols] = dot(x_ref[...], w_ref[:, cols]).astype(bf16)


def project(values, weights):
    return pl.pallas_call(
        project_kernel,
        out_shape=jax.ShapeDtypeStruct((values.shape[0], 3 * HALF), bf16),
        grid=(1,),
        in_specs=[VMEM, QKV_COLS],
        out_specs=VMEM,
        compiler_params=params(32),
        cost_estimate=COST,
        name="project",
    )(values, weights)


def back_project_kernel(first, g_own, g_other, w_own, w_other, out_ref):
    rows = slice(first, first + out_ref.shape[0])
    for at in range(0, D, HALF):
        cols = slice(at, at + HALF)
        value = dot_nt(g_own[rows, :], w_own[cols, :]) + dot_nt(g_other[rows, :], w_other[cols, :])
        out_ref[:, cols] = value.astype(out_ref.dtype)


def back_project(g_own, g_other, w_own, w_other, first, rows, dtype):
    return pl.pallas_call(
        functools.partial(back_project_kernel, first),
        out_shape=jax.ShapeDtypeStruct((rows, D), dtype),
        grid=(1,),
        in_specs=[VMEM, VMEM, QKV_COLS, QKV_COLS],
        out_specs=VMEM,
        compiler_params=params(40),
        cost_estimate=COST,
        name="back_project",
    )(g_own, g_other, w_own, w_other)


def back_first_kernel(
    tok_ref, part_ref, sent_ref, last_ref, mid_ref, gain_ref, out_ref, gain_grad_ref
):
    total = jnp.zeros((1, D), f32)
    for r in range(0, tok_ref.shape[0], ROWS):
        span = slice(r, r + ROWS)
        unit, inverse = norm_parts(tok_ref[span, :].astype(f32))
        sent = sent_ref[span, :] if r < OWN else last_ref[r - OWN : r - OWN + ROWS, :]
        grad = part_ref[span, :] + sent.astype(f32)
        total = total + jnp.sum(grad * unit, axis=0, keepdims=True)
        back = mid_ref[span, :] + norm_back(grad, unit, inverse, gain_ref[...])
        out_ref[span, :] = back.astype(bf16)
    gain_grad_ref[...] = total


def back_first(tokens, part, sent, last, grad_middle, gain):
    return pl.pallas_call(
        back_first_kernel,
        out_shape=(
            jax.ShapeDtypeStruct(tokens.shape, bf16),
            jax.ShapeDtypeStruct((1, D), f32),
        ),
        in_specs=[VMEM] * 6,
        out_specs=(VMEM,) * 2,
        compiler_params=params(32),
        cost_estimate=COST,
        name="back_first",
    )(tokens, part, sent, last, grad_middle, gain)


def weight_grad_kernel(
    ndp, nz, info, x_own, x_par, g_own, g_par, a_own, a_par, b_own, b_par,
    keep_ref, send_ref,
):
    block = D // ndp
    rows = block // nz
    z = info[ndp]
    half = ndp // 2
    for p in range(ndp):
        cols = pl.ds(pl.multiple_of(info[p] * block, block), block)
        qkv = dot(x_own[:, cols].T, g_own[...]) + dot(x_par[:, cols].T, g_par[...])
        out = dot(a_own[:, cols].T, b_own[...]) + dot(a_par[:, cols].T, b_par[...])
        qkv = qkv.astype(bf16)
        out = out.astype(bf16)
        dst = keep_ref if p < half else send_ref
        for b in range(nz):
            span = slice(b * rows, (b + 1) * rows)
            r = swap_bits(z ^ b, bits_of(nz))
            dst[p % half, r, :, : 3 * HALF] = qkv[span]
            dst[p % half, r, :, 3 * HALF :] = out[span]


def weight_grads(links, info, x_own, x_par, g_own, g_par, a_own, a_par, b_own, b_par):
    ndp, nz = links.ndp, links.nz
    rows = D // (ndp * nz)
    line = 4 * HALF
    out = jax.ShapeDtypeStruct((ndp // 2, nz, rows, line), bf16)
    return pl.pallas_call(
        functools.partial(weight_grad_kernel, ndp, nz),
        out_shape=(out, out),
        in_specs=[SMEM] + [VMEM] * 8,
        out_specs=(VMEM, VMEM),
        compiler_params=params(48),
        cost_estimate=COST,
        name="weight_grads",
    )(info, x_own, x_par, g_own, g_par, a_own, a_par, b_own, b_par)


def place_kernel(ndp, order, *refs):
    out = refs[ndp]
    b = pl.program_id(0)
    for p in range(ndp):

        @pl.when(order[b] == p)
        def _(p=p):
            out[...] = refs[p][...]


def place(links, order, pieces):
    block, cols = pieces[0].shape
    ndp = links.ndp
    return pl.pallas_call(
        functools.partial(place_kernel, ndp),
        out_shape=jax.ShapeDtypeStruct((ndp * block, cols), pieces[0].dtype),
        grid_spec=pltpu.PrefetchScalarGridSpec(
            num_scalar_prefetch=1,
            grid=(ndp,),
            in_specs=[VMEM] * ndp,
            out_specs=pl.BlockSpec((block, cols), lambda b, order: (b, 0)),
        ),
        compiler_params=params(16),
        cost_estimate=COST,
        name="place",
    )(order, *pieces)


def add_b(left, right):
    return (left.astype(f32) + right.astype(f32)).astype(bf16)


def in_order(links, values):
    ndp, nz = values.shape[:2]
    inner = values.shape[2:]
    bits = links.dp_bits + links.mp_bits - 1
    split = values.reshape((2,) * bits + inner)
    for axis in range(links.dp_bits):
        mine = (links.dp >> (links.dp_bits - 1 - axis)) & 1
        split = jnp.where(mine == 0, split, jnp.flip(split, axis))
    for axis in range(links.dp_bits, bits):
        mine = (links.z >> (bits - 1 - axis)) & 1
        split = jnp.where(mine == 0, split, jnp.flip(split, axis))
    dp_axes, z_axes = list(range(links.dp_bits)), list(range(links.dp_bits, bits))
    rest = list(range(bits, split.ndim))
    split = jnp.where(
        links.core == 0,
        split.transpose(dp_axes[::-1] + z_axes[::-1] + rest),
        split.transpose(dp_axes + z_axes[::-1] + rest),
    )
    return split.reshape(values.shape)


def pack(pieces):
    sizes = [piece.size for piece in pieces]
    packed = jnp.concatenate([piece.reshape(-1) for piece in pieces])
    return jnp.pad(packed, (0, -packed.shape[0] % 128)).reshape(-1, 128), sizes


def merge_kernel(inner, bit, here_ref, there_ref, out):
    count = here_ref.shape[0]
    for i in range(count):
        if inner:
            at, other = 2 * i + bit[0], 2 * i + 1 - bit[0]
        else:
            at, other = bit[0] * count + i, (1 - bit[0]) * count + i
        out[at] = here_ref[i]
        out[other] = there_ref[i]


def merge(here, there, bit, inner):
    shape = (2 * here.shape[0], *here.shape[1:])
    return pl.pallas_call(
        functools.partial(merge_kernel, inner),
        out_shape=jax.ShapeDtypeStruct(shape, here.dtype),
        in_specs=[SMEM, VMEM, VMEM],
        out_specs=VMEM,
        compiler_params=params(16),
        cost_estimate=COST,
        name="merge",
    )(bit.astype(jnp.int32).reshape(1), here, there)


def join_small(links, current, received, index, bit):
    return merge(current, received, (index >> bit) & 1, False)


class Live:
    pass


def fence(live, transfers=(), waits=()):
    held = dict(vars(live))
    tree = (held, [t.state for t in transfers], [t.received for t in waits])
    leaves, form = jax.tree.flatten(tree)
    held, states, received = jax.tree.unflatten(form, lax.optimization_barrier(leaves))
    vars(live).update(held)
    for t, state in zip(transfers, states):
        t.state = state
    for t, values in zip(waits, received):
        t.received = values
    for t in waits:
        t.join()


class Gather:
    def __init__(self, links, values):
        self.links = links
        self.state = [values[None]]
        self.kind = None

    def along_z(self, bit, first=0, last=None):
        self.kind, self.bit, self.span = "z", bit, slice(first, last)
        self.received = [self.links.mp_swap(piece, bit) for piece in self.state[self.span]]

    def along_dp(self, level):
        self.kind = "d"
        self.received = [self.links.fan(piece, level) for piece in self.state]

    def last_dp(self, first, last):
        if first == 0:
            self.count = len(self.state)
        last = self.count if last is None else last
        self.kind = "d"
        self.received = [self.links.fan(piece, 0) for piece in self.state[first:last]]

    def join(self):
        if self.kind == "d":
            self.state = self.state + self.received
        else:
            mine = (self.links.mp >> self.bit) & 1
            joined = [
                merge(piece, received, mine, True)
                for piece, received in zip(self.state[self.span], self.received)
            ]
            self.state = self.state[: self.span.start] + joined + (
                [] if self.span.stop is None else self.state[self.span.stop :]
            )
        self.received = None

    def first_z(self):
        for bit in reversed(range(2, self.links.mp_bits)):
            if self.received is not None:
                self.join()
            self.along_z(bit)

    def along_z_but_last(self, first, last):
        for bit in reversed(range(2, self.links.mp_bits)):
            if self.received is not None:
                self.join()
            self.along_z(bit, first, last)

    def first_dp(self):
        self.received = None
        for level in reversed(range(1, self.links.dp_bits)):
            if self.received is not None:
                self.join()
            self.along_dp(level)

    received = None

    def blocks(self):
        return [piece.reshape(-1, piece.shape[2]) for piece in self.state]


def add_kernel(axis, keep_ref, recv_ref, *outs):
    part = keep_ref.shape[axis] // len(outs)
    for i, out in enumerate(outs):
        span = (slice(None),) * axis + (slice(i * part, (i + 1) * part),)
        total = keep_ref[span].astype(f32) + recv_ref[span].astype(f32)
        out[...] = total.astype(out.dtype)


def add_split(keep, received, axis):
    shape = list(keep.shape)
    if axis is None:
        outs = (jax.ShapeDtypeStruct(shape, f32),)
    else:
        shape[axis] //= 2
        outs = (jax.ShapeDtypeStruct(shape, keep.dtype),) * 2
    return pl.pallas_call(
        functools.partial(add_kernel, axis or 0),
        out_shape=outs,
        in_specs=[VMEM] * 2,
        out_specs=(VMEM,) * len(outs),
        compiler_params=params(32),
        cost_estimate=COST,
        name="add_split",
    )(keep, received)


class Scatter:
    def __init__(self, links, keep, send):
        self.links = links
        self.state = [keep, send]
        self.steps = [("d", level) for level in range(links.dp_bits)]
        self.steps += [("z", bit) for bit in range(1, links.mp_bits)]
        self.result = None

    def start(self):
        kind, index = self.steps[0]
        swap = self.links.mp_swap if kind == "z" else self.links.fan
        self.received = swap(self.state[1], index)

    def join(self):
        self.steps.pop(0)
        keep, received = self.state[0], self.received
        if not self.steps:
            self.result = add_split(keep, received, None)[0][0, 0]
            self.state = []
            return
        self.state = list(add_split(keep, received, 1 if self.steps[0][0] == "z" else 0))

    def finish(self):
        while self.steps:
            self.start()
            self.join()


def body(
    tokens, cotangent, first_gain, second_gain, w_query, w_key, w_value, w_out, w_up, w_down,
    state_rate, state_in, state_out, state_bank, prev_link,
):
    links = Links()
    ndp, nmp, nz = links.ndp, links.nmp, links.nz
    rows = tokens.shape[0]
    per_window = LEN // BLK
    place_in = links.mp % per_window
    window = links.dp * (nmp // per_window) + links.mp // per_window
    link = lax.dynamic_index_in_dim(prev_link, window, keepdims=False)
    info = jnp.stack([links.block_at(p) for p in range(ndp)] + [links.z, links.core]).astype(jnp.int32)
    order = []
    for b in range(ndp):
        far = links.dp ^ b
        order.append(jnp.where(links.core == 0, swap_bits(far, links.dp_bits), far))
    order = jnp.stack(order).astype(jnp.int32)
    attend_info = jnp.stack([links.core, (place_in != 0).astype(jnp.int32)]).astype(jnp.int32)

    channels = state_rate.shape[0]
    maps_here = state_rate.shape[1]
    banks_here = state_bank.shape[0]

    def full_map(values):
        values = values.reshape(ndp, nmp, maps_here, channels).transpose(0, 2, 1, 3)
        return values.reshape(NS, 8, 128)

    def halves(values):
        values = values.reshape(values.shape[0], -1, 2, HALF)
        keep = jnp.where(links.core == 0, values[:, :, 0], values[:, :, 1])
        send = jnp.where(links.core == 0, values[:, :, 1], values[:, :, 0])
        return keep.reshape(keep.shape[0], -1), send.reshape(send.shape[0], -1)

    mats_keep, mats_send = halves(jnp.stack([w_query, w_key, w_value, w_out], 1).astype(bf16))
    chunk = FF // nmp
    groups = 2 if chunk >= 256 else 1
    width = chunk // groups
    both = jnp.stack([w_up, w_down.T], 1).astype(bf16)
    both = both.reshape(both.shape[0], 2, nz, 2, groups, width).transpose(0, 3, 4, 1, 2, 5)
    feed_rows = both.reshape(both.shape[0], -1)

    def chip_rows(keep, send):
        return by_core(links, keep, links.core_swap(send), 0)

    pieces = [
        first_gain, second_gain, state_rate.T, state_in.T, state_out.T,
        state_bank.transpose(0, 2, 1),
    ]
    small, sizes = pack(pieces)
    v = Live()
    v.tokens, v.cotangent = tokens, cotangent
    small = small[None]
    v.small = join_small(links, small, links.core_swap(small), links.mp, 0)
    attn = Gather(links, chip_rows(mats_keep, mats_send))
    v.feed_rows = feed_rows
    fence(v, [attn])

    attn.first_z()
    for bit in range(1, links.mp_bits):
        v.small = join_small(links, v.small, links.mp_swap(v.small, bit), links.mp, bit)
    fence(v, [attn], [attn])

    feed_weights = lax.all_gather(v.feed_rows, AXES, axis=0, tiled=True)
    del v.feed_rows
    attn.along_z(1)
    for bit in range(links.dp_bits):
        v.small = join_small(links, v.small, links.dp_swap(v.small, bit), links.dp, bit)
    small = v.small.reshape(ndp, nmp, -1)
    del v.small
    starts = [sum(sizes[:i]) for i in range(len(sizes))]
    gain_one, gain_two, rate, gain_in, gain_out, banks = (
        small[:, :, a : a + n] for a, n in zip(starts, sizes)
    )
    v.gain_one = lax.reduce_precision(gain_one.reshape(1, D), 8, 7)
    v.gain_two = lax.reduce_precision(gain_two.reshape(1, D), 8, 7)
    v.rate, v.gain_in, v.gain_out = full_map(rate), full_map(gain_in), full_map(gain_out)
    banks = banks.reshape(ndp, nmp, banks_here, NS, channels)
    bank = lax.dynamic_index_in_dim(banks, link // banks_here, 0, keepdims=False)
    bank = lax.dynamic_index_in_dim(bank, link % banks_here, 1, keepdims=False)
    v.initial = bank.transpose(1, 0, 2).reshape(NS, 8, 128)
    fence(v, [attn], [attn])

    half_blocks = float(BLK)
    v.scal = jnp.stack(
        [place_in.astype(f32) * half_blocks - CTX, (place_in != 0).astype(f32)]
    )
    v.steps, v.steps_back = [], []
    for bit in range(bits_of(per_window)):
        mine = ((links.mp >> bit) & 1).astype(f32)
        inside = (place_in % (1 << bit)).astype(f32)
        span = jnp.float32(half_blocks * (1 << bit))
        v.steps.append(jnp.stack([mine, inside * half_blocks, span]))
        v.steps_back.append(
            jnp.stack([mine, ((1 << bit) - 1 - inside) * half_blocks, span])
        )

    def exchange(bit):
        received = links.mp_swap(v.total, bit)
        v.total, v.before = exchange_step(v.steps[bit], v.total, received, v.before, v.rate)

    attn.first_dp()
    v.normed_b, tail = norm_first(v.tokens, v.gain_one)
    v.tail = links.window_shift(tail, 1)
    v.total = scan_tail(v.tail, scan_own(v.normed_b, v.rate), v.rate)
    v.before = jnp.zeros_like(v.total)
    exchange(0)
    fence(v, [attn], [attn])

    attn.last_dp(0, None)
    for bit in range(1, bits_of(per_window)):
        exchange(bit)
    v.inputs_kv = context_states(
        v.scal, v.tail, v.normed_b, v.before, v.initial, v.rate, v.gain_in, v.gain_out
    )
    v.cot_t = v.cotangent.T
    fence(v, [attn], [attn])

    v.w_own = place(links, order, attn.blocks())
    attn.state = []
    v.w_other = links.core_swap(v.w_own)
    v.qkv_own = project(v.inputs_kv, v.w_own)
    v.cot_par, v.cot_par_t = links.core_swap(v.cotangent), links.core_swap(v.cot_t)
    v.inputs_par = links.core_swap(v.inputs_kv)
    fence(v)
    v.qkv_other = project(v.inputs_kv, v.w_other)
    v.attended = attend(attend_info, v.qkv_own, v.qkv_other)
    v.middle, v.second_b, v.second_t = middle_norm(
        attend_info, v.attended, v.tokens, v.w_own, v.w_other, v.gain_two
    )
    v.attended_par = links.core_swap(v.attended)
    v.second_par, v.second_par_t = links.core_swap(v.second_b), links.core_swap(v.second_t)
    v.feed_weights = feed_weights
    fence(v)

    scatters = []
    earlier = None
    for g in range(groups):
        last = g == groups - 1
        acts = (
            v.second_b, v.second_par, v.cotangent, v.cot_par,
            v.second_t, v.second_par_t, v.cot_t, v.cot_par_t,
        )
        *v.sums, keep, send = feed(
            links, info, acts, v.feed_weights, nz * width, g, groups, earlier, last
        )
        waits = list(scatters)
        scatters.append(Scatter(links, keep, send))
        fence(v, scatters, waits)
        if not last:
            scatters[g].start()
        earlier = v.sums
    first, second = scatters[0], scatters[-1]
    both = [first, second] if groups > 1 else [first]
    v.mix_own, v.mix_par, v.back_own, back_par = v.sums
    del v.sums, v.feed_weights, v.cot_t, v.cot_par, v.cot_par_t, v.second_b, v.second_par
    del v.second_t, v.second_par_t

    for scatter in both:
        scatter.start()
    v.back_recv = links.core_swap(back_par)
    v.grad_middle, v.branch_own, branch_other, v.grad_attended, v.grad_gain_two = back_middle(
        attend_info, v.middle, v.back_own, v.back_recv, v.cotangent, v.gain_two, v.w_own,
        v.w_other,
    )
    v.branch_par = links.core_swap(branch_other)
    v.g_own, v.g_other = attend_back(attend_info, v.qkv_own, v.qkv_other, v.grad_attended)
    v.g_par = links.core_swap(v.g_other)
    v.grad_context = back_project(v.g_own, v.g_other, v.w_own, v.w_other, 0, CTX, bf16)
    v.lows = state_low(v.grad_context, v.rate)
    fence(v, both, both)

    def exchange_back(bit):
        received = links.mp_swap(v.total, bit)
        v.total, v.after = exchange_back_step(
            v.steps_back[bit], v.total, received, v.after, v.rate
        )

    for scatter in both:
        scatter.start()
    v.total = v.lows[0]
    v.after = jnp.zeros_like(v.total)
    exchange_back(0)
    mats = Scatter(
        links,
        *weight_grads(
            links, info, v.inputs_kv, v.inputs_par, v.g_own, v.g_par, v.attended,
            v.attended_par, v.branch_own, v.branch_par,
        ),
    )
    fence(v, [*both, mats], both)

    mats.start()
    for scatter in both:
        scatter.start()
    for bit in range(1, bits_of(per_window)):
        exchange_back(bit)
    sums = state_sums(
        v.scal, v.grad_context, v.tail, v.before, v.lows, v.initial, v.rate, v.gain_in, v.gain_out
    )

    def by_owner(values):
        values = values.reshape(ndp, maps_here, nmp, channels).transpose(0, 2, 1, 3)
        return values.reshape(ndp, nmp, -1)

    chosen = jnp.arange(ndp * banks_here, dtype=jnp.int32) == link
    bank_share = sums[3].reshape(NS, nmp, channels).transpose(1, 0, 2)[None]
    bank_share = jnp.where(chosen[:, None, None, None], bank_share, 0.0)
    bank_share = bank_share.reshape(ndp, banks_here, nmp, NS * channels).transpose(0, 2, 1, 3)
    shares = jnp.concatenate(
        [
            by_owner(sums[0]),
            by_owner(sums[1]),
            by_owner(sums[2]),
            bank_share.reshape(ndp, nmp, -1),
            v.grad_gain_two.reshape(ndp, nmp, -1),
        ],
        2,
    ).astype(bf16)
    share_len = shares.shape[2]
    mat_rows = D // (ndp * nz)
    shares = jnp.pad(shares, ((0, 0), (0, 0), (0, -share_len % (128 * mat_rows))))
    shares = shares.reshape(ndp, nz, 2, mat_rows, -1)
    shares_keep = jnp.where(links.core == 0, shares[:, :, 0], shares[:, :, 1])
    shares_send = jnp.where(links.core == 0, shares[:, :, 1], shares[:, :, 0])
    shares = in_order(links, add_b(shares_keep, links.core_swap(shares_send)))
    small = Scatter(links, shares[: ndp // 2], shares[ndp // 2 :])
    small.start()
    v.part = back_project(v.g_own, v.g_other, v.w_own, v.w_other, CTX, BLK, f32)
    fence(v, [*both, mats, small], [*both, mats, small])

    mats.state = [jnp.concatenate([a, b], -1) for a, b in zip(mats.state, small.state)]
    mats.start()
    late = [second] if second.steps else []
    for scatter in late:
        scatter.start()
    tail_sent = sent_tail(v.grad_context, v.after, v.rate, v.gain_in, v.gain_out)
    v.last_sent = links.window_shift(tail_sent, -1)
    v.own_sent = sent_own(v.after, v.rate, v.gain_in, v.gain_out)
    fence(v, [*both, mats], [mats, *late])
    mats.start()
    v.grad_tokens, grad_gain_one = back_first(
        v.tokens, v.part, v.own_sent, v.last_sent, v.grad_middle, v.gain_one
    )
    v.gain_parts = grad_gain_one.reshape(ndp * nmp, -1)
    v.mix_recv = links.core_swap(v.mix_par)
    fence(v, [*both, mats], [mats])
    gain_parts = lax.all_to_all(v.gain_parts, AXES, split_axis=0, concat_axis=0, tiled=True)
    v.share_one = jnp.sum(gain_parts, axis=0)
    mats.start()
    for scatter in both:
        scatter.finish()
    v.mixed = (v.middle + (v.mix_own + v.mix_recv.astype(f32))).astype(bf16)
    mats.join()
    mats.finish()
    grad_tokens = v.grad_tokens
    mixed, share_one = v.mixed, v.share_one
    mats_share = mats.result
    grad_up = jnp.concatenate([scatter.result[0] for scatter in both], 1)
    grad_down = jnp.concatenate([scatter.result[1] for scatter in both], 1).T

    line = 4 * HALF
    flat = mats_share[:, line:].reshape(-1)[:share_len]
    map_size = maps_here * channels
    grad_maps = [
        flat[i * map_size : (i + 1) * map_size].reshape(maps_here, channels).T for i in range(3)
    ]
    bank_end = share_len - D // (ndp * nmp)
    grad_bank = flat[3 * map_size : bank_end].reshape(banks_here, NS, channels)
    grad_bank = grad_bank.transpose(0, 2, 1)
    share_two = flat[bank_end:]
    mine_rows = mats_share[:, :line].reshape(2, mat_rows // 2, 4, HALF)
    rows_keep = jnp.where(links.core == 0, mine_rows[0], mine_rows[1])
    rows_send = jnp.where(links.core == 0, mine_rows[1], mine_rows[0])
    grad_rows = by_core(links, rows_keep, links.core_swap(rows_send), 2)
    return (
        mixed, grad_tokens, share_one, share_two,
        grad_rows[:, 0], grad_rows[:, 1], grad_rows[:, 2], grad_rows[:, 3],
        grad_up, grad_down, grad_maps[0], grad_maps[1], grad_maps[2], grad_bank,
    )


def solution(mesh):
    split = P(AXES, None)
    gain = P(AXES)
    maps = P("mp", "dp")
    bank = P("dp", "mp", None)
    return jax.shard_map(
        body,
        mesh=mesh,
        in_specs=(
            split, split, gain, gain, split, split, split, split, split, P(None, AXES),
            maps, maps, maps, bank, P(),
        ),
        out_specs=(
            split, split, gain, gain, split, split, split, split, P("dp", "mp"), P("mp", "dp"),
            maps, maps, maps, bank,
        ),
        check_vma=False,
    )
```

time: 541 us -> 396 us (0.73)
  Pallas kernels: 216 us -> 148 us
  other arithmetic: 62.3 us -> 17.8 us
  matrix products: 38.9 us -> 0 us
  local copies, waits for them, and re-layouts: 51.2 us -> 27.6 us
  between operations: 4.81 us -> 17.6 us
  waiting for transfers between devices: 98.9 us -> 110 us
  starting transfers between devices: 60.5 us -> 67.9 us
    pallas_call x6 -> x42, Pallas kernels: 184 us -> 119 us  [the longest x2 46.3 us: feed(): pl.pallas_call(functools.partial(feed_kernel, ndp, nz, width, index, grou...]
    dot_general x16 -> x0, matrix products: 38.9 us -> none  [the longest x6 16.3 us: dot_nt(): return lax.dot_general(left, right, NT, preferred_element_type=f32)]
    convert_element_type x7 -> x1, other arithmetic: 13.4 us -> 1.2 us  [add_b(): return (left.astype(f32) + right.astype(f32)).astype(bf16)]
    slice x18 -> x4, local copies, waits for them, and re-layouts: 11.5 us -> 0.05 us  [the longest x3 0.04 us: body(): small = Scatter(links, shares[:ndp // 2], shares[ndp // 2:])]
    concatenate x9 -> x3, other arithmetic: 10.3 us -> 1.9 us  [the longest x1 1.79 us: body(): grad_up = jnp.concatenate([scatter.result[0] for scatter in both], 1)]
    all_to_all x1, waiting for transfers between devices: 0.01 us -> 8.28 us  [body(): lax.all_to_all(v.gain_parts, AXES, split_axis=0, concat_axis=0, tiled=True)]
    ppermute x51 -> x45, starting transfers between devices: 55.3 us -> 63.3 us  [send(): return lax.ppermute(values, AXES, pairs)]
    select_n x21 -> x6, other arithmetic: 7.21 us -> 0.38 us  [the longest x4 0.25 us: in_order(): split = jnp.where(mine == 0, split, jnp.flip(split, axis))]
  transfers between devices with their start and end apart: 52 -> 47, of which waited for: 17 -> 23; matrix products, arithmetic and copies ran while one was open for 26% -> 7% of each run, Pallas kernels for 36% -> 31%
where the time goes in v2:
time: 396 us; the launch traced here: 390 us
  Pallas kernels  148 us (37%)
  waiting for transfers between devices  110 us (28%)
  starting transfers between devices  67.9 us (17%)
  local copies, waits for them, and re-layouts  27.6 us (7%)
  other arithmetic  17.8 us (4%)
  between operations  17.6 us (4%)
    ppermute x45, waiting for transfers between devices, send(): return lax.ppermute(values, AXES, pairs)  98.5 us
    ppermute x45, starting transfers between devices, send(): return lax.ppermute(values, AXES, pairs)  63.3 us
    pallas_call x2, Pallas kernels, feed(): pl.pallas_call(functools.partial(feed_kernel, ndp, nz, width, index, grou...  46.3 us
    unnamed x118, local copies, waits for them, and re-layouts  14.7 us
    pallas_call x1, Pallas kernels, attend_back(): pl.pallas_call(attend_back_kernel, out_shape=(out, out), in_specs=[SMEM]...  12 us
    pallas_call x2, Pallas kernels, back_project(): pl.pallas_call(functools.partial(back_project_kernel, first), out_shape=j...  11.4 us
    pallas_call x1, Pallas kernels, weight_grads(): pl.pallas_call(functools.partial(weight_grad_kernel, ndp, nz), out_shape=...  10.9 us
    all_to_all x1, waiting for transfers between devices, body(): lax.all_to_all(v.gain_parts, AXES, split_axis=0, concat_axis=0, tiled=True)  8.28 us
  transfers between devices with their start and end apart: 47, of which 23 were waited for; matrix products, arithmetic and copies ran while one was open for 7% of the time, Pallas kernels for 31%

profile of v2, /device:TPU:0, one launch (start us, length us, event | category | flops | bytes accessed | tf_op | source)
XLA Modules:
  0.0 389.6 jit_solution(7564864111770911515)
XLA Ops:
  15.6 4.1 %collective-permute-start.4 = (bf16[1,64,2048]{2,1,0:T(8,128)(2,1)S(1)}, bf16[1,64,2048]{2,1,0:T(8,128)(2,1)S(1)}, u32[]{:S(2)}, u32[]{:S(2)}) collective-permute-start(bf16[1,64,2048]{2,1,0:T(8,128)(2,1)S(1)} %maximum_select_fusion.1.here_ref), channel_id=1, source_target_pairs={{0,4},{1,5},{2,6},{3,7},{4,0},{5,1},{6,2},{7,3},{8,12},{9,13},{10,... | collective-permute-start | bytes 786440 | tf_op jit(solution)/shard_map/ppermute | solution.py:70
  19.7 1.6 collective-permute-start.2
  21.3 4.9 %collective-permute-done.2.there_ref = f32[2,29,128]{2,1,0:T(8,128)S(1)} collective-permute-done((f32[2,29,128]{2,1,0:T(8,128)S(1)}, f32[2,29,128]{2,1,0:T(8,128)S(1)}, u32[]{:S(2)}, u32[]{:S(2)}) %collective-permute-start.2) | collective-permute-done | bytes 29728 | tf_op jit(solution)/shard_map/ppermute | solution.py:70
  26.2 2.4 collective-permute-start.3
  28.6 6.0 %collective-permute-done.3.there_ref = f32[4,29,128]{2,1,0:T(8,128)S(1)} collective-permute-done((f32[4,29,128]{2,1,0:T(8,128)S(1)}, f32[4,29,128]{2,1,0:T(8,128)S(1)}, u32[]{:S(2)}, u32[]{:S(2)}) %collective-permute-start.3) | collective-permute-done | bytes 59424 | tf_op jit(solution)/shard_map/ppermute | solution.py:70
  34.7 1.6 collective-permute-start.5
  36.3 3.4 collective-permute-done.5.there_ref
  39.7 1.6 collective-permute-start.6
  50.5 16.8 %collective-permute-done.7.there_ref = bf16[2,64,2048]{2,1,0:T(8,128)(2,1)S(1)} collective-permute-done((bf16[2,64,2048]{2,1,0:T(8,128)(2,1)S(1)}, bf16[2,64,2048]{2,1,0:T(8,128)(2,1)S(1)}, u32[]{:S(2)}, u32[]{:S(2)}) %collective-permute-start.7) | collective-permute-done | bytes 524320 | tf_op jit(solution)/shard_map/ppermute | solution.py:70
  73.3 4.9 %scan_own.1.own_ref = f32[2,16,8,128]{3,2,1,0:T(8,128)S(1)} custom-call(bf16[512,1024]{1,0:T(8,128)(2,1)S(1)} %copy-done.21, f32[16,8,128]{2,1,0:T(8,128)S(1)} %bitcast.163), custom_call_target="tpu_custom_call" | custom-call | flops 1 | bytes 1 | tf_op jit(solution)/shard_map/scan_own/pallas_call | solution.py:162
  78.2 1.6 scan_tail.1.total_ref
  79.8 4.3 %collective-permute-start.9 = (f32[2,16,8,128]{3,2,1,0:T(8,128)S(1)}, f32[2,16,8,128]{3,2,1,0:T(8,128)S(1)}, u32[]{:S(2)}, u32[]{:S(2)}) collective-permute-start(f32[2,16,8,128]{3,2,1,0:T(8,128)S(1)} %scan_tail.1.total_ref), channel_id=1, source_target_pairs={{0,1},{1,0},{2,3},{3,2},{4,5},{5,4},{6,7},{7,6},{8,9},{9,8},{10,11... | collective-permute-start | bytes 393224 | tf_op jit(solution)/shard_map/ppermute | solution.py:70
  85.7 6.7 %collective-permute-done.10 = bf16[4,64,2048]{2,1,0:T(8,128)(2,1)} collective-permute-done((bf16[4,64,2048]{2,1,0:T(8,128)(2,1)}, bf16[4,64,2048]{2,1,0:T(8,128)(2,1)}, u32[]{:S(2)}, u32[]{:S(2)}) %collective-permute-start.10) | collective-permute-done | bytes 1048608 | tf_op jit(solution)/shard_map/ppermute | solution.py:70
  92.5 1.5 collective-permute-start.13
  94.7 12.2 %collective-permute-done.11.recv_ref = f32[2,16,8,128]{3,2,1,0:T(8,128)S(1)} collective-permute-done((f32[2,16,8,128]{3,2,1,0:T(8,128)S(1)}, f32[2,16,8,128]{3,2,1,0:T(8,128)S(1)}, u32[]{:S(2)}, u32[]{:S(2)}) %collective-permute-start.11) | collective-permute-done | bytes 131104 | tf_op jit(solution)/shard_map/ppermute | solution.py:70
  107.8 1.3 copy.71
  109.1 7.7 %collective-permute-done.12.recv_ref = f32[2,16,8,128]{3,2,1,0:T(8,128)S(1)} collective-permute-done((f32[2,16,8,128]{3,2,1,0:T(8,128)S(1)}, f32[2,16,8,128]{3,2,1,0:T(8,128)S(1)}, u32[]{:S(2)}, u32[]{:S(2)}) %collective-permute-start.12) | collective-permute-done | bytes 131104 | tf_op jit(solution)/shard_map/ppermute | solution.py:70
  119.3 2.7 context_states.1.x_ref.x_own
  122.1 5.2 %place.1.w_ref.o_own.w_own = bf16[1024,2048]{1,0:T(8,128)(2,1)} custom-call(s32[4]{0:T(128)S(1)} %pad_add_fusion.1.order, bf16[256,2048]{1,0:T(8,128)(2,1)} %bitcast.41.refs_0_, bf16[256,2048]{1,0:T(8,128)(2,1)} %bitcast.42.refs_1_, bf16[256,2048]{1,0:T(8,128)(2,1)} %bitcast.43.refs_2_, bf16[256,2048]{1,0:T(8,128)(2,1)} %bitcast.44.refs_3_), custom_call_target="tpu_custom_call" | custom-call | flops 1 | bytes 1 | tf_op jit(solution)/shard_map/place/pallas_call | solution.py:921
  128.4 4.1 %project.2.own_ref = bf16[640,1536]{1,0:T(8,128)(2,1)S(1)} custom-call(bf16[640,1024]{1,0:T(8,128)(2,1)S(1)} %context_states.1.x_ref.x_own, bf16[1024,2048]{1,0:T(8,128)(2,1)} %place.1.w_ref.o_own.w_own), custom_call_target="tpu_custom_call" | custom-call | flops 1 | bytes 1 | tf_op jit(solution)/shard_map/project/pallas_call | solution.py:807
  132.5 7.0 %collective-permute-done.15.c_par = bf16[512,1024]{1,0:T(8,128)(2,1)} collective-permute-done((bf16[512,1024]{1,0:T(8,128)(2,1)S(1)}, bf16[512,1024]{1,0:T(8,128)(2,1)}, u32[]{:S(2)}, u32[]{:S(2)}) %collective-permute-start.15) | collective-permute-done | bytes 1048608 | tf_op jit(solution)/shard_map/ppermute | solution.py:70
  139.9 4.1 %project.3.other_ref = bf16[640,1536]{1,0:T(8,128)(2,1)S(1)} custom-call(bf16[640,1024]{1,0:T(8,128)(2,1)S(1)} %context_states.1.x_ref.x_own, bf16[1024,2048]{1,0:T(8,128)(2,1)} %collective-permute-done.18.w_ref.o_other.w_other), custom_call_target="tpu_custom_call" | custom-call | flops 1 | bytes 1 | tf_op jit(solution)/shard_map/project/pallas_call | solution.py:807
  144.0 8.0 %attend.1.att_ref.a_own = bf16[512,1024]{1,0:T(8,128)(2,1)S(1)} custom-call(s32[2]{0:T(128)S(1)} %pad_add_fusion.info, bf16[640,1536]{1,0:T(8,128)(2,1)S(1)} %project.2.own_ref, bf16[640,1536]{1,0:T(8,128)(2,1)S(1)} %project.3.other_ref), custom_call_target="tpu_custom_call" | custom-call | flops 1 | bytes 1 | tf_op jit(solution)/shard_map/attend/pallas_call | solution.py:451
  153.3 5.2 %middle_norm.1 = (f32[512,1024]{1,0:T(8,128)S(1)}, bf16[512,1024]{1,0:T(8,128)(2,1)}, bf16[1024,512]{1,0:T(8,128)(2,1)}) custom-call(s32[2]{0:T(128)S(1)} %pad_add_fusion.info, bf16[512,1024]{1,0:T(8,128)(2,1)S(1)} %attend.1.att_ref.a_own, bf16[512,1024]{1,0:T(8,128)(2,1)S(1)} %copy-done.11, bf16[1024,2048]{1,0:T(8,128)(2,1)} %place.1.w_ref.o_own.w_own, ...), custom_call_target="tpu_custom_call" | custom-call | flops 1 | bytes 1 | tf_op jit(solution)/shard_map/middle_norm/pallas_call | solution.py:742
  158.5 1.4 copy-done.13
  161.1 1.7 collective-permute-done.20.s_par
  162.9 3.1 collective-permute-done.21.st_par
  166.0 3.5 all-gather.2.cloned.1.call-done.rest_0_
  169.5 23.5 %feed_first.1 = (f32[1024,1024]{1,0:T(8,128)}, f32[1024,1024]{1,0:T(8,128)}, bf16[2,4,2,256,256]{4,3,2,1,0:T(8,128)(2,1)}, bf16[2,4,2,256,256]{4,3,2,1,0:T(8,128)(2,1)}) custom-call(s32[6]{0:T(128)} %stack.159.info, bf16[512,1024]{1,0:T(8,128)(2,1)} %get-tuple-element.502.s_own, bf16[512,1024]{1,0:T(8,128)(2,1)} %collective-permute-done.20.s_par, ...), custom_call_target="tpu_custom_call" | custom-call | flops 1 | bytes 1 | tf_op jit(solution)/shard_map/feed_first/pallas_call | solution.py:651
  193.1 4.0 %collective-permute-start.22 = (bf16[2,4,2,256,256]{4,3,2,1,0:T(8,128)(2,1)}, bf16[2,4,2,256,256]{4,3,2,1,0:T(8,128)(2,1)}, u32[]{:S(2)}, u32[]{:S(2)}) collective-permute-start(bf16[2,4,2,256,256]{4,3,2,1,0:T(8,128)(2,1)} %get-tuple-element.520), channel_id=1, source_target_pairs={{0,8},{1,17},{2,10},{3,19},{4,12},{5,21},{6,14},{7,23},{8,0},{9,25... | collective-permute-start | bytes 6291464 | tf_op jit(solution)/shard_map/ppermute | solution.py:70
  197.1 22.8 %feed_last.1 = (f32[512,1024]{1,0:T(8,128)}, bf16[512,1024]{1,0:T(8,128)(2,1)}, f32[512,1024]{1,0:T(8,128)}, bf16[512,1024]{1,0:T(8,128)(2,1)}, bf16[2,4,2,256,2...) custom-call(s32[6]{0:T(128)} %stack.159.info, bf16[512,1024]{1,0:T(8,128)(2,1)} %get-tuple-element.502.s_own, ...), custom_call_target="tpu_custom_call" | custom-call | flops 1 | bytes 1 | tf_op jit(solution)/shard_map/feed_last/pallas_call | solution.py:651
  219.8 1.6 collective-permute-done.22.recv_ref
  221.4 2.1 collective-permute-start.27
  224.3 1.6 copy-done.14
  225.9 1.6 copy-done.25
  227.5 4.4 %back_middle.1 = (f32[512,1024]{1,0:T(8,128)S(1)}, bf16[512,512]{1,0:T(8,128)(2,1)S(1)}, bf16[512,512]{1,0:T(8,128)(2,1)S(1)}, bf16[512,1024]{1,0:T(8,128)(2,1)S(1)}, f32[1,1024]{1,0:T(1,128)S(1)}) custom-call(s32[2]{0:T(128)S(1)} %pad_add_fusion.info, f32[512,1024]{1,0:T(8,128)S(1)} %copy-done.14, f32[512,1024]{1,0:T(8,128)S(1)} %copy-done.25, ...), custom_call_target="tpu_custom_call" | custom-call | flops 1 | bytes 1 | tf_op jit(solution)/shard_map/back_middle/pallas_call | solution.py:781
  231.9 1.3 copy-done.29
  233.2 12.0 %attend_back.1 = (bf16[640,1536]{1,0:T(8,128)(2,1)S(1)}, bf16[640,1536]{1,0:T(8,128)(2,1)S(1)}) custom-call(s32[2]{0:T(128)S(1)} %pad_add_fusion.info, bf16[640,1536]{1,0:T(8,128)(2,1)S(1)} %copy-done.3, bf16[640,1536]{1,0:T(8,128)(2,1)S(1)} %copy-done.5, bf16[512,1024]{1,0:T(8,128)(2,1)S(1)} %get-tuple-element.537.grad_ref), custom_call_target="tpu_custom_call" | custom-call | flops 1 | bytes 1 | tf_op jit(solution)/shard_map/attend_back/pallas_call | solution.py:502
  245.4 3.3 add_split.13
  249.3 1.4 collective-permute-start.24
  250.6 5.1 %back_project.2.g_ref = bf16[128,1024]{1,0:T(8,128)(2,1)S(1)} custom-call(bf16[640,1536]{1,0:T(8,128)(2,1)S(1)} %get-tuple-element.615.g_own, bf16[640,1536]{1,0:T(8,128)(2,1)S(1)} %get-tuple-element.614.g_other, bf16[1024,2048]{1,0:T(8,128)(2,1)} %place.1.w_ref.o_own.w_own, bf16[1024,2048]{1,0:T(8,128)(2,1)} %collective-permute-done.18.w_ref.o_other.w_other), custom_call_target="tpu_custom_call" | custom-call | flops 1 | bytes 1 | tf_op jit(solution)/shard_map/back_project/pallas_call | solution.py:828
  255.8 1.5 state_low.1.lows_ref
  257.3 6.3 %collective-permute-done.26.recv_ref = bf16[1,4,2,256,256]{4,3,2,1,0:T(8,128)(2,1)S(1)} collective-permute-done((bf16[1,4,2,256,256]{4,3,2,1,0:T(8,128)(2,1)S(1)}, bf16[1,4,2,256,256]{4,3,2,1,0:T(8,128)(2,1)S(1)}, u32[]{:S(2)}, u32[]{:S(2)}) %collective-permute-start.26) | collective-permute-done | bytes 1048608 | tf_op jit(solution)/shard_map/ppermute | solution.py:70
  264.9 4.2 %collective-permute-start.29 = (bf16[1,2,2,256,256]{4,3,2,1,0:T(8,128)(2,1)S(1)}, bf16[1,2,2,256,256]{4,3,2,1,0:T(8,128)(2,1)S(1)}, u32[]{:S(2)}, u32[]{:S(2)}) collective-permute-start(bf16[1,2,2,256,256]{4,3,2,1,0:T(8,128)(2,1)S(1)} %get-tuple-element.598), channel_id=1, source_target_pairs={{0,2},{1,3},{2,0},{3,1},{4,6},{5,7},{6,4},{7,5},{8,10},{9,11},{10,... | collective-permute-start | bytes 1572872 | tf_op jit(solution)/shard_map/ppermute | solution.py:70
  270.0 10.9 %weight_grads.1 = (bf16[2,4,64,2048]{3,2,1,0:T(8,128)(2,1)}, bf16[2,4,64,2048]{3,2,1,0:T(8,128)(2,1)}) custom-call(s32[6]{0:T(128)S(1)} %copy-done.41, bf16[640,1024]{1,0:T(8,128)(2,1)S(1)} %context_states.1.x_ref.x_own, bf16[640,1024]{1,0:T(8,128)(2,1)} %collective-permute-done.17.x_par, bf16[640,1536]{1,0:T(8,128)(2,1)} %copy-done, ...), custom_call_target="tpu_custom_call" | custom-call | flops 1 | bytes 1 | tf_op jit(solution)/shard_map/weight_grads/pallas_call | solution.py:897
  281.7 4.0 %state_sums.1 = f32[4,16,8,128]{3,2,1,0:T(8,128)S(1)} custom-call(f32[2]{0:T(128)S(1)} %pad_maximum_fusion.11.scal, bf16[128,1024]{1,0:T(8,128)(2,1)S(1)} %back_project.2.g_ref, bf16[128,1024]{1,0:T(8,128)(2,1)S(1)} %copy-done.24, f32[2,16,8,128]{3,2,1,0:T(8,128)S(1)} %copy-done.36, f32[2,16,8,128]{3,2,1,0:T(8,128)S(1)} %state_low.1.lows_ref, ...), custom_call_target="tpu_custom_call" | custom-call | flops 1 | bytes 1 | tf_op jit(solution)/shard_map/state_sums/pallas_call | solution.py:339
  286.3 1.6 collective-permute-start.36
  290.2 1.8 collective-permute-start.35
  292.2 7.9 %collective-permute-start.34 = (bf16[1,1,2,256,256]{4,3,2,1,0:T(8,128)(2,1)S(1)}, bf16[1,1,2,256,256]{4,3,2,1,0:T(8,128)(2,1)S(1)}, u32[]{:S(2)}, u32[]{:S(2)}) collective-permute-start(bf16[1,1,2,256,256]{4,3,2,1,0:T(8,128)(2,1)S(1)} %get-tuple-element.635), channel_id=1, source_target_pairs={{0,4},{1,5},{2,6},{3,7},{4,0},{5,1},{6,2},{7,3},{8,12},{9,13},{10,... | collective-permute-start | bytes 786440 | tf_op jit(solution)/shard_map/ppermute | solution.py:70
  303.8 7.9 %collective-permute-done.31.recv_ref = f32[16,8,128]{2,1,0:T(8,128)S(1)} collective-permute-done((f32[16,8,128]{2,1,0:T(8,128)S(1)}, f32[16,8,128]{2,1,0:T(8,128)S(1)}, u32[]{:S(2)}, u32[]{:S(2)}) %collective-permute-start.31) | collective-permute-done | bytes 65568 | tf_op jit(solution)/shard_map/ppermute | solution.py:70
  312.3 7.9 %collective-permute-start.32 = (f32[16,8,128]{2,1,0:T(8,128)S(1)}, f32[16,8,128]{2,1,0:T(8,128)S(1)}, u32[]{:S(2)}, u32[]{:S(2)}) collective-permute-start(f32[16,8,128]{2,1,0:T(8,128)S(1)} %get-tuple-element.610.total_ref), channel_id=1, source_target_pairs={{0,4},{1,5},{2,6},{3,7},{4,0},{5,1},{6,2},{7,3},{8,12},{9,13},{10,... | collective-permute-start | bytes 196616 | tf_op jit(solution)/shard_map/ppermute | solution.py:70
  320.1 6.3 %back_project.3.part_ref = f32[512,1024]{1,0:T(8,128)S(1)} custom-call(bf16[640,1536]{1,0:T(8,128)(2,1)S(1)} %copy-done.1, bf16[640,1536]{1,0:T(8,128)(2,1)S(1)} %copy-done.17, bf16[1024,2048]{1,0:T(8,128)(2,1)} %place.1.w_ref.o_own.w_own, bf16[1024,2048]{1,0:T(8,128)(2,1)} %collective-permute-done.18.w_ref.o_other.w_other), custom_call_target="tpu_custom_call" | custom-call | flops 1 | bytes 1 | tf_op jit(solution)/shard_map/back_project/pallas_call | solution.py:828
  328.4 1.7 collective-permute-start.39
  330.4 3.6 sent_own.1.sent_ref
  334.0 2.1 sent_tail.1
  337.5 5.9 %collective-permute-done.40.recv_ref = bf16[1,1,2,256,256]{4,3,2,1,0:T(8,128)(2,1)S(1)} collective-permute-done((bf16[1,1,2,256,256]{4,3,2,1,0:T(8,128)(2,1)S(1)}, bf16[1,1,2,256,256]{4,3,2,1,0:T(8,128)(2,1)S(1)}, u32[]{:S(2)}, u32[]{:S(2)}) %collective-permute-start.40) | collective-permute-done | bytes 262176 | tf_op jit(solution)/shard_map/ppermute | solution.py:70
  343.9 1.9 collective-permute-start.41
  348.0 2.7 back_first.1
  352.4 2.0 copy.82
  356.3 1.8 pad_maximum_fusion.1
  358.1 3.6 collective-permute-done.42.recv_ref
  362.7 4.5 %all-to-all-start = ((f32[32,1,32]{2,1,0:T(1,128)}), f32[32,1,32]{2,1,0:T(1,128)S(1)}, u32[]{:S(2)}, u32[]{:S(2)}) async-start(f32[32,1,32]{2,1,0:T(1,128)} %bitcast.73), calls=%async_computation | async-start | bytes 32768 | tf_op jit(solution)/shard_map/all_to_all | solution.py:1373
  367.3 3.4 add_convert_fusion
  370.7 8.3 %all-to-all-done = f32[32,1,32]{2,1,0:T(1,128)S(1)} async-done(((f32[32,1,32]{2,1,0:T(1,128)}), f32[32,1,32]{2,1,0:T(1,128)S(1)}, u32[]{:S(2)}, u32[]{:S(2)}) %all-to-all-start) | async-done | bytes 4128 | tf_op jit(solution)/shard_map/all_to_all | solution.py:1373
  (281 shorter events, 56.9 us)
Async XLA Ops:
  7.3 162.3 %all-gather.2.cloned.1.call-start = ((), (), s32[]{:S(2)}) async-start(), calls=%async_computation.1 | async-start | bytes 17301504 | tf_op jit(solution)/shard_map/all_gather | solution.py:1189
  12.5 3.1 collective-permute-start.1
  13.1 2.4 collective-permute-start
  13.9 27.5 %copy-start.54 = (s32[4]{0:T(128)S(1)}, s32[4]{0:T(128)}, u32[]{:S(2)}) copy-start(s32[4]{0:T(128)} %param.29) | copy-start | bytes 52
  15.6 19.1 %collective-permute-start.4 = (bf16[1,64,2048]{2,1,0:T(8,128)(2,1)S(1)}, bf16[1,64,2048]{2,1,0:T(8,128)(2,1)S(1)}, u32[]{:S(2)}, u32[]{:S(2)}) collective-permute-start(bf16[1,64,2048]{2,1,0:T(8,128)(2,1)S(1)} %maximum_select_fusion.1.here_ref), channel_id=1, source_target_pairs={{0,4},{1,5},{2,6},{3,7},{4,0},{5,1},{6,2},{7,3},{8,12},{9,13},{10,... | collective-permute-start | bytes 786440 | tf_op jit(solution)/shard_map/ppermute | solution.py:70
  19.7 6.5 %collective-permute-start.2 = (f32[2,29,128]{2,1,0:T(8,128)S(1)}, f32[2,29,128]{2,1,0:T(8,128)S(1)}, u32[]{:S(2)}, u32[]{:S(2)}) collective-permute-start(f32[2,29,128]{2,1,0:T(8,128)S(1)} %merge.7.here_ref), channel_id=1, source_target_pairs={{0,2},{1,3},{2,0},{3,1},{4,6},{5,7},{6,4},{7,5},{8,10},{9,11},{10,... | collective-permute-start | bytes 89096 | tf_op jit(solution)/shard_map/ppermute | solution.py:70
  26.2 8.4 %collective-permute-start.3 = (f32[4,29,128]{2,1,0:T(8,128)S(1)}, f32[4,29,128]{2,1,0:T(8,128)S(1)}, u32[]{:S(2)}, u32[]{:S(2)}) collective-permute-start(f32[4,29,128]{2,1,0:T(8,128)S(1)} %merge.8.here_ref), channel_id=1, source_target_pairs={{0,4},{1,5},{2,6},{3,7},{4,0},{5,1},{6,2},{7,3},{8,12},{9,13},{10,... | collective-permute-start | bytes 178184 | tf_op jit(solution)/shard_map/ppermute | solution.py:70
  34.7 5.0 %collective-permute-start.5 = (f32[8,29,128]{2,1,0:T(8,128)S(1)}, f32[8,29,128]{2,1,0:T(8,128)S(1)}, u32[]{:S(2)}, u32[]{:S(2)}) collective-permute-start(f32[8,29,128]{2,1,0:T(8,128)S(1)} %merge.9.here_ref), channel_id=1, source_target_pairs={{0,8},{1,9},{2,10},{3,11},{4,12},{5,13},{6,14},{7,15},{8,0},{9,1},... | collective-permute-start | bytes 356360 | tf_op jit(solution)/shard_map/ppermute | solution.py:70
  39.7 6.6 %collective-permute-start.6 = (f32[16,29,128]{2,1,0:T(8,128)S(1)}, f32[16,29,128]{2,1,0:T(8,128)S(1)}, u32[]{:S(2)}, u32[]{:S(2)}) collective-permute-start(f32[16,29,128]{2,1,0:T(8,128)S(1)} %merge.10.here_ref), channel_id=1, source_target_pairs={{0,16},{1,17},{2,18},{3,19},{4,20},{5,21},{6,22},{7,23},{8,24},{9,... | collective-permute-start | bytes 712712 | tf_op jit(solution)/shard_map/ppermute | solution.py:70
  43.9 23.4 %collective-permute-start.7 = (bf16[2,64,2048]{2,1,0:T(8,128)(2,1)S(1)}, bf16[2,64,2048]{2,1,0:T(8,128)(2,1)S(1)}, u32[]{:S(2)}, u32[]{:S(2)}) collective-permute-start(bf16[2,64,2048]{2,1,0:T(8,128)(2,1)S(1)} %merge.12.here_ref), channel_id=1, source_target_pairs={{0,2},{1,3},{2,0},{3,1},{4,6},{5,7},{6,4},{7,5},{8,10},{9,11},{10,... | collective-permute-start | bytes 1572872 | tf_op jit(solution)/shard_map/ppermute | solution.py:70
  46.4 21.9 %copy-start.10 = (bf16[512,1024]{1,0:T(8,128)(2,1)S(1)}, bf16[512,1024]{1,0:T(8,128)(2,1)}, u32[]{:S(2)}) copy-start(bf16[512,1024]{1,0:T(8,128)(2,1)} %tok_ref.1) | copy-start | bytes 3145732
  68.3 39.4 %copy-start.6 = (bf16[512,1024]{1,0:T(8,128)(2,1)S(1)}, bf16[512,1024]{1,0:T(8,128)(2,1)}, u32[]{:S(2)}) copy-start(bf16[512,1024]{1,0:T(8,128)(2,1)} %cot_ref) | copy-start | bytes 3145732
  68.3 24.1 %collective-permute-start.10 = (bf16[4,64,2048]{2,1,0:T(8,128)(2,1)}, bf16[4,64,2048]{2,1,0:T(8,128)(2,1)}, u32[]{:S(2)}, u32[]{:S(2)}) collective-permute-start(bf16[4,64,2048]{2,1,0:T(8,128)(2,1)} %merge.13), channel_id=1, source_target_pairs={{0,16},{1,9},{2,18},{3,11},{4,20},{5,13},{6,22},{7,15},{8,24},{9,1... | collective-permute-start | bytes 3145736 | tf_op jit(solution)/shard_map/ppermute | solution.py:70
  70.0 8.2 %collective-permute-start.8 = (bf16[128,1024]{1,0:T(8,128)(2,1)S(1)}, bf16[128,1024]{1,0:T(8,128)(2,1)S(1)}, u32[]{:S(2)}, u32[]{:S(2)}) collective-permute-start(bf16[128,1024]{1,0:T(8,128)(2,1)S(1)} %get-tuple-element.366), channel_id=1, source_target_pairs={{0,1},{1,2},{2,3},{3,4},{4,5},{5,6},{6,7},{8,9},{9,10},{10,11},{11... | collective-permute-start | bytes 786440 | tf_op jit(solution)/shard_map/ppermute | solution.py:70
  78.2 39.8 %copy-start.23 = (bf16[128,1024]{1,0:T(8,128)(2,1)}, bf16[128,1024]{1,0:T(8,128)(2,1)S(1)}, u32[]{:S(2)}) copy-start(bf16[128,1024]{1,0:T(8,128)(2,1)S(1)} %collective-permute-done.8.x_ref) | copy-start | bytes 786436
  79.8 5.3 %collective-permute-start.9 = (f32[2,16,8,128]{3,2,1,0:T(8,128)S(1)}, f32[2,16,8,128]{3,2,1,0:T(8,128)S(1)}, u32[]{:S(2)}, u32[]{:S(2)}) collective-permute-start(f32[2,16,8,128]{3,2,1,0:T(8,128)S(1)} %scan_tail.1.total_ref), channel_id=1, source_target_pairs={{0,1},{1,0},{2,3},{3,2},{4,5},{5,4},{6,7},{7,6},{8,9},{9,8},{10,11... | collective-permute-start | bytes 393224 | tf_op jit(solution)/shard_map/ppermute | solution.py:70
  92.5 29.6 %collective-permute-start.13 = (bf16[4,64,2048]{2,1,0:T(8,128)(2,1)}, bf16[4,64,2048]{2,1,0:T(8,128)(2,1)}, u32[]{:S(2)}, u32[]{:S(2)}) collective-permute-start(bf16[4,64,2048]{2,1,0:T(8,128)(2,1)} %merge.13), channel_id=1, source_target_pairs={{0,8},{1,17},{2,10},{3,19},{4,12},{5,21},{6,14},{7,23},{8,0},{9,25... | collective-permute-start | bytes 3145736 | tf_op jit(solution)/shard_map/ppermute | solution.py:70
  93.9 28.1 %collective-permute-start.14 = (bf16[4,64,2048]{2,1,0:T(8,128)(2,1)}, bf16[4,64,2048]{2,1,0:T(8,128)(2,1)}, u32[]{:S(2)}, u32[]{:S(2)}) collective-permute-start(bf16[4,64,2048]{2,1,0:T(8,128)(2,1)} %collective-permute-done.10), channel_id=1, source_target_pairs={{0,8},{1,17},{2,10},{3,19},{4,12},{5,21},{6,14},{7,23},{8,0},{9,25... | collective-permute-start | bytes 3145736 | tf_op jit(solution)/shard_map/ppermute | solution.py:70
  94.5 12.4 %collective-permute-start.11 = (f32[2,16,8,128]{3,2,1,0:T(8,128)S(1)}, f32[2,16,8,128]{3,2,1,0:T(8,128)S(1)}, u32[]{:S(2)}, u32[]{:S(2)}) collective-permute-start(f32[2,16,8,128]{3,2,1,0:T(8,128)S(1)} %get-tuple-element.380.total_ref), channel_id=1, source_target_pairs={{0,2},{1,3},{2,0},{3,1},{4,6},{5,7},{6,4},{7,5},{8,10},{9,11},{10,... | collective-permute-start | bytes 393224 | tf_op jit(solution)/shard_map/ppermute | solution.py:70
  107.6 9.2 %collective-permute-start.12 = (f32[2,16,8,128]{3,2,1,0:T(8,128)S(1)}, f32[2,16,8,128]{3,2,1,0:T(8,128)S(1)}, u32[]{:S(2)}, u32[]{:S(2)}) collective-permute-start(f32[2,16,8,128]{3,2,1,0:T(8,128)S(1)} %get-tuple-element.383.total_ref), channel_id=1, source_target_pairs={{0,4},{1,5},{2,6},{3,7},{4,0},{5,1},{6,2},{7,3},{8,12},{9,13},{10,... | collective-permute-start | bytes 393224 | tf_op jit(solution)/shard_map/ppermute | solution.py:70
  127.3 12.6 %collective-permute-start.18 = (bf16[1024,2048]{1,0:T(8,128)(2,1)}, bf16[1024,2048]{1,0:T(8,128)(2,1)}, u32[]{:S(2)}, u32[]{:S(2)}) collective-permute-start(bf16[1024,2048]{1,0:T(8,128)(2,1)} %place.1.w_ref.o_own.w_own), channel_id=1, source_target_pairs={{0,1},{1,0},{2,3},{3,2},{4,5},{5,4},{6,7},{7,6},{8,9},{9,8},{10,11... | collective-permute-start | bytes 12582920 | tf_op jit(solution)/shard_map/ppermute | solution.py:70
  127.3 12.6 %collective-permute-start.17 = (bf16[640,1024]{1,0:T(8,128)(2,1)S(1)}, bf16[640,1024]{1,0:T(8,128)(2,1)}, u32[]{:S(2)}, u32[]{:S(2)}) collective-permute-start(bf16[640,1024]{1,0:T(8,128)(2,1)S(1)} %context_states.1.x_ref.x_own), channel_id=1, source_target_pairs={{0,1},{1,0},{2,3},{3,2},{4,5},{5,4},{6,7},{7,6},{8,9},{9,8},{10,11... | collective-permute-start | bytes 3932168 | tf_op jit(solution)/shard_map/ppermute | solution.py:70
  127.8 11.7 %collective-permute-start.15 = (bf16[512,1024]{1,0:T(8,128)(2,1)S(1)}, bf16[512,1024]{1,0:T(8,128)(2,1)}, u32[]{:S(2)}, u32[]{:S(2)}) collective-permute-start(bf16[512,1024]{1,0:T(8,128)(2,1)S(1)} %copy-done.6), channel_id=1, source_target_pairs={{0,1},{1,0},{2,3},{3,2},{4,5},{5,4},{6,7},{7,6},{8,9},{9,8},{10,11... | collective-permute-start | bytes 3145736 | tf_op jit(solution)/shard_map/ppermute | solution.py:70
  127.9 12.1 %collective-permute-start.16 = (bf16[1024,512]{1,0:T(8,128)(2,1)}, bf16[1024,512]{1,0:T(8,128)(2,1)}, u32[]{:S(2)}, u32[]{:S(2)}) collective-permute-start(bf16[1024,512]{1,0:T(8,128)(2,1)} %bitcast.36.ct_own), channel_id=1, source_target_pairs={{0,1},{1,0},{2,3},{3,2},{4,5},{5,4},{6,7},{7,6},{8,9},{9,8},{10,11... | collective-permute-start | bytes 3145736 | tf_op jit(solution)/shard_map/ppermute | solution.py:70
  159.9 3.0 collective-permute-start.20
  160.0 6.0 %collective-permute-start.21 = (bf16[1024,512]{1,0:T(8,128)(2,1)}, bf16[1024,512]{1,0:T(8,128)(2,1)}, u32[]{:S(2)}, u32[]{:S(2)}) collective-permute-start(bf16[1024,512]{1,0:T(8,128)(2,1)} %get-tuple-element.505.st_own), channel_id=1, source_target_pairs={{0,1},{1,0},{2,3},{3,2},{4,5},{5,4},{6,7},{7,6},{8,9},{9,8},{10,11... | collective-permute-start | bytes 3145736 | tf_op jit(solution)/shard_map/ppermute | solution.py:70
  160.4 5.6 %collective-permute-start.19 = (bf16[512,1024]{1,0:T(8,128)(2,1)S(1)}, bf16[512,1024]{1,0:T(8,128)(2,1)}, u32[]{:S(2)}, u32[]{:S(2)}) collective-permute-start(bf16[512,1024]{1,0:T(8,128)(2,1)S(1)} %attend.1.att_ref.a_own), channel_id=1, source_target_pairs={{0,1},{1,0},{2,3},{3,2},{4,5},{5,4},{6,7},{7,6},{8,9},{9,8},{10,11... | collective-permute-start | bytes 3145736 | tf_op jit(solution)/shard_map/ppermute | solution.py:70
  193.0 31.2 %copy-start.7 = (bf16[512,1024]{1,0:T(8,128)(2,1)S(1)}, bf16[512,1024]{1,0:T(8,128)(2,1)}, u32[]{:S(2)}) copy-start(bf16[512,1024]{1,0:T(8,128)(2,1)} %cot_ref) | copy-start | bytes 3145732
  193.1 28.3 %collective-permute-start.22 = (bf16[2,4,2,256,256]{4,3,2,1,0:T(8,128)(2,1)}, bf16[2,4,2,256,256]{4,3,2,1,0:T(8,128)(2,1)}, u32[]{:S(2)}, u32[]{:S(2)}) collective-permute-start(bf16[2,4,2,256,256]{4,3,2,1,0:T(8,128)(2,1)} %get-tuple-element.520), channel_id=1, source_target_pairs={{0,8},{1,17},{2,10},{3,19},{4,12},{5,21},{6,14},{7,23},{8,0},{9,25... | collective-permute-start | bytes 6291464 | tf_op jit(solution)/shard_map/ppermute | solution.py:70
  221.4 11.8 %copy-start.3 = (bf16[640,1536]{1,0:T(8,128)(2,1)S(1)}, bf16[640,1536]{1,0:T(8,128)(2,1)}, u32[]{:S(2)}) copy-start(bf16[640,1536]{1,0:T(8,128)(2,1)} %copy-done.2) | copy-start | bytes 5898244
  221.4 11.8 %copy-start.5 = (bf16[640,1536]{1,0:T(8,128)(2,1)S(1)}, bf16[640,1536]{1,0:T(8,128)(2,1)}, u32[]{:S(2)}) copy-start(bf16[640,1536]{1,0:T(8,128)(2,1)} %copy-done.4) | copy-start | bytes 5898244
  221.4 2.9 collective-permute-start.23
  221.4 42.2 %collective-permute-start.27 = (bf16[2,4,2,256,256]{4,3,2,1,0:T(8,128)(2,1)}, bf16[2,4,2,256,256]{4,3,2,1,0:T(8,128)(2,1)S(1)}, u32[]{:S(2)}, u32[]{:S(2)}) collective-permute-start(bf16[2,4,2,256,256]{4,3,2,1,0:T(8,128)(2,1)} %get-tuple-element.562), channel_id=1, source_target_pairs={{0,8},{1,17},{2,10},{3,19},{4,12},{5,21},{6,14},{7,23},{8,0},{9,25... | collective-permute-start | bytes 6291464 | tf_op jit(solution)/shard_map/ppermute | solution.py:70
  233.2 12.2 %copy-start.28 = (bf16[2,4,2,256,256]{4,3,2,1,0:T(8,128)(2,1)S(1)}, bf16[2,4,2,256,256]{4,3,2,1,0:T(8,128)(2,1)}, u32[]{:S(2)}) copy-start(bf16[2,4,2,256,256]{4,3,2,1,0:T(8,128)(2,1)} %get-tuple-element.557.keep_ref) | copy-start | bytes 6291460
  245.2 18.3 %collective-permute-start.25 = (bf16[640,1536]{1,0:T(8,128)(2,1)S(1)}, bf16[640,1536]{1,0:T(8,128)(2,1)}, u32[]{:S(2)}, u32[]{:S(2)}) collective-permute-start(bf16[640,1536]{1,0:T(8,128)(2,1)S(1)} %get-tuple-element.614.g_other), channel_id=1, source_target_pairs={{0,1},{1,0},{2,3},{3,2},{4,5},{5,4},{6,7},{7,6},{8,9},{9,8},{10,11... | collective-permute-start | bytes 5898248 | tf_op jit(solution)/shard_map/ppermute | solution.py:70
  248.7 14.9 %collective-permute-start.26 = (bf16[1,4,2,256,256]{4,3,2,1,0:T(8,128)(2,1)S(1)}, bf16[1,4,2,256,256]{4,3,2,1,0:T(8,128)(2,1)S(1)}, u32[]{:S(2)}, u32[]{:S(2)}) collective-permute-start(bf16[1,4,2,256,256]{4,3,2,1,0:T(8,128)(2,1)S(1)} %get-tuple-element.560), channel_id=1, source_target_pairs={{0,16},{1,9},{2,18},{3,11},{4,20},{5,13},{6,22},{7,15},{8,24},{9,1... | collective-permute-start | bytes 3145736 | tf_op jit(solution)/shard_map/ppermute | solution.py:70
  249.3 14.3 %collective-permute-start.24 = (bf16[512,512]{1,0:T(8,128)(2,1)S(1)}, bf16[512,512]{1,0:T(8,128)(2,1)S(1)}, u32[]{:S(2)}, u32[]{:S(2)}) collective-permute-start(bf16[512,512]{1,0:T(8,128)(2,1)S(1)} %get-tuple-element.534), channel_id=1, source_target_pairs={{0,1},{1,0},{2,3},{3,2},{4,5},{5,4},{6,7},{7,6},{8,9},{9,8},{10,11... | collective-permute-start | bytes 1572872 | tf_op jit(solution)/shard_map/ppermute | solution.py:70
  250.6 13.0 %copy-start.27 = (bf16[2,4,2,256,256]{4,3,2,1,0:T(8,128)(2,1)S(1)}, bf16[2,4,2,256,256]{4,3,2,1,0:T(8,128)(2,1)}, u32[]{:S(2)}) copy-start(bf16[2,4,2,256,256]{4,3,2,1,0:T(8,128)(2,1)} %get-tuple-element.599.keep_ref) | copy-start | bytes 6291460
  255.8 26.0 %copy-start.18 = (bf16[128,1024]{1,0:T(8,128)(2,1)}, bf16[128,1024]{1,0:T(8,128)(2,1)S(1)}, u32[]{:S(2)}) copy-start(bf16[128,1024]{1,0:T(8,128)(2,1)S(1)} %back_project.2.g_ref) | copy-start | bytes 786436
  264.1 17.6 %collective-permute-start.30 = (bf16[1,4,2,256,256]{4,3,2,1,0:T(8,128)(2,1)S(1)}, bf16[1,4,2,256,256]{4,3,2,1,0:T(8,128)(2,1)S(1)}, u32[]{:S(2)}, u32[]{:S(2)}) collective-permute-start(bf16[1,4,2,256,256]{4,3,2,1,0:T(8,128)(2,1)S(1)} %get-tuple-element.602), channel_id=1, source_target_pairs={{0,16},{1,9},{2,18},{3,11},{4,20},{5,13},{6,22},{7,15},{8,24},{9,1... | collective-permute-start | bytes 3145736 | tf_op jit(solution)/shard_map/ppermute | solution.py:70
  264.9 16.0 %copy-start.37 = (bf16[1,2,2,256,256]{4,3,2,1,0:T(8,128)(2,1)}, bf16[1,2,2,256,256]{4,3,2,1,0:T(8,128)(2,1)S(1)}, u32[]{:S(2)}) copy-start(bf16[1,2,2,256,256]{4,3,2,1,0:T(8,128)(2,1)S(1)} %get-tuple-element.632.keep_ref) | copy-start | bytes 1572868
  264.9 16.8 %collective-permute-start.29 = (bf16[1,2,2,256,256]{4,3,2,1,0:T(8,128)(2,1)S(1)}, bf16[1,2,2,256,256]{4,3,2,1,0:T(8,128)(2,1)S(1)}, u32[]{:S(2)}, u32[]{:S(2)}) collective-permute-start(bf16[1,2,2,256,256]{4,3,2,1,0:T(8,128)(2,1)S(1)} %get-tuple-element.598), channel_id=1, source_target_pairs={{0,2},{1,3},{2,0},{3,1},{4,6},{5,7},{6,4},{7,5},{8,10},{9,11},{10,... | collective-permute-start | bytes 1572872 | tf_op jit(solution)/shard_map/ppermute | solution.py:70
  269.1 11.8 %collective-permute-start.28 = (f32[16,8,128]{2,1,0:T(8,128)S(1)}, f32[16,8,128]{2,1,0:T(8,128)S(1)}, u32[]{:S(2)}, u32[]{:S(2)}) collective-permute-start(f32[16,8,128]{2,1,0:T(8,128)S(1)} %slice_bitcast_fusion.10.total_ref), channel_id=1, source_target_pairs={{0,1},{1,0},{2,3},{3,2},{4,5},{5,4},{6,7},{7,6},{8,9},{9,8},{10,11... | collective-permute-start | bytes 196616 | tf_op jit(solution)/shard_map/ppermute | solution.py:70
  286.3 41.4 %collective-permute-start.36 = (bf16[2,4,64,2048]{3,2,1,0:T(8,128)(2,1)}, bf16[2,4,64,2048]{3,2,1,0:T(8,128)(2,1)S(1)}, u32[]{:S(2)}, u32[]{:S(2)}) collective-permute-start(bf16[2,4,64,2048]{3,2,1,0:T(8,128)(2,1)} %get-tuple-element.641), channel_id=1, source_target_pairs={{0,8},{1,17},{2,10},{3,19},{4,12},{5,21},{6,14},{7,23},{8,0},{9,25... | collective-permute-start | bytes 6291464 | tf_op jit(solution)/shard_map/ppermute | solution.py:70
  288.6 12.3 %collective-permute-start.33 = (bf16[4,4,64,128]{3,2,1,0:T(8,128)(2,1)}, bf16[4,4,64,128]{3,2,1,0:T(8,128)(2,1)}, u32[]{:S(2)}, u32[]{:S(2)}) collective-permute-start(bf16[4,4,64,128]{3,2,1,0:T(8,128)(2,1)} %fusion.1), channel_id=1, source_target_pairs={{0,1},{1,0},{2,3},{3,2},{4,5},{5,4},{6,7},{7,6},{8,9},{9,8},{10,11... | collective-permute-start | bytes 786440 | tf_op jit(solution)/shard_map/ppermute | solution.py:70
  290.2 37.5 %collective-permute-start.35 = (bf16[1,2,2,256,256]{4,3,2,1,0:T(8,128)(2,1)S(1)}, bf16[1,2,2,256,256]{4,3,2,1,0:T(8,128)(2,1)S(1)}, u32[]{:S(2)}, u32[]{:S(2)}) collective-permute-start(bf16[1,2,2,256,256]{4,3,2,1,0:T(8,128)(2,1)S(1)} %get-tuple-element.639), channel_id=1, source_target_pairs={{0,2},{1,3},{2,0},{3,1},{4,6},{5,7},{6,4},{7,5},{8,10},{9,11},{10,... | collective-permute-start | bytes 1572872 | tf_op jit(solution)/shard_map/ppermute | solution.py:70
  292.1 19.5 %copy-start.42 = (f32[3]{0:T(128)S(1)}, f32[3]{0:T(128)}, u32[]{:S(2)}) copy-start(f32[3]{0:T(128)} %get-tuple-element.606.scal) | copy-start | bytes 40
  292.2 35.5 %collective-permute-start.34 = (bf16[1,1,2,256,256]{4,3,2,1,0:T(8,128)(2,1)S(1)}, bf16[1,1,2,256,256]{4,3,2,1,0:T(8,128)(2,1)S(1)}, u32[]{:S(2)}, u32[]{:S(2)}) collective-permute-start(bf16[1,1,2,256,256]{4,3,2,1,0:T(8,128)(2,1)S(1)} %get-tuple-element.635), channel_id=1, source_target_pairs={{0,4},{1,5},{2,6},{3,7},{4,0},{5,1},{6,2},{7,3},{8,12},{9,13},{10,... | collective-permute-start | bytes 786440 | tf_op jit(solution)/shard_map/ppermute | solution.py:70
  300.0 11.6 %collective-permute-start.31 = (f32[16,8,128]{2,1,0:T(8,128)S(1)}, f32[16,8,128]{2,1,0:T(8,128)S(1)}, u32[]{:S(2)}, u32[]{:S(2)}) collective-permute-start(f32[16,8,128]{2,1,0:T(8,128)S(1)} %get-tuple-element.607.total_ref), channel_id=1, source_target_pairs={{0,2},{1,3},{2,0},{3,1},{4,6},{5,7},{6,4},{7,5},{8,10},{9,11},{10,... | collective-permute-start | bytes 196616 | tf_op jit(solution)/shard_map/ppermute | solution.py:70
  300.9 19.2 %copy-start.17 = (bf16[640,1536]{1,0:T(8,128)(2,1)S(1)}, bf16[640,1536]{1,0:T(8,128)(2,1)}, u32[]{:S(2)}) copy-start(bf16[640,1536]{1,0:T(8,128)(2,1)} %copy-done.16) | copy-start | bytes 5898244
  302.1 18.0 %copy-start.1 = (bf16[640,1536]{1,0:T(8,128)(2,1)S(1)}, bf16[640,1536]{1,0:T(8,128)(2,1)}, u32[]{:S(2)}) copy-start(bf16[640,1536]{1,0:T(8,128)(2,1)} %copy-done) | copy-start | bytes 5898244
  302.5 25.2 %collective-permute-start.37 = (bf16[2,4,64,128]{3,2,1,0:T(8,128)(2,1)S(1)}, bf16[2,4,64,128]{3,2,1,0:T(8,128)(2,1)S(1)}, u32[]{:S(2)}, u32[]{:S(2)}) collective-permute-start(bf16[2,4,64,128]{3,2,1,0:T(8,128)(2,1)S(1)} %bitcast.198), channel_id=1, source_target_pairs={{0,8},{1,17},{2,10},{3,19},{4,12},{5,21},{6,14},{7,23},{8,0},{9,25... | collective-permute-start | bytes 393224 | tf_op jit(solution)/shard_map/ppermute | solution.py:70
  312.2 14.2 %copy-start.43 = (f32[3]{0:T(128)S(1)}, f32[3]{0:T(128)}, u32[]{:S(2)}) copy-start(f32[3]{0:T(128)} %get-tuple-element.605.scal) | copy-start | bytes 40
  312.2 15.5 %copy-start.26 = (bf16[2,4,64,2048]{3,2,1,0:T(8,128)(2,1)S(1)}, bf16[2,4,64,2048]{3,2,1,0:T(8,128)(2,1)}, u32[]{:S(2)}) copy-start(bf16[2,4,64,2048]{3,2,1,0:T(8,128)(2,1)} %get-tuple-element.658.keep_ref) | copy-start | bytes 6291460
  312.3 14.2 %collective-permute-start.32 = (f32[16,8,128]{2,1,0:T(8,128)S(1)}, f32[16,8,128]{2,1,0:T(8,128)S(1)}, u32[]{:S(2)}, u32[]{:S(2)}) collective-permute-start(f32[16,8,128]{2,1,0:T(8,128)S(1)} %get-tuple-element.610.total_ref), channel_id=1, source_target_pairs={{0,4},{1,5},{2,6},{3,7},{4,0},{5,1},{6,2},{7,3},{8,12},{9,13},{10,... | collective-permute-start | bytes 196616 | tf_op jit(solution)/shard_map/ppermute | solution.py:70
  328.4 15.6 %collective-permute-start.39 = (bf16[1,4,64,2176]{3,2,1,0:T(8,128)(2,1)S(1)}, bf16[1,4,64,2176]{3,2,1,0:T(8,128)(2,1)S(1)}, u32[]{:S(2)}, u32[]{:S(2)}) collective-permute-start(bf16[1,4,64,2176]{3,2,1,0:T(8,128)(2,1)S(1)} %constant_dynamic-update-slice_fusion.4), channel_id=1, source_target_pairs={{0,16},{1,9},{2,18},{3,11},{4,20},{5,13},{6,22},{7,15},{8,24},{9,1... | collective-permute-start | bytes 3342344 | tf_op jit(solution)/shard_map/ppermute | solution.py:70
  330.1 13.2 %collective-permute-start.40 = (bf16[1,1,2,256,256]{4,3,2,1,0:T(8,128)(2,1)S(1)}, bf16[1,1,2,256,256]{4,3,2,1,0:T(8,128)(2,1)S(1)}, u32[]{:S(2)}, u32[]{:S(2)}) collective-permute-start(bf16[1,1,2,256,256]{4,3,2,1,0:T(8,128)(2,1)S(1)} %get-tuple-element.657), channel_id=1, source_target_pairs={{0,4},{1,5},{2,6},{3,7},{4,0},{5,1},{6,2},{7,3},{8,12},{9,13},{10,... | collective-permute-start | bytes 786440 | tf_op jit(solution)/shard_map/ppermute | solution.py:70
  336.1 7.3 %collective-permute-start.38 = (bf16[128,1024]{1,0:T(8,128)(2,1)S(1)}, bf16[128,1024]{1,0:T(8,128)(2,1)S(1)}, u32[]{:S(2)}, u32[]{:S(2)}) collective-permute-start(bf16[128,1024]{1,0:T(8,128)(2,1)S(1)} %sent_tail.1), channel_id=1, source_target_pairs={{1,0},{2,1},{3,2},{4,3},{5,4},{6,5},{7,6},{9,8},{10,9},{11,10},{12... | collective-permute-start | bytes 786440 | tf_op jit(solution)/shard_map/ppermute | solution.py:70
  343.9 17.8 %collective-permute-start.41 = (bf16[512,1024]{1,0:T(8,128)(2,1)}, bf16[512,1024]{1,0:T(8,128)(2,1)}, u32[]{:S(2)}, u32[]{:S(2)}) collective-permute-start(bf16[512,1024]{1,0:T(8,128)(2,1)} %get-tuple-element.676), channel_id=1, source_target_pairs={{0,1},{1,0},{2,3},{3,2},{4,5},{5,4},{6,7},{7,6},{8,9},{9,8},{10,11... | collective-permute-start | bytes 3145736 | tf_op jit(solution)/shard_map/ppermute | solution.py:70
  346.9 14.7 %collective-permute-start.42 = (bf16[1,2,64,2176]{3,2,1,0:T(8,128)(2,1)}, bf16[1,2,64,2176]{3,2,1,0:T(8,128)(2,1)S(1)}, u32[]{:S(2)}, u32[]{:S(2)}) collective-permute-start(bf16[1,2,64,2176]{3,2,1,0:T(8,128)(2,1)} %get-tuple-element.680), channel_id=1, source_target_pairs={{0,2},{1,3},{2,0},{3,1},{4,6},{5,7},{6,4},{7,5},{8,10},{9,11},{10,... | collective-permute-start | bytes 1671176 | tf_op jit(solution)/shard_map/ppermute | solution.py:70
  351.5 15.7 %copy-start.15 = (f32[512,1024]{1,0:T(8,128)S(1)}, f32[512,1024]{1,0:T(8,128)}, u32[]{:S(2)}) copy-start(f32[512,1024]{1,0:T(8,128)} %copy-done.13) | copy-start | bytes 6291460
  362.5 17.1 %collective-permute-start.43 = (bf16[1,1,64,2176]{3,2,1,0:T(8,128)(2,1)}, bf16[1,1,64,2176]{3,2,1,0:T(8,128)(2,1)S(1)}, u32[]{:S(2)}, u32[]{:S(2)}) collective-permute-start(bf16[1,1,64,2176]{3,2,1,0:T(8,128)(2,1)} %get-tuple-element.689), channel_id=1, source_target_pairs={{0,4},{1,5},{2,6},{3,7},{4,0},{5,1},{6,2},{7,3},{8,12},{9,13},{10,... | collective-permute-start | bytes 835592 | tf_op jit(solution)/shard_map/ppermute | solution.py:70
  362.7 16.2 %all-to-all-start = ((f32[32,1,32]{2,1,0:T(1,128)}), f32[32,1,32]{2,1,0:T(1,128)S(1)}, u32[]{:S(2)}, u32[]{:S(2)}) async-start(f32[32,1,32]{2,1,0:T(1,128)} %bitcast.73), calls=%async_computation | async-start | bytes 32768 | tf_op jit(solution)/shard_map/all_to_all | solution.py:1373
  379.7 1.8 collective-permute-start.44
  (38 other events, 183.5 us)
Sparse Core Ops, SparseCore 0:
  34.8 134.6 all-gather.1

commit v3 on v2

--- a/solution.py
+++ b/solution.py
@@ -23,7 +23,7 @@
 bf16 = jnp.bfloat16
 VMEM = pl.BlockSpec(memory_space=pltpu.VMEM)
 SMEM = pl.BlockSpec(memory_space=pltpu.SMEM)
-ANY = pl.BlockSpec(memory_space=pl.ANY)
+ANY = pl.BlockSpec(memory_space=pltpu.HBM)
 QKV_COLS = pl.BlockSpec((D, 3 * HALF), lambda i: (0, 0))
 OUT_COLS = pl.BlockSpec((D, HALF), lambda i: (0, 3))
 NT = (((1,), (1,)), ((), ()))
@@ -32,6 +32,14 @@
 
 def params(mib):
     return pltpu.CompilerParams(vmem_limit_bytes=mib * 1024 * 1024)
+
+
+def in_hbm(values):
+    return pltpu.with_memory_space_constraint(values, pltpu.HBM)
+
+
+def in_vmem(values):
+    return pltpu.with_memory_space_constraint(values, pltpu.VMEM)
 
 
 COST = pl.CostEstimate(flops=1, bytes_accessed=1, transcendentals=0)
@@ -165,7 +173,7 @@
         in_specs=[VMEM, VMEM],
         out_specs=VMEM,
         scratch_shapes=[pltpu.VMEM((OWN, 8, 128), f32)],
-        compiler_params=params(24),
+        compiler_params=params(6),
         cost_estimate=COST,
         name="scan_own",
     )(values, rate)
@@ -178,7 +186,7 @@
         in_specs=[VMEM] * 3,
         out_specs=VMEM,
         scratch_shapes=[pltpu.VMEM((CTX, 8, 128), f32)],
-        compiler_params=params(24),
+        compiler_params=params(4),
         cost_estimate=COST,
         name="scan_tail",
     )(values, own, rate)
@@ -204,7 +212,7 @@
         out_shape=(STATE, STATE),
         in_specs=[SMEM] + [VMEM] * 4,
         out_specs=(VMEM, VMEM),
-        compiler_params=params(16),
+        compiler_params=params(3),
         cost_estimate=COST,
         name="exchange_step",
     )(scal, total, received, before, rate)
@@ -227,7 +235,7 @@
         out_shape=(one, one),
         in_specs=[SMEM] + [VMEM] * 4,
         out_specs=(VMEM, VMEM),
-        compiler_params=params(16),
+        compiler_params=params(3),
         cost_estimate=COST,
         name="exchange_back_step",
     )(scal, total, received, after, rate)
@@ -261,7 +269,7 @@
         in_specs=[SMEM] + [VMEM] * 7,
         out_specs=VMEM,
         scratch_shapes=[pltpu.VMEM((CTX, 8, 128), f32)] * 2,
-        compiler_params=params(24),
+        compiler_params=params(6),
         cost_estimate=COST,
         name="context_states",
     )(scal, tail, own, before, initial, rate, gain_in, gain_out)
@@ -291,7 +299,7 @@
         in_specs=[VMEM] * 2,
         out_specs=VMEM,
         scratch_shapes=[pltpu.VMEM((CTX, 8, 128), f32)],
-        compiler_params=params(16),
+        compiler_params=params(3),
         cost_estimate=COST,
         name="state_low",
     )(grad_context, rate)
@@ -342,7 +350,7 @@
         in_specs=[SMEM] + [VMEM] * 8,
         out_specs=VMEM,
         scratch_shapes=[pltpu.VMEM((CTX, 8, 128), f32)] * 2,
-        compiler_params=params(24),
+        compiler_params=params(4),
         cost_estimate=COST,
         name="state_sums",
     )(scal, grad_context, tail, start, lows, initial, rate, gain_in, gain_out)
@@ -373,7 +381,7 @@
         in_specs=[VMEM] * 5,
         out_specs=VMEM,
         scratch_shapes=[pltpu.VMEM((CTX, 8, 128), f32)] * 2,
-        compiler_params=params(24),
+        compiler_params=params(4),
         cost_estimate=COST,
         name="sent_tail",
     )(grad_context, after, rate, gain_in, gain_out)
@@ -399,7 +407,7 @@
         in_specs=[VMEM] * 4,
         out_specs=VMEM,
         scratch_shapes=[pltpu.VMEM((OWN, 8, 128), f32)],
-        compiler_params=params(24),
+        compiler_params=params(6),
         cost_estimate=COST,
         name="sent_own",
     )(after, rate, gain_in, gain_out)
@@ -453,7 +461,7 @@
         out_shape=jax.ShapeDtypeStruct((BLK, D), bf16),
         in_specs=[SMEM] + [VMEM] * 2,
         out_specs=VMEM,
-        compiler_params=params(32),
+        compiler_params=params(14),
         cost_estimate=COST,
         name="attend",
     )(info, own, other)
@@ -505,7 +513,7 @@
         in_specs=[SMEM] + [VMEM] * 3,
         out_specs=(VMEM, VMEM),
         scratch_shapes=[pltpu.VMEM((2, CTX + QT, HD), f32)],
-        compiler_params=params(32),
+        compiler_params=params(18),
         cost_estimate=COST,
         name="attend_back",
     )(info, own, other, grad)
@@ -518,61 +526,40 @@
 
 
 def feed_kernel(
-    ndp, nz, width, index, groups, earlier, last, info, s_own, s_par, c_own, c_par, st_own, st_par, ct_own, ct_par,
-    *rest
+    ndp, nz, width, index, groups, earlier, last, info, s_own, s_par, c_own, c_par,
+    st_own, st_par, ct_own, ct_par, weights, *rest
 ):
     rows = s_own.shape[0]
-    tokens = 2 * rows
     block = D // ndp
     group = nz * width
     half = ndp // 2
-    weights, *rest = rest
+    s, c = (s_own, s_par), (c_own, c_par)
     if earlier:
         m_in, g_in, *rest = rest
     if last:
-        m_own, m_par, g_own, g_par, keep_out, send_out, *rest = rest
+        m_own, m_par, g_own, g_par, *rest = rest
     else:
-        m_out, g_out, keep_out, send_out, *rest = rest
-    s, c, st, ct, w, act, gh, acc_m, acc_g, keep, send, sems, out_sems = rest
+        m_out, g_out, *rest = rest
+    parts, (st, ct, w, act, gh, sems) = rest[:4], rest[4:]
     at = [pl.multiple_of(info[p] * block, block) for p in range(ndp)]
     z = info[ndp]
-    copies = {}
-    count = [0]
-
-    def start(name, src, dst):
-        sem = sems.at[count[0]]
-        count[0] += 1
-        copy = pltpu.make_async_copy(src, dst, sem)
+    copies = []
+
+    def start(src, dst):
+        copy = pltpu.make_async_copy(src, dst, sems.at[len(copies)])
         copy.start()
-        copies.setdefault(name, []).append(copy)
-
-    def wait(name):
-        for copy in copies.pop(name):
-            copy.wait()
-
-    def rows_of(name, own, par, dst):
+        copies.append(copy)
+
+    at_core = pl.multiple_of((info[ndp + 1] * groups + index) * 2 * group, 128)
+    start(weights.at[:, pl.ds(at_core, 2 * group)], w)
+    for own, par, dst in ((st_own, st_par, st), (ct_own, ct_par, ct)):
         for p in range(ndp):
             for i, src in enumerate((own, par)):
                 start(
-                    name,
                     src.at[pl.ds(at[p], block), :],
                     dst.at[p * block : (p + 1) * block, i * rows : (i + 1) * rows],
                 )
-
-    for i, src in enumerate((s_own, s_par)):
-        start("s", src, s.at[i * rows : (i + 1) * rows, :])
-    at_core = pl.multiple_of((info[ndp + 1] * groups + index) * 2 * group, 128)
-    start("w", weights.at[:, pl.ds(at_core, 2 * group)], w)
-    for i, src in enumerate((c_own, c_par)):
-        start("c", src, c.at[i * rows : (i + 1) * rows, :])
-    rows_of("st", st_own, st_par, st)
-    rows_of("ct", ct_own, ct_par, ct)
-    if earlier:
-        start("m", m_in, acc_m)
-        start("g", g_in, acc_g)
-    wait("s")
-    wait("w")
-    wait("c")
+    copies[0].wait()
 
     @pl.loop(0, nz)
     def _(b):
@@ -580,57 +567,44 @@
         down = pl.ds(pl.multiple_of(group + b * width, width), width)
         for i in range(2):
             part = slice(i * rows, (i + 1) * rows)
-            hidden = jnp.dot(s[part, :], w[:, up], preferred_element_type=f32)
-            grad = jnp.dot(c[part, :], w[:, down], preferred_element_type=f32)
+            hidden = jnp.dot(s[i][...], w[:, up], preferred_element_type=f32)
+            grad = jnp.dot(c[i][...], w[:, down], preferred_element_type=f32)
             active, slope = gelu_parts(hidden)
             act[part, up] = active.astype(bf16)
             gh[part, up] = (grad * slope).astype(bf16)
 
-    wait("st")
-    wait("ct")
+    for copy in copies[1:]:
+        copy.wait()
 
     @pl.loop(0, nz)
     def _(r):
         cols = pl.ds(pl.multiple_of((z ^ swap_bits(r, bits_of(nz))) * width, width), width)
-        for part, dst in ((0, keep), (1, send)):
+        for part in range(2):
             span = slice(part * half * block, (part + 1) * half * block)
             up = jnp.dot(st[span, :], gh[:, cols], preferred_element_type=f32).astype(bf16)
             down = jnp.dot(ct[span, :], act[:, cols], preferred_element_type=f32).astype(bf16)
             for p in range(half):
-                dst[p, r, 0] = up[p * block : (p + 1) * block]
-                dst[p, r, 1] = down[p * block : (p + 1) * block]
-
-    outs = [
-        pltpu.make_async_copy(keep, keep_out, out_sems.at[0]),
-        pltpu.make_async_copy(send, send_out, out_sems.at[1]),
-    ]
-    for copy in outs:
-        copy.start()
-    if earlier:
-        wait("m")
-        wait("g")
-    for name, left, acc, first in (("g", gh, acc_g, 0), ("m", act, acc_m, group)):
+                far = p >= half // 2
+                dst = parts[2 * part + far]
+                q = p - far * (half // 2)
+                dst[q, r, 0] = up[p * block : (p + 1) * block]
+                dst[q, r, 1] = down[p * block : (p + 1) * block]
+
+    for name, left, first in (("g", gh, 0), ("m", act, group)):
         for p in range(ndp):
             right = w[p * block : (p + 1) * block, first : first + group]
+            cols = slice(p * block, (p + 1) * block)
             for i in range(2):
                 part = slice(i * rows, (i + 1) * rows)
                 value = lax.dot_general(left[part, :], right, NT, preferred_element_type=f32)
-                cols = slice(p * block, (p + 1) * block)
                 if earlier:
-                    value = value + acc[part, cols]
+                    value = value + (g_in if name == "g" else m_in)[part, cols]
                 if not last:
-                    acc[part, cols] = value
+                    (g_out if name == "g" else m_out)[part, cols] = value
                 elif i == 0:
                     (g_own if name == "g" else m_own)[:, cols] = value
                 else:
                     (g_par if name == "g" else m_par)[:, cols] = value.astype(bf16)
-    if not last:
-        outs.append(pltpu.make_async_copy(acc_m, m_out, out_sems.at[2]))
-        outs.append(pltpu.make_async_copy(acc_g, g_out, out_sems.at[3]))
-        for copy in outs[2:]:
-            copy.start()
-    for copy in outs:
-        copy.wait()
 
 
 def feed(links, info, acts, weights, group, index, groups, earlier, last):
@@ -640,38 +614,32 @@
     block = D // ndp
     width = group // nz
     half = ndp // 2
-    full = jax.ShapeDtypeStruct((tokens, D), f32)
+    full = pltpu.VMEM((tokens, D), f32)
     own = jax.ShapeDtypeStruct((rows, D), f32)
     par = jax.ShapeDtypeStruct((rows, D), bf16)
-    grads = jax.ShapeDtypeStruct((half, nz, 2, block, width), bf16)
-    out_shape = (own, par, own, par, grads, grads) if last else (full, full, grads, grads)
-    out_specs = (VMEM,) * 4 + (ANY,) * 2 if last else (ANY,) * 4
-    inputs = (info, *acts, weights) + (tuple(earlier) if earlier else ())
-    n_copies = 4 * ndp + 7
+    grads = tuple(
+        jax.ShapeDtypeStruct((count, nz, 2, block, width), bf16)
+        for count in (half // 2, half - half // 2) * 2
+    )
+    out_shape = (own, par, own, par, *grads) if last else (full, full, *grads)
+    earlier = tuple(earlier) if earlier else ()
     return pl.pallas_call(
         functools.partial(feed_kernel, ndp, nz, width, index, groups, bool(earlier), last),
         out_shape=out_shape,
-        in_specs=[SMEM] + [ANY] * (len(inputs) - 1),
-        out_specs=out_specs,
+        in_specs=[SMEM] + [VMEM] * len(acts) + [ANY] + [VMEM] * len(earlier),
+        out_specs=(VMEM,) * len(out_shape),
         scratch_shapes=[
-            pltpu.VMEM((tokens, D), bf16),
-            pltpu.VMEM((tokens, D), bf16),
             pltpu.VMEM((D, tokens), bf16),
             pltpu.VMEM((D, tokens), bf16),
             pltpu.VMEM((D, 2 * group), bf16),
             pltpu.VMEM((tokens, group), bf16),
             pltpu.VMEM((tokens, group), bf16),
-            pltpu.VMEM((tokens, D), f32),
-            pltpu.VMEM((tokens, D), f32),
-            pltpu.VMEM((half, nz, 2, block, width), bf16),
-            pltpu.VMEM((half, nz, 2, block, width), bf16),
-            pltpu.SemaphoreType.DMA((n_copies,)),
-            pltpu.SemaphoreType.DMA((4,)),
+            pltpu.SemaphoreType.DMA((4 * ndp + 1,)),
         ],
-        compiler_params=params(58),
+        compiler_params=params(22),
         cost_estimate=COST,
         name="feed_last" if last else "feed_first",
-    )(*inputs)
+    )(info, *map(in_vmem, acts), in_hbm(weights), *map(in_vmem, earlier))
 
 
 def norm_parts(values):
@@ -717,7 +685,7 @@
         ),
         in_specs=[VMEM] * 2,
         out_specs=(VMEM, VMEM),
-        compiler_params=params(16),
+        compiler_params=params(5),
         cost_estimate=COST,
         name="norm_first",
     )(tokens, gain)
@@ -743,16 +711,16 @@
         middle_kernel,
         out_shape=(
             jax.ShapeDtypeStruct((rows, D), f32),
-            jax.ShapeDtypeStruct((rows, D), bf16),
-            jax.ShapeDtypeStruct((D, rows), bf16),
+            pltpu.VMEM((rows, D), bf16),
+            pltpu.VMEM((D, rows), bf16),
         ),
         grid=(1,),
         in_specs=[SMEM, VMEM, VMEM, OUT_COLS, OUT_COLS, VMEM],
         out_specs=(VMEM,) * 3,
-        compiler_params=params(32),
+        compiler_params=params(16),
         cost_estimate=COST,
         name="middle_norm",
-    )(info, attended, tokens, o_own, o_other, gain)
+    )(info, attended, tokens, in_hbm(o_own), in_hbm(o_other), gain)
 
 
 def back_middle_kernel(
@@ -791,10 +759,10 @@
         in_specs=[SMEM] + [VMEM] * 5 + [OUT_COLS] * 2,
         out_specs=(VMEM,) * 5,
         scratch_shapes=[pltpu.VMEM((rows, D), bf16)],
-        compiler_params=params(40),
+        compiler_params=params(22),
         cost_estimate=COST,
         name="back_middle",
-    )(info, middle, own, received, cotangent, gain, o_own, o_other)
+    )(info, middle, own, received, cotangent, gain, in_hbm(o_own), in_hbm(o_other))
 
 
 def project_kernel(x_ref, w_ref, out_ref):
@@ -810,10 +778,10 @@
         grid=(1,),
         in_specs=[VMEM, QKV_COLS],
         out_specs=VMEM,
-        compiler_params=params(32),
+        compiler_params=params(16),
         cost_estimate=COST,
         name="project",
-    )(values, weights)
+    )(values, in_hbm(weights))
 
 
 def back_project_kernel(first, g_own, g_other, w_own, w_other, out_ref):
@@ -831,10 +799,10 @@
         grid=(1,),
         in_specs=[VMEM, VMEM, QKV_COLS, QKV_COLS],
         out_specs=VMEM,
-        compiler_params=params(40),
+        compiler_params=params(26),
         cost_estimate=COST,
         name="back_project",
-    )(g_own, g_other, w_own, w_other)
+    )(g_own, g_other, in_hbm(w_own), in_hbm(w_other))
 
 
 def back_first_kernel(
@@ -861,14 +829,14 @@
         ),
         in_specs=[VMEM] * 6,
         out_specs=(VMEM,) * 2,
-        compiler_params=params(32),
+        compiler_params=params(14),
         cost_estimate=COST,
         name="back_first",
     )(tokens, part, sent, last, grad_middle, gain)
 
 
 def weight_grad_kernel(
-    ndp, nz, info, x_own, x_par, g_own, g_par, a_own, a_par, b_own, b_par,
+    ndp, nz, info, x_own, x_par, g_own, g_par, a_own, a_par, b_own, b_par, shares,
     keep_ref, send_ref,
 ):
     block = D // ndp
@@ -877,32 +845,92 @@
     half = ndp // 2
     for p in range(ndp):
         cols = pl.ds(pl.multiple_of(info[p] * block, block), block)
-        qkv = dot(x_own[:, cols].T, g_own[...]) + dot(x_par[:, cols].T, g_par[...])
+        grad = dot(x_own[:, cols].T, g_own[...]) + dot(x_par[:, cols].T, g_par[...])
         out = dot(a_own[:, cols].T, b_own[...]) + dot(a_par[:, cols].T, b_par[...])
-        qkv = qkv.astype(bf16)
+        grad = grad.astype(bf16)
         out = out.astype(bf16)
         dst = keep_ref if p < half else send_ref
         for b in range(nz):
+            r = swap_bits(z ^ b, bits_of(nz))
             span = slice(b * rows, (b + 1) * rows)
-            r = swap_bits(z ^ b, bits_of(nz))
-            dst[p % half, r, :, : 3 * HALF] = qkv[span]
-            dst[p % half, r, :, 3 * HALF :] = out[span]
-
-
-def weight_grads(links, info, x_own, x_par, g_own, g_par, a_own, a_par, b_own, b_par):
+            dst[p % half, r, :, : 3 * HALF] = grad[span]
+            dst[p % half, r, :, 3 * HALF : 4 * HALF] = out[span]
+            dst[p % half, r, :, 4 * HALF :] = shares[p, r]
+
+
+def weight_grads(links, info, x_own, x_par, g_own, g_par, a_own, a_par, b_own, b_par, shares):
     ndp, nz = links.ndp, links.nz
-    rows = D // (ndp * nz)
-    line = 4 * HALF
-    out = jax.ShapeDtypeStruct((ndp // 2, nz, rows, line), bf16)
+    line = 4 * HALF + shares.shape[3]
+    out = jax.ShapeDtypeStruct((ndp // 2, nz, D // (ndp * nz), line), bf16)
     return pl.pallas_call(
         functools.partial(weight_grad_kernel, ndp, nz),
         out_shape=(out, out),
-        in_specs=[SMEM] + [VMEM] * 8,
+        in_specs=[SMEM] + [VMEM] * 9,
         out_specs=(VMEM, VMEM),
-        compiler_params=params(48),
+        compiler_params=params(24),
         cost_estimate=COST,
         name="weight_grads",
-    )(info, x_own, x_par, g_own, g_par, a_own, a_par, b_own, b_par)
+    )(info, x_own, x_par, g_own, g_par, a_own, a_par, b_own, b_par, shares)
+
+
+def shares_kernel(ndp, nmp, maps, info, owner, sums_ref, gain_ref, out):
+    for p in range(ndp):
+        d = info[p]
+        mine = (owner[0] == d).astype(f32)
+        for m in range(nmp):
+            r = swap_bits(info[ndp] ^ (m // 2), bits_of(nmp // 2))
+            other = (m % 2) ^ info[ndp + 1]
+            place_of = jnp.where(other == 0, p, swap_bits(p, bits_of(ndp)))
+            to = out.at[other, place_of, r]
+            for i in range(3):
+                rows = sums_ref[i, pl.ds(d * maps, maps), m, :]
+                to[i * maps : (i + 1) * maps, :] = rows
+            to[3 * maps : 3 * maps + NS, :] = sums_ref[3, :, m, :] * mine
+            to[3 * maps + NS :, :] = jnp.zeros((to.shape[0] - 3 * maps - NS, 128), f32)
+            to[3 * maps + NS : 3 * maps + NS + 1, :] = gain_ref[pl.ds(d, 1), m, :]
+
+
+def pack_shares(links, info, owner, sums, gain, maps, lines):
+    out = jax.ShapeDtypeStruct((2, links.ndp, links.nz, lines, 128), f32)
+    return pl.pallas_call(
+        functools.partial(shares_kernel, links.ndp, links.nmp, maps),
+        out_shape=out,
+        in_specs=[SMEM, SMEM, VMEM, VMEM],
+        out_specs=VMEM,
+        compiler_params=params(3),
+        cost_estimate=COST,
+        name="pack_shares",
+    )(info, owner, sums, gain)
+
+
+def prepare_kernel(nz, groups, core, q_ref, k_ref, v_ref, o_ref, up_ref, down_ref, keep, send, feed):
+    for i, ref in enumerate((q_ref, k_ref, v_ref, o_ref)):
+        to = slice(i * HALF, (i + 1) * HALF)
+        keep[:, to] = ref[:, pl.ds(pl.multiple_of(core[0] * HALF, HALF), HALF)].astype(bf16)
+        send[:, to] = ref[:, pl.ds(pl.multiple_of((1 - core[0]) * HALF, HALF), HALF)].astype(bf16)
+    width = FF // (2 * nz * groups)
+    at = 0
+    for c in range(2):
+        for g in range(groups):
+            for ref in (up_ref, down_ref):
+                for b in range(nz):
+                    first = ((b * 2 + c) * groups + g) * width
+                    feed[:, at : at + width] = ref[:, first : first + width].astype(bf16)
+                    at += width
+
+
+def prepare(links, groups, core, mats, up, down):
+    rows = up.shape[0]
+    part = jax.ShapeDtypeStruct((rows, 4 * HALF), bf16)
+    return pl.pallas_call(
+        functools.partial(prepare_kernel, links.nz, groups),
+        out_shape=(part, part, jax.ShapeDtypeStruct((rows, 2 * FF), bf16)),
+        in_specs=[SMEM] + [VMEM] * 6,
+        out_specs=(VMEM,) * 3,
+        compiler_params=params(5),
+        cost_estimate=COST,
+        name="prepare",
+    )(core, *(in_hbm(values) for values in (*mats, up, down)))
 
 
 def place_kernel(ndp, order, *refs):
@@ -920,14 +948,14 @@
     ndp = links.ndp
     return pl.pallas_call(
         functools.partial(place_kernel, ndp),
-        out_shape=jax.ShapeDtypeStruct((ndp * block, cols), pieces[0].dtype),
+        out_shape=pltpu.HBM((ndp * block, cols), pieces[0].dtype),
         grid_spec=pltpu.PrefetchScalarGridSpec(
             num_scalar_prefetch=1,
             grid=(ndp,),
             in_specs=[VMEM] * ndp,
             out_specs=pl.BlockSpec((block, cols), lambda b, order: (b, 0)),
         ),
-        compiler_params=params(16),
+        compiler_params=params(12),
         cost_estimate=COST,
         name="place",
     )(order, *pieces)
@@ -937,7 +965,7 @@
     return (left.astype(f32) + right.astype(f32)).astype(bf16)
 
 
-def in_order(links, values):
+def in_order(links, values, core):
     ndp, nz = values.shape[:2]
     inner = values.shape[2:]
     bits = links.dp_bits + links.mp_bits - 1
@@ -950,11 +978,7 @@
         split = jnp.where(mine == 0, split, jnp.flip(split, axis))
     dp_axes, z_axes = list(range(links.dp_bits)), list(range(links.dp_bits, bits))
     rest = list(range(bits, split.ndim))
-    split = jnp.where(
-        links.core == 0,
-        split.transpose(dp_axes[::-1] + z_axes[::-1] + rest),
-        split.transpose(dp_axes + z_axes[::-1] + rest),
-    )
+    split = split.transpose((dp_axes if core else dp_axes[::-1]) + z_axes[::-1] + rest)
     return split.reshape(values.shape)
 
 
@@ -982,7 +1006,7 @@
         out_shape=jax.ShapeDtypeStruct(shape, here.dtype),
         in_specs=[SMEM, VMEM, VMEM],
         out_specs=VMEM,
-        compiler_params=params(16),
+        compiler_params=params(6),
         cost_estimate=COST,
         name="merge",
     )(bit.astype(jnp.int32).reshape(1), here, there)
@@ -992,18 +1016,41 @@
     return merge(current, received, (index >> bit) & 1, False)
 
 
+def pack_shares_plain(links, owner, row, banks_here, sums, gain, maps):
+    ndp, nmp = links.ndp, links.nmp
+    channels = gain.shape[2]
+
+    def by_owner(values):
+        values = values.reshape(ndp, maps, nmp, channels)
+        return values.transpose(0, 2, 1, 3)
+
+    bank = sums[3].reshape(NS, nmp, channels).transpose(1, 0, 2)
+    here = jnp.arange(ndp * banks_here, dtype=jnp.int32) == owner * banks_here + row
+    bank = jnp.where(here[:, None, None, None], bank[None], 0.0)
+    bank = bank.reshape(ndp, banks_here, nmp, NS, channels).transpose(0, 2, 1, 3, 4)
+    bank = bank.reshape(ndp, nmp, banks_here * NS, channels)
+    lines = [by_owner(sums[0]), by_owner(sums[1]), by_owner(sums[2]), bank, gain[:, :, None]]
+    shares = jnp.concatenate(lines, 2)
+    rows = D // (ndp * links.nz)
+    shares = shares.reshape(ndp, nmp, -1)
+    shares = jnp.pad(shares, ((0, 0), (0, 0), (0, -shares.shape[2] % (128 * rows))))
+    shares = shares.reshape(ndp, nmp // 2, 2, rows, -1)
+    parts = [in_order(links, shares[:, :, c], c) for c in range(2)]
+    return jnp.where(links.core == 0, jnp.stack(parts), jnp.stack(parts[::-1]))
+
+
 class Live:
     pass
 
 
 def fence(live, transfers=(), waits=()):
     held = dict(vars(live))
-    tree = (held, [t.state for t in transfers], [t.received for t in waits])
+    tree = (held, [t.outgoing for t in transfers], [t.received for t in waits])
     leaves, form = jax.tree.flatten(tree)
     held, states, received = jax.tree.unflatten(form, lax.optimization_barrier(leaves))
     vars(live).update(held)
     for t, state in zip(transfers, states):
-        t.state = state
+        t.outgoing = state
     for t, values in zip(waits, received):
         t.received = values
     for t in waits:
@@ -1023,6 +1070,11 @@
     def along_dp(self, level):
         self.kind = "d"
         self.received = [self.links.fan(piece, level) for piece in self.state]
+
+    def more_dp(self):
+        self.count = 2 * len(self.state)
+        self.ahead = [self.links.fan(piece, 0) for piece in self.state]
+        self.received = self.received + self.ahead
 
     def last_dp(self, first, last):
         if first == 0:
@@ -1030,6 +1082,14 @@
         last = self.count if last is None else last
         self.kind = "d"
         self.received = [self.links.fan(piece, 0) for piece in self.state[first:last]]
+
+    @property
+    def outgoing(self):
+        return self.state
+
+    @outgoing.setter
+    def outgoing(self, values):
+        self.state = values
 
     def join(self):
         if self.kind == "d":
@@ -1078,9 +1138,28 @@
         out[...] = total.astype(out.dtype)
 
 
-def add_split(keep, received, axis):
+def mix_kernel(middle_ref, own_ref, recv_ref, out_ref):
+    total = middle_ref[...] + (own_ref[...] + recv_ref[...].astype(f32))
+    out_ref[...] = total.astype(bf16)
+
+
+def mix(middle, own, received):
+    return pl.pallas_call(
+        mix_kernel,
+        out_shape=jax.ShapeDtypeStruct(middle.shape, bf16),
+        in_specs=[VMEM] * 3,
+        out_specs=VMEM,
+        compiler_params=params(10),
+        cost_estimate=COST,
+        name="mix",
+    )(middle, own, received)
+
+
+def add_split(keep, received, axis, dtype=None):
     shape = list(keep.shape)
-    if axis is None:
+    if axis is False:
+        outs = (jax.ShapeDtypeStruct(shape, dtype or keep.dtype),)
+    elif axis is None:
         outs = (jax.ShapeDtypeStruct(shape, f32),)
     else:
         shape[axis] //= 2
@@ -1090,16 +1169,16 @@
         out_shape=outs,
         in_specs=[VMEM] * 2,
         out_specs=(VMEM,) * len(outs),
-        compiler_params=params(32),
+        compiler_params=params(10),
         cost_estimate=COST,
         name="add_split",
     )(keep, received)
 
 
 class Scatter:
-    def __init__(self, links, keep, send):
+    def __init__(self, links, keep, send, *far):
         self.links = links
-        self.state = [keep, send]
+        self.state = [keep, send, *far]
         self.steps = [("d", level) for level in range(links.dp_bits)]
         self.steps += [("z", bit) for bit in range(1, links.mp_bits)]
         self.result = None
@@ -1107,16 +1186,49 @@
     def start(self):
         kind, index = self.steps[0]
         swap = self.links.mp_swap if kind == "z" else self.links.fan
-        self.received = swap(self.state[1], index)
+        self.received = [swap(part, index) for part in self.state[1::2]]
+
+    @property
+    def outgoing(self):
+        return self.state[1::2]
+
+    @outgoing.setter
+    def outgoing(self, values):
+        self.state[1::2] = values
+
+    def start_far(self):
+        self.received = [self.links.fan(self.state.pop(), 0)]
+        self.parts = "far"
+
+    def start_near(self):
+        self.received = [self.links.fan(self.state[1], 0)]
+        self.parts = "near"
+
+    parts = None
 
     def join(self):
+        if self.parts == "far":
+            self.parts = None
+            keep_far = self.state.pop()
+            self.state.append(add_split(keep_far, self.received[0], False)[0])
+            return
+        keep, received = self.state[0], self.received
         self.steps.pop(0)
-        keep, received = self.state[0], self.received
-        if not self.steps:
-            self.result = add_split(keep, received, None)[0][0, 0]
+        if self.parts == "near":
+            self.parts = None
+            received, far = lax.optimization_barrier((received[0], self.state[2]))
+            self.state = [add_split(keep, received, False)[0], far]
+        elif len(received) == 2:
+            self.state = [
+                add_split(keep, received[0], False)[0],
+                add_split(self.state[2], received[1], False)[0],
+            ]
+        elif not self.steps:
+            self.result = add_split(keep, received[0], None)[0][0, 0]
             self.state = []
-            return
-        self.state = list(add_split(keep, received, 1 if self.steps[0][0] == "z" else 0))
+        else:
+            axis = 1 if self.steps[0][0] == "z" else 0
+            self.state = list(add_split(keep, received[0], axis))
 
     def finish(self):
         while self.steps:
@@ -1151,19 +1263,13 @@
         values = values.reshape(ndp, nmp, maps_here, channels).transpose(0, 2, 1, 3)
         return values.reshape(NS, 8, 128)
 
-    def halves(values):
-        values = values.reshape(values.shape[0], -1, 2, HALF)
-        keep = jnp.where(links.core == 0, values[:, :, 0], values[:, :, 1])
-        send = jnp.where(links.core == 0, values[:, :, 1], values[:, :, 0])
-        return keep.reshape(keep.shape[0], -1), send.reshape(send.shape[0], -1)
-
-    mats_keep, mats_send = halves(jnp.stack([w_query, w_key, w_value, w_out], 1).astype(bf16))
     chunk = FF // nmp
     groups = 2 if chunk >= 256 else 1
     width = chunk // groups
-    both = jnp.stack([w_up, w_down.T], 1).astype(bf16)
-    both = both.reshape(both.shape[0], 2, nz, 2, groups, width).transpose(0, 3, 4, 1, 2, 5)
-    feed_rows = both.reshape(both.shape[0], -1)
+    mats_keep, mats_send, feed_rows = prepare(
+        links, groups, links.core.astype(jnp.int32).reshape(1),
+        (w_query, w_key, w_value, w_out), w_up, w_down.T,
+    )
 
     def chip_rows(keep, send):
         return by_core(links, keep, links.core_swap(send), 0)
@@ -1173,7 +1279,7 @@
         state_bank.transpose(0, 2, 1),
     ]
     small, sizes = pack(pieces)
-    v = Live()
+    v, u = Live(), Live()
     v.tokens, v.cotangent = tokens, cotangent
     small = small[None]
     v.small = join_small(links, small, links.core_swap(small), links.mp, 0)
@@ -1181,16 +1287,17 @@
     v.feed_rows = feed_rows
     fence(v, [attn])
 
-    attn.first_z()
     for bit in range(1, links.mp_bits):
         v.small = join_small(links, v.small, links.mp_swap(v.small, bit), links.mp, bit)
-    fence(v, [attn], [attn])
+    fence(v, [attn])
 
     feed_weights = lax.all_gather(v.feed_rows, AXES, axis=0, tiled=True)
     del v.feed_rows
-    attn.along_z(1)
+    attn.first_z()
     for bit in range(links.dp_bits):
         v.small = join_small(links, v.small, links.dp_swap(v.small, bit), links.dp, bit)
+    fence(v, [attn], [attn])
+    attn.along_z(1)
     small = v.small.reshape(ndp, nmp, -1)
     del v.small
     starts = [sum(sizes[:i]) for i in range(len(sizes))]
@@ -1199,13 +1306,11 @@
     )
     v.gain_one = lax.reduce_precision(gain_one.reshape(1, D), 8, 7)
     v.gain_two = lax.reduce_precision(gain_two.reshape(1, D), 8, 7)
-    v.rate, v.gain_in, v.gain_out = full_map(rate), full_map(gain_in), full_map(gain_out)
+    u.rate, u.gain_in, u.gain_out = full_map(rate), full_map(gain_in), full_map(gain_out)
     banks = banks.reshape(ndp, nmp, banks_here, NS, channels)
     bank = lax.dynamic_index_in_dim(banks, link // banks_here, 0, keepdims=False)
     bank = lax.dynamic_index_in_dim(bank, link % banks_here, 1, keepdims=False)
-    v.initial = bank.transpose(1, 0, 2).reshape(NS, 8, 128)
-    fence(v, [attn], [attn])
-
+    u.initial = bank.transpose(1, 0, 2).reshape(NS, 8, 128)
     half_blocks = float(BLK)
     v.scal = jnp.stack(
         [place_in.astype(f32) * half_blocks - CTX, (place_in != 0).astype(f32)]
@@ -1222,39 +1327,43 @@
 
     def exchange(bit):
         received = links.mp_swap(v.total, bit)
-        v.total, v.before = exchange_step(v.steps[bit], v.total, received, v.before, v.rate)
+        v.total, v.before = exchange_step(v.steps[bit], v.total, received, v.before, u.rate)
+
+    u.normed_b, tail = norm_first(v.tokens, v.gain_one)
+    u.tail = links.window_shift(tail, 1)
+    v.total = scan_own(u.normed_b, u.rate)
+    fence(v, [attn], [attn])
 
     attn.first_dp()
-    v.normed_b, tail = norm_first(v.tokens, v.gain_one)
-    v.tail = links.window_shift(tail, 1)
-    v.total = scan_tail(v.tail, scan_own(v.normed_b, v.rate), v.rate)
+    attn.more_dp()
+    v.total = scan_tail(u.tail, v.total, u.rate)
     v.before = jnp.zeros_like(v.total)
-    exchange(0)
+    for bit in range(2):
+        exchange(bit)
+    v.cot_t = v.cotangent.T
+    v.cot_par = links.core_swap(v.cotangent)
     fence(v, [attn], [attn])
-
-    attn.last_dp(0, None)
-    for bit in range(1, bits_of(per_window)):
+    attn.last_dp(max(ndp // 4, 1), None)
+    for bit in range(2, bits_of(per_window)):
         exchange(bit)
     v.inputs_kv = context_states(
-        v.scal, v.tail, v.normed_b, v.before, v.initial, v.rate, v.gain_in, v.gain_out
+        v.scal, u.tail, u.normed_b, v.before, u.initial, u.rate, u.gain_in, u.gain_out
     )
-    v.cot_t = v.cotangent.T
+    v.cot_par_t = links.core_swap(v.cot_t)
     fence(v, [attn], [attn])
 
     v.w_own = place(links, order, attn.blocks())
     attn.state = []
     v.w_other = links.core_swap(v.w_own)
     v.qkv_own = project(v.inputs_kv, v.w_own)
-    v.cot_par, v.cot_par_t = links.core_swap(v.cotangent), links.core_swap(v.cot_t)
+    fence(v)
     v.inputs_par = links.core_swap(v.inputs_kv)
-    fence(v)
-    v.qkv_other = project(v.inputs_kv, v.w_other)
-    v.attended = attend(attend_info, v.qkv_own, v.qkv_other)
-    v.middle, v.second_b, v.second_t = middle_norm(
+    u.qkv_other = project(v.inputs_kv, v.w_other)
+    v.attended = attend(attend_info, v.qkv_own, u.qkv_other)
+    u.middle, u.second_b, u.second_t = middle_norm(
         attend_info, v.attended, v.tokens, v.w_own, v.w_other, v.gain_two
     )
-    v.attended_par = links.core_swap(v.attended)
-    v.second_par, v.second_par_t = links.core_swap(v.second_b), links.core_swap(v.second_t)
+    u.second_par, u.second_par_t = links.core_swap(u.second_b), links.core_swap(u.second_t)
     v.feed_weights = feed_weights
     fence(v)
 
@@ -1263,137 +1372,134 @@
     for g in range(groups):
         last = g == groups - 1
         acts = (
-            v.second_b, v.second_par, v.cotangent, v.cot_par,
-            v.second_t, v.second_par_t, v.cot_t, v.cot_par_t,
+            u.second_b, u.second_par, v.cotangent, v.cot_par,
+            u.second_t, u.second_par_t, v.cot_t, v.cot_par_t,
         )
-        *v.sums, keep, send = feed(
+        *u.sums, keep, keep_far, send, send_far = feed(
             links, info, acts, v.feed_weights, nz * width, g, groups, earlier, last
         )
+        if g == 0:
+            v.attended_par = links.core_swap(v.attended)
         waits = list(scatters)
-        scatters.append(Scatter(links, keep, send))
+        scatters.append(Scatter(links, keep, send, keep_far, send_far))
         fence(v, scatters, waits)
         if not last:
             scatters[g].start()
-        earlier = v.sums
+        earlier = u.sums
     first, second = scatters[0], scatters[-1]
     both = [first, second] if groups > 1 else [first]
-    v.mix_own, v.mix_par, v.back_own, back_par = v.sums
-    del v.sums, v.feed_weights, v.cot_t, v.cot_par, v.cot_par_t, v.second_b, v.second_par
-    del v.second_t, v.second_par_t
-
-    for scatter in both:
-        scatter.start()
+    u.mix_own, v.mix_par, u.back_own, back_par = u.sums
+    del v.feed_weights, v.cot_t, v.cot_par, v.cot_par_t
+
+    split = groups > 1 and ndp >= 4
+    if split:
+        first.start()
+        second.start_far()
+    else:
+        second.start()
     v.back_recv = links.core_swap(back_par)
     v.grad_middle, v.branch_own, branch_other, v.grad_attended, v.grad_gain_two = back_middle(
-        attend_info, v.middle, v.back_own, v.back_recv, v.cotangent, v.gain_two, v.w_own,
+        attend_info, u.middle, u.back_own, v.back_recv, v.cotangent, v.gain_two, v.w_own,
         v.w_other,
     )
     v.branch_par = links.core_swap(branch_other)
-    v.g_own, v.g_other = attend_back(attend_info, v.qkv_own, v.qkv_other, v.grad_attended)
-    v.g_par = links.core_swap(v.g_other)
-    v.grad_context = back_project(v.g_own, v.g_other, v.w_own, v.w_other, 0, CTX, bf16)
-    v.lows = state_low(v.grad_context, v.rate)
+    v.grad_gain_two = v.grad_gain_two.reshape(ndp, nmp, -1)
+    gain_len = v.grad_gain_two.shape[2]
+    v.grad_gain_two = jnp.pad(v.grad_gain_two, ((0, 0), (0, 0), (0, channels - gain_len)))
+    v.g_own, v.g_other = attend_back(attend_info, v.qkv_own, u.qkv_other, v.grad_attended)
     fence(v, both, both)
 
     def exchange_back(bit):
         received = links.mp_swap(v.total, bit)
         v.total, v.after = exchange_back_step(
-            v.steps_back[bit], v.total, received, v.after, v.rate
+            v.steps_back[bit], v.total, received, v.after, u.rate
         )
+
+    if split:
+        second.start_near()
+    v.g_par = links.core_swap(v.g_other)
+    v.grad_context = back_project(v.g_own, v.g_other, v.w_own, v.w_other, 0, CTX, bf16)
+    v.lows = state_low(v.grad_context, u.rate)
+    v.total = v.lows[0]
+    v.after = jnp.zeros_like(v.total)
+    sums = state_sums(
+        v.scal, v.grad_context, u.tail, v.before, v.lows, u.initial, u.rate, u.gain_in, u.gain_out
+    )
+    bank_owner = link // banks_here
+    mat_rows = D // (ndp * nz)
+    whole_lines = channels == 128 and banks_here == 1
+    if whole_lines:
+        shares = pack_shares(
+            links, info, bank_owner.reshape(1), sums, v.grad_gain_two, maps_here, mat_rows
+        )
+    else:
+        shares = pack_shares_plain(
+            links, bank_owner, link % banks_here, banks_here, sums, v.grad_gain_two, maps_here
+        )
+    v.shares = add_split(shares[0], links.core_swap(shares[1].astype(bf16)), False, bf16)[0]
+    for bit in range(2):
+        exchange_back(bit)
+    fence(v, both, [second] if split else [])
 
     for scatter in both:
         scatter.start()
-    v.total = v.lows[0]
-    v.after = jnp.zeros_like(v.total)
-    exchange_back(0)
     mats = Scatter(
         links,
         *weight_grads(
             links, info, v.inputs_kv, v.inputs_par, v.g_own, v.g_par, v.attended,
-            v.attended_par, v.branch_own, v.branch_par,
+            v.attended_par, v.branch_own, v.branch_par, v.shares,
         ),
     )
+    for bit in range(2, bits_of(per_window)):
+        exchange_back(bit)
     fence(v, [*both, mats], both)
 
     mats.start()
     for scatter in both:
         scatter.start()
-    for bit in range(1, bits_of(per_window)):
-        exchange_back(bit)
-    sums = state_sums(
-        v.scal, v.grad_context, v.tail, v.before, v.lows, v.initial, v.rate, v.gain_in, v.gain_out
+    tail_sent = sent_tail(v.grad_context, v.after, u.rate, u.gain_in, u.gain_out)
+    v.last_sent = links.window_shift(tail_sent, -1)
+    v.own_sent = sent_own(v.after, u.rate, u.gain_in, u.gain_out)
+    v.part = back_project(v.g_own, v.g_other, v.w_own, v.w_other, CTX, BLK, f32)
+    v.grad_tokens, grad_gain_one = back_first(
+        v.tokens, v.part, v.own_sent, v.last_sent, v.grad_middle, v.gain_one
     )
-
-    def by_owner(values):
-        values = values.reshape(ndp, maps_here, nmp, channels).transpose(0, 2, 1, 3)
-        return values.reshape(ndp, nmp, -1)
-
-    chosen = jnp.arange(ndp * banks_here, dtype=jnp.int32) == link
-    bank_share = sums[3].reshape(NS, nmp, channels).transpose(1, 0, 2)[None]
-    bank_share = jnp.where(chosen[:, None, None, None], bank_share, 0.0)
-    bank_share = bank_share.reshape(ndp, banks_here, nmp, NS * channels).transpose(0, 2, 1, 3)
-    shares = jnp.concatenate(
-        [
-            by_owner(sums[0]),
-            by_owner(sums[1]),
-            by_owner(sums[2]),
-            bank_share.reshape(ndp, nmp, -1),
-            v.grad_gain_two.reshape(ndp, nmp, -1),
-        ],
-        2,
-    ).astype(bf16)
-    share_len = shares.shape[2]
-    mat_rows = D // (ndp * nz)
-    shares = jnp.pad(shares, ((0, 0), (0, 0), (0, -share_len % (128 * mat_rows))))
-    shares = shares.reshape(ndp, nz, 2, mat_rows, -1)
-    shares_keep = jnp.where(links.core == 0, shares[:, :, 0], shares[:, :, 1])
-    shares_send = jnp.where(links.core == 0, shares[:, :, 1], shares[:, :, 0])
-    shares = in_order(links, add_b(shares_keep, links.core_swap(shares_send)))
-    small = Scatter(links, shares[: ndp // 2], shares[ndp // 2 :])
-    small.start()
-    v.part = back_project(v.g_own, v.g_other, v.w_own, v.w_other, CTX, BLK, f32)
-    fence(v, [*both, mats, small], [*both, mats, small])
-
-    mats.state = [jnp.concatenate([a, b], -1) for a, b in zip(mats.state, small.state)]
+    v.gain_parts = grad_gain_one.reshape(ndp * nmp, -1)
+    fence(v, [*both, mats], [mats, *both])
     mats.start()
     late = [second] if second.steps else []
     for scatter in late:
         scatter.start()
-    tail_sent = sent_tail(v.grad_context, v.after, v.rate, v.gain_in, v.gain_out)
-    v.last_sent = links.window_shift(tail_sent, -1)
-    v.own_sent = sent_own(v.after, v.rate, v.gain_in, v.gain_out)
+    gain_parts = lax.all_to_all(v.gain_parts, AXES, split_axis=0, concat_axis=0, tiled=True)
+    v.share_one = jnp.sum(gain_parts, axis=0)
+    v.mix_recv = links.core_swap(v.mix_par)
     fence(v, [*both, mats], [mats, *late])
     mats.start()
-    v.grad_tokens, grad_gain_one = back_first(
-        v.tokens, v.part, v.own_sent, v.last_sent, v.grad_middle, v.gain_one
-    )
-    v.gain_parts = grad_gain_one.reshape(ndp * nmp, -1)
-    v.mix_recv = links.core_swap(v.mix_par)
-    fence(v, [*both, mats], [mats])
-    gain_parts = lax.all_to_all(v.gain_parts, AXES, split_axis=0, concat_axis=0, tiled=True)
-    v.share_one = jnp.sum(gain_parts, axis=0)
-    mats.start()
+    v.mixed = mix(u.middle, u.mix_own, v.mix_recv)
     for scatter in both:
         scatter.finish()
-    v.mixed = (v.middle + (v.mix_own + v.mix_recv.astype(f32))).astype(bf16)
+    v.results = [scatter.result for scatter in both]
+    fence(v, [mats], [mats])
+    mats.start()
+    grad_up = jnp.concatenate([result[0] for result in v.results], 1)
+    grad_down = jnp.concatenate([result[1] for result in v.results], 1).T
     mats.join()
     mats.finish()
     grad_tokens = v.grad_tokens
     mixed, share_one = v.mixed, v.share_one
     mats_share = mats.result
-    grad_up = jnp.concatenate([scatter.result[0] for scatter in both], 1)
-    grad_down = jnp.concatenate([scatter.result[1] for scatter in both], 1).T
-
     line = 4 * HALF
-    flat = mats_share[:, line:].reshape(-1)[:share_len]
-    map_size = maps_here * channels
+    extra = mats_share[:, line:]
+    if not whole_lines:
+        lines = 3 * maps_here + banks_here * NS + 1
+        extra = extra.reshape(-1)[: lines * channels].reshape(lines, channels)
     grad_maps = [
-        flat[i * map_size : (i + 1) * map_size].reshape(maps_here, channels).T for i in range(3)
+        extra[i * maps_here : (i + 1) * maps_here].T for i in range(3)
     ]
-    bank_end = share_len - D // (ndp * nmp)
-    grad_bank = flat[3 * map_size : bank_end].reshape(banks_here, NS, channels)
+    bank_end = 3 * maps_here + banks_here * NS
+    grad_bank = extra[3 * maps_here : bank_end].reshape(banks_here, NS, channels)
     grad_bank = grad_bank.transpose(0, 2, 1)
-    share_two = flat[bank_end:]
+    share_two = extra[bank_end, :gain_len]
     mine_rows = mats_share[:, :line].reshape(2, mat_rows // 2, 4, HALF)
     rows_keep = jnp.where(links.core == 0, mine_rows[0], mine_rows[1])
     rows_send = jnp.where(links.core == 0, mine_rows[1], mine_rows[0])

time: 396 us -> 383 us (0.967)
  waiting for transfers between devices: 110 us -> 89.9 us
  blocking collectives: 0 us -> 14.2 us
  other arithmetic: 17.8 us -> 5.43 us
  Pallas kernels: 148 us -> 160 us
  starting transfers between devices: 67.9 us -> 60.5 us
    all_to_all x0 -> x1, blocking collectives: none -> 14.2 us  [body(): lax.all_to_all(v.gain_parts, AXES, split_axis=0, concat_axis=0, tiled=True)]
    ppermute x45 -> x46, waiting for transfers between devices: 98.5 us -> 89.7 us  [send(): return lax.ppermute(values, AXES, pairs)]
    pallas_call x13 -> x15, Pallas kernels: 6.9 us -> 15.3 us  [add_split(): pl.pallas_call(functools.partial(add_kernel, axis or 0), out_shape=outs,...]
    all_to_all x1 -> x0, waiting for transfers between devices: 8.28 us -> none  [body(): lax.all_to_all(v.gain_parts, AXES, split_axis=0, concat_axis=0, tiled=True)]
    unnamed x118 -> x155, local copies, waits for them, and re-layouts: 14.7 us -> 21.9 us
    pallas_call x1 -> x4, Pallas kernels: 5.23 us -> 11.5 us  [the longest x1 5.24 us: place(): pl.pallas_call(functools.partial(place_kernel, ndp), out_shape=pltpu.HBM(...]
    convert_element_type x2 -> x0, other arithmetic: 4.63 us -> none  [the longest x1 3.42 us: body(): v.mixed = (v.middle + (v.mix_own + v.mix_recv.astype(f32))).astype(bf16)]
    all_to_all x1 -> x0, starting transfers between devices: 4.51 us -> none  [body(): lax.all_to_all(v.gain_parts, AXES, split_axis=0, concat_axis=0, tiled=True)]
  transfers between devices with their start and end apart: 47 -> 47, of which waited for: 23 -> 26; matrix products, arithmetic and copies ran while one was open for 7% -> 4% of each run, Pallas kernels for 31% -> 40%
where the time goes in v3:
time: 383 us; the launch traced here: 378 us
  Pallas kernels  160 us (42%)
  waiting for transfers between devices  89.9 us (23%)
  starting transfers between devices  60.5 us (16%)
  local copies, waits for them, and re-layouts  30.8 us (8%)
  between operations  17.2 us (4%)
  blocking collectives  14.2 us (4%)
  other arithmetic  5.43 us (1%)
    ppermute x46, waiting for transfers between devices, send(): return lax.ppermute(values, AXES, pairs)  89.7 us
    ppermute x46, starting transfers between devices, send(): return lax.ppermute(values, AXES, pairs)  60.4 us
    pallas_call x2, Pallas kernels, feed(): pl.pallas_call(functools.partial(feed_kernel, ndp, nz, width, index, grou...  42.3 us
    unnamed x155, local copies, waits for them, and re-layouts  21.9 us
    pallas_call x15, Pallas kernels, add_split(): pl.pallas_call(functools.partial(add_kernel, axis or 0), out_shape=outs,...  15.3 us
    all_to_all x1, blocking collectives, body(): lax.all_to_all(v.gain_parts, AXES, split_axis=0, concat_axis=0, tiled=True)  14.2 us
    pallas_call x1, Pallas kernels, attend_back(): pl.pallas_call(attend_back_kernel, out_shape=(out, out), in_specs=[SMEM]...  11.8 us
    pallas_call x2, Pallas kernels, back_project(): pl.pallas_call(functools.partial(back_project_kernel, first), out_shape=j...  11.4 us
  transfers between devices with their start and end apart: 47, of which 26 were waited for; matrix products, arithmetic and copies ran while one was open for 4% of the time, Pallas kernels for 40%

profile of v3, /device:TPU:0, one launch (start us, length us, event | category | flops | bytes accessed | tf_op | source)
XLA Modules:
  0.0 378.1 jit_solution(9810829291192479636)
XLA Ops:
  7.2 2.3 prepare.1
  12.2 2.8 collective-permute-start.2
  15.0 1.9 collective-permute-done.2.there_ref
  16.9 3.0 collective-permute-start.3
  19.9 2.5 collective-permute-done.3.there_ref
  22.5 1.6 collective-permute-start.4
  24.2 2.6 collective-permute-start.6
  27.6 1.6 collective-permute-start.5
  30.5 3.5 collective-permute-done.5.there_ref
  34.0 2.7 collective-permute-done.6.there_ref
  37.7 5.3 %collective-permute-start.7 = (bf16[2,64,2048]{2,1,0:T(8,128)(2,1)}, bf16[2,64,2048]{2,1,0:T(8,128)(2,1)}, u32[]{:S(2)}, u32[]{:S(2)}) collective-permute-start(bf16[2,64,2048]{2,1,0:T(8,128)(2,1)} %merge.12.here_ref), channel_id=1, source_target_pairs={{0,2},{1,3},{2,0},{3,1},{4,6},{5,7},{6,4},{7,5},{8,10},{9,11},{10,... | collective-permute-start | bytes 1572872 | tf_op jit(solution)/shard_map/ppermute | solution.py:78
  44.6 2.0 fusion.1
  46.6 4.5 %scan_own.1.own_ref = f32[2,16,8,128]{3,2,1,0:T(8,128)S(1)} custom-call(bf16[512,1024]{1,0:T(8,128)(2,1)S(1)} %get-tuple-element.302.x_ref.own_ref, f32[16,8,128]{2,1,0:T(8,128)S(1)} %bitcast.107), custom_call_target="tpu_custom_call" | custom-call | flops 1 | bytes 1 | tf_op jit(solution)/shard_map/scan_own/pallas_call | solution.py:170
  51.2 8.4 %collective-permute-done.7.there_ref = bf16[2,64,2048]{2,1,0:T(8,128)(2,1)} collective-permute-done((bf16[2,64,2048]{2,1,0:T(8,128)(2,1)}, bf16[2,64,2048]{2,1,0:T(8,128)(2,1)}, u32[]{:S(2)}, u32[]{:S(2)}) %collective-permute-start.7) | collective-permute-done | bytes 524320 | tf_op jit(solution)/shard_map/ppermute | solution.py:78
  59.6 2.4 merge.13
  64.0 2.1 collective-permute-start.8
  67.9 1.6 scan_tail.1.total_ref
  69.5 7.1 %collective-permute-start.9 = (f32[2,16,8,128]{3,2,1,0:T(8,128)S(1)}, f32[2,16,8,128]{3,2,1,0:T(8,128)S(1)}, u32[]{:S(2)}, u32[]{:S(2)}) collective-permute-start(f32[2,16,8,128]{3,2,1,0:T(8,128)S(1)} %scan_tail.1.total_ref), channel_id=1, source_target_pairs={{0,1},{1,0},{2,3},{3,2},{4,5},{5,4},{6,7},{7,6},{8,9},{9,8},{10,11... | collective-permute-start | bytes 393224 | tf_op jit(solution)/shard_map/ppermute | solution.py:78
  79.0 2.7 collective-permute-start.10
  82.3 5.1 %collective-permute-done.10.recv_ref = f32[2,16,8,128]{3,2,1,0:T(8,128)S(1)} collective-permute-done((f32[2,16,8,128]{3,2,1,0:T(8,128)S(1)}, f32[2,16,8,128]{3,2,1,0:T(8,128)S(1)}, u32[]{:S(2)}, u32[]{:S(2)}) %collective-permute-start.10) | collective-permute-done | bytes 131104 | tf_op jit(solution)/shard_map/ppermute | solution.py:78
  92.4 7.2 %collective-permute-done.13 = bf16[4,64,2048]{2,1,0:T(8,128)(2,1)} collective-permute-done((bf16[4,64,2048]{2,1,0:T(8,128)(2,1)}, bf16[4,64,2048]{2,1,0:T(8,128)(2,1)}, u32[]{:S(2)}, u32[]{:S(2)}) %collective-permute-start.13) | collective-permute-done | bytes 1048608 | tf_op jit(solution)/shard_map/ppermute | solution.py:78
  103.7 2.7 collective-permute-start.14
  107.3 14.5 %collective-permute-done.14.recv_ref = f32[2,16,8,128]{3,2,1,0:T(8,128)S(1)} collective-permute-done((f32[2,16,8,128]{3,2,1,0:T(8,128)S(1)}, f32[2,16,8,128]{3,2,1,0:T(8,128)S(1)}, u32[]{:S(2)}, u32[]{:S(2)}) %collective-permute-start.14) | collective-permute-done | bytes 131104 | tf_op jit(solution)/shard_map/ppermute | solution.py:78
  124.1 2.7 context_states.1.x_ref.x_own
  126.9 5.2 %collective-permute-done.16 = bf16[4,64,2048]{2,1,0:T(8,128)(2,1)} collective-permute-done((bf16[4,64,2048]{2,1,0:T(8,128)(2,1)}, bf16[4,64,2048]{2,1,0:T(8,128)(2,1)}, u32[]{:S(2)}, u32[]{:S(2)}) %collective-permute-start.16) | collective-permute-done | bytes 1048608 | tf_op jit(solution)/shard_map/ppermute | solution.py:78
  132.0 5.2 %place.1.w_ref.o_own.w_own = bf16[1024,2048]{1,0:T(8,128)(2,1)} custom-call(s32[4]{0:T(128)S(1)} %pad_add_fusion.1.order, bf16[256,2048]{1,0:T(8,128)(2,1)} %bitcast.41.refs_0_, bf16[256,2048]{1,0:T(8,128)(2,1)} %bitcast.42.refs_1_, bf16[256,2048]{1,0:T(8,128)(2,1)} %bitcast.43.refs_2_, bf16[256,2048]{1,0:T(8,128)(2,1)} %bitcast.44.refs_3_), custom_call_target="tpu_custom_call" | custom-call | flops 1 | bytes 1 | tf_op jit(solution)/shard_map/place/pallas_call | solution.py:949
  137.3 4.2 %project.2.own_ref = bf16[640,1536]{1,0:T(8,128)(2,1)S(1)} custom-call(bf16[640,1024]{1,0:T(8,128)(2,1)S(1)} %context_states.1.x_ref.x_own, bf16[1024,2048]{1,0:T(8,128)(2,1)} %place.1.w_ref.o_own.w_own), custom_call_target="tpu_custom_call" | custom-call | flops 1 | bytes 1 | tf_op jit(solution)/shard_map/project/pallas_call | solution.py:775
  141.5 3.5 collective-permute-done.17.w_ref.o_other.w_other
  145.2 4.5 %project.3.other_ref = bf16[640,1536]{1,0:T(8,128)(2,1)S(1)} custom-call(bf16[640,1024]{1,0:T(8,128)(2,1)S(1)} %context_states.1.x_ref.x_own, bf16[1024,2048]{1,0:T(8,128)(2,1)} %collective-permute-done.17.w_ref.o_other.w_other), custom_call_target="tpu_custom_call" | custom-call | flops 1 | bytes 1 | tf_op jit(solution)/shard_map/project/pallas_call | solution.py:775
  149.8 8.0 %attend.1.att_ref.a_own = bf16[512,1024]{1,0:T(8,128)(2,1)S(1)} custom-call(s32[2]{0:T(128)S(1)} %pad_add_fusion.info, bf16[640,1536]{1,0:T(8,128)(2,1)S(1)} %project.2.own_ref, bf16[640,1536]{1,0:T(8,128)(2,1)S(1)} %project.3.other_ref), custom_call_target="tpu_custom_call" | custom-call | flops 1 | bytes 1 | tf_op jit(solution)/shard_map/attend/pallas_call | solution.py:459
  159.0 5.2 %middle_norm.1 = (f32[512,1024]{1,0:T(8,128)S(1)}, bf16[512,1024]{1,0:T(8,128)(2,1)}, bf16[1024,512]{1,0:T(8,128)(2,1)}) custom-call(s32[2]{0:T(128)S(1)} %pad_add_fusion.info, bf16[512,1024]{1,0:T(8,128)(2,1)S(1)} %attend.1.att_ref.a_own, bf16[512,1024]{1,0:T(8,128)(2,1)S(1)} %copy-done.11, bf16[1024,2048]{1,0:T(8,128)(2,1)} %place.1.w_ref.o_own.w_own, ...), custom_call_target="tpu_custom_call" | custom-call | flops 1 | bytes 1 | tf_op jit(solution)/shard_map/middle_norm/pallas_call | solution.py:710
  166.7 2.0 collective-permute-done.20.s_par
  172.7 21.0 %feed_first.1 = (f32[1024,1024]{1,0:T(8,128)S(1)}, f32[1024,1024]{1,0:T(8,128)S(1)}, bf16[1,4,2,256,256]{4,3,2,1,0:T(8,128)(2,1)S(1)}, bf16[1,4,2,256,256]{4,3,2...) custom-call(s32[6]{0:T(128)S(1)} %stack.127.info, ...), custom_call_target="tpu_custom_call" | custom-call | flops 1 | bytes 1 | tf_op jit(solution)/shard_map/feed_first/pallas_call | solution.py:626
  194.8 1.9 collective-permute-start.23
  196.7 21.3 %feed_last.1 = (f32[512,1024]{1,0:T(8,128)S(1)}, bf16[512,1024]{1,0:T(8,128)(2,1)}, f32[512,1024]{1,0:T(8,128)S(1)}, bf16[512,1024]{1,0:T(8,128)(2,1)S(1)}, bf16...) custom-call(s32[6]{0:T(128)S(1)} %stack.127.info, ...), custom_call_target="tpu_custom_call" | custom-call | flops 1 | bytes 1 | tf_op jit(solution)/shard_map/feed_last/pallas_call | solution.py:626
  219.2 1.5 collective-permute-done.23.recv_ref
  221.9 1.8 collective-permute-start.26
  224.0 4.6 %back_middle.1 = (f32[512,1024]{1,0:T(8,128)S(1)}, bf16[512,512]{1,0:T(8,128)(2,1)S(1)}, bf16[512,512]{1,0:T(8,128)(2,1)}, bf16[512,1024]{1,0:T(8,128)(2,1)S(1)}, f32[1,1024]{1,0:T(1,128)S(1)}) custom-call(s32[2]{0:T(128)S(1)} %pad_add_fusion.info, f32[512,1024]{1,0:T(8,128)S(1)} %copy-done.14, f32[512,1024]{1,0:T(8,128)S(1)} %get-tuple-element.429.own_ref, ...), custom_call_target="tpu_custom_call" | custom-call | flops 1 | bytes 1 | tf_op jit(solution)/shard_map/back_middle/pallas_call | solution.py:749
  229.4 11.8 %attend_back.1 = (bf16[640,1536]{1,0:T(8,128)(2,1)S(1)}, bf16[640,1536]{1,0:T(8,128)(2,1)S(1)}) custom-call(s32[2]{0:T(128)S(1)} %pad_add_fusion.info, bf16[640,1536]{1,0:T(8,128)(2,1)S(1)} %copy-done.1, bf16[640,1536]{1,0:T(8,128)(2,1)S(1)} %copy-done.3, bf16[512,1024]{1,0:T(8,128)(2,1)S(1)} %get-tuple-element.437.grad_ref), custom_call_target="tpu_custom_call" | custom-call | flops 1 | bytes 1 | tf_op jit(solution)/shard_map/attend_back/pallas_call | solution.py:510
  243.8 3.1 collective-permute-done.26.recv_ref
  246.9 1.6 collective-permute-start.32
  248.4 1.5 copy-done.17
  250.0 5.0 %back_project.2.g_ref = bf16[128,1024]{1,0:T(8,128)(2,1)S(1)} custom-call(bf16[640,1536]{1,0:T(8,128)(2,1)S(1)} %get-tuple-element.513.g_own, bf16[640,1536]{1,0:T(8,128)(2,1)S(1)} %copy-done.17, bf16[1024,2048]{1,0:T(8,128)(2,1)} %place.1.w_ref.o_own.w_own, bf16[1024,2048]{1,0:T(8,128)(2,1)} %collective-permute-done.17.w_ref.o_other.w_other), custom_call_target="tpu_custom_call" | custom-call | flops 1 | bytes 1 | tf_op jit(solution)/shard_map/back_project/pallas_call | solution.py:796
  257.0 4.0 %state_sums.1.sums_ref = f32[4,16,8,128]{3,2,1,0:T(8,128)S(1)} custom-call(f32[2]{0:T(128)S(1)} %copy-done.69, bf16[128,1024]{1,0:T(8,128)(2,1)S(1)} %back_project.2.g_ref, bf16[128,1024]{1,0:T(8,128)(2,1)S(1)} %copy-done.29, f32[2,16,8,128]{3,2,1,0:T(8,128)S(1)} %copy-done.51, f32[2,16,8,128]{3,2,1,0:T(8,128)S(1)} %state_low.1.lows_ref, ...), custom_call_target="tpu_custom_call" | custom-call | flops 1 | bytes 1 | tf_op jit(solution)/shard_map/state_sums/pallas_call | solution.py:347
  266.7 1.6 add_split.19
  269.0 1.7 collective-permute-start.35
  271.8 2.4 collective-permute-start.33
  274.2 9.5 %weight_grads.1 = (bf16[2,4,64,2176]{3,2,1,0:T(8,128)(2,1)S(1)}, bf16[2,4,64,2176]{3,2,1,0:T(8,128)(2,1)}) custom-call(s32[6]{0:T(128)S(1)} %stack.127.info, bf16[640,1024]{1,0:T(8,128)(2,1)S(1)} %context_states.1.x_ref.x_own, bf16[640,1024]{1,0:T(8,128)(2,1)} %collective-permute-done.18.x_par, bf16[640,1536]{1,0:T(8,128)(2,1)S(1)} %get-tuple-element.513.g_own, ...), custom_call_target="tpu_custom_call" | custom-call | flops 1 | bytes 1 | tf_op jit(solution)/shard_map/weight_grads/pallas_call | solution.py:865
  287.3 3.6 collective-permute-start.39
  291.0 2.1 sent_tail.1
  296.0 3.8 %sent_own.1.sent_ref = bf16[384,1024]{1,0:T(8,128)(2,1)S(1)} custom-call(f32[16,8,128]{2,1,0:T(8,128)S(1)} %get-tuple-element.511.after_ref, f32[16,8,128]{2,1,0:T(8,128)S(1)} %bitcast.119, f32[16,8,128]{2,1,0:T(8,128)S(1)} %bitcast.132, f32[16,8,128]{2,1,0:T(8,128)S(1)} %bitcast.136), custom_call_target="tpu_custom_call" | custom-call | flops 1 | bytes 1 | tf_op jit(solution)/shard_map/sent_own/pallas_call | solution.py:404
  299.8 6.4 %back_project.3.part_ref = f32[512,1024]{1,0:T(8,128)S(1)} custom-call(bf16[640,1536]{1,0:T(8,128)(2,1)S(1)} %get-tuple-element.513.g_own, bf16[640,1536]{1,0:T(8,128)(2,1)S(1)} %copy-done.18, bf16[1024,2048]{1,0:T(8,128)(2,1)} %place.1.w_ref.o_own.w_own, bf16[1024,2048]{1,0:T(8,128)(2,1)} %collective-permute-done.17.w_ref.o_other.w_other), custom_call_target="tpu_custom_call" | custom-call | flops 1 | bytes 1 | tf_op jit(solution)/shard_map/back_project/pallas_call | solution.py:796
  306.3 2.6 back_first.1
  309.7 2.0 collective-permute-done.38.recv_ref
  311.6 1.6 collective-permute-done.37.recv_ref
  313.3 3.0 add_split.24
  316.9 2.0 add_split.23
  319.6 2.8 collective-permute-start.42
  322.4 14.2 %all_to_all.9 = f32[32,1,32]{2,1,0:T(1,128)S(1)} all-to-all(f32[32,1,32]{2,1,0:T(1,128)S(1)} %bitcast.144), channel_id=1, replica_groups=mesh['dp'=4,'mp'=8] {'dp','mp'}, dimensions={0} | all-to-all | bytes 8192 | tf_op jit(solution)/shard_map/all_to_all | solution.py:1473
  337.2 1.7 add_split.27
  341.4 2.5 mix.1
  344.9 8.4 %collective-permute-done.43.recv_ref = bf16[1,2,64,2176]{3,2,1,0:T(8,128)(2,1)S(1)} collective-permute-done((bf16[1,2,64,2176]{3,2,1,0:T(8,128)(2,1)S(1)}, bf16[1,2,64,2176]{3,2,1,0:T(8,128)(2,1)S(1)}, u32[]{:S(2)}, u32[]{:S(2)}) %collective-permute-start.43) | collective-permute-done | bytes 557088 | tf_op jit(solution)/shard_map/ppermute | solution.py:78
  353.4 2.0 collective-permute-start.44
  357.4 10.5 %collective-permute-done.44.recv_ref = bf16[1,1,64,2176]{3,2,1,0:T(8,128)(2,1)S(1)} collective-permute-done((bf16[1,1,64,2176]{3,2,1,0:T(8,128)(2,1)S(1)}, bf16[1,1,64,2176]{3,2,1,0:T(8,128)(2,1)S(1)}, u32[]{:S(2)}, u32[]{:S(2)}) %collective-permute-start.44) | collective-permute-done | bytes 278560 | tf_op jit(solution)/shard_map/ppermute | solution.py:78
  (284 shorter events, 66.7 us)
Async XLA Ops:
  7.2 159.1 %all-gather.2.cloned.1.call-start = ((), (), s32[]{:S(2)}) async-start(), calls=%async_computation.1 | async-start | bytes 17301504 | tf_op jit(solution)/shard_map/all_gather | solution.py:1294
  9.6 2.6 collective-permute-start.1
  10.9 1.2 collective-permute-start
  12.2 4.7 %collective-permute-start.2 = (f32[2,29,128]{2,1,0:T(8,128)S(1)}, f32[2,29,128]{2,1,0:T(8,128)S(1)}, u32[]{:S(2)}, u32[]{:S(2)}) collective-permute-start(f32[2,29,128]{2,1,0:T(8,128)S(1)} %merge.7.here_ref), channel_id=1, source_target_pairs={{0,2},{1,3},{2,0},{3,1},{4,6},{5,7},{6,4},{7,5},{8,10},{9,11},{10,... | collective-permute-start | bytes 89096 | tf_op jit(solution)/shard_map/ppermute | solution.py:78
  16.9 5.5 %collective-permute-start.3 = (f32[4,29,128]{2,1,0:T(8,128)S(1)}, f32[4,29,128]{2,1,0:T(8,128)S(1)}, u32[]{:S(2)}, u32[]{:S(2)}) collective-permute-start(f32[4,29,128]{2,1,0:T(8,128)S(1)} %merge.8.here_ref), channel_id=1, source_target_pairs={{0,4},{1,5},{2,6},{3,7},{4,0},{5,1},{6,2},{7,3},{8,12},{9,13},{10,... | collective-permute-start | bytes 178184 | tf_op jit(solution)/shard_map/ppermute | solution.py:78
  22.5 20.7 %copy-start.10 = (bf16[512,1024]{1,0:T(8,128)(2,1)S(1)}, bf16[512,1024]{1,0:T(8,128)(2,1)}, u32[]{:S(2)}) copy-start(bf16[512,1024]{1,0:T(8,128)(2,1)} %tok_ref.1) | copy-start | bytes 3145732
  22.5 5.0 %collective-permute-start.4 = (f32[8,29,128]{2,1,0:T(8,128)S(1)}, f32[8,29,128]{2,1,0:T(8,128)S(1)}, u32[]{:S(2)}, u32[]{:S(2)}) collective-permute-start(f32[8,29,128]{2,1,0:T(8,128)S(1)} %merge.9.here_ref), channel_id=1, source_target_pairs={{0,8},{1,9},{2,10},{3,11},{4,12},{5,13},{6,14},{7,15},{8,0},{9,1},... | collective-permute-start | bytes 356360 | tf_op jit(solution)/shard_map/ppermute | solution.py:78
  24.2 98.9 %copy-start.68 = (f32[2]{0:T(128)}, f32[2]{0:T(128)S(1)}, u32[]{:S(2)}) copy-start(f32[2]{0:T(128)S(1)} %pad_maximum_fusion.8.scal) | copy-start | bytes 28
  24.2 12.5 %collective-permute-start.6 = (bf16[1,64,2048]{2,1,0:T(8,128)(2,1)S(1)}, bf16[1,64,2048]{2,1,0:T(8,128)(2,1)S(1)}, u32[]{:S(2)}, u32[]{:S(2)}) collective-permute-start(bf16[1,64,2048]{2,1,0:T(8,128)(2,1)S(1)} %maximum_select_fusion.1.here_ref), channel_id=1, source_target_pairs={{0,4},{1,5},{2,6},{3,7},{4,0},{5,1},{6,2},{7,3},{8,12},{9,13},{10,... | collective-permute-start | bytes 786440 | tf_op jit(solution)/shard_map/ppermute | solution.py:78
  27.6 6.4 %collective-permute-start.5 = (f32[16,29,128]{2,1,0:T(8,128)S(1)}, f32[16,29,128]{2,1,0:T(8,128)S(1)}, u32[]{:S(2)}, u32[]{:S(2)}) collective-permute-start(f32[16,29,128]{2,1,0:T(8,128)S(1)} %merge.10.here_ref), channel_id=1, source_target_pairs={{0,16},{1,17},{2,18},{3,19},{4,20},{5,21},{6,22},{7,23},{8,24},{9,... | collective-permute-start | bytes 712712 | tf_op jit(solution)/shard_map/ppermute | solution.py:78
  29.3 48.4 %copy-start.66 = (f32[3]{0:T(128)}, f32[3]{0:T(128)S(1)}, u32[]{:S(2)}) copy-start(f32[3]{0:T(128)S(1)} %pad_maximum_fusion.9.scal) | copy-start | bytes 40
  37.6 22.0 %copy-start.4 = (bf16[512,1024]{1,0:T(8,128)(2,1)S(1)}, bf16[512,1024]{1,0:T(8,128)(2,1)}, u32[]{:S(2)}) copy-start(bf16[512,1024]{1,0:T(8,128)(2,1)} %cot_ref) | copy-start | bytes 3145732
  37.7 21.9 %collective-permute-start.7 = (bf16[2,64,2048]{2,1,0:T(8,128)(2,1)}, bf16[2,64,2048]{2,1,0:T(8,128)(2,1)}, u32[]{:S(2)}, u32[]{:S(2)}) collective-permute-start(bf16[2,64,2048]{2,1,0:T(8,128)(2,1)} %merge.12.here_ref), channel_id=1, source_target_pairs={{0,2},{1,3},{2,0},{3,1},{4,6},{5,7},{6,4},{7,5},{8,10},{9,11},{10,... | collective-permute-start | bytes 1572872 | tf_op jit(solution)/shard_map/ppermute | solution.py:78
  44.6 25.0 %copy-start.25 = (bf16[512,1024]{1,0:T(8,128)(2,1)}, bf16[512,1024]{1,0:T(8,128)(2,1)S(1)}, u32[]{:S(2)}) copy-start(bf16[512,1024]{1,0:T(8,128)(2,1)S(1)} %get-tuple-element.302.x_ref.own_ref) | copy-start | bytes 3145732
  51.1 12.9 %copy-start.54 = (f32[2,16,8,128]{3,2,1,0:T(8,128)}, f32[2,16,8,128]{3,2,1,0:T(8,128)S(1)}, u32[]{:S(2)}) copy-start(f32[2,16,8,128]{3,2,1,0:T(8,128)S(1)} %scan_own.1.own_ref) | copy-start | bytes 393220
  59.6 31.8 %collective-permute-start.11 = (bf16[512,1024]{1,0:T(8,128)(2,1)S(1)}, bf16[512,1024]{1,0:T(8,128)(2,1)S(1)}, u32[]{:S(2)}, u32[]{:S(2)}) collective-permute-start(bf16[512,1024]{1,0:T(8,128)(2,1)S(1)} %copy-done.4), channel_id=1, source_target_pairs={{0,1},{1,0},{2,3},{3,2},{4,5},{5,4},{6,7},{7,6},{8,9},{9,8},{10,11... | collective-permute-start | bytes 3145736 | tf_op jit(solution)/shard_map/ppermute | solution.py:78
  62.0 37.9 %copy-start.76 = (s32[4]{0:T(128)S(1)}, s32[4]{0:T(128)}, u32[]{:S(2)}) copy-start(s32[4]{0:T(128)} %param.29) | copy-start | bytes 52
  62.0 30.3 %collective-permute-start.12 = (bf16[4,64,2048]{2,1,0:T(8,128)(2,1)}, bf16[4,64,2048]{2,1,0:T(8,128)(2,1)}, u32[]{:S(2)}, u32[]{:S(2)}) collective-permute-start(bf16[4,64,2048]{2,1,0:T(8,128)(2,1)} %merge.13), channel_id=1, source_target_pairs={{0,16},{1,9},{2,18},{3,11},{4,20},{5,13},{6,22},{7,15},{8,24},{9,1... | collective-permute-start | bytes 3145736 | tf_op jit(solution)/shard_map/ppermute | solution.py:78
  63.2 36.4 %collective-permute-start.13 = (bf16[4,64,2048]{2,1,0:T(8,128)(2,1)}, bf16[4,64,2048]{2,1,0:T(8,128)(2,1)}, u32[]{:S(2)}, u32[]{:S(2)}) collective-permute-start(bf16[4,64,2048]{2,1,0:T(8,128)(2,1)} %merge.13), channel_id=1, source_target_pairs={{0,8},{1,17},{2,10},{3,19},{4,12},{5,21},{6,14},{7,23},{8,0},{9,25... | collective-permute-start | bytes 3145736 | tf_op jit(solution)/shard_map/ppermute | solution.py:78
  64.0 3.0 collective-permute-start.8
  69.5 8.1 %collective-permute-start.9 = (f32[2,16,8,128]{3,2,1,0:T(8,128)S(1)}, f32[2,16,8,128]{3,2,1,0:T(8,128)S(1)}, u32[]{:S(2)}, u32[]{:S(2)}) collective-permute-start(f32[2,16,8,128]{3,2,1,0:T(8,128)S(1)} %scan_tail.1.total_ref), channel_id=1, source_target_pairs={{0,1},{1,0},{2,3},{3,2},{4,5},{5,4},{6,7},{7,6},{8,9},{9,8},{10,11... | collective-permute-start | bytes 393224 | tf_op jit(solution)/shard_map/ppermute | solution.py:78
  79.0 8.4 %collective-permute-start.10 = (f32[2,16,8,128]{3,2,1,0:T(8,128)S(1)}, f32[2,16,8,128]{3,2,1,0:T(8,128)S(1)}, u32[]{:S(2)}, u32[]{:S(2)}) collective-permute-start(f32[2,16,8,128]{3,2,1,0:T(8,128)S(1)} %get-tuple-element.309.total_ref), channel_id=1, source_target_pairs={{0,2},{1,3},{2,0},{3,1},{4,6},{5,7},{6,4},{7,5},{8,10},{9,11},{10,... | collective-permute-start | bytes 393224 | tf_op jit(solution)/shard_map/ppermute | solution.py:78
  82.3 44.6 %copy-start.8 = (bf16[512,1024]{0,1:T(8,128)(2,1)}, bf16[512,1024]{0,1:T(8,128)(2,1)S(1)}, u32[]{:S(2)}) copy-start(bf16[512,1024]{0,1:T(8,128)(2,1)S(1)} %copy.41) | copy-start | bytes 3145732
  99.6 27.3 %collective-permute-start.15 = (bf16[1024,512]{1,0:T(8,128)(2,1)S(1)}, bf16[1024,512]{1,0:T(8,128)(2,1)S(1)}, u32[]{:S(2)}, u32[]{:S(2)}) collective-permute-start(bf16[1024,512]{1,0:T(8,128)(2,1)S(1)} %bitcast.120), channel_id=1, source_target_pairs={{0,1},{1,0},{2,3},{3,2},{4,5},{5,4},{6,7},{7,6},{8,9},{9,8},{10,11... | collective-permute-start | bytes 3145736 | tf_op jit(solution)/shard_map/ppermute | solution.py:78
  99.6 32.4 %collective-permute-start.16 = (bf16[4,64,2048]{2,1,0:T(8,128)(2,1)}, bf16[4,64,2048]{2,1,0:T(8,128)(2,1)}, u32[]{:S(2)}, u32[]{:S(2)}) collective-permute-start(bf16[4,64,2048]{2,1,0:T(8,128)(2,1)} %collective-permute-done.12), channel_id=1, source_target_pairs={{0,8},{1,17},{2,10},{3,19},{4,12},{5,21},{6,14},{7,23},{8,0},{9,25... | collective-permute-start | bytes 3145736 | tf_op jit(solution)/shard_map/ppermute | solution.py:78
  102.5 20.7 %copy-start.26 = (bf16[512,1024]{1,0:T(8,128)(2,1)S(1)}, bf16[512,1024]{1,0:T(8,128)(2,1)}, u32[]{:S(2)}) copy-start(bf16[512,1024]{1,0:T(8,128)(2,1)} %copy-done.25) | copy-start | bytes 3145732
  103.7 18.1 %collective-permute-start.14 = (f32[2,16,8,128]{3,2,1,0:T(8,128)S(1)}, f32[2,16,8,128]{3,2,1,0:T(8,128)S(1)}, u32[]{:S(2)}, u32[]{:S(2)}) collective-permute-start(f32[2,16,8,128]{3,2,1,0:T(8,128)S(1)} %get-tuple-element.325.total_ref), channel_id=1, source_target_pairs={{0,4},{1,5},{2,6},{3,7},{4,0},{5,1},{6,2},{7,3},{8,12},{9,13},{10,... | collective-permute-start | bytes 393224 | tf_op jit(solution)/shard_map/ppermute | solution.py:78
  106.4 25.6 %copy-start.46 = (f32[16,8,128]{2,1,0:T(8,128)}, f32[16,8,128]{2,1,0:T(8,128)S(1)}, u32[]{:S(2)}) copy-start(f32[16,8,128]{2,1,0:T(8,128)S(1)} %dynamic-slice_bitcast_fusion.initial_ref) | copy-start | bytes 196612
  107.3 19.5 %copy-start.36 = (f32[4,32,128]{2,1,0:T(8,128)}, f32[4,32,128]{2,1,0:T(8,128)S(1)}, u32[]{:S(2)}) copy-start(f32[4,32,128]{2,1,0:T(8,128)S(1)} %get-tuple-element.634) | copy-start | bytes 196612
  137.3 7.7 %collective-permute-start.17 = (bf16[1024,2048]{1,0:T(8,128)(2,1)}, bf16[1024,2048]{1,0:T(8,128)(2,1)}, u32[]{:S(2)}, u32[]{:S(2)}) collective-permute-start(bf16[1024,2048]{1,0:T(8,128)(2,1)} %place.1.w_ref.o_own.w_own), channel_id=1, source_target_pairs={{0,1},{1,0},{2,3},{3,2},{4,5},{5,4},{6,7},{7,6},{8,9},{9,8},{10,11... | collective-permute-start | bytes 12582920 | tf_op jit(solution)/shard_map/ppermute | solution.py:78
  145.0 21.1 %collective-permute-start.18 = (bf16[640,1024]{1,0:T(8,128)(2,1)S(1)}, bf16[640,1024]{1,0:T(8,128)(2,1)}, u32[]{:S(2)}, u32[]{:S(2)}) collective-permute-start(bf16[640,1024]{1,0:T(8,128)(2,1)S(1)} %context_states.1.x_ref.x_own), channel_id=1, source_target_pairs={{0,1},{1,0},{2,3},{3,2},{4,5},{5,4},{6,7},{7,6},{8,9},{9,8},{10,11... | collective-permute-start | bytes 3932168 | tf_op jit(solution)/shard_map/ppermute | solution.py:78
  165.6 3.1 collective-permute-start.20
  166.1 4.1 %collective-permute-start.21 = (bf16[1024,512]{1,0:T(8,128)(2,1)}, bf16[1024,512]{1,0:T(8,128)(2,1)}, u32[]{:S(2)}, u32[]{:S(2)}) collective-permute-start(bf16[1024,512]{1,0:T(8,128)(2,1)} %get-tuple-element.395.st_own), channel_id=1, source_target_pairs={{0,1},{1,0},{2,3},{3,2},{4,5},{5,4},{6,7},{7,6},{8,9},{9,8},{10,11... | collective-permute-start | bytes 3145736 | tf_op jit(solution)/shard_map/ppermute | solution.py:78
  166.3 28.4 %collective-permute-start.19 = (bf16[512,1024]{1,0:T(8,128)(2,1)}, bf16[512,1024]{1,0:T(8,128)(2,1)}, u32[]{:S(2)}, u32[]{:S(2)}) collective-permute-start(bf16[512,1024]{1,0:T(8,128)(2,1)} %copy-done.6), channel_id=1, source_target_pairs={{0,1},{1,0},{2,3},{3,2},{4,5},{5,4},{6,7},{7,6},{8,9},{9,8},{10,11... | collective-permute-start | bytes 3145736 | tf_op jit(solution)/shard_map/ppermute | solution.py:78
  172.7 24.0 %copy-start.21 = (bf16[512,1024]{1,0:T(8,128)(2,1)S(1)}, bf16[512,1024]{1,0:T(8,128)(2,1)}, u32[]{:S(2)}) copy-start(bf16[512,1024]{1,0:T(8,128)(2,1)} %copy-done.19) | copy-start | bytes 3145732
  172.7 24.0 %copy-start.24 = (bf16[1024,512]{1,0:T(8,128)(2,1)S(1)}, bf16[1024,512]{1,0:T(8,128)(2,1)}, u32[]{:S(2)}) copy-start(bf16[1024,512]{1,0:T(8,128)(2,1)} %copy-done.22) | copy-start | bytes 3145732
  194.7 23.5 %collective-permute-start.22 = (bf16[1,4,2,256,256]{4,3,2,1,0:T(8,128)(2,1)S(1)}, bf16[1,4,2,256,256]{4,3,2,1,0:T(8,128)(2,1)S(1)}, u32[]{:S(2)}, u32[]{:S(2)}) collective-permute-start(bf16[1,4,2,256,256]{4,3,2,1,0:T(8,128)(2,1)S(1)} %get-tuple-element.418), channel_id=1, source_target_pairs={{0,8},{1,17},{2,10},{3,19},{4,12},{5,21},{6,14},{7,23},{8,0},{9,25... | collective-permute-start | bytes 3145736 | tf_op jit(solution)/shard_map/ppermute | solution.py:78
  194.8 25.9 %collective-permute-start.23 = (bf16[1,4,2,256,256]{4,3,2,1,0:T(8,128)(2,1)S(1)}, bf16[1,4,2,256,256]{4,3,2,1,0:T(8,128)(2,1)S(1)}, u32[]{:S(2)}, u32[]{:S(2)}) collective-permute-start(bf16[1,4,2,256,256]{4,3,2,1,0:T(8,128)(2,1)S(1)} %get-tuple-element.419), channel_id=1, source_target_pairs={{0,8},{1,17},{2,10},{3,19},{4,12},{5,21},{6,14},{7,23},{8,0},{9,25... | collective-permute-start | bytes 3145736 | tf_op jit(solution)/shard_map/ppermute | solution.py:78
  218.1 5.8 %collective-permute-start.24 = (bf16[512,1024]{1,0:T(8,128)(2,1)S(1)}, bf16[512,1024]{1,0:T(8,128)(2,1)S(1)}, u32[]{:S(2)}, u32[]{:S(2)}) collective-permute-start(bf16[512,1024]{1,0:T(8,128)(2,1)S(1)} %get-tuple-element.426), channel_id=1, source_target_pairs={{0,1},{1,0},{2,3},{3,2},{4,5},{5,4},{6,7},{7,6},{8,9},{9,8},{10,11... | collective-permute-start | bytes 3145736 | tf_op jit(solution)/shard_map/ppermute | solution.py:78
  221.9 24.9 %collective-permute-start.26 = (bf16[1,4,2,256,256]{4,3,2,1,0:T(8,128)(2,1)}, bf16[1,4,2,256,256]{4,3,2,1,0:T(8,128)(2,1)}, u32[]{:S(2)}, u32[]{:S(2)}) collective-permute-start(bf16[1,4,2,256,256]{4,3,2,1,0:T(8,128)(2,1)} %add_split.15), channel_id=1, source_target_pairs={{0,16},{1,9},{2,18},{3,11},{4,20},{5,13},{6,22},{7,15},{8,24},{9,1... | collective-permute-start | bytes 3145736 | tf_op jit(solution)/shard_map/ppermute | solution.py:78
  223.7 23.1 %collective-permute-start.27 = (bf16[1,4,2,256,256]{4,3,2,1,0:T(8,128)(2,1)}, bf16[1,4,2,256,256]{4,3,2,1,0:T(8,128)(2,1)}, u32[]{:S(2)}, u32[]{:S(2)}) collective-permute-start(bf16[1,4,2,256,256]{4,3,2,1,0:T(8,128)(2,1)} %get-tuple-element.454), channel_id=1, source_target_pairs={{0,8},{1,17},{2,10},{3,19},{4,12},{5,21},{6,14},{7,23},{8,0},{9,25... | collective-permute-start | bytes 3145736 | tf_op jit(solution)/shard_map/ppermute | solution.py:78
  229.4 14.3 %collective-permute-start.25 = (bf16[512,512]{1,0:T(8,128)(2,1)}, bf16[512,512]{1,0:T(8,128)(2,1)}, u32[]{:S(2)}, u32[]{:S(2)}) collective-permute-start(bf16[512,512]{1,0:T(8,128)(2,1)} %get-tuple-element.435), channel_id=1, source_target_pairs={{0,1},{1,0},{2,3},{3,2},{4,5},{5,4},{6,7},{7,6},{8,9},{9,8},{10,11... | collective-permute-start | bytes 1572872 | tf_op jit(solution)/shard_map/ppermute | solution.py:78
  246.9 22.1 %collective-permute-start.30 = (bf16[640,1536]{1,0:T(8,128)(2,1)}, bf16[640,1536]{1,0:T(8,128)(2,1)S(1)}, u32[]{:S(2)}, u32[]{:S(2)}) collective-permute-start(bf16[640,1536]{1,0:T(8,128)(2,1)} %copy-done.16), channel_id=1, source_target_pairs={{0,1},{1,0},{2,3},{3,2},{4,5},{5,4},{6,7},{7,6},{8,9},{9,8},{10,11... | collective-permute-start | bytes 5898248 | tf_op jit(solution)/shard_map/ppermute | solution.py:78
  246.9 22.1 %collective-permute-start.32 = (bf16[1,4,2,256,256]{4,3,2,1,0:T(8,128)(2,1)}, bf16[1,4,2,256,256]{4,3,2,1,0:T(8,128)(2,1)S(1)}, u32[]{:S(2)}, u32[]{:S(2)}) collective-permute-start(bf16[1,4,2,256,256]{4,3,2,1,0:T(8,128)(2,1)} %copy-done.72), channel_id=1, source_target_pairs={{0,8},{1,17},{2,10},{3,19},{4,12},{5,21},{6,14},{7,23},{8,0},{9,25... | collective-permute-start | bytes 3145736 | tf_op jit(solution)/shard_map/ppermute | solution.py:78
  256.5 6.4 %collective-permute-start.28 = (f32[16,8,128]{2,1,0:T(8,128)S(1)}, f32[16,8,128]{2,1,0:T(8,128)S(1)}, u32[]{:S(2)}, u32[]{:S(2)}) collective-permute-start(f32[16,8,128]{2,1,0:T(8,128)S(1)} %slice_bitcast_fusion.10.total_ref), channel_id=1, source_target_pairs={{0,1},{1,0},{2,3},{3,2},{4,5},{5,4},{6,7},{7,6},{8,9},{9,8},{10,11... | collective-permute-start | bytes 196616 | tf_op jit(solution)/shard_map/ppermute | solution.py:78
  262.5 6.4 %collective-permute-start.31 = (bf16[4,4,64,128]{3,2,1,0:T(8,128)(2,1)S(1)}, bf16[4,4,64,128]{3,2,1,0:T(8,128)(2,1)S(1)}, u32[]{:S(2)}, u32[]{:S(2)}) collective-permute-start(bf16[4,4,64,128]{3,2,1,0:T(8,128)(2,1)S(1)} %fusion), channel_id=1, source_target_pairs={{0,1},{1,0},{2,3},{3,2},{4,5},{5,4},{6,7},{7,6},{8,9},{9,8},{10,11... | collective-permute-start | bytes 786440 | tf_op jit(solution)/shard_map/ppermute | solution.py:78
  263.7 4.6 %collective-permute-start.29 = (f32[16,8,128]{2,1,0:T(8,128)S(1)}, f32[16,8,128]{2,1,0:T(8,128)S(1)}, u32[]{:S(2)}, u32[]{:S(2)}) collective-permute-start(f32[16,8,128]{2,1,0:T(8,128)S(1)} %get-tuple-element.461.total_ref), channel_id=1, source_target_pairs={{0,2},{1,3},{2,0},{3,1},{4,6},{5,7},{6,4},{7,5},{8,10},{9,11},{10,... | collective-permute-start | bytes 196616 | tf_op jit(solution)/shard_map/ppermute | solution.py:78
  269.0 14.9 %copy-start.70 = (f32[3]{0:T(128)S(1)}, f32[3]{0:T(128)}, u32[]{:S(2)}) copy-start(f32[3]{0:T(128)} %get-tuple-element.484.scal) | copy-start | bytes 40
  269.0 17.0 %copy-start.39 = (bf16[1,4,2,256,256]{4,3,2,1,0:T(8,128)(2,1)S(1)}, bf16[1,4,2,256,256]{4,3,2,1,0:T(8,128)(2,1)}, u32[]{:S(2)}) copy-start(bf16[1,4,2,256,256]{4,3,2,1,0:T(8,128)(2,1)} %copy-done.38) | copy-start | bytes 3145732
  269.0 16.5 %collective-permute-start.35 = (bf16[1,4,2,256,256]{4,3,2,1,0:T(8,128)(2,1)S(1)}, bf16[1,4,2,256,256]{4,3,2,1,0:T(8,128)(2,1)S(1)}, u32[]{:S(2)}, u32[]{:S(2)}) collective-permute-start(bf16[1,4,2,256,256]{4,3,2,1,0:T(8,128)(2,1)S(1)} %add_split.19), channel_id=1, source_target_pairs={{0,16},{1,9},{2,18},{3,11},{4,20},{5,13},{6,22},{7,15},{8,24},{9,1... | collective-permute-start | bytes 3145736 | tf_op jit(solution)/shard_map/ppermute | solution.py:78
  270.7 14.8 %collective-permute-start.34 = (bf16[1,2,2,256,256]{4,3,2,1,0:T(8,128)(2,1)S(1)}, bf16[1,2,2,256,256]{4,3,2,1,0:T(8,128)(2,1)S(1)}, u32[]{:S(2)}, u32[]{:S(2)}) collective-permute-start(bf16[1,2,2,256,256]{4,3,2,1,0:T(8,128)(2,1)S(1)} %get-tuple-element.505), channel_id=1, source_target_pairs={{0,2},{1,3},{2,0},{3,1},{4,6},{5,7},{6,4},{7,5},{8,10},{9,11},{10,... | collective-permute-start | bytes 1572872 | tf_op jit(solution)/shard_map/ppermute | solution.py:78
  271.8 12.2 %collective-permute-start.33 = (f32[16,8,128]{2,1,0:T(8,128)S(1)}, f32[16,8,128]{2,1,0:T(8,128)S(1)}, u32[]{:S(2)}, u32[]{:S(2)}) collective-permute-start(f32[16,8,128]{2,1,0:T(8,128)S(1)} %get-tuple-element.485.total_ref), channel_id=1, source_target_pairs={{0,4},{1,5},{2,6},{3,7},{4,0},{5,1},{6,2},{7,3},{8,12},{9,13},{10,... | collective-permute-start | bytes 196616 | tf_op jit(solution)/shard_map/ppermute | solution.py:78
  285.5 27.8 %collective-permute-start.37 = (bf16[2,4,64,2176]{3,2,1,0:T(8,128)(2,1)}, bf16[2,4,64,2176]{3,2,1,0:T(8,128)(2,1)}, u32[]{:S(2)}, u32[]{:S(2)}) collective-permute-start(bf16[2,4,64,2176]{3,2,1,0:T(8,128)(2,1)} %get-tuple-element.530), channel_id=1, source_target_pairs={{0,8},{1,17},{2,10},{3,19},{4,12},{5,21},{6,14},{7,23},{8,0},{9,25... | collective-permute-start | bytes 6684680 | tf_op jit(solution)/shard_map/ppermute | solution.py:78
  286.3 13.5 %copy-start.18 = (bf16[640,1536]{1,0:T(8,128)(2,1)S(1)}, bf16[640,1536]{1,0:T(8,128)(2,1)}, u32[]{:S(2)}) copy-start(bf16[640,1536]{1,0:T(8,128)(2,1)} %copy-done.16) | copy-start | bytes 5898244
  287.3 24.3 %collective-permute-start.39 = (bf16[1,2,2,256,256]{4,3,2,1,0:T(8,128)(2,1)}, bf16[1,2,2,256,256]{4,3,2,1,0:T(8,128)(2,1)}, u32[]{:S(2)}, u32[]{:S(2)}) collective-permute-start(bf16[1,2,2,256,256]{4,3,2,1,0:T(8,128)(2,1)} %get-tuple-element.529), channel_id=1, source_target_pairs={{0,2},{1,3},{2,0},{3,1},{4,6},{5,7},{6,4},{7,5},{8,10},{9,11},{10,... | collective-permute-start | bytes 1572872 | tf_op jit(solution)/shard_map/ppermute | solution.py:78
  293.1 13.2 %collective-permute-start.36 = (bf16[128,1024]{1,0:T(8,128)(2,1)S(1)}, bf16[128,1024]{1,0:T(8,128)(2,1)S(1)}, u32[]{:S(2)}, u32[]{:S(2)}) collective-permute-start(bf16[128,1024]{1,0:T(8,128)(2,1)S(1)} %sent_tail.1), channel_id=1, source_target_pairs={{1,0},{2,1},{3,2},{4,3},{5,4},{6,5},{7,6},{9,8},{10,9},{11,10},{12... | collective-permute-start | bytes 786440 | tf_op jit(solution)/shard_map/ppermute | solution.py:78
  295.8 15.8 %collective-permute-start.38 = (bf16[1,1,2,256,256]{4,3,2,1,0:T(8,128)(2,1)}, bf16[1,1,2,256,256]{4,3,2,1,0:T(8,128)(2,1)}, u32[]{:S(2)}, u32[]{:S(2)}) collective-permute-start(bf16[1,1,2,256,256]{4,3,2,1,0:T(8,128)(2,1)} %get-tuple-element.525), channel_id=1, source_target_pairs={{0,4},{1,5},{2,6},{3,7},{4,0},{5,1},{6,2},{7,3},{8,12},{9,13},{10,... | collective-permute-start | bytes 786440 | tf_op jit(solution)/shard_map/ppermute | solution.py:78
  316.2 20.9 %collective-permute-start.41 = (bf16[1,4,64,2176]{3,2,1,0:T(8,128)(2,1)}, bf16[1,4,64,2176]{3,2,1,0:T(8,128)(2,1)}, u32[]{:S(2)}, u32[]{:S(2)}) collective-permute-start(bf16[1,4,64,2176]{3,2,1,0:T(8,128)(2,1)} %get-tuple-element.539), channel_id=1, source_target_pairs={{0,16},{1,9},{2,18},{3,11},{4,20},{5,13},{6,22},{7,15},{8,24},{9,1... | collective-permute-start | bytes 3342344 | tf_op jit(solution)/shard_map/ppermute | solution.py:78
  316.7 20.4 %collective-permute-start.40 = (bf16[512,1024]{1,0:T(8,128)(2,1)}, bf16[512,1024]{1,0:T(8,128)(2,1)}, u32[]{:S(2)}, u32[]{:S(2)}) collective-permute-start(bf16[512,1024]{1,0:T(8,128)(2,1)} %get-tuple-element.533), channel_id=1, source_target_pairs={{0,1},{1,0},{2,3},{3,2},{4,5},{5,4},{6,7},{7,6},{8,9},{9,8},{10,11... | collective-permute-start | bytes 3145736 | tf_op jit(solution)/shard_map/ppermute | solution.py:78
  316.9 24.4 %copy-start.15 = (f32[512,1024]{1,0:T(8,128)S(1)}, f32[512,1024]{1,0:T(8,128)}, u32[]{:S(2)}) copy-start(f32[512,1024]{1,0:T(8,128)} %copy-done.13) | copy-start | bytes 6291460
  319.6 17.6 %collective-permute-start.42 = (bf16[1,1,2,256,256]{4,3,2,1,0:T(8,128)(2,1)}, bf16[1,1,2,256,256]{4,3,2,1,0:T(8,128)(2,1)}, u32[]{:S(2)}, u32[]{:S(2)}) collective-permute-start(bf16[1,1,2,256,256]{4,3,2,1,0:T(8,128)(2,1)} %get-tuple-element.536), channel_id=1, source_target_pairs={{0,4},{1,5},{2,6},{3,7},{4,0},{5,1},{6,2},{7,3},{8,12},{9,13},{10,... | collective-permute-start | bytes 786440 | tf_op jit(solution)/shard_map/ppermute | solution.py:78
  338.8 14.5 %collective-permute-start.43 = (bf16[1,2,64,2176]{3,2,1,0:T(8,128)(2,1)S(1)}, bf16[1,2,64,2176]{3,2,1,0:T(8,128)(2,1)S(1)}, u32[]{:S(2)}, u32[]{:S(2)}) collective-permute-start(bf16[1,2,64,2176]{3,2,1,0:T(8,128)(2,1)S(1)} %get-tuple-element.550), channel_id=1, source_target_pairs={{0,2},{1,3},{2,0},{3,1},{4,6},{5,7},{6,4},{7,5},{8,10},{9,11},{10,... | collective-permute-start | bytes 1671176 | tf_op jit(solution)/shard_map/ppermute | solution.py:78
  353.4 14.5 %collective-permute-start.44 = (bf16[1,1,64,2176]{3,2,1,0:T(8,128)(2,1)S(1)}, bf16[1,1,64,2176]{3,2,1,0:T(8,128)(2,1)S(1)}, u32[]{:S(2)}, u32[]{:S(2)}) collective-permute-start(bf16[1,1,64,2176]{3,2,1,0:T(8,128)(2,1)S(1)} %get-tuple-element.557), channel_id=1, source_target_pairs={{0,4},{1,5},{2,6},{3,7},{4,0},{5,1},{6,2},{7,3},{8,12},{9,13},{10,... | collective-permute-start | bytes 835592 | tf_op jit(solution)/shard_map/ppermute | solution.py:78
  368.6 1.6 collective-permute-start.45
  (60 other events, 306.3 us)
Sparse Core Ops, SparseCore 0:
  22.6 143.6 all-gather.1

commit v4 on v3

--- a/solution.py
+++ b/solution.py
@@ -527,13 +527,15 @@
 
 def feed_kernel(
     ndp, nz, width, index, groups, earlier, last, info, s_own, s_par, c_own, c_par,
-    st_own, st_par, ct_own, ct_par, weights, *rest
+    st_own, st_par, ct_own, ct_par, *rest
 ):
     rows = s_own.shape[0]
     block = D // ndp
     group = nz * width
     half = ndp // 2
     s, c = (s_own, s_par), (c_own, c_par)
+    count = ndp if index else 1
+    weights, rest = rest[:count], rest[count:]
     if earlier:
         m_in, g_in, *rest = rest
     if last:
@@ -550,8 +552,12 @@
         copy.start()
         copies.append(copy)
 
-    at_core = pl.multiple_of((info[ndp + 1] * groups + index) * 2 * group, 128)
-    start(weights.at[:, pl.ds(at_core, 2 * group)], w)
+    if index:
+        for p in range(ndp):
+            start(weights[p], w.at[pl.ds(at[p], block), :])
+    else:
+        at_core = pl.multiple_of(info[ndp + 1] * 2 * group, 128)
+        start(weights[0].at[:, pl.ds(at_core, 2 * group)], w)
     for own, par, dst in ((st_own, st_par, st), (ct_own, ct_par, ct)):
         for p in range(ndp):
             for i, src in enumerate((own, par)):
@@ -559,7 +565,8 @@
                     src.at[pl.ds(at[p], block), :],
                     dst.at[p * block : (p + 1) * block, i * rows : (i + 1) * rows],
                 )
-    copies[0].wait()
+    for copy in copies[:count]:
+        copy.wait()
 
     @pl.loop(0, nz)
     def _(b):
@@ -573,7 +580,7 @@
             act[part, up] = active.astype(bf16)
             gh[part, up] = (grad * slope).astype(bf16)
 
-    for copy in copies[1:]:
+    for copy in copies[count:]:
         copy.wait()
 
     @pl.loop(0, nz)
@@ -626,7 +633,7 @@
     return pl.pallas_call(
         functools.partial(feed_kernel, ndp, nz, width, index, groups, bool(earlier), last),
         out_shape=out_shape,
-        in_specs=[SMEM] + [VMEM] * len(acts) + [ANY] + [VMEM] * len(earlier),
+        in_specs=[SMEM] + [VMEM] * len(acts) + [ANY] * len(weights) + [VMEM] * len(earlier),
         out_specs=(VMEM,) * len(out_shape),
         scratch_shapes=[
             pltpu.VMEM((D, tokens), bf16),
@@ -634,12 +641,12 @@
             pltpu.VMEM((D, 2 * group), bf16),
             pltpu.VMEM((tokens, group), bf16),
             pltpu.VMEM((tokens, group), bf16),
-            pltpu.SemaphoreType.DMA((4 * ndp + 1,)),
+            pltpu.SemaphoreType.DMA((5 * ndp,)),
         ],
-        compiler_params=params(22),
+        compiler_params=params(30),
         cost_estimate=COST,
         name="feed_last" if last else "feed_first",
-    )(info, *map(in_vmem, acts), in_hbm(weights), *map(in_vmem, earlier))
+    )(info, *map(in_vmem, acts), *map(in_hbm, weights), *map(in_vmem, earlier))
 
 
 def norm_parts(values):
@@ -759,7 +766,7 @@
         in_specs=[SMEM] + [VMEM] * 5 + [OUT_COLS] * 2,
         out_specs=(VMEM,) * 5,
         scratch_shapes=[pltpu.VMEM((rows, D), bf16)],
-        compiler_params=params(22),
+        compiler_params=params(30),
         cost_estimate=COST,
         name="back_middle",
     )(info, middle, own, received, cotangent, gain, in_hbm(o_own), in_hbm(o_other))
@@ -903,7 +910,9 @@
     )(info, owner, sums, gain)
 
 
-def prepare_kernel(nz, groups, core, q_ref, k_ref, v_ref, o_ref, up_ref, down_ref, keep, send, feed):
+def prepare_kernel(
+    nz, groups, core, q_ref, k_ref, v_ref, o_ref, up_ref, down_ref, keep, send, feed, *late
+):
     for i, ref in enumerate((q_ref, k_ref, v_ref, o_ref)):
         to = slice(i * HALF, (i + 1) * HALF)
         keep[:, to] = ref[:, pl.ds(pl.multiple_of(core[0] * HALF, HALF), HALF)].astype(bf16)
@@ -911,22 +920,30 @@
     width = FF // (2 * nz * groups)
     at = 0
     for c in range(2):
-        for g in range(groups):
-            for ref in (up_ref, down_ref):
-                for b in range(nz):
-                    first = ((b * 2 + c) * groups + g) * width
-                    feed[:, at : at + width] = ref[:, first : first + width].astype(bf16)
-                    at += width
+        for ref in (up_ref, down_ref):
+            for b in range(nz):
+                first = (b * 2 + c) * groups * width
+                feed[:, at : at + width] = ref[:, first : first + width].astype(bf16)
+                at += width
+    for i, out in enumerate(late):
+        at = 0
+        for ref in (up_ref, down_ref):
+            for b in range(nz):
+                first = ((b * 2 + (core[0] ^ i)) * groups + 1) * width
+                span = pl.ds(pl.multiple_of(first, width), width)
+                out[:, at : at + width] = ref[:, span].astype(bf16)
+                at += width
 
 
 def prepare(links, groups, core, mats, up, down):
     rows = up.shape[0]
     part = jax.ShapeDtypeStruct((rows, 4 * HALF), bf16)
+    late = (jax.ShapeDtypeStruct((rows, FF // 2), bf16),) * 2 if groups > 1 else ()
     return pl.pallas_call(
         functools.partial(prepare_kernel, links.nz, groups),
-        out_shape=(part, part, jax.ShapeDtypeStruct((rows, 2 * FF), bf16)),
+        out_shape=(part, part, jax.ShapeDtypeStruct((rows, 2 * FF // groups), bf16), *late),
         in_specs=[SMEM] + [VMEM] * 6,
-        out_specs=(VMEM,) * 3,
+        out_specs=(VMEM,) * (3 + len(late)),
         compiler_params=params(5),
         cost_estimate=COST,
         name="prepare",
@@ -1266,7 +1283,7 @@
     chunk = FF // nmp
     groups = 2 if chunk >= 256 else 1
     width = chunk // groups
-    mats_keep, mats_send, feed_rows = prepare(
+    mats_keep, mats_send, feed_rows, *late_rows = prepare(
         links, groups, links.core.astype(jnp.int32).reshape(1),
         (w_query, w_key, w_value, w_out), w_up, w_down.T,
     )
@@ -1285,7 +1302,8 @@
     v.small = join_small(links, small, links.core_swap(small), links.mp, 0)
     attn = Gather(links, chip_rows(mats_keep, mats_send))
     v.feed_rows = feed_rows
-    fence(v, [attn])
+    late_feeds = [Gather(links, chip_rows(*late_rows))] if late_rows else []
+    fence(v, [attn, *late_feeds])
 
     for bit in range(1, links.mp_bits):
         v.small = join_small(links, v.small, links.mp_swap(v.small, bit), links.mp, bit)
@@ -1341,55 +1359,67 @@
     for bit in range(2):
         exchange(bit)
     v.cot_t = v.cotangent.T
-    v.cot_par = links.core_swap(v.cotangent)
-    fence(v, [attn], [attn])
+    fence(v, [attn, *late_feeds], [attn])
     attn.last_dp(max(ndp // 4, 1), None)
     for bit in range(2, bits_of(per_window)):
         exchange(bit)
     v.inputs_kv = context_states(
         v.scal, u.tail, u.normed_b, v.before, u.initial, u.rate, u.gain_in, u.gain_out
     )
-    v.cot_par_t = links.core_swap(v.cot_t)
-    fence(v, [attn], [attn])
-
+    fence(v, [attn, *late_feeds], [attn])
+
+    for gather in late_feeds:
+        gather.first_z()
     v.w_own = place(links, order, attn.blocks())
     attn.state = []
     v.w_other = links.core_swap(v.w_own)
     v.qkv_own = project(v.inputs_kv, v.w_own)
-    fence(v)
+    u.cot_par, u.cot_par_t = links.core_swap(v.cotangent), links.core_swap(v.cot_t)
+    fence(v, late_feeds, late_feeds)
+    for gather in late_feeds:
+        gather.along_z(1)
     v.inputs_par = links.core_swap(v.inputs_kv)
     u.qkv_other = project(v.inputs_kv, v.w_other)
     v.attended = attend(attend_info, v.qkv_own, u.qkv_other)
+    fence(v, late_feeds, late_feeds)
+    for gather in late_feeds:
+        gather.first_dp()
     u.middle, u.second_b, u.second_t = middle_norm(
         attend_info, v.attended, v.tokens, v.w_own, v.w_other, v.gain_two
     )
     u.second_par, u.second_par_t = links.core_swap(u.second_b), links.core_swap(u.second_t)
     v.feed_weights = feed_weights
-    fence(v)
+    fence(v, late_feeds, late_feeds)
 
     scatters = []
     earlier = None
     for g in range(groups):
         last = g == groups - 1
         acts = (
-            u.second_b, u.second_par, v.cotangent, v.cot_par,
-            u.second_t, u.second_par_t, v.cot_t, v.cot_par_t,
+            u.second_b, u.second_par, v.cotangent, u.cot_par,
+            u.second_t, u.second_par_t, v.cot_t, u.cot_par_t,
         )
+        if g == 0:
+            weights = [v.feed_weights]
+            for gather in late_feeds:
+                gather.last_dp(0, None)
+        else:
+            weights = late_feeds[0].blocks()
         *u.sums, keep, keep_far, send, send_far = feed(
-            links, info, acts, v.feed_weights, nz * width, g, groups, earlier, last
+            links, info, acts, weights, nz * width, g, groups, earlier, last
         )
         if g == 0:
             v.attended_par = links.core_swap(v.attended)
         waits = list(scatters)
         scatters.append(Scatter(links, keep, send, keep_far, send_far))
-        fence(v, scatters, waits)
+        fence(v, scatters, waits + (late_feeds if not last else []))
         if not last:
             scatters[g].start()
         earlier = u.sums
     first, second = scatters[0], scatters[-1]
     both = [first, second] if groups > 1 else [first]
     u.mix_own, v.mix_par, u.back_own, back_par = u.sums
-    del v.feed_weights, v.cot_t, v.cot_par, v.cot_par_t
+    del v.feed_weights, v.cot_t
 
     split = groups > 1 and ndp >= 4
     if split:

time: 383 us -> 380 us (level)
  waiting for transfers between devices: 89.9 us -> 84.2 us
    ppermute x46 -> x52, waiting for transfers between devices: 89.7 us -> 84.2 us  [send(): return lax.ppermute(values, AXES, pairs)]
    ppermute x46 -> x52, starting transfers between devices: 60.4 us -> 64.3 us  [send(): return lax.ppermute(values, AXES, pairs)]
    unnamed x155 -> x145, local copies, waits for them, and re-layouts: 21.9 us -> 18.9 us
  transfers between devices with their start and end apart: 47 -> 53, of which waited for: 26 -> 26; matrix products, arithmetic and copies ran while one was open for 4% -> 4% of each run, Pallas kernels for 40% -> 41%
where the time goes in v4:
time: 380 us; the launch traced here: 376 us
  Pallas kernels  161 us (42%)
  waiting for transfers between devices  84.2 us (22%)
  starting transfers between devices  64.3 us (17%)
  local copies, waits for them, and re-layouts  28.2 us (7%)
  between operations  17.3 us (5%)
  blocking collectives  14 us (4%)
  other arithmetic  6.82 us (2%)
    ppermute x52, waiting for transfers between devices, send(): return lax.ppermute(values, AXES, pairs)  84.2 us
    ppermute x52, starting transfers between devices, send(): return lax.ppermute(values, AXES, pairs)  64.3 us
    pallas_call x2, Pallas kernels, feed(): pl.pallas_call(functools.partial(feed_kernel, ndp, nz, width, index, grou...  45.1 us
    unnamed x145, local copies, waits for them, and re-layouts  18.9 us
    pallas_call x15, Pallas kernels, add_split(): pl.pallas_call(functools.partial(add_kernel, axis or 0), out_shape=outs,...  15.3 us
    all_to_all x1, blocking collectives, body(): lax.all_to_all(v.gain_parts, AXES, split_axis=0, concat_axis=0, tiled=True)  14 us
    pallas_call x1, Pallas kernels, attend_back(): pl.pallas_call(attend_back_kernel, out_shape=(out, out), in_specs=[SMEM]...  11.8 us
    pallas_call x2, Pallas kernels, back_project(): pl.pallas_call(functools.partial(back_project_kernel, first), out_shape=j...  11.4 us
  transfers between devices with their start and end apart: 53, of which 26 were waited for; matrix products, arithmetic and copies ran while one was open for 4% of the time, Pallas kernels for 41%

profile of v4, /device:TPU:0, one launch (start us, length us, event | category | flops | bytes accessed | tf_op | source)
XLA Modules:
  0.0 375.8 jit_solution(3505792503469295463)
XLA Ops:
  7.2 2.2 prepare.1
  13.1 2.9 collective-permute-start.3
  16.0 1.9 collective-permute-done.3.there_ref
  17.9 3.0 collective-permute-start.4
  21.0 2.3 collective-permute-done.4.there_ref
  23.4 1.8 collective-permute-start.5
  25.2 2.6 collective-permute-start.7
  28.4 1.8 collective-permute-start.6
  31.5 3.3 collective-permute-done.6.there_ref
  34.9 2.7 collective-permute-done.7.there_ref
  37.8 2.6 collective-permute-start.8
  41.2 1.8 fusion.1
  43.0 4.5 %scan_own.1.own_ref = f32[2,16,8,128]{3,2,1,0:T(8,128)S(1)} custom-call(bf16[512,1024]{1,0:T(8,128)(2,1)S(1)} %get-tuple-element.323.x_ref.own_ref, f32[16,8,128]{2,1,0:T(8,128)S(1)} %bitcast.113), custom_call_target="tpu_custom_call" | custom-call | flops 1 | bytes 1 | tf_op jit(solution)/shard_map/scan_own/pallas_call | solution.py:170
  48.2 7.3 %collective-permute-done.8.there_ref = bf16[2,64,2048]{2,1,0:T(8,128)(2,1)S(1)} collective-permute-done((bf16[2,64,2048]{2,1,0:T(8,128)(2,1)S(1)}, bf16[2,64,2048]{2,1,0:T(8,128)(2,1)S(1)}, u32[]{:S(2)}, u32[]{:S(2)}) %collective-permute-start.8) | collective-permute-done | bytes 524320 | tf_op jit(solution)/shard_map/ppermute | solution.py:78
  60.0 1.5 collective-permute-start.9
  62.5 1.6 scan_tail.1.total_ref
  64.8 7.5 %collective-permute-start.10 = (f32[2,16,8,128]{3,2,1,0:T(8,128)S(1)}, f32[2,16,8,128]{3,2,1,0:T(8,128)S(1)}, u32[]{:S(2)}, u32[]{:S(2)}) collective-permute-start(f32[2,16,8,128]{3,2,1,0:T(8,128)S(1)} %scan_tail.1.total_ref), channel_id=1, source_target_pairs={{0,1},{1,0},{2,3},{3,2},{4,5},{5,4},{6,7},{7,6},{8,9},{9,8},{10,11... | collective-permute-start | bytes 393224 | tf_op jit(solution)/shard_map/ppermute | solution.py:78
  74.6 2.7 collective-permute-start.11
  78.7 8.3 %collective-permute-done.11.recv_ref = f32[2,16,8,128]{3,2,1,0:T(8,128)} collective-permute-done((f32[2,16,8,128]{3,2,1,0:T(8,128)S(1)}, f32[2,16,8,128]{3,2,1,0:T(8,128)}, u32[]{:S(2)}, u32[]{:S(2)}) %collective-permute-start.11) | collective-permute-done | bytes 131104 | tf_op jit(solution)/shard_map/ppermute | solution.py:78
  88.0 4.1 %collective-permute-done.13 = bf16[4,64,2048]{2,1,0:T(8,128)(2,1)} collective-permute-done((bf16[4,64,2048]{2,1,0:T(8,128)(2,1)S(1)}, bf16[4,64,2048]{2,1,0:T(8,128)(2,1)}, u32[]{:S(2)}, u32[]{:S(2)}) %collective-permute-start.13) | collective-permute-done | bytes 1048608 | tf_op jit(solution)/shard_map/ppermute | solution.py:78
  96.2 2.7 collective-permute-start.14
  99.8 6.6 %collective-permute-done.14.recv_ref = f32[2,16,8,128]{3,2,1,0:T(8,128)S(1)} collective-permute-done((f32[2,16,8,128]{3,2,1,0:T(8,128)S(1)}, f32[2,16,8,128]{3,2,1,0:T(8,128)S(1)}, u32[]{:S(2)}, u32[]{:S(2)}) %collective-permute-start.14) | collective-permute-done | bytes 131104 | tf_op jit(solution)/shard_map/ppermute | solution.py:78
  108.7 2.7 context_states.1.x_ref.x_own
  111.8 5.0 %place.1.w_ref.o_own.w_own = bf16[1024,2048]{1,0:T(8,128)(2,1)} custom-call(s32[4]{0:T(128)S(1)} %pad_add_fusion.1.order, bf16[256,2048]{1,0:T(8,128)(2,1)S(1)} %bitcast.129, bf16[256,2048]{1,0:T(8,128)(2,1)} %bitcast.44.refs_1_, bf16[256,2048]{1,0:T(8,128)(2,1)} %bitcast.45.refs_2_, bf16[256,2048]{1,0:T(8,128)(2,1)} %bitcast.46.refs_3_), custom_call_target="tpu_custom_call" | custom-call | flops 1 | bytes 1 | tf_op jit(solution)/shard_map/place/pallas_call | solution.py:966
  116.8 2.3 collective-permute-start.17
  119.1 4.1 %project.2.own_ref = bf16[640,1536]{1,0:T(8,128)(2,1)S(1)} custom-call(bf16[640,1024]{1,0:T(8,128)(2,1)S(1)} %context_states.1.x_ref.x_own, bf16[1024,2048]{1,0:T(8,128)(2,1)} %place.1.w_ref.o_own.w_own), custom_call_target="tpu_custom_call" | custom-call | flops 1 | bytes 1 | tf_op jit(solution)/shard_map/project/pallas_call | solution.py:782
  123.2 8.8 %collective-permute-done.17.there_ref = bf16[1,64,2048]{2,1,0:T(8,128)(2,1)S(1)} collective-permute-done((bf16[1,64,2048]{2,1,0:T(8,128)(2,1)S(1)}, bf16[1,64,2048]{2,1,0:T(8,128)(2,1)S(1)}, u32[]{:S(2)}, u32[]{:S(2)}) %collective-permute-start.17) | collective-permute-done | bytes 262176 | tf_op jit(solution)/shard_map/ppermute | solution.py:78
  134.7 4.1 %project.3.other_ref = bf16[640,1536]{1,0:T(8,128)(2,1)S(1)} custom-call(bf16[640,1024]{1,0:T(8,128)(2,1)S(1)} %context_states.1.x_ref.x_own, bf16[1024,2048]{1,0:T(8,128)(2,1)} %copy-done.69), custom_call_target="tpu_custom_call" | custom-call | flops 1 | bytes 1 | tf_op jit(solution)/shard_map/project/pallas_call | solution.py:782
  138.8 8.0 %attend.1.att_ref.a_own = bf16[512,1024]{1,0:T(8,128)(2,1)S(1)} custom-call(s32[2]{0:T(128)S(1)} %pad_add_fusion.info, bf16[640,1536]{1,0:T(8,128)(2,1)S(1)} %project.2.own_ref, bf16[640,1536]{1,0:T(8,128)(2,1)S(1)} %project.3.other_ref), custom_call_target="tpu_custom_call" | custom-call | flops 1 | bytes 1 | tf_op jit(solution)/shard_map/attend/pallas_call | solution.py:459
  151.3 4.8 %middle_norm.1 = (f32[512,1024]{1,0:T(8,128)S(1)}, bf16[512,1024]{1,0:T(8,128)(2,1)}, bf16[1024,512]{1,0:T(8,128)(2,1)}) custom-call(s32[2]{0:T(128)S(1)} %pad_add_fusion.info, bf16[512,1024]{1,0:T(8,128)(2,1)S(1)} %attend.1.att_ref.a_own, bf16[512,1024]{1,0:T(8,128)(2,1)S(1)} %copy-done.10, bf16[1024,2048]{1,0:T(8,128)(2,1)} %place.1.w_ref.o_own.w_own, ...), custom_call_target="tpu_custom_call" | custom-call | flops 1 | bytes 1 | tf_op jit(solution)/shard_map/middle_norm/pallas_call | solution.py:717
  157.9 6.3 %collective-permute-done.20 = bf16[4,64,2048]{2,1,0:T(8,128)(2,1)} collective-permute-done((bf16[4,64,2048]{2,1,0:T(8,128)(2,1)S(1)}, bf16[4,64,2048]{2,1,0:T(8,128)(2,1)}, u32[]{:S(2)}, u32[]{:S(2)}) %collective-permute-start.20) | collective-permute-done | bytes 1048608 | tf_op jit(solution)/shard_map/ppermute | solution.py:78
  164.3 2.9 collective-permute-start.26
  167.4 21.3 %feed_first.1 = (f32[1024,1024]{1,0:T(8,128)S(1)}, f32[1024,1024]{1,0:T(8,128)S(1)}, bf16[1,4,2,256,256]{4,3,2,1,0:T(8,128)(2,1)S(1)}, bf16[1,4,2,256,256]{4,3,2...) custom-call(s32[6]{0:T(128)S(1)} %stack.127.info, ...), custom_call_target="tpu_custom_call" | custom-call | flops 1 | bytes 1 | tf_op jit(solution)/shard_map/feed_first/pallas_call | solution.py:633
  189.6 1.9 collective-permute-done.27
  191.5 2.0 collective-permute-start.28
  193.6 23.8 %feed_last.1 = (f32[512,1024]{1,0:T(8,128)}, bf16[512,1024]{1,0:T(8,128)(2,1)}, f32[512,1024]{1,0:T(8,128)}, bf16[512,1024]{1,0:T(8,128)(2,1)S(1)}, bf16[1,4,2,2...) custom-call(s32[6]{0:T(128)S(1)} %stack.127.info, ...), custom_call_target="tpu_custom_call" | custom-call | flops 1 | bytes 1 | tf_op jit(solution)/shard_map/feed_last/pallas_call | solution.py:633
  220.8 1.6 copy-done.25
  222.4 4.6 %back_middle.1 = (f32[512,1024]{1,0:T(8,128)S(1)}, bf16[512,512]{1,0:T(8,128)(2,1)S(1)}, bf16[512,512]{1,0:T(8,128)(2,1)}, bf16[512,1024]{1,0:T(8,128)(2,1)S(1)}, f32[1,1024]{1,0:T(1,128)S(1)}) custom-call(s32[2]{0:T(128)S(1)} %pad_add_fusion.info, f32[512,1024]{1,0:T(8,128)S(1)} %copy-done.13, f32[512,1024]{1,0:T(8,128)S(1)} %copy-done.25, ...), custom_call_target="tpu_custom_call" | custom-call | flops 1 | bytes 1 | tf_op jit(solution)/shard_map/back_middle/pallas_call | solution.py:756
  227.3 11.8 %attend_back.1 = (bf16[640,1536]{1,0:T(8,128)(2,1)S(1)}, bf16[640,1536]{1,0:T(8,128)(2,1)S(1)}) custom-call(s32[2]{0:T(128)S(1)} %pad_add_fusion.info, bf16[640,1536]{1,0:T(8,128)(2,1)S(1)} %copy-done.1, bf16[640,1536]{1,0:T(8,128)(2,1)S(1)} %copy-done.3, bf16[512,1024]{1,0:T(8,128)(2,1)S(1)} %get-tuple-element.475.grad_ref), custom_call_target="tpu_custom_call" | custom-call | flops 1 | bytes 1 | tf_op jit(solution)/shard_map/attend_back/pallas_call | solution.py:510
  245.0 1.7 collective-permute-start.38
  246.7 1.5 copy-done.16
  248.3 5.0 %back_project.2.g_ref = bf16[128,1024]{1,0:T(8,128)(2,1)S(1)} custom-call(bf16[640,1536]{1,0:T(8,128)(2,1)S(1)} %get-tuple-element.551.g_own, bf16[640,1536]{1,0:T(8,128)(2,1)S(1)} %copy-done.16, bf16[1024,2048]{1,0:T(8,128)(2,1)} %place.1.w_ref.o_own.w_own, bf16[1024,2048]{1,0:T(8,128)(2,1)} %copy-done.69), custom_call_target="tpu_custom_call" | custom-call | flops 1 | bytes 1 | tf_op jit(solution)/shard_map/back_project/pallas_call | solution.py:803
  253.3 1.5 state_low.1.lows_ref
  255.0 4.0 %state_sums.1.sums_ref = f32[4,16,8,128]{3,2,1,0:T(8,128)S(1)} custom-call(f32[2]{0:T(128)S(1)} %copy-done.63, bf16[128,1024]{1,0:T(8,128)(2,1)S(1)} %back_project.2.g_ref, bf16[128,1024]{1,0:T(8,128)(2,1)S(1)} %copy-done.21, f32[2,16,8,128]{3,2,1,0:T(8,128)S(1)} %copy-done.48, f32[2,16,8,128]{3,2,1,0:T(8,128)S(1)} %state_low.1.lows_ref, ...), custom_call_target="tpu_custom_call" | custom-call | flops 1 | bytes 1 | tf_op jit(solution)/shard_map/state_sums/pallas_call | solution.py:347
  258.9 1.5 pack_shares.1
  264.3 1.6 add_split.19
  268.2 2.4 collective-permute-start.39
  270.6 9.5 %weight_grads.1 = (bf16[2,4,64,2176]{3,2,1,0:T(8,128)(2,1)S(1)}, bf16[2,4,64,2176]{3,2,1,0:T(8,128)(2,1)}) custom-call(s32[6]{0:T(128)S(1)} %stack.127.info, bf16[640,1024]{1,0:T(8,128)(2,1)S(1)} %context_states.1.x_ref.x_own, bf16[640,1024]{1,0:T(8,128)(2,1)} %collective-permute-done.18.x_par, bf16[640,1536]{1,0:T(8,128)(2,1)S(1)} %get-tuple-element.551.g_own, ...), custom_call_target="tpu_custom_call" | custom-call | flops 1 | bytes 1 | tf_op jit(solution)/shard_map/weight_grads/pallas_call | solution.py:872
  285.5 2.8 collective-permute-start.45
  288.3 2.1 sent_tail.1
  293.8 3.8 %sent_own.1.sent_ref = bf16[384,1024]{1,0:T(8,128)(2,1)S(1)} custom-call(f32[16,8,128]{2,1,0:T(8,128)S(1)} %get-tuple-element.549.after_ref, f32[16,8,128]{2,1,0:T(8,128)S(1)} %bitcast.125, f32[16,8,128]{2,1,0:T(8,128)S(1)} %bitcast.140, f32[16,8,128]{2,1,0:T(8,128)S(1)} %bitcast.144), custom_call_target="tpu_custom_call" | custom-call | flops 1 | bytes 1 | tf_op jit(solution)/shard_map/sent_own/pallas_call | solution.py:404
  297.6 6.4 %back_project.3.part_ref = f32[512,1024]{1,0:T(8,128)S(1)} custom-call(bf16[640,1536]{1,0:T(8,128)(2,1)S(1)} %get-tuple-element.551.g_own, bf16[640,1536]{1,0:T(8,128)(2,1)S(1)} %copy-done.17, bf16[1024,2048]{1,0:T(8,128)(2,1)} %place.1.w_ref.o_own.w_own, bf16[1024,2048]{1,0:T(8,128)(2,1)} %copy-done.69), custom_call_target="tpu_custom_call" | custom-call | flops 1 | bytes 1 | tf_op jit(solution)/shard_map/back_project/pallas_call | solution.py:803
  304.1 2.6 back_first.1
  307.4 1.6 collective-permute-done.44.recv_ref
  309.0 1.5 collective-permute-done.43.recv_ref
  310.5 2.9 add_split.24
  314.8 2.0 add_split.23
  317.5 2.8 collective-permute-start.48
  320.3 14.0 %all_to_all.9 = f32[32,1,32]{2,1,0:T(1,128)S(1)} all-to-all(f32[32,1,32]{2,1,0:T(1,128)S(1)} %bitcast.154), channel_id=1, replica_groups=mesh['dp'=4,'mp'=8] {'dp','mp'}, dimensions={0} | all-to-all | bytes 8192 | tf_op jit(solution)/shard_map/all_to_all | solution.py:1503
  334.9 1.7 add_split.27
  339.1 2.5 mix.1
  342.6 8.4 %collective-permute-done.49.recv_ref = bf16[1,2,64,2176]{3,2,1,0:T(8,128)(2,1)S(1)} collective-permute-done((bf16[1,2,64,2176]{3,2,1,0:T(8,128)(2,1)S(1)}, bf16[1,2,64,2176]{3,2,1,0:T(8,128)(2,1)S(1)}, u32[]{:S(2)}, u32[]{:S(2)}) %collective-permute-start.49) | collective-permute-done | bytes 557088 | tf_op jit(solution)/shard_map/ppermute | solution.py:78
  351.1 1.5 collective-permute-start.50
  354.6 10.9 %collective-permute-done.50.recv_ref = bf16[1,1,64,2176]{3,2,1,0:T(8,128)(2,1)S(1)} collective-permute-done((bf16[1,1,64,2176]{3,2,1,0:T(8,128)(2,1)S(1)}, bf16[1,1,64,2176]{3,2,1,0:T(8,128)(2,1)S(1)}, u32[]{:S(2)}, u32[]{:S(2)}) %collective-permute-start.50) | collective-permute-done | bytes 278560 | tf_op jit(solution)/shard_map/ppermute | solution.py:78
  (289 shorter events, 70.5 us)
Async XLA Ops:
  7.2 157.1 %all-gather.2.cloned.1.call-start = ((), (), s32[]{:S(2)}) async-start(), calls=%async_computation.1 | async-start | bytes 8650752 | tf_op jit(solution)/shard_map/all_gather | solution.py:1312
  9.5 2.6 collective-permute-start.1
  10.8 1.2 collective-permute-start
  10.9 1.4 collective-permute-start.2
  13.1 4.8 %collective-permute-start.3 = (f32[2,29,128]{2,1,0:T(8,128)S(1)}, f32[2,29,128]{2,1,0:T(8,128)S(1)}, u32[]{:S(2)}, u32[]{:S(2)}) collective-permute-start(f32[2,29,128]{2,1,0:T(8,128)S(1)} %merge.9.here_ref), channel_id=1, source_target_pairs={{0,2},{1,3},{2,0},{3,1},{4,6},{5,7},{6,4},{7,5},{8,10},{9,11},{10,... | collective-permute-start | bytes 89096 | tf_op jit(solution)/shard_map/ppermute | solution.py:78
  17.9 5.4 %collective-permute-start.4 = (f32[4,29,128]{2,1,0:T(8,128)S(1)}, f32[4,29,128]{2,1,0:T(8,128)S(1)}, u32[]{:S(2)}, u32[]{:S(2)}) collective-permute-start(f32[4,29,128]{2,1,0:T(8,128)S(1)} %merge.10.here_ref), channel_id=1, source_target_pairs={{0,4},{1,5},{2,6},{3,7},{4,0},{5,1},{6,2},{7,3},{8,12},{9,13},{10,... | collective-permute-start | bytes 178184 | tf_op jit(solution)/shard_map/ppermute | solution.py:78
  23.3 17.2 %copy-start.9 = (bf16[512,1024]{1,0:T(8,128)(2,1)S(1)}, bf16[512,1024]{1,0:T(8,128)(2,1)}, u32[]{:S(2)}) copy-start(bf16[512,1024]{1,0:T(8,128)(2,1)} %tok_ref.1) | copy-start | bytes 3145732
  23.4 5.0 %collective-permute-start.5 = (f32[8,29,128]{2,1,0:T(8,128)S(1)}, f32[8,29,128]{2,1,0:T(8,128)S(1)}, u32[]{:S(2)}, u32[]{:S(2)}) collective-permute-start(f32[8,29,128]{2,1,0:T(8,128)S(1)} %merge.11.here_ref), channel_id=1, source_target_pairs={{0,8},{1,9},{2,10},{3,11},{4,12},{5,13},{6,14},{7,15},{8,0},{9,1},... | collective-permute-start | bytes 356360 | tf_op jit(solution)/shard_map/ppermute | solution.py:78
  25.2 82.5 %copy-start.62 = (f32[2]{0:T(128)}, f32[2]{0:T(128)S(1)}, u32[]{:S(2)}) copy-start(f32[2]{0:T(128)S(1)} %pad_maximum_fusion.8.scal) | copy-start | bytes 28
  25.2 12.4 %collective-permute-start.7 = (bf16[1,64,2048]{2,1,0:T(8,128)(2,1)S(1)}, bf16[1,64,2048]{2,1,0:T(8,128)(2,1)S(1)}, u32[]{:S(2)}, u32[]{:S(2)}) collective-permute-start(bf16[1,64,2048]{2,1,0:T(8,128)(2,1)S(1)} %maximum_select_fusion.1.here_ref), channel_id=1, source_target_pairs={{0,4},{1,5},{2,6},{3,7},{4,0},{5,1},{6,2},{7,3},{8,12},{9,13},{10,... | collective-permute-start | bytes 786440 | tf_op jit(solution)/shard_map/ppermute | solution.py:78
  28.4 6.4 %collective-permute-start.6 = (f32[16,29,128]{2,1,0:T(8,128)S(1)}, f32[16,29,128]{2,1,0:T(8,128)S(1)}, u32[]{:S(2)}, u32[]{:S(2)}) collective-permute-start(f32[16,29,128]{2,1,0:T(8,128)S(1)} %merge.12.here_ref), channel_id=1, source_target_pairs={{0,16},{1,17},{2,18},{3,19},{4,20},{5,21},{6,22},{7,23},{8,24},{9,... | collective-permute-start | bytes 712712 | tf_op jit(solution)/shard_map/ppermute | solution.py:78
  30.3 43.0 %copy-start.59 = (f32[3]{0:T(128)}, f32[3]{0:T(128)S(1)}, u32[]{:S(2)}) copy-start(f32[3]{0:T(128)S(1)} %pad_maximum_fusion.9.scal) | copy-start | bytes 40
  37.6 18.7 %copy-start.26 = (bf16[2,64,2048]{2,1,0:T(8,128)(2,1)}, bf16[2,64,2048]{2,1,0:T(8,128)(2,1)S(1)}, u32[]{:S(2)}) copy-start(bf16[2,64,2048]{2,1,0:T(8,128)(2,1)S(1)} %merge.14.here_ref) | copy-start | bytes 1572868
  37.8 17.8 %collective-permute-start.8 = (bf16[2,64,2048]{2,1,0:T(8,128)(2,1)S(1)}, bf16[2,64,2048]{2,1,0:T(8,128)(2,1)S(1)}, u32[]{:S(2)}, u32[]{:S(2)}) collective-permute-start(bf16[2,64,2048]{2,1,0:T(8,128)(2,1)S(1)} %merge.14.here_ref), channel_id=1, source_target_pairs={{0,2},{1,3},{2,0},{3,1},{4,6},{5,7},{6,4},{7,5},{8,10},{9,11},{10,... | collective-permute-start | bytes 1572872 | tf_op jit(solution)/shard_map/ppermute | solution.py:78
  43.0 34.3 %copy-start.4 = (bf16[512,1024]{1,0:T(8,128)(2,1)S(1)}, bf16[512,1024]{1,0:T(8,128)(2,1)}, u32[]{:S(2)}) copy-start(bf16[512,1024]{1,0:T(8,128)(2,1)} %cot_ref) | copy-start | bytes 3145732
  58.5 34.0 %copy-start.71 = (s32[4]{0:T(128)S(1)}, s32[4]{0:T(128)}, u32[]{:S(2)}) copy-start(s32[4]{0:T(128)} %param.29) | copy-start | bytes 52
  58.5 29.5 %collective-permute-start.12 = (bf16[4,64,2048]{2,1,0:T(8,128)(2,1)S(1)}, bf16[4,64,2048]{2,1,0:T(8,128)(2,1)}, u32[]{:S(2)}, u32[]{:S(2)}) collective-permute-start(bf16[4,64,2048]{2,1,0:T(8,128)(2,1)S(1)} %merge.15), channel_id=1, source_target_pairs={{0,16},{1,9},{2,18},{3,11},{4,20},{5,13},{6,22},{7,15},{8,24},{9,1... | collective-permute-start | bytes 3145736 | tf_op jit(solution)/shard_map/ppermute | solution.py:78
  59.5 32.6 %collective-permute-start.13 = (bf16[4,64,2048]{2,1,0:T(8,128)(2,1)S(1)}, bf16[4,64,2048]{2,1,0:T(8,128)(2,1)}, u32[]{:S(2)}, u32[]{:S(2)}) collective-permute-start(bf16[4,64,2048]{2,1,0:T(8,128)(2,1)S(1)} %merge.15), channel_id=1, source_target_pairs={{0,8},{1,17},{2,10},{3,19},{4,12},{5,21},{6,14},{7,23},{8,0},{9,25... | collective-permute-start | bytes 3145736 | tf_op jit(solution)/shard_map/ppermute | solution.py:78
  60.0 2.4 collective-permute-start.9
  64.8 8.5 %collective-permute-start.10 = (f32[2,16,8,128]{3,2,1,0:T(8,128)S(1)}, f32[2,16,8,128]{3,2,1,0:T(8,128)S(1)}, u32[]{:S(2)}, u32[]{:S(2)}) collective-permute-start(f32[2,16,8,128]{3,2,1,0:T(8,128)S(1)} %scan_tail.1.total_ref), channel_id=1, source_target_pairs={{0,1},{1,0},{2,3},{3,2},{4,5},{5,4},{6,7},{7,6},{8,9},{9,8},{10,11... | collective-permute-start | bytes 393224 | tf_op jit(solution)/shard_map/ppermute | solution.py:78
  74.6 12.3 %collective-permute-start.11 = (f32[2,16,8,128]{3,2,1,0:T(8,128)S(1)}, f32[2,16,8,128]{3,2,1,0:T(8,128)}, u32[]{:S(2)}, u32[]{:S(2)}) collective-permute-start(f32[2,16,8,128]{3,2,1,0:T(8,128)S(1)} %get-tuple-element.330.total_ref), channel_id=1, source_target_pairs={{0,2},{1,3},{2,0},{3,1},{4,6},{5,7},{6,4},{7,5},{8,10},{9,11},{10,... | collective-permute-start | bytes 393224 | tf_op jit(solution)/shard_map/ppermute | solution.py:78
  92.1 19.7 %collective-permute-start.15 = (bf16[4,64,2048]{2,1,0:T(8,128)(2,1)}, bf16[4,64,2048]{2,1,0:T(8,128)(2,1)}, u32[]{:S(2)}, u32[]{:S(2)}) collective-permute-start(bf16[4,64,2048]{2,1,0:T(8,128)(2,1)} %collective-permute-done.12), channel_id=1, source_target_pairs={{0,8},{1,17},{2,10},{3,19},{4,12},{5,21},{6,14},{7,23},{8,0},{9,25... | collective-permute-start | bytes 3145736 | tf_op jit(solution)/shard_map/ppermute | solution.py:78
  96.2 10.2 %collective-permute-start.14 = (f32[2,16,8,128]{3,2,1,0:T(8,128)S(1)}, f32[2,16,8,128]{3,2,1,0:T(8,128)S(1)}, u32[]{:S(2)}, u32[]{:S(2)}) collective-permute-start(f32[2,16,8,128]{3,2,1,0:T(8,128)S(1)} %get-tuple-element.347.total_ref), channel_id=1, source_target_pairs={{0,4},{1,5},{2,6},{3,7},{4,0},{5,1},{6,2},{7,3},{8,12},{9,13},{10,... | collective-permute-start | bytes 393224 | tf_op jit(solution)/shard_map/ppermute | solution.py:78
  116.8 15.2 %collective-permute-start.16 = (bf16[1024,2048]{1,0:T(8,128)(2,1)}, bf16[1024,2048]{1,0:T(8,128)(2,1)S(1)}, u32[]{:S(2)}, u32[]{:S(2)}) collective-permute-start(bf16[1024,2048]{1,0:T(8,128)(2,1)} %place.1.w_ref.o_own.w_own), channel_id=1, source_target_pairs={{0,1},{1,0},{2,3},{3,2},{4,5},{5,4},{6,7},{7,6},{8,9},{9,8},{10,11... | collective-permute-start | bytes 12582920 | tf_op jit(solution)/shard_map/ppermute | solution.py:78
  116.8 15.2 %collective-permute-start.17 = (bf16[1,64,2048]{2,1,0:T(8,128)(2,1)S(1)}, bf16[1,64,2048]{2,1,0:T(8,128)(2,1)S(1)}, u32[]{:S(2)}, u32[]{:S(2)}) collective-permute-start(bf16[1,64,2048]{2,1,0:T(8,128)(2,1)S(1)} %copy-done.40), channel_id=1, source_target_pairs={{0,4},{1,5},{2,6},{3,7},{4,0},{5,1},{6,2},{7,3},{8,12},{9,13},{10,... | collective-permute-start | bytes 786440 | tf_op jit(solution)/shard_map/ppermute | solution.py:78
  123.2 15.5 %copy-start = (bf16[640,1536]{1,0:T(8,128)(2,1)}, bf16[640,1536]{1,0:T(8,128)(2,1)S(1)}, u32[]{:S(2)}) copy-start(bf16[640,1536]{1,0:T(8,128)(2,1)S(1)} %project.2.own_ref) | copy-start | bytes 5898244
  132.0 16.0 %collective-permute-start.18 = (bf16[640,1024]{1,0:T(8,128)(2,1)S(1)}, bf16[640,1024]{1,0:T(8,128)(2,1)}, u32[]{:S(2)}, u32[]{:S(2)}) collective-permute-start(bf16[640,1024]{1,0:T(8,128)(2,1)S(1)} %context_states.1.x_ref.x_own), channel_id=1, source_target_pairs={{0,1},{1,0},{2,3},{3,2},{4,5},{5,4},{6,7},{7,6},{8,9},{9,8},{10,11... | collective-permute-start | bytes 3932168 | tf_op jit(solution)/shard_map/ppermute | solution.py:78
  134.1 13.9 %collective-permute-start.19 = (bf16[2,64,2048]{2,1,0:T(8,128)(2,1)}, bf16[2,64,2048]{2,1,0:T(8,128)(2,1)}, u32[]{:S(2)}, u32[]{:S(2)}) collective-permute-start(bf16[2,64,2048]{2,1,0:T(8,128)(2,1)} %merge.16.here_ref), channel_id=1, source_target_pairs={{0,2},{1,3},{2,0},{3,1},{4,6},{5,7},{6,4},{7,5},{8,10},{9,11},{10,... | collective-permute-start | bytes 1572872 | tf_op jit(solution)/shard_map/ppermute | solution.py:78
  149.3 15.0 %collective-permute-start.20 = (bf16[4,64,2048]{2,1,0:T(8,128)(2,1)S(1)}, bf16[4,64,2048]{2,1,0:T(8,128)(2,1)}, u32[]{:S(2)}, u32[]{:S(2)}) collective-permute-start(bf16[4,64,2048]{2,1,0:T(8,128)(2,1)S(1)} %merge.17), channel_id=1, source_target_pairs={{0,16},{1,9},{2,18},{3,11},{4,20},{5,13},{6,22},{7,15},{8,24},{9,1... | collective-permute-start | bytes 3145736 | tf_op jit(solution)/shard_map/ppermute | solution.py:78
  150.8 13.5 %collective-permute-start.23 = (bf16[512,1024]{1,0:T(8,128)(2,1)S(1)}, bf16[512,1024]{1,0:T(8,128)(2,1)}, u32[]{:S(2)}, u32[]{:S(2)}) collective-permute-start(bf16[512,1024]{1,0:T(8,128)(2,1)S(1)} %copy-done.5), channel_id=1, source_target_pairs={{0,1},{1,0},{2,3},{3,2},{4,5},{5,4},{6,7},{7,6},{8,9},{9,8},{10,11... | collective-permute-start | bytes 3145736 | tf_op jit(solution)/shard_map/ppermute | solution.py:78
  151.0 16.2 %collective-permute-start.25 = (bf16[1024,512]{1,0:T(8,128)(2,1)S(1)}, bf16[1024,512]{1,0:T(8,128)(2,1)}, u32[]{:S(2)}, u32[]{:S(2)}) collective-permute-start(bf16[1024,512]{1,0:T(8,128)(2,1)S(1)} %bitcast.126), channel_id=1, source_target_pairs={{0,1},{1,0},{2,3},{3,2},{4,5},{5,4},{6,7},{7,6},{8,9},{9,8},{10,11... | collective-permute-start | bytes 3145736 | tf_op jit(solution)/shard_map/ppermute | solution.py:78
  157.4 10.0 %collective-permute-start.22 = (bf16[512,1024]{1,0:T(8,128)(2,1)}, bf16[512,1024]{1,0:T(8,128)(2,1)}, u32[]{:S(2)}, u32[]{:S(2)}) collective-permute-start(bf16[512,1024]{1,0:T(8,128)(2,1)} %get-tuple-element.431.s_own), channel_id=1, source_target_pairs={{0,1},{1,0},{2,3},{3,2},{4,5},{5,4},{6,7},{7,6},{8,9},{9,8},{10,11... | collective-permute-start | bytes 3145736 | tf_op jit(solution)/shard_map/ppermute | solution.py:78
  157.6 9.7 %collective-permute-start.24 = (bf16[1024,512]{1,0:T(8,128)(2,1)}, bf16[1024,512]{1,0:T(8,128)(2,1)}, u32[]{:S(2)}, u32[]{:S(2)}) collective-permute-start(bf16[1024,512]{1,0:T(8,128)(2,1)} %get-tuple-element.432.st_own), channel_id=1, source_target_pairs={{0,1},{1,0},{2,3},{3,2},{4,5},{5,4},{6,7},{7,6},{8,9},{9,8},{10,11... | collective-permute-start | bytes 3145736 | tf_op jit(solution)/shard_map/ppermute | solution.py:78
  164.3 25.4 %collective-permute-start.21 = (bf16[512,1024]{1,0:T(8,128)(2,1)}, bf16[512,1024]{1,0:T(8,128)(2,1)}, u32[]{:S(2)}, u32[]{:S(2)}) collective-permute-start(bf16[512,1024]{1,0:T(8,128)(2,1)} %copy-done.6), channel_id=1, source_target_pairs={{0,1},{1,0},{2,3},{3,2},{4,5},{5,4},{6,7},{7,6},{8,9},{9,8},{10,11... | collective-permute-start | bytes 3145736 | tf_op jit(solution)/shard_map/ppermute | solution.py:78
  164.3 25.4 %collective-permute-start.26 = (bf16[4,64,2048]{2,1,0:T(8,128)(2,1)}, bf16[4,64,2048]{2,1,0:T(8,128)(2,1)}, u32[]{:S(2)}, u32[]{:S(2)}) collective-permute-start(bf16[4,64,2048]{2,1,0:T(8,128)(2,1)} %copy-done.18), channel_id=1, source_target_pairs={{0,8},{1,17},{2,10},{3,19},{4,12},{5,21},{6,14},{7,23},{8,0},{9,25... | collective-permute-start | bytes 3145736 | tf_op jit(solution)/shard_map/ppermute | solution.py:78
  167.2 24.3 %collective-permute-start.27 = (bf16[4,64,2048]{2,1,0:T(8,128)(2,1)}, bf16[4,64,2048]{2,1,0:T(8,128)(2,1)}, u32[]{:S(2)}, u32[]{:S(2)}) collective-permute-start(bf16[4,64,2048]{2,1,0:T(8,128)(2,1)} %collective-permute-done.20), channel_id=1, source_target_pairs={{0,8},{1,17},{2,10},{3,19},{4,12},{5,21},{6,14},{7,23},{8,0},{9,25... | collective-permute-start | bytes 3145736 | tf_op jit(solution)/shard_map/ppermute | solution.py:78
  191.5 26.0 %collective-permute-start.28 = (bf16[1,4,2,256,256]{4,3,2,1,0:T(8,128)(2,1)S(1)}, bf16[1,4,2,256,256]{4,3,2,1,0:T(8,128)(2,1)S(1)}, u32[]{:S(2)}, u32[]{:S(2)}) collective-permute-start(bf16[1,4,2,256,256]{4,3,2,1,0:T(8,128)(2,1)S(1)} %get-tuple-element.454), channel_id=1, source_target_pairs={{0,8},{1,17},{2,10},{3,19},{4,12},{5,21},{6,14},{7,23},{8,0},{9,25... | collective-permute-start | bytes 3145736 | tf_op jit(solution)/shard_map/ppermute | solution.py:78
  193.5 24.0 %collective-permute-start.29 = (bf16[1,4,2,256,256]{4,3,2,1,0:T(8,128)(2,1)S(1)}, bf16[1,4,2,256,256]{4,3,2,1,0:T(8,128)(2,1)S(1)}, u32[]{:S(2)}, u32[]{:S(2)}) collective-permute-start(bf16[1,4,2,256,256]{4,3,2,1,0:T(8,128)(2,1)S(1)} %get-tuple-element.455), channel_id=1, source_target_pairs={{0,8},{1,17},{2,10},{3,19},{4,12},{5,21},{6,14},{7,23},{8,0},{9,25... | collective-permute-start | bytes 3145736 | tf_op jit(solution)/shard_map/ppermute | solution.py:78
  217.5 3.3 collective-permute-start.30
  218.8 25.1 %collective-permute-start.32 = (bf16[1,4,2,256,256]{4,3,2,1,0:T(8,128)(2,1)}, bf16[1,4,2,256,256]{4,3,2,1,0:T(8,128)(2,1)}, u32[]{:S(2)}, u32[]{:S(2)}) collective-permute-start(bf16[1,4,2,256,256]{4,3,2,1,0:T(8,128)(2,1)} %add_split.15), channel_id=1, source_target_pairs={{0,16},{1,9},{2,18},{3,11},{4,20},{5,13},{6,22},{7,15},{8,24},{9,1... | collective-permute-start | bytes 3145736 | tf_op jit(solution)/shard_map/ppermute | solution.py:78
  219.3 25.6 %collective-permute-start.33 = (bf16[1,4,2,256,256]{4,3,2,1,0:T(8,128)(2,1)}, bf16[1,4,2,256,256]{4,3,2,1,0:T(8,128)(2,1)}, u32[]{:S(2)}, u32[]{:S(2)}) collective-permute-start(bf16[1,4,2,256,256]{4,3,2,1,0:T(8,128)(2,1)} %get-tuple-element.492), channel_id=1, source_target_pairs={{0,8},{1,17},{2,10},{3,19},{4,12},{5,21},{6,14},{7,23},{8,0},{9,25... | collective-permute-start | bytes 3145736 | tf_op jit(solution)/shard_map/ppermute | solution.py:78
  227.1 15.3 %collective-permute-start.31 = (bf16[512,512]{1,0:T(8,128)(2,1)}, bf16[512,512]{1,0:T(8,128)(2,1)}, u32[]{:S(2)}, u32[]{:S(2)}) collective-permute-start(bf16[512,512]{1,0:T(8,128)(2,1)} %get-tuple-element.473), channel_id=1, source_target_pairs={{0,1},{1,0},{2,3},{3,2},{4,5},{5,4},{6,7},{7,6},{8,9},{9,8},{10,11... | collective-permute-start | bytes 1572872 | tf_op jit(solution)/shard_map/ppermute | solution.py:78
  244.9 22.0 %collective-permute-start.36 = (bf16[640,1536]{1,0:T(8,128)(2,1)}, bf16[640,1536]{1,0:T(8,128)(2,1)S(1)}, u32[]{:S(2)}, u32[]{:S(2)}) collective-permute-start(bf16[640,1536]{1,0:T(8,128)(2,1)} %copy-done.15), channel_id=1, source_target_pairs={{0,1},{1,0},{2,3},{3,2},{4,5},{5,4},{6,7},{7,6},{8,9},{9,8},{10,11... | collective-permute-start | bytes 5898248 | tf_op jit(solution)/shard_map/ppermute | solution.py:78
  245.0 21.9 %collective-permute-start.38 = (bf16[1,4,2,256,256]{4,3,2,1,0:T(8,128)(2,1)}, bf16[1,4,2,256,256]{4,3,2,1,0:T(8,128)(2,1)S(1)}, u32[]{:S(2)}, u32[]{:S(2)}) collective-permute-start(bf16[1,4,2,256,256]{4,3,2,1,0:T(8,128)(2,1)} %copy-done.66), channel_id=1, source_target_pairs={{0,8},{1,17},{2,10},{3,19},{4,12},{5,21},{6,14},{7,23},{8,0},{9,25... | collective-permute-start | bytes 3145736 | tf_op jit(solution)/shard_map/ppermute | solution.py:78
  254.8 6.4 %collective-permute-start.34 = (f32[16,8,128]{2,1,0:T(8,128)S(1)}, f32[16,8,128]{2,1,0:T(8,128)S(1)}, u32[]{:S(2)}, u32[]{:S(2)}) collective-permute-start(f32[16,8,128]{2,1,0:T(8,128)S(1)} %slice_bitcast_fusion.10.total_ref), channel_id=1, source_target_pairs={{0,1},{1,0},{2,3},{3,2},{4,5},{5,4},{6,7},{7,6},{8,9},{9,8},{10,11... | collective-permute-start | bytes 196616 | tf_op jit(solution)/shard_map/ppermute | solution.py:78
  260.5 6.4 %collective-permute-start.37 = (bf16[4,4,64,128]{3,2,1,0:T(8,128)(2,1)S(1)}, bf16[4,4,64,128]{3,2,1,0:T(8,128)(2,1)S(1)}, u32[]{:S(2)}, u32[]{:S(2)}) collective-permute-start(bf16[4,4,64,128]{3,2,1,0:T(8,128)(2,1)S(1)} %fusion), channel_id=1, source_target_pairs={{0,1},{1,0},{2,3},{3,2},{4,5},{5,4},{6,7},{7,6},{8,9},{9,8},{10,11... | collective-permute-start | bytes 786440 | tf_op jit(solution)/shard_map/ppermute | solution.py:78
  261.9 4.3 %collective-permute-start.35 = (f32[16,8,128]{2,1,0:T(8,128)S(1)}, f32[16,8,128]{2,1,0:T(8,128)S(1)}, u32[]{:S(2)}, u32[]{:S(2)}) collective-permute-start(f32[16,8,128]{2,1,0:T(8,128)S(1)} %get-tuple-element.499.total_ref), channel_id=1, source_target_pairs={{0,2},{1,3},{2,0},{3,1},{4,6},{5,7},{6,4},{7,5},{8,10},{9,11},{10,... | collective-permute-start | bytes 196616 | tf_op jit(solution)/shard_map/ppermute | solution.py:78
  266.9 14.6 %copy-start.64 = (f32[3]{0:T(128)S(1)}, f32[3]{0:T(128)}, u32[]{:S(2)}) copy-start(f32[3]{0:T(128)} %get-tuple-element.522.scal) | copy-start | bytes 40
  266.9 17.3 %copy-start.33 = (bf16[1,4,2,256,256]{4,3,2,1,0:T(8,128)(2,1)S(1)}, bf16[1,4,2,256,256]{4,3,2,1,0:T(8,128)(2,1)}, u32[]{:S(2)}) copy-start(bf16[1,4,2,256,256]{4,3,2,1,0:T(8,128)(2,1)} %copy-done.32) | copy-start | bytes 3145732
  267.0 15.8 %collective-permute-start.41 = (bf16[1,4,2,256,256]{4,3,2,1,0:T(8,128)(2,1)S(1)}, bf16[1,4,2,256,256]{4,3,2,1,0:T(8,128)(2,1)S(1)}, u32[]{:S(2)}, u32[]{:S(2)}) collective-permute-start(bf16[1,4,2,256,256]{4,3,2,1,0:T(8,128)(2,1)S(1)} %add_split.19), channel_id=1, source_target_pairs={{0,16},{1,9},{2,18},{3,11},{4,20},{5,13},{6,22},{7,15},{8,24},{9,1... | collective-permute-start | bytes 3145736 | tf_op jit(solution)/shard_map/ppermute | solution.py:78
  267.3 15.5 %collective-permute-start.40 = (bf16[1,2,2,256,256]{4,3,2,1,0:T(8,128)(2,1)S(1)}, bf16[1,2,2,256,256]{4,3,2,1,0:T(8,128)(2,1)S(1)}, u32[]{:S(2)}, u32[]{:S(2)}) collective-permute-start(bf16[1,2,2,256,256]{4,3,2,1,0:T(8,128)(2,1)S(1)} %get-tuple-element.543), channel_id=1, source_target_pairs={{0,2},{1,3},{2,0},{3,1},{4,6},{5,7},{6,4},{7,5},{8,10},{9,11},{10,... | collective-permute-start | bytes 1572872 | tf_op jit(solution)/shard_map/ppermute | solution.py:78
  268.2 13.3 %collective-permute-start.39 = (f32[16,8,128]{2,1,0:T(8,128)S(1)}, f32[16,8,128]{2,1,0:T(8,128)S(1)}, u32[]{:S(2)}, u32[]{:S(2)}) collective-permute-start(f32[16,8,128]{2,1,0:T(8,128)S(1)} %get-tuple-element.523.total_ref), channel_id=1, source_target_pairs={{0,4},{1,5},{2,6},{3,7},{4,0},{5,1},{6,2},{7,3},{8,12},{9,13},{10,... | collective-permute-start | bytes 196616 | tf_op jit(solution)/shard_map/ppermute | solution.py:78
  282.8 27.8 %collective-permute-start.43 = (bf16[2,4,64,2176]{3,2,1,0:T(8,128)(2,1)}, bf16[2,4,64,2176]{3,2,1,0:T(8,128)(2,1)}, u32[]{:S(2)}, u32[]{:S(2)}) collective-permute-start(bf16[2,4,64,2176]{3,2,1,0:T(8,128)(2,1)} %get-tuple-element.568), channel_id=1, source_target_pairs={{0,8},{1,17},{2,10},{3,19},{4,12},{5,21},{6,14},{7,23},{8,0},{9,25... | collective-permute-start | bytes 6684680 | tf_op jit(solution)/shard_map/ppermute | solution.py:78
  284.5 13.0 %copy-start.17 = (bf16[640,1536]{1,0:T(8,128)(2,1)S(1)}, bf16[640,1536]{1,0:T(8,128)(2,1)}, u32[]{:S(2)}) copy-start(bf16[640,1536]{1,0:T(8,128)(2,1)} %copy-done.15) | copy-start | bytes 5898244
  285.5 23.5 %collective-permute-start.45 = (bf16[1,2,2,256,256]{4,3,2,1,0:T(8,128)(2,1)}, bf16[1,2,2,256,256]{4,3,2,1,0:T(8,128)(2,1)}, u32[]{:S(2)}, u32[]{:S(2)}) collective-permute-start(bf16[1,2,2,256,256]{4,3,2,1,0:T(8,128)(2,1)} %get-tuple-element.567), channel_id=1, source_target_pairs={{0,2},{1,3},{2,0},{3,1},{4,6},{5,7},{6,4},{7,5},{8,10},{9,11},{10,... | collective-permute-start | bytes 1572872 | tf_op jit(solution)/shard_map/ppermute | solution.py:78
  290.4 13.6 %collective-permute-start.42 = (bf16[128,1024]{1,0:T(8,128)(2,1)S(1)}, bf16[128,1024]{1,0:T(8,128)(2,1)S(1)}, u32[]{:S(2)}, u32[]{:S(2)}) collective-permute-start(bf16[128,1024]{1,0:T(8,128)(2,1)S(1)} %sent_tail.1), channel_id=1, source_target_pairs={{1,0},{2,1},{3,2},{4,3},{5,4},{6,5},{7,6},{9,8},{10,9},{11,10},{12... | collective-permute-start | bytes 786440 | tf_op jit(solution)/shard_map/ppermute | solution.py:78
  293.2 15.8 %collective-permute-start.44 = (bf16[1,1,2,256,256]{4,3,2,1,0:T(8,128)(2,1)}, bf16[1,1,2,256,256]{4,3,2,1,0:T(8,128)(2,1)}, u32[]{:S(2)}, u32[]{:S(2)}) collective-permute-start(bf16[1,1,2,256,256]{4,3,2,1,0:T(8,128)(2,1)} %get-tuple-element.563), channel_id=1, source_target_pairs={{0,4},{1,5},{2,6},{3,7},{4,0},{5,1},{6,2},{7,3},{8,12},{9,13},{10,... | collective-permute-start | bytes 786440 | tf_op jit(solution)/shard_map/ppermute | solution.py:78
  313.5 21.4 %collective-permute-start.47 = (bf16[1,4,64,2176]{3,2,1,0:T(8,128)(2,1)}, bf16[1,4,64,2176]{3,2,1,0:T(8,128)(2,1)}, u32[]{:S(2)}, u32[]{:S(2)}) collective-permute-start(bf16[1,4,64,2176]{3,2,1,0:T(8,128)(2,1)} %get-tuple-element.577), channel_id=1, source_target_pairs={{0,16},{1,9},{2,18},{3,11},{4,20},{5,13},{6,22},{7,15},{8,24},{9,1... | collective-permute-start | bytes 3342344 | tf_op jit(solution)/shard_map/ppermute | solution.py:78
  314.8 20.0 %collective-permute-start.46 = (bf16[512,1024]{1,0:T(8,128)(2,1)}, bf16[512,1024]{1,0:T(8,128)(2,1)}, u32[]{:S(2)}, u32[]{:S(2)}) collective-permute-start(bf16[512,1024]{1,0:T(8,128)(2,1)} %get-tuple-element.571), channel_id=1, source_target_pairs={{0,1},{1,0},{2,3},{3,2},{4,5},{5,4},{6,7},{7,6},{8,9},{9,8},{10,11... | collective-permute-start | bytes 3145736 | tf_op jit(solution)/shard_map/ppermute | solution.py:78
  314.8 24.2 %copy-start.14 = (f32[512,1024]{1,0:T(8,128)S(1)}, f32[512,1024]{1,0:T(8,128)}, u32[]{:S(2)}) copy-start(f32[512,1024]{1,0:T(8,128)} %copy-done.12) | copy-start | bytes 6291460
  317.5 17.4 %collective-permute-start.48 = (bf16[1,1,2,256,256]{4,3,2,1,0:T(8,128)(2,1)}, bf16[1,1,2,256,256]{4,3,2,1,0:T(8,128)(2,1)}, u32[]{:S(2)}, u32[]{:S(2)}) collective-permute-start(bf16[1,1,2,256,256]{4,3,2,1,0:T(8,128)(2,1)} %get-tuple-element.574), channel_id=1, source_target_pairs={{0,4},{1,5},{2,6},{3,7},{4,0},{5,1},{6,2},{7,3},{8,12},{9,13},{10,... | collective-permute-start | bytes 786440 | tf_op jit(solution)/shard_map/ppermute | solution.py:78
  336.5 14.5 %collective-permute-start.49 = (bf16[1,2,64,2176]{3,2,1,0:T(8,128)(2,1)S(1)}, bf16[1,2,64,2176]{3,2,1,0:T(8,128)(2,1)S(1)}, u32[]{:S(2)}, u32[]{:S(2)}) collective-permute-start(bf16[1,2,64,2176]{3,2,1,0:T(8,128)(2,1)S(1)} %get-tuple-element.588), channel_id=1, source_target_pairs={{0,2},{1,3},{2,0},{3,1},{4,6},{5,7},{6,4},{7,5},{8,10},{9,11},{10,... | collective-permute-start | bytes 1671176 | tf_op jit(solution)/shard_map/ppermute | solution.py:78
  351.1 14.4 %collective-permute-start.50 = (bf16[1,1,64,2176]{3,2,1,0:T(8,128)(2,1)S(1)}, bf16[1,1,64,2176]{3,2,1,0:T(8,128)(2,1)S(1)}, u32[]{:S(2)}, u32[]{:S(2)}) collective-permute-start(bf16[1,1,64,2176]{3,2,1,0:T(8,128)(2,1)S(1)} %get-tuple-element.595), channel_id=1, source_target_pairs={{0,4},{1,5},{2,6},{3,7},{4,0},{5,1},{6,2},{7,3},{8,12},{9,13},{10,... | collective-permute-start | bytes 835592 | tf_op jit(solution)/shard_map/ppermute | solution.py:78
  366.3 1.6 collective-permute-start.51
  (61 other events, 316.5 us)
Sparse Core Ops, SparseCore 0:
  23.5 92.6 all-gather.1

commit v5 on v4

--- a/solution.py
+++ b/solution.py
@@ -1026,7 +1026,7 @@
         compiler_params=params(6),
         cost_estimate=COST,
         name="merge",
-    )(bit.astype(jnp.int32).reshape(1), here, there)
+    )(bit.astype(jnp.int32).reshape(1), *map(in_hbm if here.dtype == bf16 else in_vmem, (here, there)))
 
 
 def join_small(links, current, received, index, bit):
@@ -1436,7 +1436,7 @@
     v.grad_gain_two = v.grad_gain_two.reshape(ndp, nmp, -1)
     gain_len = v.grad_gain_two.shape[2]
     v.grad_gain_two = jnp.pad(v.grad_gain_two, ((0, 0), (0, 0), (0, channels - gain_len)))
-    v.g_own, v.g_other = attend_back(attend_info, v.qkv_own, u.qkv_other, v.grad_attended)
+    u.g_own, u.g_other = attend_back(attend_info, v.qkv_own, u.qkv_other, v.grad_attended)
     fence(v, both, both)
 
     def exchange_back(bit):
@@ -1447,8 +1447,8 @@
 
     if split:
         second.start_near()
-    v.g_par = links.core_swap(v.g_other)
-    v.grad_context = back_project(v.g_own, v.g_other, v.w_own, v.w_other, 0, CTX, bf16)
+    v.g_par = links.core_swap(u.g_other)
+    v.grad_context = back_project(u.g_own, u.g_other, v.w_own, v.w_other, 0, CTX, bf16)
     v.lows = state_low(v.grad_context, u.rate)
     v.total = v.lows[0]
     v.after = jnp.zeros_like(v.total)
@@ -1471,12 +1471,13 @@
         exchange_back(bit)
     fence(v, both, [second] if split else [])
 
+    u.mix_recv = links.core_swap(v.mix_par)
     for scatter in both:
         scatter.start()
     mats = Scatter(
         links,
         *weight_grads(
-            links, info, v.inputs_kv, v.inputs_par, v.g_own, v.g_par, v.attended,
+            links, info, v.inputs_kv, v.inputs_par, u.g_own, v.g_par, v.attended,
             v.attended_par, v.branch_own, v.branch_par, v.shares,
         ),
     )
@@ -1490,7 +1491,7 @@
     tail_sent = sent_tail(v.grad_context, v.after, u.rate, u.gain_in, u.gain_out)
     v.last_sent = links.window_shift(tail_sent, -1)
     v.own_sent = sent_own(v.after, u.rate, u.gain_in, u.gain_out)
-    v.part = back_project(v.g_own, v.g_other, v.w_own, v.w_other, CTX, BLK, f32)
+    v.part = back_project(u.g_own, u.g_other, v.w_own, v.w_other, CTX, BLK, f32)
     v.grad_tokens, grad_gain_one = back_first(
         v.tokens, v.part, v.own_sent, v.last_sent, v.grad_middle, v.gain_one
     )
@@ -1502,10 +1503,9 @@
         scatter.start()
     gain_parts = lax.all_to_all(v.gain_parts, AXES, split_axis=0, concat_axis=0, tiled=True)
     v.share_one = jnp.sum(gain_parts, axis=0)
-    v.mix_recv = links.core_swap(v.mix_par)
     fence(v, [*both, mats], [mats, *late])
     mats.start()
-    v.mixed = mix(u.middle, u.mix_own, v.mix_recv)
+    v.mixed = mix(u.middle, u.mix_own, u.mix_recv)
     for scatter in both:
         scatter.finish()
     v.results = [scatter.result for scatter in both]

time: 380 us -> 379 us (level)
  local copies, waits for them, and re-layouts: 28.2 us -> 21.9 us
  Pallas kernels: 161 us -> 167 us
    unnamed x145 -> x137, local copies, waits for them, and re-layouts: 18.9 us -> 12.6 us
  transfers between devices with their start and end apart: 53 -> 53, of which waited for: 26 -> 25; matrix products, arithmetic and copies ran while one was open for 4% -> 4% of each run, Pallas kernels for 41% -> 43%
where the time goes in v5:
time: 379 us; the launch traced here: 375 us
  Pallas kernels  167 us (44%)
  waiting for transfers between devices  86.4 us (23%)
  starting transfers between devices  60.6 us (16%)
  local copies, waits for them, and re-layouts  21.9 us (6%)
  between operations  17.3 us (5%)
  blocking collectives  14.6 us (4%)
  other arithmetic  6.9 us (2%)
    ppermute x52, waiting for transfers between devices, send(): return lax.ppermute(values, AXES, pairs)  86.3 us
    ppermute x52, starting transfers between devices, send(): return lax.ppermute(values, AXES, pairs)  60.6 us
    pallas_call x2, Pallas kernels, feed(): pl.pallas_call(functools.partial(feed_kernel, ndp, nz, width, index, grou...  45.2 us
    pallas_call x15, Pallas kernels, add_split(): pl.pallas_call(functools.partial(add_kernel, axis or 0), out_shape=outs,...  15.1 us
    all_to_all x1, blocking collectives, body(): lax.all_to_all(v.gain_parts, AXES, split_axis=0, concat_axis=0, tiled=True)  14.6 us
    pallas_call x1, Pallas kernels, attend_back(): pl.pallas_call(attend_back_kernel, out_shape=(out, out), in_specs=[SMEM]...  13.1 us
    pallas_call x2, Pallas kernels, back_project(): pl.pallas_call(functools.partial(back_project_kernel, first), out_shape=j...  12.6 us
    unnamed x137, local copies, waits for them, and re-layouts  12.6 us
  transfers between devices with their start and end apart: 53, of which 25 were waited for; matrix products, arithmetic and copies ran while one was open for 4% of the time, Pallas kernels for 43%

profile of v5, /device:TPU:0, one launch (start us, length us, event | category | flops | bytes accessed | tf_op | source)
XLA Modules:
  0.0 374.8 jit_solution(3527910056430739980)
XLA Ops:
  7.2 2.3 prepare.1
  13.1 2.9 collective-permute-start.3
  16.1 1.9 collective-permute-done.3.there_ref
  18.0 3.0 collective-permute-start.4
  21.0 2.3 collective-permute-done.4.there_ref
  23.4 1.8 collective-permute-start.5
  25.3 2.6 collective-permute-start.7
  28.4 1.8 collective-permute-start.6
  31.6 3.2 collective-permute-done.6.there_ref
  34.9 2.7 collective-permute-done.7.there_ref
  39.5 2.6 collective-permute-start.8
  43.0 1.8 fusion.1
  44.8 4.5 %scan_own.1.own_ref = f32[2,16,8,128]{3,2,1,0:T(8,128)S(1)} custom-call(bf16[512,1024]{1,0:T(8,128)(2,1)S(1)} %get-tuple-element.314.x_ref.own_ref, f32[16,8,128]{2,1,0:T(8,128)S(1)} %bitcast.113), custom_call_target="tpu_custom_call" | custom-call | flops 1 | bytes 1 | tf_op jit(solution)/shard_map/scan_own/pallas_call | solution.py:170
  50.0 9.6 %collective-permute-done.8.there_ref = bf16[2,64,2048]{2,1,0:T(8,128)(2,1)} collective-permute-done((bf16[2,64,2048]{2,1,0:T(8,128)(2,1)S(1)}, bf16[2,64,2048]{2,1,0:T(8,128)(2,1)}, u32[]{:S(2)}, u32[]{:S(2)}) %collective-permute-start.8) | collective-permute-done | bytes 524320 | tf_op jit(solution)/shard_map/ppermute | solution.py:78
  60.9 1.5 collective-permute-start.12
  62.3 1.5 collective-permute-start.9
  64.8 1.6 scan_tail.1.total_ref
  67.0 5.6 %collective-permute-start.10 = (f32[2,16,8,128]{3,2,1,0:T(8,128)S(1)}, f32[2,16,8,128]{3,2,1,0:T(8,128)S(1)}, u32[]{:S(2)}, u32[]{:S(2)}) collective-permute-start(f32[2,16,8,128]{3,2,1,0:T(8,128)S(1)} %scan_tail.1.total_ref), channel_id=1, source_target_pairs={{0,1},{1,0},{2,3},{3,2},{4,5},{5,4},{6,7},{7,6},{8,9},{9,8},{10,11... | collective-permute-start | bytes 393224 | tf_op jit(solution)/shard_map/ppermute | solution.py:78
  74.9 2.7 collective-permute-start.11
  79.0 10.1 %collective-permute-done.11.recv_ref = f32[2,16,8,128]{3,2,1,0:T(8,128)} collective-permute-done((f32[2,16,8,128]{3,2,1,0:T(8,128)S(1)}, f32[2,16,8,128]{3,2,1,0:T(8,128)}, u32[]{:S(2)}, u32[]{:S(2)}) %collective-permute-start.11) | collective-permute-done | bytes 131104 | tf_op jit(solution)/shard_map/ppermute | solution.py:78
  90.1 2.0 collective-permute-done.12
  92.2 2.2 collective-permute-done.13
  98.1 2.3 collective-permute-start.14
  101.2 6.0 %collective-permute-done.14.recv_ref = f32[2,16,8,128]{3,2,1,0:T(8,128)S(1)} collective-permute-done((f32[2,16,8,128]{3,2,1,0:T(8,128)S(1)}, f32[2,16,8,128]{3,2,1,0:T(8,128)S(1)}, u32[]{:S(2)}, u32[]{:S(2)}) %collective-permute-start.14) | collective-permute-done | bytes 131104 | tf_op jit(solution)/shard_map/ppermute | solution.py:78
  109.5 2.7 context_states.1.x_ref.x_own
  112.3 4.9 %place.1.w_ref.o_own.w_own = bf16[1024,2048]{1,0:T(8,128)(2,1)} custom-call(s32[4]{0:T(128)S(1)} %pad_add_fusion.1.order, bf16[256,2048]{1,0:T(8,128)(2,1)S(1)} %bitcast.129, bf16[256,2048]{1,0:T(8,128)(2,1)} %bitcast.44.refs_1_, bf16[256,2048]{1,0:T(8,128)(2,1)} %bitcast.45.refs_2_, bf16[256,2048]{1,0:T(8,128)(2,1)} %bitcast.46.refs_3_), custom_call_target="tpu_custom_call" | custom-call | flops 1 | bytes 1 | tf_op jit(solution)/shard_map/place/pallas_call | solution.py:966
  117.2 1.6 collective-permute-start.17
  118.8 4.1 %project.2.own_ref = bf16[640,1536]{1,0:T(8,128)(2,1)S(1)} custom-call(bf16[640,1024]{1,0:T(8,128)(2,1)S(1)} %context_states.1.x_ref.x_own, bf16[1024,2048]{1,0:T(8,128)(2,1)} %place.1.w_ref.o_own.w_own), custom_call_target="tpu_custom_call" | custom-call | flops 1 | bytes 1 | tf_op jit(solution)/shard_map/project/pallas_call | solution.py:782
  122.9 9.5 %collective-permute-done.17.there_ref = bf16[1,64,2048]{2,1,0:T(8,128)(2,1)S(1)} collective-permute-done((bf16[1,64,2048]{2,1,0:T(8,128)(2,1)S(1)}, bf16[1,64,2048]{2,1,0:T(8,128)(2,1)S(1)}, u32[]{:S(2)}, u32[]{:S(2)}) %collective-permute-start.17) | collective-permute-done | bytes 262176 | tf_op jit(solution)/shard_map/ppermute | solution.py:78
  133.1 1.9 merge.16.here_ref
  135.6 4.1 %project.3.other_ref = bf16[640,1536]{1,0:T(8,128)(2,1)S(1)} custom-call(bf16[640,1024]{1,0:T(8,128)(2,1)S(1)} %context_states.1.x_ref.x_own, bf16[1024,2048]{1,0:T(8,128)(2,1)} %collective-permute-done.16.w_ref.o_other.w_other), custom_call_target="tpu_custom_call" | custom-call | flops 1 | bytes 1 | tf_op jit(solution)/shard_map/project/pallas_call | solution.py:782
  139.7 8.0 %attend.1.att_ref.a_own = bf16[512,1024]{1,0:T(8,128)(2,1)S(1)} custom-call(s32[2]{0:T(128)S(1)} %pad_add_fusion.info, bf16[640,1536]{1,0:T(8,128)(2,1)S(1)} %project.2.own_ref, bf16[640,1536]{1,0:T(8,128)(2,1)S(1)} %project.3.other_ref), custom_call_target="tpu_custom_call" | custom-call | flops 1 | bytes 1 | tf_op jit(solution)/shard_map/attend/pallas_call | solution.py:459
  151.7 4.8 %middle_norm.1 = (f32[512,1024]{1,0:T(8,128)S(1)}, bf16[512,1024]{1,0:T(8,128)(2,1)}, bf16[1024,512]{1,0:T(8,128)(2,1)}) custom-call(s32[2]{0:T(128)S(1)} %pad_add_fusion.info, bf16[512,1024]{1,0:T(8,128)(2,1)S(1)} %attend.1.att_ref.a_own, bf16[512,1024]{1,0:T(8,128)(2,1)S(1)} %copy-done.10, bf16[1024,2048]{1,0:T(8,128)(2,1)} %place.1.w_ref.o_own.w_own, ...), custom_call_target="tpu_custom_call" | custom-call | flops 1 | bytes 1 | tf_op jit(solution)/shard_map/middle_norm/pallas_call | solution.py:717
  158.4 6.8 %collective-permute-done.20 = bf16[4,64,2048]{2,1,0:T(8,128)(2,1)} collective-permute-done((bf16[4,64,2048]{2,1,0:T(8,128)(2,1)S(1)}, bf16[4,64,2048]{2,1,0:T(8,128)(2,1)}, u32[]{:S(2)}, u32[]{:S(2)}) %collective-permute-start.20) | collective-permute-done | bytes 1048608 | tf_op jit(solution)/shard_map/ppermute | solution.py:78
  167.4 21.3 %feed_first.1 = (f32[1024,1024]{1,0:T(8,128)S(1)}, f32[1024,1024]{1,0:T(8,128)S(1)}, bf16[1,4,2,256,256]{4,3,2,1,0:T(8,128)(2,1)S(1)}, bf16[1,4,2,256,256]{4,3,2...) custom-call(s32[6]{0:T(128)S(1)} %stack.127.info, ...), custom_call_target="tpu_custom_call" | custom-call | flops 1 | bytes 1 | tf_op jit(solution)/shard_map/feed_first/pallas_call | solution.py:633
  189.7 2.0 collective-permute-done.27
  193.6 23.9 %feed_last.1 = (f32[512,1024]{1,0:T(8,128)}, bf16[512,1024]{1,0:T(8,128)(2,1)}, f32[512,1024]{1,0:T(8,128)}, bf16[512,1024]{1,0:T(8,128)(2,1)S(1)}, bf16[1,4,2,2...) custom-call(s32[6]{0:T(128)S(1)} %stack.127.info, ...), custom_call_target="tpu_custom_call" | custom-call | flops 1 | bytes 1 | tf_op jit(solution)/shard_map/feed_last/pallas_call | solution.py:633
  221.1 1.6 copy-done.22
  222.6 4.6 %back_middle.1 = (f32[512,1024]{1,0:T(8,128)S(1)}, bf16[512,512]{1,0:T(8,128)(2,1)S(1)}, bf16[512,512]{1,0:T(8,128)(2,1)}, bf16[512,1024]{1,0:T(8,128)(2,1)S(1)}, f32[1,1024]{1,0:T(1,128)S(1)}) custom-call(s32[2]{0:T(128)S(1)} %pad_add_fusion.info, f32[512,1024]{1,0:T(8,128)S(1)} %copy-done.13, f32[512,1024]{1,0:T(8,128)S(1)} %copy-done.22, ...), custom_call_target="tpu_custom_call" | custom-call | flops 1 | bytes 1 | tf_op jit(solution)/shard_map/back_middle/pallas_call | solution.py:756
  227.3 13.1 %attend_back.1 = (bf16[640,1536]{1,0:T(8,128)(2,1)S(1)}, bf16[640,1536]{1,0:T(8,128)(2,1)}) custom-call(s32[2]{0:T(128)S(1)} %pad_add_fusion.info, bf16[640,1536]{1,0:T(8,128)(2,1)S(1)} %copy-done.1, bf16[640,1536]{1,0:T(8,128)(2,1)S(1)} %copy-done.3, bf16[512,1024]{1,0:T(8,128)(2,1)S(1)} %get-tuple-element.466.grad_ref), custom_call_target="tpu_custom_call" | custom-call | flops 1 | bytes 1 | tf_op jit(solution)/shard_map/attend_back/pallas_call | solution.py:510
  243.0 2.6 collective-permute-done.31.b_par
  246.5 5.6 %back_project.2.g_ref = bf16[128,1024]{1,0:T(8,128)(2,1)S(1)} custom-call(bf16[640,1536]{1,0:T(8,128)(2,1)S(1)} %get-tuple-element.484.g_own, bf16[640,1536]{1,0:T(8,128)(2,1)} %get-tuple-element.485.g_other, bf16[1024,2048]{1,0:T(8,128)(2,1)} %place.1.w_ref.o_own.w_own, bf16[1024,2048]{1,0:T(8,128)(2,1)} %collective-permute-done.16.w_ref.o_other.w_other), custom_call_target="tpu_custom_call" | custom-call | flops 1 | bytes 1 | tf_op jit(solution)/shard_map/back_project/pallas_call | solution.py:803
  252.1 1.5 state_low.1.lows_ref
  253.8 4.0 %state_sums.1.sums_ref = f32[4,16,8,128]{3,2,1,0:T(8,128)S(1)} custom-call(f32[2]{0:T(128)S(1)} %copy-done.56, bf16[128,1024]{1,0:T(8,128)(2,1)S(1)} %back_project.2.g_ref, bf16[128,1024]{1,0:T(8,128)(2,1)S(1)} %copy-done.18, f32[2,16,8,128]{3,2,1,0:T(8,128)S(1)} %copy-done.41, f32[2,16,8,128]{3,2,1,0:T(8,128)S(1)} %state_low.1.lows_ref, ...), custom_call_target="tpu_custom_call" | custom-call | flops 1 | bytes 1 | tf_op jit(solution)/shard_map/state_sums/pallas_call | solution.py:347
  257.7 1.5 pack_shares.1
  263.5 1.6 add_split.19
  268.1 2.4 collective-permute-start.39
  270.5 10.1 %weight_grads.1 = (bf16[2,4,64,2176]{3,2,1,0:T(8,128)(2,1)S(1)}, bf16[2,4,64,2176]{3,2,1,0:T(8,128)(2,1)}) custom-call(s32[6]{0:T(128)S(1)} %stack.127.info, bf16[640,1024]{1,0:T(8,128)(2,1)S(1)} %context_states.1.x_ref.x_own, bf16[640,1024]{1,0:T(8,128)(2,1)} %collective-permute-done.18.x_par, bf16[640,1536]{1,0:T(8,128)(2,1)S(1)} %get-tuple-element.484.g_own, ...), custom_call_target="tpu_custom_call" | custom-call | flops 1 | bytes 1 | tf_op jit(solution)/shard_map/weight_grads/pallas_call | solution.py:872
  282.1 1.5 collective-permute-start.43
  284.8 3.3 collective-permute-start.45
  288.1 2.1 sent_tail.1
  293.4 3.8 %sent_own.1.sent_ref = bf16[384,1024]{1,0:T(8,128)(2,1)S(1)} custom-call(f32[16,8,128]{2,1,0:T(8,128)S(1)} %get-tuple-element.536.after_ref, f32[16,8,128]{2,1,0:T(8,128)S(1)} %bitcast.125, f32[16,8,128]{2,1,0:T(8,128)S(1)} %bitcast.140, f32[16,8,128]{2,1,0:T(8,128)S(1)} %bitcast.144), custom_call_target="tpu_custom_call" | custom-call | flops 1 | bytes 1 | tf_op jit(solution)/shard_map/sent_own/pallas_call | solution.py:404
  297.2 7.0 %back_project.3.part_ref = f32[512,1024]{1,0:T(8,128)S(1)} custom-call(bf16[640,1536]{1,0:T(8,128)(2,1)S(1)} %get-tuple-element.484.g_own, bf16[640,1536]{1,0:T(8,128)(2,1)} %get-tuple-element.485.g_other, bf16[1024,2048]{1,0:T(8,128)(2,1)} %place.1.w_ref.o_own.w_own, bf16[1024,2048]{1,0:T(8,128)(2,1)} %collective-permute-done.16.w_ref.o_other.w_other), custom_call_target="tpu_custom_call" | custom-call | flops 1 | bytes 1 | tf_op jit(solution)/shard_map/back_project/pallas_call | solution.py:803
  304.2 2.6 back_first.1
  309.8 2.9 add_split.24
  314.0 1.8 add_split.23
  316.5 2.2 collective-permute-start.47
  318.8 14.6 %all_to_all.9 = f32[32,1,32]{2,1,0:T(1,128)S(1)} all-to-all(f32[32,1,32]{2,1,0:T(1,128)S(1)} %bitcast.154), channel_id=1, replica_groups=mesh['dp'=4,'mp'=8] {'dp','mp'}, dimensions={0} | all-to-all | bytes 8192 | tf_op jit(solution)/shard_map/all_to_all | solution.py:1504
  334.0 1.5 add_split.27
  336.1 1.6 copy-done.21
  337.7 2.5 mix.1
  342.2 7.7 %collective-permute-done.49.recv_ref = bf16[1,2,64,2176]{3,2,1,0:T(8,128)(2,1)S(1)} collective-permute-done((bf16[1,2,64,2176]{3,2,1,0:T(8,128)(2,1)S(1)}, bf16[1,2,64,2176]{3,2,1,0:T(8,128)(2,1)S(1)}, u32[]{:S(2)}, u32[]{:S(2)}) %collective-permute-start.49) | collective-permute-done | bytes 557088 | tf_op jit(solution)/shard_map/ppermute | solution.py:78
  350.1 2.1 collective-permute-start.50
  354.2 10.4 %collective-permute-done.50.recv_ref = bf16[1,1,64,2176]{3,2,1,0:T(8,128)(2,1)S(1)} collective-permute-done((bf16[1,1,64,2176]{3,2,1,0:T(8,128)(2,1)S(1)}, bf16[1,1,64,2176]{3,2,1,0:T(8,128)(2,1)S(1)}, u32[]{:S(2)}, u32[]{:S(2)}) %collective-permute-start.50) | collective-permute-done | bytes 278560 | tf_op jit(solution)/shard_map/ppermute | solution.py:78
  (281 shorter events, 67.1 us)
Async XLA Ops:
  7.2 158.0 %all-gather.2.cloned.1.call-start = ((), (), s32[]{:S(2)}) async-start(), calls=%async_computation.1 | async-start | bytes 8650752 | tf_op jit(solution)/shard_map/all_gather | solution.py:1312
  9.5 2.6 collective-permute-start.1
  10.8 1.2 collective-permute-start
  10.9 1.4 collective-permute-start.2
  12.1 25.5 %copy-start.64 = (bf16[1,64,2048]{2,1,0:T(8,128)(2,1)}, bf16[1,64,2048]{2,1,0:T(8,128)(2,1)S(1)}, u32[]{:S(2)}) copy-start(bf16[1,64,2048]{2,1,0:T(8,128)(2,1)S(1)} %maximum_select_fusion.1.here_ref) | copy-start | bytes 786436
  13.1 4.8 %collective-permute-start.3 = (f32[2,29,128]{2,1,0:T(8,128)S(1)}, f32[2,29,128]{2,1,0:T(8,128)S(1)}, u32[]{:S(2)}, u32[]{:S(2)}) collective-permute-start(f32[2,29,128]{2,1,0:T(8,128)S(1)} %merge.9.here_ref), channel_id=1, source_target_pairs={{0,2},{1,3},{2,0},{3,1},{4,6},{5,7},{6,4},{7,5},{8,10},{9,11},{10,... | collective-permute-start | bytes 89096 | tf_op jit(solution)/shard_map/ppermute | solution.py:78
  18.0 5.4 %collective-permute-start.4 = (f32[4,29,128]{2,1,0:T(8,128)S(1)}, f32[4,29,128]{2,1,0:T(8,128)S(1)}, u32[]{:S(2)}, u32[]{:S(2)}) collective-permute-start(f32[4,29,128]{2,1,0:T(8,128)S(1)} %merge.10.here_ref), channel_id=1, source_target_pairs={{0,4},{1,5},{2,6},{3,7},{4,0},{5,1},{6,2},{7,3},{8,12},{9,13},{10,... | collective-permute-start | bytes 178184 | tf_op jit(solution)/shard_map/ppermute | solution.py:78
  23.3 18.9 %copy-start.9 = (bf16[512,1024]{1,0:T(8,128)(2,1)S(1)}, bf16[512,1024]{1,0:T(8,128)(2,1)}, u32[]{:S(2)}) copy-start(bf16[512,1024]{1,0:T(8,128)(2,1)} %tok_ref.1) | copy-start | bytes 3145732
  23.4 5.0 %collective-permute-start.5 = (f32[8,29,128]{2,1,0:T(8,128)S(1)}, f32[8,29,128]{2,1,0:T(8,128)S(1)}, u32[]{:S(2)}, u32[]{:S(2)}) collective-permute-start(f32[8,29,128]{2,1,0:T(8,128)S(1)} %merge.11.here_ref), channel_id=1, source_target_pairs={{0,8},{1,9},{2,10},{3,11},{4,12},{5,13},{6,14},{7,15},{8,0},{9,1},... | collective-permute-start | bytes 356360 | tf_op jit(solution)/shard_map/ppermute | solution.py:78
  25.3 83.2 %copy-start.55 = (f32[2]{0:T(128)}, f32[2]{0:T(128)S(1)}, u32[]{:S(2)}) copy-start(f32[2]{0:T(128)S(1)} %pad_maximum_fusion.8.scal) | copy-start | bytes 28
  25.3 12.4 %collective-permute-start.7 = (bf16[1,64,2048]{2,1,0:T(8,128)(2,1)S(1)}, bf16[1,64,2048]{2,1,0:T(8,128)(2,1)S(1)}, u32[]{:S(2)}, u32[]{:S(2)}) collective-permute-start(bf16[1,64,2048]{2,1,0:T(8,128)(2,1)S(1)} %maximum_select_fusion.1.here_ref), channel_id=1, source_target_pairs={{0,4},{1,5},{2,6},{3,7},{4,0},{5,1},{6,2},{7,3},{8,12},{9,13},{10,... | collective-permute-start | bytes 786440 | tf_op jit(solution)/shard_map/ppermute | solution.py:78
  28.4 6.4 %collective-permute-start.6 = (f32[16,29,128]{2,1,0:T(8,128)S(1)}, f32[16,29,128]{2,1,0:T(8,128)S(1)}, u32[]{:S(2)}, u32[]{:S(2)}) collective-permute-start(f32[16,29,128]{2,1,0:T(8,128)S(1)} %merge.12.here_ref), channel_id=1, source_target_pairs={{0,16},{1,17},{2,18},{3,19},{4,20},{5,21},{6,22},{7,23},{8,24},{9,... | collective-permute-start | bytes 712712 | tf_op jit(solution)/shard_map/ppermute | solution.py:78
  30.3 43.3 %copy-start.52 = (f32[3]{0:T(128)}, f32[3]{0:T(128)S(1)}, u32[]{:S(2)}) copy-start(f32[3]{0:T(128)S(1)} %pad_maximum_fusion.9.scal) | copy-start | bytes 40
  39.4 20.2 %copy-start.23 = (bf16[2,64,2048]{2,1,0:T(8,128)(2,1)}, bf16[2,64,2048]{2,1,0:T(8,128)(2,1)S(1)}, u32[]{:S(2)}) copy-start(bf16[2,64,2048]{2,1,0:T(8,128)(2,1)S(1)} %merge.14.here_ref) | copy-start | bytes 1572868
  39.5 20.1 %collective-permute-start.8 = (bf16[2,64,2048]{2,1,0:T(8,128)(2,1)S(1)}, bf16[2,64,2048]{2,1,0:T(8,128)(2,1)}, u32[]{:S(2)}, u32[]{:S(2)}) collective-permute-start(bf16[2,64,2048]{2,1,0:T(8,128)(2,1)S(1)} %merge.14.here_ref), channel_id=1, source_target_pairs={{0,2},{1,3},{2,0},{3,1},{4,6},{5,7},{6,4},{7,5},{8,10},{9,11},{10,... | collective-permute-start | bytes 1572872 | tf_op jit(solution)/shard_map/ppermute | solution.py:78
  44.8 32.9 %copy-start.4 = (bf16[512,1024]{1,0:T(8,128)(2,1)S(1)}, bf16[512,1024]{1,0:T(8,128)(2,1)}, u32[]{:S(2)}) copy-start(bf16[512,1024]{1,0:T(8,128)(2,1)} %cot_ref) | copy-start | bytes 3145732
  60.8 33.5 %copy-start.67 = (s32[4]{0:T(128)S(1)}, s32[4]{0:T(128)}, u32[]{:S(2)}) copy-start(s32[4]{0:T(128)} %param.29) | copy-start | bytes 52
  60.9 31.3 %collective-permute-start.12 = (bf16[4,64,2048]{2,1,0:T(8,128)(2,1)S(1)}, bf16[4,64,2048]{2,1,0:T(8,128)(2,1)}, u32[]{:S(2)}, u32[]{:S(2)}) collective-permute-start(bf16[4,64,2048]{2,1,0:T(8,128)(2,1)S(1)} %merge.15), channel_id=1, source_target_pairs={{0,16},{1,9},{2,18},{3,11},{4,20},{5,13},{6,22},{7,15},{8,24},{9,1... | collective-permute-start | bytes 3145736 | tf_op jit(solution)/shard_map/ppermute | solution.py:78
  62.3 32.0 %collective-permute-start.13 = (bf16[4,64,2048]{2,1,0:T(8,128)(2,1)S(1)}, bf16[4,64,2048]{2,1,0:T(8,128)(2,1)}, u32[]{:S(2)}, u32[]{:S(2)}) collective-permute-start(bf16[4,64,2048]{2,1,0:T(8,128)(2,1)S(1)} %merge.15), channel_id=1, source_target_pairs={{0,8},{1,17},{2,10},{3,19},{4,12},{5,21},{6,14},{7,23},{8,0},{9,25... | collective-permute-start | bytes 3145736 | tf_op jit(solution)/shard_map/ppermute | solution.py:78
  62.3 2.4 collective-permute-start.9
  67.0 6.6 %collective-permute-start.10 = (f32[2,16,8,128]{3,2,1,0:T(8,128)S(1)}, f32[2,16,8,128]{3,2,1,0:T(8,128)S(1)}, u32[]{:S(2)}, u32[]{:S(2)}) collective-permute-start(f32[2,16,8,128]{3,2,1,0:T(8,128)S(1)} %scan_tail.1.total_ref), channel_id=1, source_target_pairs={{0,1},{1,0},{2,3},{3,2},{4,5},{5,4},{6,7},{7,6},{8,9},{9,8},{10,11... | collective-permute-start | bytes 393224 | tf_op jit(solution)/shard_map/ppermute | solution.py:78
  74.9 14.2 %collective-permute-start.11 = (f32[2,16,8,128]{3,2,1,0:T(8,128)S(1)}, f32[2,16,8,128]{3,2,1,0:T(8,128)}, u32[]{:S(2)}, u32[]{:S(2)}) collective-permute-start(f32[2,16,8,128]{3,2,1,0:T(8,128)S(1)} %get-tuple-element.321.total_ref), channel_id=1, source_target_pairs={{0,2},{1,3},{2,0},{3,1},{4,6},{5,7},{6,4},{7,5},{8,10},{9,11},{10,... | collective-permute-start | bytes 393224 | tf_op jit(solution)/shard_map/ppermute | solution.py:78
  94.3 17.9 %collective-permute-start.15 = (bf16[4,64,2048]{2,1,0:T(8,128)(2,1)}, bf16[4,64,2048]{2,1,0:T(8,128)(2,1)}, u32[]{:S(2)}, u32[]{:S(2)}) collective-permute-start(bf16[4,64,2048]{2,1,0:T(8,128)(2,1)} %collective-permute-done.12), channel_id=1, source_target_pairs={{0,8},{1,17},{2,10},{3,19},{4,12},{5,21},{6,14},{7,23},{8,0},{9,25... | collective-permute-start | bytes 3145736 | tf_op jit(solution)/shard_map/ppermute | solution.py:78
  98.1 9.2 %collective-permute-start.14 = (f32[2,16,8,128]{3,2,1,0:T(8,128)S(1)}, f32[2,16,8,128]{3,2,1,0:T(8,128)S(1)}, u32[]{:S(2)}, u32[]{:S(2)}) collective-permute-start(f32[2,16,8,128]{3,2,1,0:T(8,128)S(1)} %get-tuple-element.338.total_ref), channel_id=1, source_target_pairs={{0,4},{1,5},{2,6},{3,7},{4,0},{5,1},{6,2},{7,3},{8,12},{9,13},{10,... | collective-permute-start | bytes 393224 | tf_op jit(solution)/shard_map/ppermute | solution.py:78
  117.2 15.2 %collective-permute-start.16 = (bf16[1024,2048]{1,0:T(8,128)(2,1)}, bf16[1024,2048]{1,0:T(8,128)(2,1)}, u32[]{:S(2)}, u32[]{:S(2)}) collective-permute-start(bf16[1024,2048]{1,0:T(8,128)(2,1)} %place.1.w_ref.o_own.w_own), channel_id=1, source_target_pairs={{0,1},{1,0},{2,3},{3,2},{4,5},{5,4},{6,7},{7,6},{8,9},{9,8},{10,11... | collective-permute-start | bytes 12582920 | tf_op jit(solution)/shard_map/ppermute | solution.py:78
  117.2 15.2 %collective-permute-start.17 = (bf16[1,64,2048]{2,1,0:T(8,128)(2,1)S(1)}, bf16[1,64,2048]{2,1,0:T(8,128)(2,1)S(1)}, u32[]{:S(2)}, u32[]{:S(2)}) collective-permute-start(bf16[1,64,2048]{2,1,0:T(8,128)(2,1)S(1)} %copy-done.63), channel_id=1, source_target_pairs={{0,4},{1,5},{2,6},{3,7},{4,0},{5,1},{6,2},{7,3},{8,12},{9,13},{10,... | collective-permute-start | bytes 786440 | tf_op jit(solution)/shard_map/ppermute | solution.py:78
  122.9 16.8 %copy-start = (bf16[640,1536]{1,0:T(8,128)(2,1)}, bf16[640,1536]{1,0:T(8,128)(2,1)S(1)}, u32[]{:S(2)}) copy-start(bf16[640,1536]{1,0:T(8,128)(2,1)S(1)} %project.2.own_ref) | copy-start | bytes 5898244
  132.4 16.5 %collective-permute-start.18 = (bf16[640,1024]{1,0:T(8,128)(2,1)S(1)}, bf16[640,1024]{1,0:T(8,128)(2,1)}, u32[]{:S(2)}, u32[]{:S(2)}) collective-permute-start(bf16[640,1024]{1,0:T(8,128)(2,1)S(1)} %context_states.1.x_ref.x_own), channel_id=1, source_target_pairs={{0,1},{1,0},{2,3},{3,2},{4,5},{5,4},{6,7},{7,6},{8,9},{9,8},{10,11... | collective-permute-start | bytes 3932168 | tf_op jit(solution)/shard_map/ppermute | solution.py:78
  135.0 14.0 %collective-permute-start.19 = (bf16[2,64,2048]{2,1,0:T(8,128)(2,1)}, bf16[2,64,2048]{2,1,0:T(8,128)(2,1)}, u32[]{:S(2)}, u32[]{:S(2)}) collective-permute-start(bf16[2,64,2048]{2,1,0:T(8,128)(2,1)} %merge.16.here_ref), channel_id=1, source_target_pairs={{0,2},{1,3},{2,0},{3,1},{4,6},{5,7},{6,4},{7,5},{8,10},{9,11},{10,... | collective-permute-start | bytes 1572872 | tf_op jit(solution)/shard_map/ppermute | solution.py:78
  150.2 15.0 %collective-permute-start.20 = (bf16[4,64,2048]{2,1,0:T(8,128)(2,1)S(1)}, bf16[4,64,2048]{2,1,0:T(8,128)(2,1)}, u32[]{:S(2)}, u32[]{:S(2)}) collective-permute-start(bf16[4,64,2048]{2,1,0:T(8,128)(2,1)S(1)} %merge.17), channel_id=1, source_target_pairs={{0,16},{1,9},{2,18},{3,11},{4,20},{5,13},{6,22},{7,15},{8,24},{9,1... | collective-permute-start | bytes 3145736 | tf_op jit(solution)/shard_map/ppermute | solution.py:78
  151.2 14.0 %collective-permute-start.23 = (bf16[512,1024]{1,0:T(8,128)(2,1)S(1)}, bf16[512,1024]{1,0:T(8,128)(2,1)}, u32[]{:S(2)}, u32[]{:S(2)}) collective-permute-start(bf16[512,1024]{1,0:T(8,128)(2,1)S(1)} %copy-done.5), channel_id=1, source_target_pairs={{0,1},{1,0},{2,3},{3,2},{4,5},{5,4},{6,7},{7,6},{8,9},{9,8},{10,11... | collective-permute-start | bytes 3145736 | tf_op jit(solution)/shard_map/ppermute | solution.py:78
  151.2 14.7 %collective-permute-start.25 = (bf16[1024,512]{1,0:T(8,128)(2,1)S(1)}, bf16[1024,512]{1,0:T(8,128)(2,1)}, u32[]{:S(2)}, u32[]{:S(2)}) collective-permute-start(bf16[1024,512]{1,0:T(8,128)(2,1)S(1)} %bitcast.126), channel_id=1, source_target_pairs={{0,1},{1,0},{2,3},{3,2},{4,5},{5,4},{6,7},{7,6},{8,9},{9,8},{10,11... | collective-permute-start | bytes 3145736 | tf_op jit(solution)/shard_map/ppermute | solution.py:78
  157.8 9.5 %collective-permute-start.22 = (bf16[512,1024]{1,0:T(8,128)(2,1)}, bf16[512,1024]{1,0:T(8,128)(2,1)}, u32[]{:S(2)}, u32[]{:S(2)}) collective-permute-start(bf16[512,1024]{1,0:T(8,128)(2,1)} %get-tuple-element.422.s_own), channel_id=1, source_target_pairs={{0,1},{1,0},{2,3},{3,2},{4,5},{5,4},{6,7},{7,6},{8,9},{9,8},{10,11... | collective-permute-start | bytes 3145736 | tf_op jit(solution)/shard_map/ppermute | solution.py:78
  157.9 9.5 %collective-permute-start.24 = (bf16[1024,512]{1,0:T(8,128)(2,1)}, bf16[1024,512]{1,0:T(8,128)(2,1)}, u32[]{:S(2)}, u32[]{:S(2)}) collective-permute-start(bf16[1024,512]{1,0:T(8,128)(2,1)} %get-tuple-element.423.st_own), channel_id=1, source_target_pairs={{0,1},{1,0},{2,3},{3,2},{4,5},{5,4},{6,7},{7,6},{8,9},{9,8},{10,11... | collective-permute-start | bytes 3145736 | tf_op jit(solution)/shard_map/ppermute | solution.py:78
  165.2 24.5 %collective-permute-start.21 = (bf16[512,1024]{1,0:T(8,128)(2,1)}, bf16[512,1024]{1,0:T(8,128)(2,1)}, u32[]{:S(2)}, u32[]{:S(2)}) collective-permute-start(bf16[512,1024]{1,0:T(8,128)(2,1)} %copy-done.6), channel_id=1, source_target_pairs={{0,1},{1,0},{2,3},{3,2},{4,5},{5,4},{6,7},{7,6},{8,9},{9,8},{10,11... | collective-permute-start | bytes 3145736 | tf_op jit(solution)/shard_map/ppermute | solution.py:78
  165.2 24.5 %collective-permute-start.26 = (bf16[4,64,2048]{2,1,0:T(8,128)(2,1)}, bf16[4,64,2048]{2,1,0:T(8,128)(2,1)}, u32[]{:S(2)}, u32[]{:S(2)}) collective-permute-start(bf16[4,64,2048]{2,1,0:T(8,128)(2,1)} %copy-done.15), channel_id=1, source_target_pairs={{0,8},{1,17},{2,10},{3,19},{4,12},{5,21},{6,14},{7,23},{8,0},{9,25... | collective-permute-start | bytes 3145736 | tf_op jit(solution)/shard_map/ppermute | solution.py:78
  165.9 25.8 %collective-permute-start.27 = (bf16[4,64,2048]{2,1,0:T(8,128)(2,1)}, bf16[4,64,2048]{2,1,0:T(8,128)(2,1)}, u32[]{:S(2)}, u32[]{:S(2)}) collective-permute-start(bf16[4,64,2048]{2,1,0:T(8,128)(2,1)} %collective-permute-done.20), channel_id=1, source_target_pairs={{0,8},{1,17},{2,10},{3,19},{4,12},{5,21},{6,14},{7,23},{8,0},{9,25... | collective-permute-start | bytes 3145736 | tf_op jit(solution)/shard_map/ppermute | solution.py:78
  191.6 26.1 %collective-permute-start.28 = (bf16[1,4,2,256,256]{4,3,2,1,0:T(8,128)(2,1)S(1)}, bf16[1,4,2,256,256]{4,3,2,1,0:T(8,128)(2,1)S(1)}, u32[]{:S(2)}, u32[]{:S(2)}) collective-permute-start(bf16[1,4,2,256,256]{4,3,2,1,0:T(8,128)(2,1)S(1)} %get-tuple-element.445), channel_id=1, source_target_pairs={{0,8},{1,17},{2,10},{3,19},{4,12},{5,21},{6,14},{7,23},{8,0},{9,25... | collective-permute-start | bytes 3145736 | tf_op jit(solution)/shard_map/ppermute | solution.py:78
  192.2 25.5 %collective-permute-start.29 = (bf16[1,4,2,256,256]{4,3,2,1,0:T(8,128)(2,1)S(1)}, bf16[1,4,2,256,256]{4,3,2,1,0:T(8,128)(2,1)S(1)}, u32[]{:S(2)}, u32[]{:S(2)}) collective-permute-start(bf16[1,4,2,256,256]{4,3,2,1,0:T(8,128)(2,1)S(1)} %get-tuple-element.446), channel_id=1, source_target_pairs={{0,8},{1,17},{2,10},{3,19},{4,12},{5,21},{6,14},{7,23},{8,0},{9,25... | collective-permute-start | bytes 3145736 | tf_op jit(solution)/shard_map/ppermute | solution.py:78
  217.6 3.4 collective-permute-start.30
  219.0 26.6 %collective-permute-start.32 = (bf16[1,4,2,256,256]{4,3,2,1,0:T(8,128)(2,1)}, bf16[1,4,2,256,256]{4,3,2,1,0:T(8,128)(2,1)}, u32[]{:S(2)}, u32[]{:S(2)}) collective-permute-start(bf16[1,4,2,256,256]{4,3,2,1,0:T(8,128)(2,1)} %add_split.15), channel_id=1, source_target_pairs={{0,16},{1,9},{2,18},{3,11},{4,20},{5,13},{6,22},{7,15},{8,24},{9,1... | collective-permute-start | bytes 3145736 | tf_op jit(solution)/shard_map/ppermute | solution.py:78
  219.9 25.7 %collective-permute-start.33 = (bf16[1,4,2,256,256]{4,3,2,1,0:T(8,128)(2,1)}, bf16[1,4,2,256,256]{4,3,2,1,0:T(8,128)(2,1)}, u32[]{:S(2)}, u32[]{:S(2)}) collective-permute-start(bf16[1,4,2,256,256]{4,3,2,1,0:T(8,128)(2,1)} %get-tuple-element.481), channel_id=1, source_target_pairs={{0,8},{1,17},{2,10},{3,19},{4,12},{5,21},{6,14},{7,23},{8,0},{9,25... | collective-permute-start | bytes 3145736 | tf_op jit(solution)/shard_map/ppermute | solution.py:78
  240.5 25.3 %collective-permute-start.36 = (bf16[640,1536]{1,0:T(8,128)(2,1)}, bf16[640,1536]{1,0:T(8,128)(2,1)}, u32[]{:S(2)}, u32[]{:S(2)}) collective-permute-start(bf16[640,1536]{1,0:T(8,128)(2,1)} %get-tuple-element.485.g_other), channel_id=1, source_target_pairs={{0,1},{1,0},{2,3},{3,2},{4,5},{5,4},{6,7},{7,6},{8,9},{9,8},{10,11... | collective-permute-start | bytes 5898248 | tf_op jit(solution)/shard_map/ppermute | solution.py:78
  240.5 5.0 %collective-permute-start.31 = (bf16[512,512]{1,0:T(8,128)(2,1)}, bf16[512,512]{1,0:T(8,128)(2,1)}, u32[]{:S(2)}, u32[]{:S(2)}) collective-permute-start(bf16[512,512]{1,0:T(8,128)(2,1)} %get-tuple-element.464), channel_id=1, source_target_pairs={{0,1},{1,0},{2,3},{3,2},{4,5},{5,4},{6,7},{7,6},{8,9},{9,8},{10,11... | collective-permute-start | bytes 1572872 | tf_op jit(solution)/shard_map/ppermute | solution.py:78
  245.6 20.2 %collective-permute-start.38 = (bf16[1,4,2,256,256]{4,3,2,1,0:T(8,128)(2,1)}, bf16[1,4,2,256,256]{4,3,2,1,0:T(8,128)(2,1)S(1)}, u32[]{:S(2)}, u32[]{:S(2)}) collective-permute-start(bf16[1,4,2,256,256]{4,3,2,1,0:T(8,128)(2,1)} %copy-done.59), channel_id=1, source_target_pairs={{0,8},{1,17},{2,10},{3,19},{4,12},{5,21},{6,14},{7,23},{8,0},{9,25... | collective-permute-start | bytes 3145736 | tf_op jit(solution)/shard_map/ppermute | solution.py:78
  253.6 6.4 %collective-permute-start.34 = (f32[16,8,128]{2,1,0:T(8,128)S(1)}, f32[16,8,128]{2,1,0:T(8,128)S(1)}, u32[]{:S(2)}, u32[]{:S(2)}) collective-permute-start(f32[16,8,128]{2,1,0:T(8,128)S(1)} %slice_bitcast_fusion.10.total_ref), channel_id=1, source_target_pairs={{0,1},{1,0},{2,3},{3,2},{4,5},{5,4},{6,7},{7,6},{8,9},{9,8},{10,11... | collective-permute-start | bytes 196616 | tf_op jit(solution)/shard_map/ppermute | solution.py:78
  259.3 6.4 %collective-permute-start.37 = (bf16[4,4,64,128]{3,2,1,0:T(8,128)(2,1)S(1)}, bf16[4,4,64,128]{3,2,1,0:T(8,128)(2,1)S(1)}, u32[]{:S(2)}, u32[]{:S(2)}) collective-permute-start(bf16[4,4,64,128]{3,2,1,0:T(8,128)(2,1)S(1)} %fusion), channel_id=1, source_target_pairs={{0,1},{1,0},{2,3},{3,2},{4,5},{5,4},{6,7},{7,6},{8,9},{9,8},{10,11... | collective-permute-start | bytes 786440 | tf_op jit(solution)/shard_map/ppermute | solution.py:78
  260.7 4.4 %collective-permute-start.35 = (f32[16,8,128]{2,1,0:T(8,128)S(1)}, f32[16,8,128]{2,1,0:T(8,128)S(1)}, u32[]{:S(2)}, u32[]{:S(2)}) collective-permute-start(f32[16,8,128]{2,1,0:T(8,128)S(1)} %get-tuple-element.488.total_ref), channel_id=1, source_target_pairs={{0,2},{1,3},{2,0},{3,1},{4,6},{5,7},{6,4},{7,5},{8,10},{9,11},{10,... | collective-permute-start | bytes 196616 | tf_op jit(solution)/shard_map/ppermute | solution.py:78
  265.8 14.8 %copy-start.57 = (f32[3]{0:T(128)S(1)}, f32[3]{0:T(128)}, u32[]{:S(2)}) copy-start(f32[3]{0:T(128)} %get-tuple-element.511.scal) | copy-start | bytes 40
  265.8 17.8 %copy-start.29 = (bf16[1,4,2,256,256]{4,3,2,1,0:T(8,128)(2,1)S(1)}, bf16[1,4,2,256,256]{4,3,2,1,0:T(8,128)(2,1)}, u32[]{:S(2)}) copy-start(bf16[1,4,2,256,256]{4,3,2,1,0:T(8,128)(2,1)} %copy-done.28) | copy-start | bytes 3145732
  265.8 16.3 %collective-permute-start.41 = (bf16[1,4,2,256,256]{4,3,2,1,0:T(8,128)(2,1)S(1)}, bf16[1,4,2,256,256]{4,3,2,1,0:T(8,128)(2,1)S(1)}, u32[]{:S(2)}, u32[]{:S(2)}) collective-permute-start(bf16[1,4,2,256,256]{4,3,2,1,0:T(8,128)(2,1)S(1)} %add_split.19), channel_id=1, source_target_pairs={{0,16},{1,9},{2,18},{3,11},{4,20},{5,13},{6,22},{7,15},{8,24},{9,1... | collective-permute-start | bytes 3145736 | tf_op jit(solution)/shard_map/ppermute | solution.py:78
  267.0 15.1 %collective-permute-start.40 = (bf16[1,2,2,256,256]{4,3,2,1,0:T(8,128)(2,1)S(1)}, bf16[1,2,2,256,256]{4,3,2,1,0:T(8,128)(2,1)S(1)}, u32[]{:S(2)}, u32[]{:S(2)}) collective-permute-start(bf16[1,2,2,256,256]{4,3,2,1,0:T(8,128)(2,1)S(1)} %get-tuple-element.530), channel_id=1, source_target_pairs={{0,2},{1,3},{2,0},{3,1},{4,6},{5,7},{6,4},{7,5},{8,10},{9,11},{10,... | collective-permute-start | bytes 1572872 | tf_op jit(solution)/shard_map/ppermute | solution.py:78
  268.1 12.5 %collective-permute-start.39 = (f32[16,8,128]{2,1,0:T(8,128)S(1)}, f32[16,8,128]{2,1,0:T(8,128)S(1)}, u32[]{:S(2)}, u32[]{:S(2)}) collective-permute-start(f32[16,8,128]{2,1,0:T(8,128)S(1)} %get-tuple-element.512.total_ref), channel_id=1, source_target_pairs={{0,4},{1,5},{2,6},{3,7},{4,0},{5,1},{6,2},{7,3},{8,12},{9,13},{10,... | collective-permute-start | bytes 196616 | tf_op jit(solution)/shard_map/ppermute | solution.py:78
  282.1 27.8 %collective-permute-start.43 = (bf16[2,4,64,2176]{3,2,1,0:T(8,128)(2,1)}, bf16[2,4,64,2176]{3,2,1,0:T(8,128)(2,1)}, u32[]{:S(2)}, u32[]{:S(2)}) collective-permute-start(bf16[2,4,64,2176]{3,2,1,0:T(8,128)(2,1)} %get-tuple-element.552), channel_id=1, source_target_pairs={{0,8},{1,17},{2,10},{3,19},{4,12},{5,21},{6,14},{7,23},{8,0},{9,25... | collective-permute-start | bytes 6684680 | tf_op jit(solution)/shard_map/ppermute | solution.py:78
  284.8 24.0 %collective-permute-start.45 = (bf16[1,2,2,256,256]{4,3,2,1,0:T(8,128)(2,1)}, bf16[1,2,2,256,256]{4,3,2,1,0:T(8,128)(2,1)}, u32[]{:S(2)}, u32[]{:S(2)}) collective-permute-start(bf16[1,2,2,256,256]{4,3,2,1,0:T(8,128)(2,1)} %get-tuple-element.551), channel_id=1, source_target_pairs={{0,2},{1,3},{2,0},{3,1},{4,6},{5,7},{6,4},{7,5},{8,10},{9,11},{10,... | collective-permute-start | bytes 1572872 | tf_op jit(solution)/shard_map/ppermute | solution.py:78
  290.2 14.0 %collective-permute-start.42 = (bf16[128,1024]{1,0:T(8,128)(2,1)S(1)}, bf16[128,1024]{1,0:T(8,128)(2,1)S(1)}, u32[]{:S(2)}, u32[]{:S(2)}) collective-permute-start(bf16[128,1024]{1,0:T(8,128)(2,1)S(1)} %sent_tail.1), channel_id=1, source_target_pairs={{1,0},{2,1},{3,2},{4,3},{5,4},{6,5},{7,6},{9,8},{10,9},{11,10},{12... | collective-permute-start | bytes 786440 | tf_op jit(solution)/shard_map/ppermute | solution.py:78
  293.0 15.8 %collective-permute-start.44 = (bf16[1,1,2,256,256]{4,3,2,1,0:T(8,128)(2,1)}, bf16[1,1,2,256,256]{4,3,2,1,0:T(8,128)(2,1)}, u32[]{:S(2)}, u32[]{:S(2)}) collective-permute-start(bf16[1,1,2,256,256]{4,3,2,1,0:T(8,128)(2,1)} %get-tuple-element.547), channel_id=1, source_target_pairs={{0,4},{1,5},{2,6},{3,7},{4,0},{5,1},{6,2},{7,3},{8,12},{9,13},{10,... | collective-permute-start | bytes 786440 | tf_op jit(solution)/shard_map/ppermute | solution.py:78
  312.8 23.3 %copy-start.14 = (f32[512,1024]{1,0:T(8,128)S(1)}, f32[512,1024]{1,0:T(8,128)}, u32[]{:S(2)}) copy-start(f32[512,1024]{1,0:T(8,128)} %copy-done.12) | copy-start | bytes 6291460
  312.8 21.2 %collective-permute-start.46 = (bf16[1,4,64,2176]{3,2,1,0:T(8,128)(2,1)}, bf16[1,4,64,2176]{3,2,1,0:T(8,128)(2,1)}, u32[]{:S(2)}, u32[]{:S(2)}) collective-permute-start(bf16[1,4,64,2176]{3,2,1,0:T(8,128)(2,1)} %get-tuple-element.560), channel_id=1, source_target_pairs={{0,16},{1,9},{2,18},{3,11},{4,20},{5,13},{6,22},{7,15},{8,24},{9,1... | collective-permute-start | bytes 3342344 | tf_op jit(solution)/shard_map/ppermute | solution.py:78
  314.0 22.1 %collective-permute-start.48 = (bf16[512,1024]{1,0:T(8,128)(2,1)}, bf16[512,1024]{1,0:T(8,128)(2,1)}, u32[]{:S(2)}, u32[]{:S(2)}) collective-permute-start(bf16[512,1024]{1,0:T(8,128)(2,1)} %get-tuple-element.525), channel_id=1, source_target_pairs={{0,1},{1,0},{2,3},{3,2},{4,5},{5,4},{6,7},{7,6},{8,9},{9,8},{10,11... | collective-permute-start | bytes 3145736 | tf_op jit(solution)/shard_map/ppermute | solution.py:78
  316.5 17.4 %collective-permute-start.47 = (bf16[1,1,2,256,256]{4,3,2,1,0:T(8,128)(2,1)}, bf16[1,1,2,256,256]{4,3,2,1,0:T(8,128)(2,1)}, u32[]{:S(2)}, u32[]{:S(2)}) collective-permute-start(bf16[1,1,2,256,256]{4,3,2,1,0:T(8,128)(2,1)} %get-tuple-element.557), channel_id=1, source_target_pairs={{0,4},{1,5},{2,6},{3,7},{4,0},{5,1},{6,2},{7,3},{8,12},{9,13},{10,... | collective-permute-start | bytes 786440 | tf_op jit(solution)/shard_map/ppermute | solution.py:78
  335.5 14.5 %collective-permute-start.49 = (bf16[1,2,64,2176]{3,2,1,0:T(8,128)(2,1)S(1)}, bf16[1,2,64,2176]{3,2,1,0:T(8,128)(2,1)S(1)}, u32[]{:S(2)}, u32[]{:S(2)}) collective-permute-start(bf16[1,2,64,2176]{3,2,1,0:T(8,128)(2,1)S(1)} %get-tuple-element.570), channel_id=1, source_target_pairs={{0,2},{1,3},{2,0},{3,1},{4,6},{5,7},{6,4},{7,5},{8,10},{9,11},{10,... | collective-permute-start | bytes 1671176 | tf_op jit(solution)/shard_map/ppermute | solution.py:78
  350.1 14.5 %collective-permute-start.50 = (bf16[1,1,64,2176]{3,2,1,0:T(8,128)(2,1)S(1)}, bf16[1,1,64,2176]{3,2,1,0:T(8,128)(2,1)S(1)}, u32[]{:S(2)}, u32[]{:S(2)}) collective-permute-start(bf16[1,1,64,2176]{3,2,1,0:T(8,128)(2,1)S(1)} %get-tuple-element.577), channel_id=1, source_target_pairs={{0,4},{1,5},{2,6},{3,7},{4,0},{5,1},{6,2},{7,3},{8,12},{9,13},{10,... | collective-permute-start | bytes 835592 | tf_op jit(solution)/shard_map/ppermute | solution.py:78
  365.3 1.6 collective-permute-start.51
  (57 other events, 336.2 us)
Sparse Core Ops, SparseCore 0:
  23.5 92.2 all-gather.1
